TPU v7x, 32 devices: a whole 2x2x4 slice. The times are simulated.
32 devices in a mesh: seq: 32 (over z, y, x, core), head: 1.
Axes of the slice: x: 2, y: 2, z: 4, core: 2. Of those that a mesh axis runs over, the one named last changes fastest.
Arguments:
- queries: bfloat16 [8192, 4096], P('seq', 'head'), may hold values from -6 to 6
- keys: bfloat16 [8192, 4096], P('seq', 'head'), may hold values from -6 to 6
- values: bfloat16 [8192, 4096], P('seq', 'head'), may hold values from -6 to 6
- gate: bfloat16 [8192, 4096], P('seq', 'head'), may hold values from -6 to 6
- residual: bfloat16 [8192, 4096], P('seq', 'head'), may hold values from -40 to 40
- log_decay: float32 [8192, 32], P('seq', 'head'), may hold values from -1 to 0, as said below
- out_weight: bfloat16 [4096, 4096], P('seq', 'head'), may hold values from -0.09375 to 0.09375
- norm_gain: bfloat16 [4096], P('head'), may hold values from 0.099609375 to 1.8984375
- kv_weight: bfloat16 [4096, 2048], P('seq', 'head'), may hold values from -0.09375 to 0.09375
Outputs:
- cache_keys: bfloat16 [8192, 1024], P('seq', 'head')
- cache_values: bfloat16 [8192, 1024], P('seq', 'head')
Inputs may be any that keep to these rules, and one draw needn't show every extreme that they name: `log_decay`: every entry is negative.
All inputs are finite; a program needn't handle non-finite values.
Results may differ from a plain program's by a relative error of at most 0.015.
Values may be sent and summed in bfloat16 or wider, within the bound.
No kernel may reach another device: no remote copies, remote signals or barrier semaphores. Data moves between devices by JAX's collectives and lax.ppermute only.
A program may use at most 192 MiB of HBM per device.

v0:
```python
import jax
import jax.numpy as jnp
from jax import lax
from jax.sharding import PartitionSpec as P

HIGHEST = lax.Precision.HIGHEST


def entering(part, axis, combine, identity):
    place = lax.axis_index(axis)
    gathered = jax.tree.map(lambda a: lax.all_gather(a, axis), part)
    state = jax.tree.map(lambda a, e: jnp.zeros_like(a) + jnp.asarray(e, a.dtype), part, identity)

    def one(step, state):
        return combine(
            state, jax.tree.map(lambda a: lax.dynamic_index_in_dim(a, step, 0, False), gathered)
        )

    return lax.fori_loop(0, place, one, state)


def local_retention(queries, keys, values, log_decay, block):
    tokens, heads, width = queries.shape
    count = tokens // block

    def to_blocks(array):
        return array.reshape((count, block) + array.shape[1:])

    lower = jnp.arange(block)[:, None] >= jnp.arange(block)[None, :]

    def advance(carry, inputs):
        state, offset = carry
        query_block, key_block, value_block, decay_block = inputs
        within = jnp.cumsum(decay_block, axis=0)
        spread = within[:, None, :] - within[None, :, :]
        factor = jnp.where(
            lower[:, :, None], jnp.exp(jnp.where(lower[:, :, None], spread, 0.0)), 0.0
        )
        scores = jnp.einsum(
            "ihd,jhd->hij", query_block, key_block, preferred_element_type=jnp.float32
        )
        weighted = scores * jnp.transpose(factor, (2, 0, 1))
        values_wide = value_block.astype(jnp.float32)
        intra = jnp.einsum("hij,jhd->ihd", weighted, values_wide, precision=HIGHEST)
        query_wide = query_block.astype(jnp.float32)
        carried = jnp.exp(within)[:, :, None] * jnp.einsum(
            "ihd,hde->ihe", query_wide, state, precision=HIGHEST
        )
        ending = within[-1]
        key_wide = key_block.astype(jnp.float32) * jnp.exp(ending[None, :] - within)[:, :, None]
        fresh = jnp.exp(ending)[:, None, None] * state + jnp.einsum(
            "jhd,jhe->hde", key_wide, values_wide, precision=HIGHEST
        )
        return ((fresh, offset + ending), (intra + carried, offset[None, :] + within))

    start = (jnp.zeros((heads, width, width), jnp.float32), jnp.zeros((heads,), jnp.float32))
    final, stacked = lax.scan(
        advance,
        start,
        (to_blocks(queries), to_blocks(keys), to_blocks(values), to_blocks(log_decay)),
    )
    return (
        stacked[0].reshape(tokens, heads, width),
        stacked[1].reshape(tokens, heads),
        final[0],
        final[1],
    )


def combine_states(earlier, later):
    return (earlier[0] * later[0], later[0][:, None, None] * earlier[1] + later[1])


def on_device(queries, keys, values, gate, residual, log_decay, out_weight, norm_gain, kv_weight):
    tokens = queries.shape[0]
    heads = log_decay.shape[1]
    width = queries.shape[1] // heads
    shaped = [array.reshape(tokens, heads, width) for array in (queries, keys, values)]
    partial_out, running, state, offset = local_retention(
        shaped[0], shaped[1], shaped[2], log_decay, min(512, tokens)
    )
    identity = (jnp.ones((heads,), jnp.float32), jnp.zeros((heads, width, width), jnp.float32))
    scan_decay, incoming = entering((jnp.exp(offset), state), "seq", combine_states, identity)
    retained = partial_out + jnp.exp(running)[:, :, None] * jnp.einsum(
        "thd,hde->the", shaped[0].astype(jnp.float32), incoming, precision=HIGHEST
    )
    scale = lax.rsqrt(jnp.mean(retained * retained, axis=2, keepdims=True) + 1e-06)
    mixed = (
        jax.nn.silu(gate.astype(jnp.float32)) * (retained * scale).reshape(tokens, heads * width)
    ).astype(jnp.bfloat16)
    all_heads = lax.all_gather(mixed, "head", axis=1, tiled=True)
    out_full, kv_full = (
        lax.all_gather(out_weight, "seq", axis=0, tiled=True),
        lax.all_gather(kv_weight, "seq", axis=0, tiled=True),
    )
    branch = jnp.dot(all_heads, out_full, preferred_element_type=jnp.float32)
    hidden = (residual.astype(jnp.float32) + branch).astype(jnp.bfloat16)
    wide = hidden.astype(jnp.float32)
    squares = lax.psum(jnp.sum(wide * wide, axis=1), "head")
    features = wide.shape[1] * lax.axis_size("head")
    inverse = lax.rsqrt(squares[:, None] / features + 1e-06)
    local_norm = (wide * inverse * norm_gain.astype(jnp.float32)[None, :]).astype(jnp.bfloat16)
    normalized = lax.all_gather(local_norm, "head", axis=1, tiled=True)
    projected = jnp.dot(normalized, kv_full, preferred_element_type=jnp.float32)
    cache_heads = kv_weight.shape[1] // (2 * width)
    arranged = projected.reshape(tokens, cache_heads, 2, width)
    cache_keys = arranged[:, :, 0, :].reshape(tokens, cache_heads * width).astype(jnp.bfloat16)
    cache_values = arranged[:, :, 1, :].reshape(tokens, cache_heads * width).astype(jnp.bfloat16)
    return (cache_keys, cache_values)


def solution(mesh):
    placed = (
        P("seq", "head"),
        P("seq", "head"),
        P("seq", "head"),
        P("seq", "head"),
        P("seq", "head"),
        P("seq", "head"),
        P("seq", "head"),
        P("head"),
        P("seq", "head"),
    )
    return jax.shard_map(
        on_device,
        mesh=mesh,
        in_specs=placed,
        out_specs=(P("seq", "head"), P("seq", "head")),
        check_vma=False,
    )
```

profile of v0, /device:TPU:24, one launch (start us, length us, event | category | flops | bytes accessed | tf_op | source)
XLA Modules:
  0.0 716.9 jit_solution(18183290038021456993)
XLA Ops:
  7.2 0.0 copy-start
  7.2 0.0 all-gather.10.cloned.1.call-start
  7.2 0.9 copy_bitcast_fusion.1
  8.1 0.6 reduce-window.6
  8.7 0.2 slice_reduce_fusion
  8.9 0.1 fusion.51
  9.0 0.2 slice_reduce_fusion.1
  9.2 0.1 bitcast_exponential_fusion
  9.3 4.1 copy.74
  13.4 5.9 fusion.39
  19.3 0.0 all-gather.10.cloned.1.call-update
  19.4 0.0 all-gather.6.cloned.1.call-start
  19.4 0.7 all-gather.6.cloned.1.call-update
  20.1 0.0 all-gather.8.cloned.1.call-start
  20.2 0.7 all-gather.8.cloned.1.call-update
  20.9 0.0 copy-done.4
  20.9 33.5 %all-gather.1 = f32[32,1,32]{2,1,0:T(1,128)S(1)} all-gather(f32[1,1,32]{2,1,0:T(1,128)S(1)} %bitcast.92), channel_id=1, replica_groups=mesh['seq'=32,'head'=1] {'seq'}, dimensions={0}, use_global_device_ids=true | all-gather | bytes 4224 | tf_op jit(solution)/shard_map/all_gather | solution.py:11
  54.4 0.0 copy-done
  54.4 0.0 copy-start.2
  54.4 3.8 fusion.29
  58.2 0.0 copy-done.2
  58.2 1.2 fusion.31
  59.4 0.3 copy-done.3
  59.8 9.0 %fusion = f32[32,256,128]{1,2,0:T(8,128)} fusion(f32[32,256,256]{2,1,0:T(8,128)S(1)} %fusion.31, f32[32,256]{1,0:T(8,128)S(1)} %get-tuple-element.100, pred[256,256]{1,0:T(8,128)(4,1)S(1)} %iota_compare_fusion, bf16[256,4096]{1,0:T(8,128)(2,1)S(1)} %copy-done.3), kind=kOutput, calls=%fused_computation.2 | convolution fusion | flops 3229614080 | bytes 14778368 | tf_op jit(solution)/shard_map/while/body/eval_jaxpr/hij,jhd->ihd/dot_general | solution.py:44
  68.8 306.0 %all-gather.10.cloned.1.call-done = f32[1024,128,128]{2,1,0:T(8,128)} async-done(((f32[32,128,128]{2,1,0:T(8,128)}), f32[1024,128,128]{2,1,0:T(8,128)}) %all-gather.10.cloned.1.call-update) | async-done | bytes 67108880 | tf_op jit(solution)/shard_map/all_gather | solution.py:11
  374.8 1.6 broadcast.54
  376.4 93.0 %while.3 = (s32[]{:T(128)}, f32[32,128,128]{2,1,0:T(8,128)}, s32[]{:T(128)}, f32[32,32]{1,0:T(8,128)S(1)}, f32[32,32,128,128]{3,2,1,0:T(8,128)}, /*index=5*/s32[]{:T(128)}, s32[]{:T(128)}, s32[]{:T(128)}) while((s32[]{:T(128)}, f32[32,128,128]{2,1,0:T(8,128)}, s32[]{:T(128)}, f32[32,32]{1,0:T(8,128)S(1)}, f32[32,32,128,128]{3,2,1,0:T(8,128)}, ...), condition=%wide.region_3.4_spmd, body=%wide.region_2.3_spmd.sunk | while | flops 1048581 | bytes 6291967 | solution.py:19
  376.4 3.8 bitcast_add_fusion.2
  380.3 3.8 bitcast_add_fusion.2
  384.1 4.0 bitcast_add_fusion.2
  388.1 4.0 bitcast_add_fusion.2
  392.2 3.9 bitcast_add_fusion.2
  396.0 3.9 bitcast_add_fusion.2
  399.9 3.8 bitcast_add_fusion.2
  403.7 3.8 bitcast_add_fusion.2
  407.6 3.8 bitcast_add_fusion.2
  411.4 3.8 bitcast_add_fusion.2
  415.3 3.8 bitcast_add_fusion.2
  419.1 4.1 bitcast_add_fusion.2
  423.2 3.8 bitcast_add_fusion.2
  427.1 3.8 bitcast_add_fusion.2
  430.9 3.8 bitcast_add_fusion.2
  434.8 3.8 bitcast_add_fusion.2
  438.6 3.8 bitcast_add_fusion.2
  442.4 3.8 bitcast_add_fusion.2
  446.3 3.8 bitcast_add_fusion.2
  450.1 3.9 bitcast_add_fusion.2
  454.1 3.8 bitcast_add_fusion.2
  457.9 3.8 bitcast_add_fusion.2
  461.7 3.8 bitcast_add_fusion.2
  465.6 3.8 bitcast_add_fusion.2
  469.4 6.9 multiply_reduce_fusion
  476.3 2.3 broadcast_multiply_fusion
  478.6 5.6 copy.65
  484.3 86.4 %all-gather.6.cloned.1.call-done = bf16[4096,4096]{1,0:T(8,128)(2,1)} async-done(((bf16[128,4096]{1,0:T(8,128)(2,1)}), bf16[4096,4096]{1,0:T(8,128)(2,1)}) %all-gather.6.cloned.1.call-update) | async-done | bytes 33554448 | tf_op jit(solution)/shard_map/all_gather | solution.py:93
  570.7 19.0 %fusion.11 = (f32[256]{0:T(256)S(1)}, bf16[256,4096]{1,0:T(8,128)(2,1)}) fusion(bf16[4096,4096]{1,0:T(8,128)(2,1)} %all-gather.6.cloned.1.call-done, f32[256,4096]{1,0:T(8,128)} %copy.65, bf16[256,4096]{1,0:T(8,128)(2,1)} %param.14, bf16[256,4096]{1,0:T(8,128)(2,1)} %param.15), kind=kOutput, calls=%fused_computation.18 | convolution fusion | flops 8603566080 | bytes 44041216 | tf_op jit(solution)/shard_map/dot_general | solution.py:96
  589.7 96.9 %all-gather.8.cloned.1.call-done = bf16[4096,2048]{1,0:T(8,128)(2,1)} async-done(((bf16[128,2048]{1,0:T(8,128)(2,1)}), bf16[4096,2048]{1,0:T(8,128)(2,1)}) %all-gather.8.cloned.1.call-update) | async-done | bytes 16777232 | tf_op jit(solution)/shard_map/all_gather | solution.py:94
  686.6 10.9 %convolution_convert_fusion = bf16[256,2048]{1,0:T(8,128)(2,1)S(1)} fusion(bf16[4096,2048]{1,0:T(8,128)(2,1)} %all-gather.8.cloned.1.call-done, bf16[256,4096]{1,0:T(8,128)(2,1)} %get-tuple-element.104, f32[4096]{0:T(1024)S(1)} %convert_element_type.44, f32[256]{0:T(256)S(1)} %add_rsqrt_fusion.1), kind=kOutput, calls=%fused_computation.34 | convolution fusion | flops 4299685888 | bytes 19940352 | tf_op jit(solution)/shard_map/dot_general | solution.py:104
  697.6 0.8 reshape.80
  698.4 2.3 fusion.52
  700.7 3.6 copy.72
  704.3 2.0 copy.68
  706.3 2.0 copy.73
  708.3 2.0 copy.69
  (35 shorter events, 0.2 us)
Async XLA Ops:
  7.2 47.2 %copy-start = (bf16[256,4096]{1,0:T(8,128)(2,1)S(1)}, bf16[256,4096]{1,0:T(8,128)(2,1)}, u32[]{:S(2)}) copy-start(bf16[256,4096]{1,0:T(8,128)(2,1)} %param.11) | copy-start | bytes 6291460
  7.2 367.6 %all-gather.10.cloned.1.call-start = ((), (), s32[]{:S(2)}) async-start(), calls=%async_computation.2 | async-start | bytes 69206016 | tf_op jit(solution)/shard_map/all_gather | solution.py:11
  19.3 1.5 copy-start.4
  19.4 551.3 %all-gather.6.cloned.1.call-start = ((), (), s32[]{:S(2)}) async-start(), calls=%async_computation | async-start | bytes 34603008 | tf_op jit(solution)/shard_map/all_gather | solution.py:93
  20.1 666.5 %all-gather.8.cloned.1.call-start = ((), (), s32[]{:S(2)}) async-start(), calls=%async_computation.1 | async-start | bytes 17301504 | tf_op jit(solution)/shard_map/all_gather | solution.py:94
  54.4 3.8 copy-start.2
  58.2 1.6 copy-start.3
  700.7 9.7 %copy-start.1 = (bf16[256,4096]{1,0:T(8,128)(2,1)S(1)}, bf16[256,4096]{1,0:T(8,128)(2,1)}, u32[]{:S(2)}) copy-start(bf16[256,4096]{1,0:T(8,128)(2,1)} %param.11) | copy-start | bytes 6291460
Sparse Core Ops, SparseCore 0:
  19.5 355.2 all-gather.9
  377.7 192.9 all-gather.5
  573.5 113.0 all-gather.7
where the time goes:
time: 721 us; the launch traced here: 717 us
  waiting for transfers between devices  491 us (68%)
  other arithmetic  96 us (13%)
  matrix products  56.8 us (8%)
  blocking collectives  33.5 us (5%)
  local copies, waits for them, and re-layouts  25.8 us (4%)
  between operations  13.9 us (2%)
    all_gather x1, waiting for transfers between devices, entering(): gathered = jax.tree.map(lambda a: lax.all_gather(a, axis), part)  306 us
    all_gather x1, waiting for transfers between devices, on_device(): lax.all_gather(kv_weight, 'seq', axis=0, tiled=True)  96.9 us
    add x24, other arithmetic, combine_states(): later[0][:, None, None] * earlier[1] + later[1]  92.9 us
    all_gather x1, waiting for transfers between devices, on_device(): lax.all_gather(out_weight, 'seq', axis=0, tiled=True)  86.4 us
    all_gather x1, blocking collectives, entering(): gathered = jax.tree.map(lambda a: lax.all_gather(a, axis), part)  33.5 us
    dot_general x1, matrix products, on_device(): branch = jnp.dot(all_heads, out_full, preferred_element_type=jnp.float32)  19 us
  transfers between devices with their start and end apart: 3, of which 3 were waited for; matrix products, arithmetic and copies ran while one was open for 20% of the time, Pallas kernels for 0%

commit v1 on v0

--- a/solution.py
+++ b/solution.py
@@ -1,9 +1,298 @@
+import functools
+import math
+
 import jax
 import jax.numpy as jnp
 from jax import lax
+from jax.experimental import pallas as pl
+from jax.experimental.pallas import tpu as pltpu
+from jax.sharding import Mesh
 from jax.sharding import PartitionSpec as P
 
+F32, BF16 = jnp.float32, jnp.bfloat16
 HIGHEST = lax.Precision.HIGHEST
+NORM_EPS = 1e-06
+DECAY_ROWS = 16
+FAR = ("z", "y")
+PLANE = ("y", "x", "c")
+SEQ = ("z", "y", "x", "c")
+VMEM_LIMIT = 48 * 1024 * 1024
+
+
+def params():
+    return pltpu.CompilerParams(vmem_limit_bytes=VMEM_LIMIT)
+
+
+def split_rows(total):
+    high = total.astype(BF16).astype(F32)
+    middle = (total - high).astype(BF16).astype(F32)
+    low = total - high - middle
+    row = lax.broadcasted_iota(jnp.int32, (DECAY_ROWS, total.shape[1]), 0)
+    rows = jnp.where(row == 0, high, jnp.where(row == 1, middle, jnp.where(row == 2, low, 0.0)))
+    return rows.astype(BF16)
+
+
+def join_rows(rows):
+    return jnp.sum(rows.astype(F32), axis=0, keepdims=True)
+
+
+def dot(a, b, contract):
+    return lax.dot_general(a, b, (contract, ((), ())), preferred_element_type=F32)
+
+
+def state_kernel(width, key_ref, value_ref, within_ref, state_ref):
+    tokens = key_ref.shape[0]
+    within = within_ref[0]
+    ending = within[tokens - 1 : tokens, :]
+    fade = jnp.exp(ending - within)
+    for head in range(state_ref.shape[0]):
+        columns = slice(head * width, (head + 1) * width)
+        faded = (key_ref[:, columns].astype(F32) * fade[:, head : head + 1]).astype(BF16)
+        state = dot(faded, value_ref[:, columns], ((0,), (0,)))
+        state_ref[head, :width, :] = state.astype(BF16)
+        total = jnp.broadcast_to(ending[:, head : head + 1], (1, width))
+        state_ref[head, width:, :] = split_rows(total)
+
+
+def intra_kernel(width, query_ref, key_ref, value_ref, within_ref, across_ref, out_ref):
+    tokens = query_ref.shape[0]
+    within, across = within_ref[0], across_ref[0]
+    lower = lax.broadcasted_iota(jnp.int32, (tokens, tokens), 0) >= lax.broadcasted_iota(
+        jnp.int32, (tokens, tokens), 1
+    )
+    for head in range(within.shape[1]):
+        columns = slice(head * width, (head + 1) * width)
+        scores = dot(query_ref[:, columns], key_ref[:, columns], ((1,), (1,)))
+        spread = within[:, head : head + 1] - across[head : head + 1, :]
+        weighted = jnp.where(lower, scores * jnp.exp(jnp.where(lower, spread, 0.0)), 0.0)
+        out_ref[:, columns] = dot(weighted.astype(BF16), value_ref[:, columns], ((1,), (0,)))
+
+
+def mix_kernel(width, query_ref, gate_ref, intra_ref, within_ref, state_ref, out_ref):
+    reach = jnp.exp(within_ref[0])
+    for head in range(state_ref.shape[0]):
+        columns = slice(head * width, (head + 1) * width)
+        carried = dot(query_ref[:, columns], state_ref[head], ((1,), (0,)))
+        retained = intra_ref[:, columns] + reach[:, head : head + 1] * carried
+        scale = lax.rsqrt(jnp.mean(retained * retained, axis=1, keepdims=True) + NORM_EPS)
+        gate = gate_ref[:, columns].astype(F32)
+        out_ref[:, columns] = (gate / (1.0 + jnp.exp(-gate)) * (retained * scale)).astype(BF16)
+
+
+def total_kernel(width, parts_ref, out_ref):
+    state = jnp.zeros((width, width), F32)
+    total = jnp.zeros((1, width), F32)
+    for place in range(parts_ref.shape[0]):
+        ending = join_rows(parts_ref[place, 0, width:, :])
+        state = jnp.exp(ending) * state + parts_ref[place, 0, :width, :].astype(F32)
+        total = total + ending
+    out_ref[0, :width, :] = state.astype(BF16)
+    out_ref[0, width:, :] = split_rows(total)
+
+
+def prefix_kernel(width, planes, parts_ref, *refs):
+    plane_refs, out_ref = refs[:planes], refs[planes]
+    state = jnp.zeros((width, width), F32)
+    reach = jnp.zeros((1, width), F32)
+    for ref in plane_refs:
+        state = state + jnp.exp(reach) * ref[0, :width, :].astype(F32)
+        reach = reach + join_rows(ref[0, width:, :])
+    for place in range(parts_ref.shape[0]):
+        out_ref[place, 0] = state.astype(BF16)
+        ending = join_rows(parts_ref[place, 0, width:, :])
+        state = jnp.exp(ending) * state + parts_ref[place, 0, :width, :].astype(F32)
+
+
+def head_blocks(tokens, columns):
+    return pl.BlockSpec((tokens, columns), lambda i: (0, i))
+
+
+def group_blocks(shape):
+    return pl.BlockSpec((1,) + shape, lambda i: (i, 0, 0))
+
+
+def local_states(keys, values, within, width):
+    tokens, groups, per = keys.shape[0], within.shape[0], within.shape[2]
+    wide = head_blocks(tokens, per * width)
+    rows = width + DECAY_ROWS
+    return pl.pallas_call(
+        functools.partial(state_kernel, width),
+        grid=(groups,),
+        in_specs=[wide, wide, group_blocks((tokens, per))],
+        out_specs=pl.BlockSpec((per, rows, width), lambda i: (i, 0, 0)),
+        out_shape=jax.ShapeDtypeStruct((groups * per, rows, width), BF16),
+        compiler_params=params(),
+        name="local_states",
+    )(keys, values, within)
+
+
+def local_intra(queries, keys, values, within, across, width):
+    tokens, groups, per = keys.shape[0], within.shape[0], within.shape[2]
+    wide = head_blocks(tokens, per * width)
+    return pl.pallas_call(
+        functools.partial(intra_kernel, width),
+        grid=(groups,),
+        in_specs=[wide, wide, wide, group_blocks((tokens, per)), group_blocks((per, tokens))],
+        out_specs=wide,
+        out_shape=jax.ShapeDtypeStruct(queries.shape, F32),
+        compiler_params=params(),
+        name="local_intra",
+    )(queries, keys, values, within, across)
+
+
+def mix(queries, gate, intra, within, states, width):
+    tokens, groups, per = queries.shape[0], within.shape[0], within.shape[2]
+    wide = head_blocks(tokens, per * width)
+    return pl.pallas_call(
+        functools.partial(mix_kernel, width),
+        grid=(groups,),
+        in_specs=[
+            wide,
+            wide,
+            wide,
+            group_blocks((tokens, per)),
+            pl.BlockSpec((per, width, width), lambda i: (i, 0, 0)),
+        ],
+        out_specs=wide,
+        out_shape=jax.ShapeDtypeStruct(queries.shape, BF16),
+        compiler_params=params(),
+        name="mix",
+    )(queries, gate, intra, within, states)
+
+
+def plane_total(parts, width):
+    places, heads, rows, _ = parts.shape
+    return pl.pallas_call(
+        functools.partial(total_kernel, width),
+        grid=(heads,),
+        in_specs=[pl.BlockSpec((places, 1, rows, width), lambda i: (0, i, 0, 0))],
+        out_specs=pl.BlockSpec((1, rows, width), lambda i: (i, 0, 0)),
+        out_shape=jax.ShapeDtypeStruct((heads, rows, width), BF16),
+        compiler_params=params(),
+        name="plane_total",
+    )(parts)
+
+
+def plane_prefix(parts, planes, width):
+    places, heads, rows, _ = parts.shape
+    return pl.pallas_call(
+        functools.partial(prefix_kernel, width, len(planes)),
+        grid=(heads,),
+        in_specs=[pl.BlockSpec((places, 1, rows, width), lambda i: (0, i, 0, 0))]
+        + [pl.BlockSpec((1, rows, width), lambda i: (i, 0, 0))] * len(planes),
+        out_specs=pl.BlockSpec((places, 1, width, width), lambda i: (0, i, 0, 0)),
+        out_shape=jax.ShapeDtypeStruct((places, heads, width, width), BF16),
+        compiler_params=params(),
+        name="plane_prefix",
+    )(parts, *planes)
+
+
+def swap(array, devices, distance):
+    return lax.ppermute(array, SEQ, [(i, i ^ distance) for i in range(devices)])
+
+
+def pick(array, index, axis):
+    return lax.dynamic_index_in_dim(array, index, axis, keepdims=False)
+
+
+def shared_on_device(
+    sizes, queries, keys, values, gate, residual, log_decay, out_weight, norm_gain, kv_weight
+):
+    depth, near = sizes[0], sizes[2] * sizes[3]
+    devices = math.prod(sizes)
+    far, places = sizes[0] * sizes[1], sizes[1] * near
+    tokens, heads = log_decay.shape
+    width = queries.shape[1] // heads
+    model = out_weight.shape[1]
+    rows = out_weight.shape[0]
+    cache = kv_weight.shape[1] // 2
+    core, side = lax.axis_index("c"), lax.axis_index("x")
+    here = 2 * side + core
+
+    def columns_of(array, place):
+        shaped = array.reshape(array.shape[0], far, near, model // (far * near))
+        return pick(shaped, place, 2).reshape(array.shape[0], model // near)
+
+    with jax.named_scope("out_weight_gather"):
+        shard = jnp.zeros((near, rows, model // near), BF16)
+        for other in range(near):
+            piece = columns_of(out_weight, here ^ other)
+            if other:
+                piece = swap(piece, devices, other)
+            shard = lax.dynamic_update_index_in_dim(shard, piece, here ^ other, 0)
+        out_full = lax.all_gather(
+            shard.reshape(near * rows, model // near), FAR, axis=0, tiled=True
+        )
+    with jax.named_scope("kv_weight_gather"):
+        shaped = kv_weight.reshape(rows, cache // width, 2, width)
+        mine = pick(shaped, core, 2).reshape(rows, cache)
+        other = swap(pick(shaped, 1 - core, 2).reshape(rows, cache), devices, 1)
+        kv_full = lax.all_gather(jnp.stack([mine, other]), FAR, axis=0)
+        kv_mine = kv_full[:, 0].reshape(far * rows, cache)
+        kv_other = kv_full[:, 1].reshape(far * rows, cache)
+
+    with jax.named_scope("residual_exchange"):
+        residuals = [columns_of(residual, here)]
+        for other in range(1, near):
+            residuals.append(swap(columns_of(residual, here ^ other), devices, other))
+
+    per = heads // places
+    running = jnp.cumsum(log_decay, axis=0)
+    within = running.reshape(tokens, places, per).transpose(1, 0, 2)
+    across = running.T.reshape(places, per, tokens)
+    with jax.named_scope("state_scan"):
+        states = local_states(keys, values, within, width)
+        states = states.reshape((places, per) + states.shape[1:])
+        parts = lax.all_to_all(states, PLANE, 0, 0, tiled=True)
+        total = plane_total(parts, width)
+        step = devices // depth
+        planes = [
+            lax.ppermute(total, SEQ, [(i, i + d * step) for i in range(devices - d * step)])
+            for d in range(1, depth)
+        ]
+        entering = lax.all_to_all(plane_prefix(parts, planes, width), PLANE, 0, 0, tiled=True)
+        entering = entering.reshape(heads, width, width)
+    intra = local_intra(queries, keys, values, within, across, width)
+    mixed = mix(queries, gate, intra, within, entering, width)
+
+    with jax.named_scope("mixed_exchange"):
+        mixes = [mixed, swap(mixed, devices, 1), swap(mixed, devices, 2)]
+        mixes.append(swap(mixes[2], devices, 1))
+
+    with jax.named_scope("out_projection"):
+        gain = pick(norm_gain.reshape(far, near, model // (far * near)), here, 1)
+        gain = gain.reshape(1, model // near).astype(F32)
+        squares, scaled = [], []
+        for block, start in zip(mixes, residuals):
+            branch = jnp.dot(block, out_full, preferred_element_type=F32)
+            hidden = (start.astype(F32) + branch).astype(BF16).astype(F32)
+            squares.append(jnp.sum(hidden * hidden, axis=1))
+            scaled.append((hidden * gain).astype(BF16))
+        squares = jnp.stack(squares)
+        squares = squares + swap(squares, devices, 1)[jnp.array([1, 0, 3, 2])]
+        squares = squares[:2] + swap(squares[2:], devices, 2)
+        inverse = lax.rsqrt(squares / model + NORM_EPS)
+
+    with jax.named_scope("cache_projection"):
+
+        def partial(block, received):
+            return jnp.dot(block, kv_mine, preferred_element_type=F32) + jnp.dot(
+                received, kv_other, preferred_element_type=F32
+            )
+
+        received = swap(jnp.stack([scaled[3], scaled[2], scaled[1], scaled[0]]), devices, 1)
+        away = [
+            partial(scaled[2], received[0]).astype(BF16),
+            partial(scaled[3], received[1]).astype(BF16),
+        ]
+        back = swap(jnp.stack(away), devices, 2)
+        home = [partial(scaled[0], received[2]), partial(scaled[1], received[3])]
+        done = [
+            ((home[i] + back[i].astype(F32)) * inverse[i][:, None]).astype(BF16) for i in range(2)
+        ]
+        swapped = swap(done[1], devices, 1)
+        first = core == 0
+        return (jnp.where(first, done[0], swapped), jnp.where(first, swapped, done[0]))
 
 
 def entering(part, axis, combine, identity):
@@ -109,18 +398,24 @@
     return (cache_keys, cache_values)
 
 
+def sequence_sizes(devices):
+    return (devices // 8, 2, 2, 2)
+
+
 def solution(mesh):
-    placed = (
-        P("seq", "head"),
-        P("seq", "head"),
-        P("seq", "head"),
-        P("seq", "head"),
-        P("seq", "head"),
-        P("seq", "head"),
-        P("seq", "head"),
-        P("head"),
-        P("seq", "head"),
-    )
+    devices, split = mesh.shape["seq"], mesh.shape["head"]
+    if split == 1 and devices % 8 == 0:
+        sizes = sequence_sizes(devices)
+        fine = Mesh(mesh.devices.reshape(sizes + (1,)), SEQ + ("head",))
+        tokens, copied = P(SEQ, "head"), P("head")
+        return jax.shard_map(
+            functools.partial(shared_on_device, sizes),
+            mesh=fine,
+            in_specs=(tokens,) * 7 + (copied, tokens),
+            out_specs=(tokens, tokens),
+            check_vma=False,
+        )
+    placed = (P("seq", "head"),) * 7 + (P("head"), P("seq", "head"))
     return jax.shard_map(
         on_device,
         mesh=mesh,

time: 721 us -> 307 us (0.43)
  waiting for transfers between devices: 491 us -> 143 us
  other arithmetic: 96 us -> 7.3 us
  matrix products: 56.8 us -> 29.3 us
  Pallas kernels: 0 us -> 24.5 us
  starting transfers between devices: 0.12 us -> 17.8 us
  local copies, waits for them, and re-layouts: 25.8 us -> 40.4 us
  blocking collectives: 33.5 us -> 26 us
    all_gather x3 -> x2, waiting for transfers between devices: 489 us -> 52 us  [the longest x1 48.8 us: shared_on_device(): kv_full = lax.all_gather(jnp.stack([mine, other]), FAR, axis=0)]
    add x25 -> x1, other arithmetic: 92.9 us -> 0.01 us  [shared_on_device(): squares = squares + swap(squares, devices, 1)[jnp.array([1, 0, 3, 2])]]
    ppermute x0 -> x18, waiting for transfers between devices: none -> 88.8 us  [the longest x15 63 us: swap(): return lax.ppermute(array, SEQ, [(i, i ^ distance) for i in range(devices)])]
    all_gather x1 -> x0, blocking collectives: 33.5 us -> none  [entering(): gathered = jax.tree.map(lambda a: lax.all_gather(a, axis), part)]
    dot_general x7 -> x12, matrix products: 56.8 us -> 29.3 us  [the longest x4 18.9 us: shared_on_device(): branch = jnp.dot(block, out_full, preferred_element_type=F32)]
    all_to_all x0 -> x1, blocking collectives: none -> 26 us  [shared_on_device(): parts = lax.all_to_all(states, PLANE, 0, 0, tiled=True)]
    pallas_call x0 -> x5, Pallas kernels: none -> 24.5 us  [the longest x1 8.68 us: local_intra(): pl.pallas_call(functools.partial(intra_kernel, width), grid=(groups,), in...]
    dynamic_slice x0 -> x3, local copies, waits for them, and re-layouts: none -> 15.7 us  [pick(): return lax.dynamic_index_in_dim(array, index, axis, keepdims=False)]
  transfers between devices with their start and end apart: 3 -> 21, of which waited for: 3 -> 12; matrix products, arithmetic and copies ran while one was open for 20% -> 22% of each run, Pallas kernels for 0% -> 8%
where the time goes in v1:
time: 307 us; the launch traced here: 303 us
  waiting for transfers between devices  143 us (47%)
  local copies, waits for them, and re-layouts  40.4 us (13%)
  matrix products  29.3 us (10%)
  blocking collectives  26 us (8%)
  Pallas kernels  24.5 us (8%)
  starting transfers between devices  17.8 us (6%)
  between operations  14.6 us (5%)
  other arithmetic  7.3 us (2%)
    ppermute x15, waiting for transfers between devices, swap(): return lax.ppermute(array, SEQ, [(i, i ^ distance) for i in range(devices)])  63 us
    all_gather x1, waiting for transfers between devices, shared_on_device(): kv_full = lax.all_gather(jnp.stack([mine, other]), FAR, axis=0)  48.8 us
    all_to_all x1, blocking collectives, shared_on_device(): parts = lax.all_to_all(states, PLANE, 0, 0, tiled=True)  26 us
    ppermute x3, waiting for transfers between devices, shared_on_device(): lax.ppermute(total, SEQ, [(i, i + d * step) for i in range(devices - d *...  25.8 us
    dot_general x4, matrix products, shared_on_device(): branch = jnp.dot(block, out_full, preferred_element_type=F32)  18.9 us
    dynamic_slice x3, local copies, waits for them, and re-layouts, pick(): return lax.dynamic_index_in_dim(array, index, axis, keepdims=False)  15.7 us
    unnamed x35, local copies, waits for them, and re-layouts  9.91 us
    ppermute x15, starting transfers between devices, swap(): return lax.ppermute(array, SEQ, [(i, i ^ distance) for i in range(devices)])  9.61 us
  transfers between devices with their start and end apart: 21, of which 12 were waited for; matrix products, arithmetic and copies ran while one was open for 22% of the time, Pallas kernels for 8%

profile of v1, /device:TPU:24, one launch (start us, length us, event | category | flops | bytes accessed | tf_op | source)
XLA Modules:
  0.0 302.5 jit_solution(13418450561307757668)
XLA Ops:
  7.2 1.6 copy.62
  9.1 1.6 collective-permute-start.4
  11.4 6.8 %collective-permute-done.4 = bf16[128,1024]{0,1:T(8,128)(2,1)S(1)} collective-permute-done((bf16[128,1024]{0,1:T(8,128)(2,1)S(1)}, bf16[128,1024]{0,1:T(8,128)(2,1)S(1)}, u32[]{:S(2)}, u32[]{:S(2)}) %collective-permute-start.4) | collective-permute-done | bytes 262176 | tf_op jit(solution)/shard_map/out_weight_gather/ppermute | solution.py:191
  18.3 0.8 copy.65
  19.1 3.9 %collective-permute-done.5 = bf16[128,1024]{0,1:T(8,128)(2,1)S(1)} collective-permute-done((bf16[128,1024]{0,1:T(8,128)(2,1)S(1)}, bf16[128,1024]{0,1:T(8,128)(2,1)S(1)}, u32[]{:S(2)}, u32[]{:S(2)}) %collective-permute-start.5) | collective-permute-done | bytes 262176 | tf_op jit(solution)/shard_map/out_weight_gather/ppermute | solution.py:191
  23.0 0.8 copy.66
  23.8 1.1 constant_dynamic-update-slice_fusion.1
  25.0 1.0 constant_dynamic-update-slice_fusion
  26.0 1.0 copy-done.7
  27.0 0.6 reduce-window.6
  28.3 6.6 %local_states.1 = bf16[32,144,128]{2,1,0:T(8,128)(2,1)S(1)} custom-call(bf16[256,4096]{1,0:T(8,128)(2,1)S(1)} %copy-done.2, bf16[256,4096]{1,0:T(8,128)(2,1)} %value_ref.3, f32[8,256,4]{2,1,0:T(8,128)S(1)} %bitcast.109), custom_call_target="tpu_custom_call" | custom-call | tf_op jit(solution)/shard_map/state_scan/local_states/pallas_call | solution.py:118
  34.8 26.0 %all_to_all.10.parts_ref = bf16[8,4,144,128]{3,2,1,0:T(8,128)(2,1)S(1)} all-to-all(bf16[8,4,144,128]{3,2,1,0:T(8,128)(2,1)S(1)} %bitcast.112), channel_id=1, replica_groups=mesh['z'=4,'y'=2,'x'=2,'c'=2,'head'=1] {'y','x','c'}, dimensions={0} | all-to-all | bytes 2359296 | tf_op jit(solution)/shard_map/state_scan/all_to_all | solution.py:246
  61.3 1.3 collective-permute-start
  62.6 1.3 collective-permute-start.1
  63.9 1.3 collective-permute-start.2
  65.2 9.8 %collective-permute-done.refs_0_ = bf16[4,144,128]{2,1,0:T(8,128)(2,1)S(1)} collective-permute-done((bf16[4,144,128]{2,1,0:T(8,128)(2,1)S(1)}, bf16[4,144,128]{2,1,0:T(8,128)(2,1)S(1)}, u32[]{:S(2)}, u32[]{:S(2)}) %collective-permute-start) | collective-permute-done | bytes 147488 | tf_op jit(solution)/shard_map/state_scan/ppermute | solution.py:250
  75.1 16.0 %collective-permute-done.1.refs_1_ = bf16[4,144,128]{2,1,0:T(8,128)(2,1)S(1)} collective-permute-done((bf16[4,144,128]{2,1,0:T(8,128)(2,1)S(1)}, bf16[4,144,128]{2,1,0:T(8,128)(2,1)S(1)}, u32[]{:S(2)}, u32[]{:S(2)}) %collective-permute-start.1) | collective-permute-done | bytes 147488 | tf_op jit(solution)/shard_map/state_scan/ppermute | solution.py:250
  91.0 0.6 plane_prefix.1
  91.7 1.0 copy-done.4
  92.6 4.2 %all-to-all-start.1 = ((bf16[8,4,128,128]{3,2,1,0:T(8,128)(2,1)}), bf16[8,4,128,128]{3,2,1,0:T(8,128)(2,1)}, u32[]{:S(2)}, u32[]{:S(2)}) async-start(bf16[8,4,128,128]{3,2,1,0:T(8,128)(2,1)} %copy-done.4), calls=%async_computation.1 | async-start | bytes 2097152 | tf_op jit(solution)/shard_map/state_scan/all_to_all | solution.py:253
  96.9 2.2 copy.67
  99.1 1.1 constant_dynamic-slice_fusion.1
  100.6 1.2 collective-permute-done.6
  101.9 0.8 pad_maximum_fusion.2
  102.7 2.0 copy.68
  104.9 1.6 copy-done.3
  106.5 8.7 %local_intra.1.intra_ref = f32[256,4096]{1,0:T(8,128)} custom-call(bf16[256,4096]{1,0:T(8,128)(2,1)S(1)} %copy-done.3, bf16[256,4096]{1,0:T(8,128)(2,1)S(1)} %copy-done.2, bf16[256,4096]{1,0:T(8,128)(2,1)} %value_ref.3, f32[8,256,4]{2,1,0:T(8,128)S(1)} %bitcast.110, f32[8,4,256]{2,1,0:T(4,128)S(1)} %reduce_window_sum.21.across_ref), custom_call_target="tpu_custom_call" | custom-call | tf_op jit(solution)/shard_map/local_intra/pallas_call | solution.py:132
  115.2 1.8 all-to-all-done.1
  117.0 8.2 %mix.1 = bf16[256,4096]{1,0:T(8,128)(2,1)S(1)} custom-call(bf16[256,4096]{1,0:T(8,128)(2,1)} %query_ref.3, bf16[256,4096]{1,0:T(8,128)(2,1)} %gate_ref.1, f32[256,4096]{1,0:T(8,128)} %local_intra.1.intra_ref, f32[8,256,4]{2,1,0:T(8,128)S(1)} %bitcast.111, bf16[32,128,128]{2,1,0:T(8,128)(2,1)} %bitcast.4.state_ref), custom_call_target="tpu_custom_call" | custom-call | tf_op jit(solution)/shard_map/mix/pallas_call | solution.py:146
  125.2 1.3 collective-permute-start.8
  126.5 4.4 %reshape.104 = bf16[256,8,4,128]{3,2,1,0:T(4,128)(2,1)} reshape(bf16[256,4096]{1,0:T(8,128)(2,1)} %param.14) | data formatting | bytes 4194304 | tf_op jit(solution)/shard_map/residual_exchange/reshape | solution.py:213
  130.9 14.5 %dynamic-slice_reduce_fusion.1 = (bf16[256,8,128]{2,1,0:T(8,128)(2,1)S(1)}, bf16[256,8,128]{2,1,0:T(8,128)(2,1)S(1)}, bf16[256,8,128]{2,1,0:T(8,128)(2,1)S(1)}, bf16[256,8,1,128]{3,2,1,0:T(2,128)(2,1)S(1)}) fusion(bf16[256,8,4,128]{3,2,1,0:T(4,128)(2,1)} %reshape.104, s32[]{:T(128)S(6)} %select_n.50, s32[]{:T(128)S(6)} %select_n.51, s32[]{:T(128)S(6)} %select_n.49, ...), kind=kLoop, calls=%fused_computation.40 | loop fusion | bytes 4194320 | tf_op jit(solution)/shard_map/residual_exchange/jit(dynamic_index_in_dim)/dynamic_slice | solution.py:195
  145.4 0.9 copy.90
  146.3 0.8 collective-permute-start.10
  147.1 0.9 copy.91
  148.3 1.2 collective-permute-start.11
  149.5 24.4 %collective-permute-done.8 = bf16[256,4096]{1,0:T(8,128)(2,1)} collective-permute-done((bf16[256,4096]{1,0:T(8,128)(2,1)S(1)}, bf16[256,4096]{1,0:T(8,128)(2,1)}, u32[]{:S(2)}, u32[]{:S(2)}) %collective-permute-start.8) | collective-permute-done | bytes 2097184 | tf_op jit(solution)/shard_map/mixed_exchange/ppermute | solution.py:191
  173.9 1.1 copy_convert_fusion
  175.0 0.5 collective-permute-start.12
  175.5 3.2 %all-gather.4.cloned.1.call-done = bf16[4096,1024]{1,0:T(8,128)(2,1)} async-done(((bf16[512,1024]{1,0:T(8,128)(2,1)}), bf16[4096,1024]{1,0:T(8,128)(2,1)}) %all-gather.4.cloned.1.call-update) | async-done | bytes 8388624 | tf_op jit(solution)/shard_map/out_weight_gather/all_gather | solution.py:223
  178.7 6.1 %fusion.4 = bf16[256,1024]{1,0:T(8,128)(2,1)S(1)} fusion(bf16[256,4096]{1,0:T(8,128)(2,1)S(1)} %mix.1, bf16[4096,1024]{1,0:T(8,128)(2,1)} %all-gather.4.cloned.1.call-done, f32[32,8,8,128]{3,2,1,0:T(8,128)} %bitcast.129), kind=kOutput, calls=%fused_computation.20 | convolution fusion | flops 2148007936 | bytes 12058624 | tf_op jit(solution)/shard_map/out_projection/dot_general | solution.py:267
  185.1 4.2 %fusion.17 = (f32[256]{0:T(256)S(1)}, bf16[256,1024]{1,0:T(8,128)(2,1)S(1)}) fusion(bf16[256,1024]{1,0:T(8,128)(2,1)} %collective-permute-done.10, bf16[256,4096]{1,0:T(8,128)(2,1)} %collective-permute-done.8, bf16[4096,1024]{1,0:T(8,128)(2,1)S(1)} %copy-done.14), kind=kOutput, calls=%fused_computation.33 | convolution fusion | flops 2149056256 | bytes 11535360 | tf_op jit(solution)/shard_map/out_projection/dot_general | solution.py:267
  189.4 4.6 %collective-permute-done.7 = bf16[256,1024]{1,0:T(8,128)(2,1)} collective-permute-done((bf16[256,1024]{1,0:T(8,128)(2,1)}, bf16[256,1024]{1,0:T(8,128)(2,1)}, u32[]{:S(2)}, u32[]{:S(2)}) %collective-permute-start.7) | collective-permute-done | bytes 524320 | tf_op jit(solution)/shard_map/residual_exchange/ppermute | solution.py:191
  194.0 4.1 %fusion.5 = bf16[256,1024]{1,0:T(8,128)(2,1)S(1)} fusion(bf16[256,4096]{1,0:T(8,128)(2,1)} %collective-permute-done.9, bf16[4096,1024]{1,0:T(8,128)(2,1)S(1)} %copy-done.14, bf16[256,1024]{1,0:T(8,128)(2,1)} %collective-permute-done.7), kind=kOutput, calls=%fused_computation.21 | convolution fusion | flops 2148270080 | bytes 11534336 | tf_op jit(solution)/shard_map/out_projection/dot_general | solution.py:267
  198.1 4.4 %fusion.19 = (f32[256]{0:T(256)S(1)}, bf16[256,1024]{1,0:T(8,128)(2,1)S(1)}) fusion(bf16[256,1024]{1,0:T(8,128)(2,1)} %collective-permute-done.11, bf16[256,4096]{1,0:T(8,128)(2,1)} %collective-permute-done.12, bf16[4096,1024]{1,0:T(8,128)(2,1)S(1)} %copy-done.14), kind=kOutput, calls=%fused_computation.35 | convolution fusion | flops 2149056256 | bytes 11535360 | tf_op jit(solution)/shard_map/out_projection/dot_general | solution.py:267
  203.0 1.6 pad_maximum_fusion
  204.6 1.0 collective-permute-start.13
  205.6 48.8 %all-gather.6.cloned.1.call-done = bf16[16,128,1024]{2,1,0:T(8,128)(2,1)} async-done(((bf16[2,128,1024]{2,1,0:T(8,128)(2,1)}), bf16[16,128,1024]{2,1,0:T(8,128)(2,1)}) %all-gather.6.cloned.1.call-update) | async-done | bytes 4194320 | tf_op jit(solution)/shard_map/kv_weight_gather/all_gather | solution.py:230
  254.4 2.9 fusion.36
  257.5 0.7 fusion.23
  258.2 0.6 copy-done.11
  258.8 0.7 fusion.26
  259.5 1.8 fusion.11
  261.3 1.8 fusion.10
  263.1 1.3 pad_maximum_fusion.1
  264.4 1.5 collective-permute-start.14
  265.9 0.6 gather_fusion
  266.5 0.6 collective-permute-start.16
  267.1 0.7 fusion.20
  267.8 22.0 %collective-permute-done.16 = f32[2,256]{1,0:T(2,128)S(1)} collective-permute-done((f32[2,256]{1,0:T(2,128)S(1)}, f32[2,256]{1,0:T(2,128)S(1)}, u32[]{:S(2)}, u32[]{:S(2)}) %collective-permute-start.16) | collective-permute-done | bytes 2080 | tf_op jit(solution)/shard_map/out_projection/ppermute | solution.py:191
  289.8 2.0 fusion.9
  291.9 0.7 fusion.30
  292.6 2.0 fusion.6
  294.7 1.0 broadcast_select_fusion
  (74 shorter events, 4.0 us)
Async XLA Ops:
  7.2 19.8 %copy-start = (f32[256,32]{0,1:T(8,128)S(1)}, f32[256,32]{0,1:T(8,128)}, u32[]{:S(2)}) copy-start(f32[256,32]{0,1:T(8,128)} %param.15) | copy-start | bytes 98308
  7.2 171.5 %all-gather.4.cloned.1.call-start = ((), (), s32[]{:S(2)}) async-start(), calls=%async_computation.2 | async-start | bytes 9437184 | tf_op jit(solution)/shard_map/out_weight_gather/all_gather | solution.py:223
  9.0 2.3 collective-permute-start.3
  9.1 9.2 %collective-permute-start.4 = (bf16[128,1024]{0,1:T(8,128)(2,1)S(1)}, bf16[128,1024]{0,1:T(8,128)(2,1)S(1)}, u32[]{:S(2)}, u32[]{:S(2)}) collective-permute-start(bf16[128,1024]{0,1:T(8,128)(2,1)S(1)} %bitcast.139), channel_id=1, source_target_pairs={{0,2},{1,3},{2,0},{3,1},{4,6},{5,7},{6,4},{7,5},{8,10},{9,11},{10,... | collective-permute-start | bytes 786440 | tf_op jit(solution)/shard_map/out_weight_gather/ppermute | solution.py:191
  10.6 12.3 %collective-permute-start.5 = (bf16[128,1024]{0,1:T(8,128)(2,1)S(1)}, bf16[128,1024]{0,1:T(8,128)(2,1)S(1)}, u32[]{:S(2)}, u32[]{:S(2)}) collective-permute-start(bf16[128,1024]{0,1:T(8,128)(2,1)S(1)} %bitcast.138), channel_id=1, source_target_pairs={{0,3},{1,2},{2,1},{3,0},{4,7},{5,6},{6,5},{7,4},{8,11},{9,10},{10,... | collective-permute-start | bytes 786440 | tf_op jit(solution)/shard_map/out_weight_gather/ppermute | solution.py:191
  23.8 4.4 %copy-start.2 = (bf16[256,4096]{1,0:T(8,128)(2,1)S(1)}, bf16[256,4096]{1,0:T(8,128)(2,1)}, u32[]{:S(2)}) copy-start(bf16[256,4096]{1,0:T(8,128)(2,1)} %key_ref.3) | copy-start | bytes 6291460
  25.9 1.0 copy-start.7
  61.3 13.7 %collective-permute-start = (bf16[4,144,128]{2,1,0:T(8,128)(2,1)S(1)}, bf16[4,144,128]{2,1,0:T(8,128)(2,1)S(1)}, u32[]{:S(2)}, u32[]{:S(2)}) collective-permute-start(bf16[4,144,128]{2,1,0:T(8,128)(2,1)S(1)} %plane_total.1), channel_id=1, source_target_pairs={{0,8},{1,9},{2,10},{3,11},{4,12},{5,13},{6,14},{7,15},{8,16},{9,17... | collective-permute-start | bytes 442376 | tf_op jit(solution)/shard_map/state_scan/ppermute | solution.py:250
  62.6 28.4 %collective-permute-start.1 = (bf16[4,144,128]{2,1,0:T(8,128)(2,1)S(1)}, bf16[4,144,128]{2,1,0:T(8,128)(2,1)S(1)}, u32[]{:S(2)}, u32[]{:S(2)}) collective-permute-start(bf16[4,144,128]{2,1,0:T(8,128)(2,1)S(1)} %plane_total.1), channel_id=1, source_target_pairs={{0,16},{1,17},{2,18},{3,19},{4,20},{5,21},{6,22},{7,23},{8,24},{9,... | collective-permute-start | bytes 442376 | tf_op jit(solution)/shard_map/state_scan/ppermute | solution.py:250
  63.9 27.1 %collective-permute-start.2 = (bf16[4,144,128]{2,1,0:T(8,128)(2,1)S(1)}, bf16[4,144,128]{2,1,0:T(8,128)(2,1)S(1)}, u32[]{:S(2)}, u32[]{:S(2)}) collective-permute-start(bf16[4,144,128]{2,1,0:T(8,128)(2,1)S(1)} %plane_total.1), channel_id=1, source_target_pairs={{0,24},{1,25},{2,26},{3,27},{4,28},{5,29},{6,30},{7,31}} | collective-permute-start | bytes 442376 | tf_op jit(solution)/shard_map/state_scan/ppermute | solution.py:250
  91.7 1.0 copy-start.4
  92.6 24.3 %all-to-all-start.1 = ((bf16[8,4,128,128]{3,2,1,0:T(8,128)(2,1)}), bf16[8,4,128,128]{3,2,1,0:T(8,128)(2,1)}, u32[]{:S(2)}, u32[]{:S(2)}) async-start(bf16[8,4,128,128]{3,2,1,0:T(8,128)(2,1)} %copy-done.4), calls=%async_computation.1 | async-start | bytes 2097152 | tf_op jit(solution)/shard_map/state_scan/all_to_all | solution.py:253
  96.9 157.6 %all-gather.6.cloned.1.call-start = ((), (), s32[]{:S(2)}) async-start(), calls=%async_computation.3 | async-start | bytes 4718592 | tf_op jit(solution)/shard_map/kv_weight_gather/all_gather | solution.py:230
  100.3 1.6 collective-permute-start.6
  104.9 1.6 copy-start.3
  125.2 48.7 %collective-permute-start.8 = (bf16[256,4096]{1,0:T(8,128)(2,1)S(1)}, bf16[256,4096]{1,0:T(8,128)(2,1)}, u32[]{:S(2)}, u32[]{:S(2)}) collective-permute-start(bf16[256,4096]{1,0:T(8,128)(2,1)S(1)} %mix.1), channel_id=1, source_target_pairs={{0,2},{1,3},{2,0},{3,1},{4,6},{5,7},{6,4},{7,5},{8,10},{9,11},{10,... | collective-permute-start | bytes 6291464 | tf_op jit(solution)/shard_map/mixed_exchange/ppermute | solution.py:191
  145.4 28.5 %copy-start.12 = (bf16[4096]{0:T(1024)(128)(2,1)S(1)}, bf16[4096]{0:T(1024)(128)(2,1)}, u32[]{:S(2)}) copy-start(bf16[4096]{0:T(1024)(128)(2,1)} %param.17) | copy-start | bytes 24580
  146.3 38.8 %collective-permute-start.10 = (bf16[256,1024]{1,0:T(8,128)(2,1)}, bf16[256,1024]{1,0:T(8,128)(2,1)}, u32[]{:S(2)}, u32[]{:S(2)}) collective-permute-start(bf16[256,1024]{1,0:T(8,128)(2,1)} %bitcast.107), channel_id=1, source_target_pairs={{0,2},{1,3},{2,0},{3,1},{4,6},{5,7},{6,4},{7,5},{8,10},{9,11},{10,... | collective-permute-start | bytes 1572872 | tf_op jit(solution)/shard_map/residual_exchange/ppermute | solution.py:191
  148.0 46.0 %collective-permute-start.7 = (bf16[256,1024]{1,0:T(8,128)(2,1)}, bf16[256,1024]{1,0:T(8,128)(2,1)}, u32[]{:S(2)}, u32[]{:S(2)}) collective-permute-start(bf16[256,1024]{1,0:T(8,128)(2,1)} %bitcast.108), channel_id=1, source_target_pairs={{0,3},{1,2},{2,1},{3,0},{4,7},{5,6},{6,5},{7,4},{8,11},{9,10},{10,... | collective-permute-start | bytes 1572872 | tf_op jit(solution)/shard_map/residual_exchange/ppermute | solution.py:191
  148.3 49.8 %collective-permute-start.11 = (bf16[256,1024]{1,0:T(8,128)(2,1)S(1)}, bf16[256,1024]{1,0:T(8,128)(2,1)}, u32[]{:S(2)}, u32[]{:S(2)}) collective-permute-start(bf16[256,1024]{1,0:T(8,128)(2,1)S(1)} %bitcast.131), channel_id=1, source_target_pairs={{0,1},{1,0},{2,3},{3,2},{4,5},{5,4},{6,7},{7,6},{8,9},{9,8},{10,11... | collective-permute-start | bytes 1572872 | tf_op jit(solution)/shard_map/residual_exchange/ppermute | solution.py:191
  173.9 20.1 %collective-permute-start.9 = (bf16[256,4096]{1,0:T(8,128)(2,1)}, bf16[256,4096]{1,0:T(8,128)(2,1)}, u32[]{:S(2)}, u32[]{:S(2)}) collective-permute-start(bf16[256,4096]{1,0:T(8,128)(2,1)} %collective-permute-done.8), channel_id=1, source_target_pairs={{0,1},{1,0},{2,3},{3,2},{4,5},{5,4},{6,7},{7,6},{8,9},{9,8},{10,11... | collective-permute-start | bytes 6291464 | tf_op jit(solution)/shard_map/mixed_exchange/ppermute | solution.py:191
  175.0 23.1 %collective-permute-start.12 = (bf16[256,4096]{1,0:T(8,128)(2,1)S(1)}, bf16[256,4096]{1,0:T(8,128)(2,1)}, u32[]{:S(2)}, u32[]{:S(2)}) collective-permute-start(bf16[256,4096]{1,0:T(8,128)(2,1)S(1)} %mix.1), channel_id=1, source_target_pairs={{0,1},{1,0},{2,3},{3,2},{4,5},{5,4},{6,7},{7,6},{8,9},{9,8},{10,11... | collective-permute-start | bytes 6291464 | tf_op jit(solution)/shard_map/mixed_exchange/ppermute | solution.py:191
  178.7 6.5 %copy-start.14 = (bf16[4096,1024]{1,0:T(8,128)(2,1)S(1)}, bf16[4096,1024]{1,0:T(8,128)(2,1)}, u32[]{:S(2)}) copy-start(bf16[4096,1024]{1,0:T(8,128)(2,1)} %all-gather.4.cloned.1.call-done) | copy-start | bytes 25165828
  189.4 13.2 %copy-start.8 = (bf16[256,1024]{1,0:T(8,128)(2,1)}, bf16[256,1024]{1,0:T(8,128)(2,1)S(1)}, u32[]{:S(2)}) copy-start(bf16[256,1024]{1,0:T(8,128)(2,1)S(1)} %get-tuple-element.8) | copy-start | bytes 1572868
  198.1 4.5 %copy-start.10 = (bf16[256,1024]{1,0:T(8,128)(2,1)}, bf16[256,1024]{1,0:T(8,128)(2,1)S(1)}, u32[]{:S(2)}) copy-start(bf16[256,1024]{1,0:T(8,128)(2,1)S(1)} %fusion.5) | copy-start | bytes 1572868
  204.6 54.9 %collective-permute-start.13 = (bf16[4,256,1024]{2,1,0:T(8,128)(2,1)}, bf16[4,256,1024]{2,1,0:T(8,128)(2,1)}, u32[]{:S(2)}, u32[]{:S(2)}) collective-permute-start(bf16[4,256,1024]{2,1,0:T(8,128)(2,1)} %pad_maximum_fusion), channel_id=1, source_target_pairs={{0,1},{1,0},{2,3},{3,2},{4,5},{5,4},{6,7},{7,6},{8,9},{9,8},{10,11... | collective-permute-start | bytes 6291464 | tf_op jit(solution)/shard_map/cache_projection/ppermute | solution.py:191
  254.4 3.0 copy-start.9
  257.3 3.9 %copy-start.5 = (bf16[8,1,128,1024]{3,2,1,0:T(8,128)(2,1)}, bf16[8,1,128,1024]{3,2,1,0:T(8,128)(2,1)S(1)}, u32[]{:S(2)}) copy-start(bf16[8,1,128,1024]{3,2,1,0:T(8,128)(2,1)S(1)} %get-tuple-element.9) | copy-start | bytes 6291460
  257.3 1.4 copy-start.11
  257.4 8.5 %collective-permute-start.15 = (f32[4,256]{1,0:T(4,128)S(1)}, f32[4,256]{1,0:T(4,128)S(1)}, u32[]{:S(2)}, u32[]{:S(2)}) collective-permute-start(f32[4,256]{1,0:T(4,128)S(1)} %pad_maximum_fusion.3), channel_id=1, source_target_pairs={{0,1},{1,0},{2,3},{3,2},{4,5},{5,4},{6,7},{7,6},{8,9},{9,8},{10,11... | collective-permute-start | bytes 12296 | tf_op jit(solution)/shard_map/out_projection/ppermute | solution.py:191
  263.1 2.8 copy-start.13
  264.4 25.4 %collective-permute-start.14 = (bf16[2,256,1024]{2,1,0:T(8,128)(2,1)}, bf16[2,256,1024]{2,1,0:T(8,128)(2,1)}, u32[]{:S(2)}, u32[]{:S(2)}) collective-permute-start(bf16[2,256,1024]{2,1,0:T(8,128)(2,1)} %pad_maximum_fusion.1), channel_id=1, source_target_pairs={{0,2},{1,3},{2,0},{3,1},{4,6},{5,7},{6,4},{7,5},{8,10},{9,11},{10,... | collective-permute-start | bytes 3145736 | tf_op jit(solution)/shard_map/cache_projection/ppermute | solution.py:191
  266.4 23.4 %copy-start.6 = (bf16[8,1,128,1024]{3,2,1,0:T(8,128)(2,1)S(1)}, bf16[8,1,128,1024]{3,2,1,0:T(8,128)(2,1)}, u32[]{:S(2)}) copy-start(bf16[8,1,128,1024]{3,2,1,0:T(8,128)(2,1)} %copy-done.5) | copy-start | bytes 6291460
  266.5 23.3 %collective-permute-start.16 = (f32[2,256]{1,0:T(2,128)S(1)}, f32[2,256]{1,0:T(2,128)S(1)}, u32[]{:S(2)}, u32[]{:S(2)}) collective-permute-start(f32[2,256]{1,0:T(2,128)S(1)} %slice.66), channel_id=1, source_target_pairs={{0,2},{1,3},{2,0},{3,1},{4,6},{5,7},{6,4},{7,5},{8,10},{9,11},{10,... | collective-permute-start | bytes 6152 | tf_op jit(solution)/shard_map/out_projection/ppermute | solution.py:191
  291.8 2.8 collective-permute-start.17
  292.6 3.1 %copy-start.1 = (f32[256,32]{0,1:T(8,128)S(1)}, f32[256,32]{0,1:T(8,128)}, u32[]{:S(2)}) copy-start(f32[256,32]{0,1:T(8,128)} %param.15) | copy-start | bytes 98308
Sparse Core Ops, SparseCore 0:
  27.1 151.5 all-gather.3
  181.4 73.0 all-gather.5

commit v2 on v0

--- a/solution.py
+++ b/solution.py
@@ -1,9 +1,503 @@
+import functools
+import math
+
 import jax
 import jax.numpy as jnp
 from jax import lax
+from jax.experimental import pallas as pl
+from jax.experimental.pallas import tpu as pltpu
+from jax.sharding import Mesh
 from jax.sharding import PartitionSpec as P
 
+F32, BF16 = jnp.float32, jnp.bfloat16
 HIGHEST = lax.Precision.HIGHEST
+NORM_EPS = 1e-06
+DECAY_ROWS = 16
+PLANE = ("y", "x", "c")
+SEQ = ("z", "y", "x", "c")
+VMEM_LIMIT = 16 * 1024 * 1024
+
+
+def split_rows(total):
+    high = total.astype(BF16).astype(F32)
+    middle = (total - high).astype(BF16).astype(F32)
+    low = total - high - middle
+    row = lax.broadcasted_iota(jnp.int32, (DECAY_ROWS, total.shape[1]), 0)
+    rows = jnp.where(row == 0, high, jnp.where(row == 1, middle, jnp.where(row == 2, low, 0.0)))
+    return rows.astype(BF16)
+
+
+def join_rows(rows):
+    return jnp.sum(rows.astype(F32), axis=0, keepdims=True)
+
+
+def dot(a, b, contract):
+    return lax.dot_general(a, b, (contract, ((), ())), preferred_element_type=F32)
+
+
+def state_kernel(width, key_ref, value_ref, within_ref, out_ref):
+    tokens = key_ref.shape[0]
+    within = within_ref[0]
+    ending = within[tokens - 1 : tokens, :]
+    fade = jnp.exp(ending - within)
+    rows = width + DECAY_ROWS
+    for head in range(within.shape[1]):
+        columns = slice(head * width, (head + 1) * width)
+        faded = (key_ref[:, columns].astype(F32) * fade[:, head : head + 1]).astype(BF16)
+        state = dot(faded, value_ref[:, columns], ((0,), (0,)))
+        out_ref[0, head * rows : head * rows + width, :] = state.astype(BF16)
+        total = jnp.broadcast_to(ending[:, head : head + 1], (1, width))
+        out_ref[0, head * rows + width : (head + 1) * rows, :] = split_rows(total)
+
+
+def intra_kernel(
+    width, query_ref, key_ref, value_ref, gate_ref, within_ref, across_ref, out_ref, open_ref
+):
+    tokens = query_ref.shape[0]
+    within, across = within_ref[0], across_ref[0]
+    lower = lax.broadcasted_iota(jnp.int32, (tokens, tokens), 0) >= lax.broadcasted_iota(
+        jnp.int32, (tokens, tokens), 1
+    )
+    for head in range(within.shape[1]):
+        columns = slice(head * width, (head + 1) * width)
+        scores = dot(query_ref[:, columns], key_ref[:, columns], ((1,), (1,)))
+        spread = within[:, head : head + 1] - across[head : head + 1, :]
+        weighted = jnp.where(lower, scores * jnp.exp(jnp.where(lower, spread, 0.0)), 0.0)
+        out_ref[:, columns] = dot(weighted.astype(BF16), value_ref[:, columns], ((1,), (0,)))
+        gate = gate_ref[:, columns].astype(F32)
+        open_ref[:, columns] = (gate / (1.0 + jnp.exp(-gate))).astype(BF16)
+
+
+def mix_kernel(width, query_ref, open_ref, intra_ref, within_ref, state_ref, *out_refs):
+    reach = jnp.exp(within_ref[0])
+    rows = out_refs[0].shape[0]
+    for head in range(state_ref.shape[0]):
+        columns = slice(head * width, (head + 1) * width)
+        carried = dot(query_ref[:, columns], state_ref[head], ((1,), (0,)))
+        retained = intra_ref[:, columns] + reach[:, head : head + 1] * carried
+        scale = lax.rsqrt(jnp.mean(retained * retained, axis=1, keepdims=True) + NORM_EPS)
+        mixed = (open_ref[:, columns].astype(F32) * (retained * scale)).astype(BF16)
+        for half, out_ref in enumerate(out_refs):
+            out_ref[:, columns] = mixed[half * rows : (half + 1) * rows]
+
+
+def total_kernel(width, parts_ref, out_ref):
+    state = jnp.zeros((width, width), F32)
+    total = jnp.zeros((1, width), F32)
+    for place in range(parts_ref.shape[0]):
+        ending = join_rows(parts_ref[place, width:, :])
+        state = jnp.exp(ending) * state + parts_ref[place, :width, :].astype(F32)
+        total = total + ending
+    out_ref[0, :width, :] = state.astype(BF16)
+    out_ref[0, width:, :] = split_rows(total)
+
+
+def prefix_kernel(width, planes, parts_ref, *refs):
+    plane_refs, out_ref = refs[:planes], refs[planes]
+    state = jnp.zeros((width, width), F32)
+    reach = jnp.zeros((1, width), F32)
+    for ref in plane_refs:
+        state = state + jnp.exp(reach) * ref[0, :width, :].astype(F32)
+        reach = reach + join_rows(ref[0, width:, :])
+    for place in range(parts_ref.shape[0]):
+        out_ref[place, 0] = state.astype(BF16)
+        ending = join_rows(parts_ref[place, width:, :])
+        state = jnp.exp(ending) * state + parts_ref[place, :width, :].astype(F32)
+
+
+def local_call(
+    name, body, grid, operands, specs, out_specs, out_shape, scalars=(), scratch=(), after=()
+):
+    taken = len(scalars) + len(operands)
+
+    def kernel(*refs):
+        body(*refs[:taken], *refs[taken + len(after) :])
+
+    return pl.pallas_call(
+        kernel,
+        grid_spec=pltpu.PrefetchScalarGridSpec(
+            num_scalar_prefetch=len(scalars),
+            grid=(grid,),
+            in_specs=list(specs) + [pl.BlockSpec(memory_space=pltpu.HBM)] * len(after),
+            out_specs=out_specs,
+            scratch_shapes=scratch,
+        ),
+        out_shape=out_shape,
+        compiler_params=pltpu.CompilerParams(vmem_limit_bytes=VMEM_LIMIT),
+        name=name,
+    )(*scalars, *operands, *after)
+
+
+def wide(rows, columns):
+    return pl.BlockSpec((rows, columns), lambda i, *_: (0, i))
+
+
+def whole(rows, columns):
+    return pl.BlockSpec((rows, columns), lambda i, *_: (0, 0))
+
+
+def group(*shape):
+    return pl.BlockSpec((1,) + shape, lambda i, *_: (i, 0, 0))
+
+
+def local_states(keys, values, within, width, after=()):
+    tokens, groups, per = keys.shape[0], within.shape[0], within.shape[2]
+    tall = per * (width + DECAY_ROWS)
+    return local_call(
+        "local_states",
+        functools.partial(state_kernel, width),
+        groups,
+        (keys, values, within),
+        (wide(tokens, per * width), wide(tokens, per * width), group(tokens, per)),
+        group(tall, width),
+        jax.ShapeDtypeStruct((groups, tall, width), BF16),
+        after=after,
+    )
+
+
+def local_intra(queries, keys, values, gate, within, across, width, after=()):
+    tokens, groups, per = keys.shape[0], within.shape[0], within.shape[2]
+    heads = wide(tokens, per * width)
+    return local_call(
+        "local_intra",
+        functools.partial(intra_kernel, width),
+        groups,
+        (queries, keys, values, gate, within, across),
+        (heads, heads, heads, heads, group(tokens, per), group(per, tokens)),
+        [heads, heads],
+        [
+            jax.ShapeDtypeStruct(queries.shape, F32),
+            jax.ShapeDtypeStruct(queries.shape, BF16),
+        ],
+        after=after,
+    )
+
+
+def mix(queries, opened, intra, within, states, width, after=()):
+    groups, tokens, per = within.shape
+    heads = wide(tokens, per * width)
+    return local_call(
+        "mix",
+        functools.partial(mix_kernel, width),
+        groups,
+        (queries, opened, intra, within, states),
+        (
+            heads,
+            heads,
+            heads,
+            group(tokens, per),
+            pl.BlockSpec((per, width, width), lambda i: (i, 0, 0)),
+        ),
+        [wide(tokens // 2, per * width)] * 2,
+        [jax.ShapeDtypeStruct((tokens // 2, queries.shape[1]), BF16)] * 2,
+        after=after,
+    )
+
+
+def plane_total(parts, heads, width, after=()):
+    places, rows = parts.shape[0], width + DECAY_ROWS
+    return local_call(
+        "plane_total",
+        functools.partial(total_kernel, width),
+        heads,
+        (parts,),
+        (pl.BlockSpec((places, rows, width), lambda i: (0, i, 0)),),
+        group(rows, width),
+        jax.ShapeDtypeStruct((heads, rows, width), BF16),
+        after=after,
+    )
+
+
+def plane_prefix(parts, planes, width, after=()):
+    places, (heads, rows, _) = parts.shape[0], planes[0].shape
+    return local_call(
+        "plane_prefix",
+        functools.partial(prefix_kernel, width, len(planes)),
+        heads,
+        (parts, *planes),
+        [pl.BlockSpec((places, rows, width), lambda i: (0, i, 0))]
+        + [group(rows, width)] * len(planes),
+        pl.BlockSpec((places, 1, width, width), lambda i: (0, i, 0, 0)),
+        jax.ShapeDtypeStruct((places, heads, width, width), BF16),
+        after=after,
+    )
+
+
+def deal_kernel(ways, block, place_ref, source_ref, *target_refs):
+    for r, target_ref in enumerate(target_refs):
+        for i in range(target_ref.shape[1] // block):
+            start = pl.multiple_of((i * ways + (place_ref[0] ^ r)) * block, block)
+            target_ref[:, i * block : (i + 1) * block] = source_ref[:, pl.ds(start, block)]
+
+
+def deal(array, place, ways, block, after=()):
+    rows, columns = array.shape
+    return local_call(
+        "deal",
+        functools.partial(deal_kernel, ways, block),
+        1,
+        (array,),
+        (whole(rows, columns),),
+        [whole(rows, columns // ways)] * ways,
+        [jax.ShapeDtypeStruct((rows, columns // ways), array.dtype)] * ways,
+        scalars=(place.reshape(1),),
+        after=after,
+    )
+
+
+def spread_kernel(block, source_ref, target_ref):
+    ways, _, columns = target_ref.shape
+    for place in range(ways):
+        for i in range(columns // block):
+            start = (i * ways + place) * block
+            target_ref[place, :, i * block : (i + 1) * block] = source_ref[:, start : start + block]
+
+
+def spread(array, ways, block, after=()):
+    rows, columns = array.shape
+    return local_call(
+        "spread",
+        functools.partial(spread_kernel, block),
+        2,
+        (array,),
+        (pl.BlockSpec((rows // 2, columns), lambda i: (i, 0)),),
+        pl.BlockSpec((ways, rows // 2, columns // ways), lambda i: (0, i, 0)),
+        jax.ShapeDtypeStruct((ways, rows, columns // ways), array.dtype),
+        after=after,
+    )
+
+
+def order_kernel(place_ref, *refs):
+    *sources, target_ref = refs
+    rows = sources[0].shape[0]
+    for r, source in enumerate(sources):
+        start = pl.multiple_of((place_ref[0] ^ r) * rows, rows)
+        target_ref[pl.ds(start, rows), :] = source[...]
+
+
+def in_order(arrays, place, after=()):
+    rows, columns = arrays[0].shape
+    tall = (len(arrays) * rows, columns)
+    return local_call(
+        "in_order",
+        order_kernel,
+        1,
+        arrays,
+        [whole(rows, columns)] * len(arrays),
+        whole(*tall),
+        jax.ShapeDtypeStruct(tall, arrays[0].dtype),
+        scalars=(place.reshape(1),),
+        after=after,
+    )
+
+
+def hold(array, after):
+    kept = pl.BlockSpec(memory_space=pltpu.HBM)
+    return pl.pallas_call(
+        lambda *refs: None,
+        in_specs=[kept] * (1 + len(after)),
+        out_specs=kept,
+        out_shape=jax.ShapeDtypeStruct(array.shape, array.dtype),
+        input_output_aliases={0: 0},
+        compiler_params=pltpu.CompilerParams(vmem_limit_bytes=VMEM_LIMIT),
+        name="hold",
+    )(array, *after)
+
+
+def resident(count):
+    return [pl.BlockSpec(memory_space=pltpu.VMEM)] * count
+
+
+def out_kernel(chips, halves, place_ref, *refs):
+    pieces = 2 * len(chips)
+    mixed, (weight_ref, start_ref, mine_ref, theirs_ref) = refs[:pieces], refs[pieces:]
+    tokens, depth = mixed[0].shape
+    step = min(depth, 512)
+    total = jnp.zeros((pieces * tokens, weight_ref.shape[1]), F32)
+    for start in range(0, depth, step):
+        left = jnp.concatenate([ref[:, start : start + step] for ref in mixed], axis=0)
+        total = total + dot(left, weight_ref[start : start + step, :], ((1,), (0,)))
+    for i in range(pieces):
+        rows = ((place_ref[0] ^ (2 * chips[i // 2] + i % 2)) * 2 + halves[i // 2]) * tokens
+        hidden = start_ref[pl.ds(pl.multiple_of(rows, tokens), tokens), :].astype(F32)
+        hidden = (hidden + total[i * tokens : (i + 1) * tokens]).astype(BF16)
+        (mine_ref, theirs_ref)[i % 2][i // 2 * tokens : (i // 2 + 1) * tokens, :] = hidden
+
+
+def out_projection(place, pieces, weight, start, after=()):
+    chips, halves, mixed = zip(*pieces)
+    mixed = [array for cores in mixed for array in cores]
+    shape = jax.ShapeDtypeStruct((len(pieces) * mixed[0].shape[0], weight.shape[1]), BF16)
+    return resident_call(
+        "out_projection",
+        functools.partial(out_kernel, chips, halves),
+        (place.reshape(1),),
+        (*mixed, weight, start),
+        [shape, shape],
+        after,
+    )
+
+
+def resident_call(name, body, scalars, operands, out_shape, after):
+    taken = len(scalars) + len(operands)
+
+    def kernel(*refs):
+        body(*refs[:taken], *refs[taken + len(after) :])
+
+    return pl.pallas_call(
+        kernel,
+        in_specs=[pl.BlockSpec(memory_space=pltpu.SMEM)] * len(scalars)
+        + resident(len(operands))
+        + [pl.BlockSpec(memory_space=pltpu.HBM)] * len(after),
+        out_specs=resident(len(out_shape)),
+        out_shape=out_shape,
+        compiler_params=pltpu.CompilerParams(vmem_limit_bytes=VMEM_LIMIT),
+        name=name,
+    )(*scalars, *operands, *after)
+
+
+def cache_kernel(width, model, joined, finish, *refs):
+    own_ref, other_ref, own_weight_ref, other_weight_ref, *refs = refs
+    added, out_refs = refs[: len(joined)], refs[len(joined) :]
+    tokens, columns = own_ref.shape[0] // 2, own_weight_ref.shape[1]
+    own, other = own_ref[...], other_ref[...]
+    total = dot(own, own_weight_ref[...], ((1,), (0,)))
+    total = total + dot(other, other_weight_ref[...], ((1,), (0,)))
+    squares = jnp.square(own.astype(F32)) + jnp.square(other.astype(F32))
+    squares = jnp.sum(squares, axis=1, keepdims=True)
+    for i in range(2):
+        rows = slice(i * tokens, (i + 1) * tokens)
+        sums, norm = total[rows], squares[rows]
+        for ref, half in zip(added, joined):
+            if half == i:
+                sums = sums + ref[:, :columns].astype(F32)
+                norm = norm + jnp.sum(ref[:, columns:].astype(F32), axis=1, keepdims=True)
+        if finish:
+            sums = (sums * lax.rsqrt(norm / model + NORM_EPS)).astype(BF16)
+            for head in range(columns // (2 * width)):
+                for kind, out_ref in enumerate(out_refs):
+                    start = (2 * head + kind) * width
+                    out_ref[rows, head * width : (head + 1) * width] = sums[:, start : start + width]
+        else:
+            high = norm.astype(BF16).astype(F32)
+            middle = (norm - high).astype(BF16).astype(F32)
+            low = norm - high - middle
+            lane = lax.broadcasted_iota(jnp.int32, (tokens, width), 1)
+            lanes = jnp.where(lane == 0, high, jnp.where(lane == 1, middle, 0.0))
+            out_refs[i][:, :columns] = sums.astype(BF16)
+            out_refs[i][:, columns:] = jnp.where(lane == 2, low, lanes).astype(BF16)
+
+
+def cache_projection(own, other, weights, width, model, added=(), finish=False, after=()):
+    tokens, columns = own.shape[0], weights[0].shape[1]
+    out = (tokens, columns // 2) if finish else (tokens // 2, columns + width)
+    return resident_call(
+        "cache_projection",
+        functools.partial(cache_kernel, width, model, [half for _, half in added], finish),
+        (),
+        (own, other, *weights, *[array for array, _ in added]),
+        [jax.ShapeDtypeStruct(out, BF16)] * 2,
+        after,
+    )
+
+
+SIZES = (4, 2, 2, 2)
+DEVICES = math.prod(SIZES)
+DEPTH = SIZES[0]
+PLACES = DEVICES // DEPTH
+
+
+def swap(array, distance):
+    return lax.ppermute(array, SEQ, [(i, i ^ distance) for i in range(DEVICES)])
+
+
+def hop(array, steps):
+    pairs = [
+        (a * PLACES + i, b * PLACES + i) for a, b in sorted(steps.items()) for i in range(PLACES)
+    ]
+    return lax.ppermute(array, SEQ, pairs)
+
+
+def shared_on_device(
+    queries, keys, values, gate, residual, log_decay, out_weight, norm_gain, kv_weight
+):
+    tokens, heads = log_decay.shape
+    width = queries.shape[1] // heads
+    model = out_weight.shape[1]
+    share = model // PLACES
+    piece = share // DEPTH
+    core = lax.axis_index("c")
+    place = 4 * lax.axis_index("y") + 2 * lax.axis_index("x") + core
+
+    with jax.named_scope("kv_weight_gather"):
+        kv_mine = lax.all_gather(kv_weight, "z", axis=0, tiled=True)
+    with jax.named_scope("out_weight_gather"):
+        dealt = deal(out_weight, place, PLACES, piece)
+        pieces = [swap(part, r) if r else part for r, part in enumerate(dealt)]
+
+    running = jnp.cumsum(log_decay, axis=0)
+    per = heads // PLACES
+    within = running.reshape(tokens, PLACES, per).transpose(1, 0, 2)
+    across = running.T.reshape(PLACES, per, tokens)
+    states = local_states(keys, values, within, width, after=(dealt[0],))
+    with jax.named_scope("state_scan"):
+        parts = lax.all_to_all(states, PLANE, 0, 0, tiled=True)
+    with jax.named_scope("residual_exchange"):
+        dealt = spread(residual, PLACES, piece, after=(states,))
+    with jax.named_scope("state_scan"):
+        total = plane_total(parts, per, width, after=(dealt,))
+        earlier = [hop(total, {a: a + d for a in range(DEPTH - d)}) for d in range(1, DEPTH)]
+    with jax.named_scope("residual_exchange"):
+        start = lax.all_to_all(hold(dealt, (total,)), PLANE, 0, 0, tiled=True)
+        start = start.reshape(-1, share)
+    intra, opened = local_intra(
+        queries, keys, values, gate, within, across, width, after=(total,)
+    )
+    with jax.named_scope("state_scan"):
+        prefix = plane_prefix(parts, earlier, width, after=(start, intra))
+    with jax.named_scope("out_weight_gather"):
+        shard = in_order(pieces, place, after=(kv_mine, total))
+        out_full = lax.all_gather(shard, "z", axis=0, tiled=True)
+    with jax.named_scope("state_scan"):
+        entering = lax.all_to_all(hold(prefix, (shard,)), PLANE, 0, 0, tiled=True)
+        entering = entering.reshape(heads, width, width)
+
+    early, late = mix(queries, opened, intra, within, entering, width)
+
+    with jax.named_scope("cache_weight"):
+        gains = norm_gain.reshape(DEPTH, PLACES, piece)
+        kv_full = []
+        for r, rows in enumerate((kv_mine, swap(kv_mine, 1))):
+            gain = lax.dynamic_index_in_dim(gains, place ^ r, 1, False).reshape(share, 1)
+            kv_full.append((rows.astype(F32) * gain.astype(F32)).astype(BF16))
+
+    def hidden_of(*halves, after=()):
+        pieces = [(chip, half, (mixed, swap(mixed, 1))) for chip, half, mixed in halves]
+        mine, theirs = out_projection(place, pieces, out_full, start, after)
+        return mine, swap(theirs, 1)
+
+    def share_of(hidden, added=(), finish=False, after=()):
+        return cache_projection(*hidden, kv_full, width, model, added, finish, after)
+
+    with jax.named_scope("projections"):
+        early_x, late_y = swap(early, 2), swap(late, 4)
+        early_far, late_far = swap(early_x, 4), swap(late_y, 2)
+        home = hidden_of((0, 0, early), (0, 1, late), after=(early_x, late_y))
+        near = hidden_of((1, 0, early_x), (2, 1, late_y), after=(home[0],))
+        late_x = swap(hold(late, (near[0], early_far, late_far)), 2)
+        early_y = swap(hold(early, (near[0], early_far, late_far)), 4)
+        far = hidden_of((3, 0, early_far), (3, 1, late_far), after=(near[0],))
+        early_far, late_far = share_of(far)
+        early_x, late_y = share_of(near, after=(early_far,))
+        late_x, early_y = hold(late_x, (early_x,)), hold(early_y, (early_x,))
+        early_x, late_y = swap(early_x, 2), swap(late_y, 4)
+        near = hidden_of((1, 1, late_x), (2, 0, early_y))
+        late_x, early_y = share_of(
+            near, [(swap(late_far, 4), 0), (swap(early_far, 2), 1)], after=(early_x, late_y)
+        )
+        late_x, early_y = swap(late_x, 2), swap(early_y, 4)
+        added = [(early_x, 0), (late_x, 1), (early_y, 0), (late_y, 1)]
+        return share_of(home, added, True)
 
 
 def entering(part, axis, combine, identity):
@@ -110,21 +604,22 @@
 
 
 def solution(mesh):
-    placed = (
-        P("seq", "head"),
-        P("seq", "head"),
-        P("seq", "head"),
-        P("seq", "head"),
-        P("seq", "head"),
-        P("seq", "head"),
-        P("seq", "head"),
-        P("head"),
-        P("seq", "head"),
-    )
+    devices, split = mesh.shape["seq"], mesh.shape["head"]
+    if split == 1 and devices == DEVICES:
+        fine = Mesh(mesh.devices.reshape(SIZES + (1,)), SEQ + ("head",))
+        placed, copied = P(SEQ, "head"), P("head")
+        return jax.shard_map(
+            shared_on_device,
+            mesh=fine,
+            in_specs=(placed,) * 7 + (copied, placed),
+            out_specs=(placed, placed),
+            check_vma=False,
+        )
+    placed = P("seq", "head")
     return jax.shard_map(
         on_device,
         mesh=mesh,
-        in_specs=placed,
-        out_specs=(P("seq", "head"), P("seq", "head")),
+        in_specs=(placed,) * 7 + (P("head"), placed),
+        out_specs=(placed, placed),
         check_vma=False,
     )

time: 721 us -> 275 us (0.38)
  waiting for transfers between devices: 491 us -> 125 us
  other arithmetic: 96 us -> 4.77 us
  matrix products: 56.8 us -> 0 us
  Pallas kernels: 0 us -> 47 us
  starting transfers between devices: 0.12 us -> 31.3 us
  blocking collectives: 33.5 us -> 19.5 us
    all_gather x3 -> x2, waiting for transfers between devices: 489 us -> 3.18 us  [the longest x1 3.16 us: shared_on_device(): kv_mine = lax.all_gather(kv_weight, 'z', axis=0, tiled=True)]
    ppermute x0 -> x35, waiting for transfers between devices: none -> 121 us  [the longest x32 106 us: swap(): return lax.ppermute(array, SEQ, [(i, i ^ distance) for i in range(DEVICES)])]
    add x25 -> x0, other arithmetic: 92.9 us -> none  [the longest x24 92.9 us: combine_states(): later[0][:, None, None] * earlier[1] + later[1]]
    dot_general x7 -> x0, matrix products: 56.8 us -> none  [the longest x1 19 us: on_device(): branch = jnp.dot(all_heads, out_full, preferred_element_type=jnp.float32)]
    pallas_call x0 -> x22, Pallas kernels: none -> 47 us  [the longest x8 25.9 us: local_call(): pl.pallas_call(kernel, grid_spec=pltpu.PrefetchScalarGridSpec(num_scalar_...]
    all_gather x1 -> x0, blocking collectives: 33.5 us -> none  [entering(): gathered = jax.tree.map(lambda a: lax.all_gather(a, axis), part)]
    ppermute x0 -> x35, starting transfers between devices: none -> 23.1 us  [the longest x32 19.3 us: swap(): return lax.ppermute(array, SEQ, [(i, i ^ distance) for i in range(DEVICES)])]
    unnamed x14 -> x72, local copies, waits for them, and re-layouts: 10 us -> 31.2 us
  transfers between devices with their start and end apart: 3 -> 39, of which waited for: 3 -> 17; matrix products, arithmetic and copies ran while one was open for 20% -> 2% of each run, Pallas kernels for 0% -> 15%
where the time goes in v2:
time: 275 us; the launch traced here: 274 us
  waiting for transfers between devices  125 us (45%)
  Pallas kernels  47 us (17%)
  local copies, waits for them, and re-layouts  31.8 us (12%)
  starting transfers between devices  31.3 us (11%)
  blocking collectives  19.5 us (7%)
  between operations  14.6 us (5%)
  other arithmetic  4.77 us (2%)
    ppermute x32, waiting for transfers between devices, swap(): return lax.ppermute(array, SEQ, [(i, i ^ distance) for i in range(DEVICES)])  106 us
    unnamed x72, local copies, waits for them, and re-layouts  31.2 us
    pallas_call x8, Pallas kernels, local_call(): pl.pallas_call(kernel, grid_spec=pltpu.PrefetchScalarGridSpec(num_scalar_...  25.9 us
    pallas_call x8, Pallas kernels, resident_call(): pl.pallas_call(kernel, in_specs=[pl.BlockSpec(memory_space=pltpu.SMEM)] *...  21.1 us
    all_to_all x1, blocking collectives, shared_on_device(): entering = lax.all_to_all(hold(prefix, (shard,)), PLANE, 0, 0, tiled=True)  19.5 us
    ppermute x32, starting transfers between devices, swap(): return lax.ppermute(array, SEQ, [(i, i ^ distance) for i in range(DEVICES)])  19.3 us
    ppermute x3, waiting for transfers between devices, hop(): return lax.ppermute(array, SEQ, pairs)  15.1 us
  transfers between devices with their start and end apart: 39, of which 17 were waited for; matrix products, arithmetic and copies ran while one was open for 2% of the time, Pallas kernels for 15%

profile of v2, /device:TPU:24, one launch (start us, length us, event | category | flops | bytes accessed | tf_op | source)
XLA Modules:
  0.0 273.7 jit_solution(4929878946583426474)
XLA Ops:
  9.3 1.2 copy-done.27
  10.5 1.0 deal.1
  12.1 1.6 copy-done.12
  13.8 5.4 %local_states.1.refs_1_ = bf16[8,576,128]{2,1,0:T(8,128)(2,1)} custom-call(bf16[256,4096]{1,0:T(8,128)(2,1)S(1)} %copy-done.10, bf16[256,4096]{1,0:T(8,128)(2,1)S(1)} %copy-done.12, f32[8,256,4]{2,1,0:T(8,128)S(1)} %bitcast.27, bf16[128,512]{1,0:T(8,128)(2,1)S(1)} %get-tuple-element.28.refs_3_.refs_1_), custom_call_target="tpu_custom_call" | custom-call | tf_op jit(solution)/shard_map/local_states/pallas_call | solution.py:116
  19.2 4.4 %all-to-all-start = ((bf16[8,576,128]{2,1,0:T(8,128)(2,1)}), bf16[8,576,128]{2,1,0:T(8,128)(2,1)}, u32[]{:S(2)}, u32[]{:S(2)}) async-start(bf16[8,576,128]{2,1,0:T(8,128)(2,1)} %local_states.1.refs_1_), calls=%async_computation | async-start | bytes 2359296 | tf_op jit(solution)/shard_map/state_scan/all_to_all | solution.py:444
  24.0 1.7 collective-permute-start.4
  25.6 1.7 collective-permute-start.6
  27.5 2.6 collective-permute-start.8
  30.1 12.6 %collective-permute-done.4.refs_3_ = bf16[128,512]{1,0:T(8,128)(2,1)S(1)} collective-permute-done((bf16[128,512]{1,0:T(8,128)(2,1)S(1)}, bf16[128,512]{1,0:T(8,128)(2,1)S(1)}, u32[]{:S(2)}, u32[]{:S(2)}) %collective-permute-start.4) | collective-permute-done | bytes 131104 | tf_op jit(solution)/shard_map/out_weight_gather/ppermute | solution.py:411
  43.7 1.6 copy-done.21
  45.8 2.2 plane_total.1.refs_6_.refs_1_.refs_10_
  48.1 1.2 collective-permute-done.8.refs_7_
  49.3 1.9 collective-permute-done.9.refs_8_
  51.2 3.2 %all-gather.3.cloned.1.call-done.refs_9_ = bf16[512,2048]{1,0:T(8,128)(2,1)} async-done(((bf16[128,2048]{1,0:T(8,128)(2,1)}), bf16[512,2048]{1,0:T(8,128)(2,1)}) %all-gather.3.cloned.1.call-update) | async-done | bytes 2097168 | tf_op jit(solution)/shard_map/kv_weight_gather/all_gather | solution.py:433
  55.3 0.9 copy-done.31
  56.2 1.2 in_order.1.refs_1_
  57.4 1.0 copy-done.8
  58.5 1.3 copy-done.4
  59.8 3.7 %all-to-all-start.1 = ((bf16[8,256,512]{2,1,0:T(8,128)(2,1)}), bf16[8,256,512]{2,1,0:T(8,128)(2,1)S(1)}, u32[]{:S(2)}, u32[]{:S(2)}) async-start(bf16[8,256,512]{2,1,0:T(8,128)(2,1)} %copy-done.4), calls=%async_computation.1 | async-start | bytes 4194304 | tf_op jit(solution)/shard_map/residual_exchange/all_to_all | solution.py:451
  63.5 1.3 collective-permute-start
  64.8 1.3 collective-permute-start.1
  66.1 1.3 collective-permute-start.2
  67.5 1.8 copy-done.11
  69.3 1.8 copy-done.13
  71.0 1.6 copy-done.14
  72.6 1.6 copy-done.22
  74.2 6.6 %local_intra.1 = (f32[256,4096]{1,0:T(8,128)S(1)}, bf16[256,4096]{1,0:T(8,128)(2,1)S(1)}) custom-call(bf16[256,4096]{1,0:T(8,128)(2,1)S(1)} %copy-done.14, bf16[256,4096]{1,0:T(8,128)(2,1)S(1)} %copy-done.11, bf16[256,4096]{1,0:T(8,128)(2,1)S(1)} %copy-done.13, bf16[256,4096]{1,0:T(8,128)(2,1)S(1)} %copy-done.22, f32[8,256,4]{2,1,0:T(8,128)S(1)} %bitcast.28, ...), custom_call_target="tpu_custom_call" | custom-call | tf_op jit(solution)/shard_map/local_intra/pallas_call | solution.py:116
  80.8 2.0 copy-done.5
  82.8 1.4 copy-done.19
  84.3 15.1 %collective-permute-done.1.refs_2_ = bf16[4,144,128]{2,1,0:T(8,128)(2,1)} collective-permute-done((bf16[4,144,128]{2,1,0:T(8,128)(2,1)S(1)}, bf16[4,144,128]{2,1,0:T(8,128)(2,1)}, u32[]{:S(2)}, u32[]{:S(2)}) %collective-permute-start.1) | collective-permute-done | bytes 147488 | tf_op jit(solution)/shard_map/state_scan/ppermute | solution.py:418
  99.4 2.2 copy-done.6
  101.7 3.0 %plane_prefix.1.refs_0_ = bf16[8,4,128,128]{3,2,1,0:T(8,128)(2,1)S(1)} custom-call(bf16[8,576,128]{2,1,0:T(8,128)(2,1)} %all-to-all-done.refs_0_, bf16[4,144,128]{2,1,0:T(8,128)(2,1)S(1)} %collective-permute-done.refs_1_, bf16[4,144,128]{2,1,0:T(8,128)(2,1)} %collective-permute-done.1.refs_2_, bf16[4,144,128]{2,1,0:T(8,128)(2,1)} %collective-permute-done.2.refs_3_, ...), custom_call_target="tpu_custom_call" | custom-call | tf_op jit(solution)/shard_map/state_scan/plane_prefix/pallas_call | solution.py:116
  104.7 19.5 %all_to_all.15 = bf16[8,4,128,128]{3,2,1,0:T(8,128)(2,1)S(1)} all-to-all(bf16[8,4,128,128]{3,2,1,0:T(8,128)(2,1)S(1)} %hold.7), channel_id=1, replica_groups=mesh['z'=4,'y'=2,'x'=2,'c'=2,'head'=1] {'y','x','c'}, dimensions={0} | all-to-all | bytes 2097152 | tf_op jit(solution)/shard_map/state_scan/all_to_all | solution.py:462
  124.2 5.9 %mix.1 = (bf16[128,4096]{1,0:T(8,128)(2,1)S(1)}, bf16[128,4096]{1,0:T(8,128)(2,1)}) custom-call(bf16[256,4096]{1,0:T(8,128)(2,1)S(1)} %copy-done.15, bf16[256,4096]{1,0:T(8,128)(2,1)S(1)} %copy-done.20, f32[256,4096]{1,0:T(8,128)S(1)} %copy-done.7, f32[8,256,4]{2,1,0:T(8,128)S(1)} %bitcast.29, bf16[32,128,128]{2,1,0:T(8,128)(2,1)S(1)} %bitcast.30), custom_call_target="tpu_custom_call" | custom-call | tf_op jit(solution)/shard_map/mix/pallas_call | solution.py:116
  131.3 1.0 copy-done.16
  132.8 21.8 %collective-permute-done.12.refs_7_.refs_1_ = bf16[128,4096]{1,0:T(8,128)(2,1)} collective-permute-done((bf16[128,4096]{1,0:T(8,128)(2,1)S(1)}, bf16[128,4096]{1,0:T(8,128)(2,1)}, u32[]{:S(2)}, u32[]{:S(2)}) %collective-permute-start.12) | collective-permute-done | bytes 1048608 | tf_op jit(solution)/shard_map/projections/ppermute | solution.py:411
  156.6 1.0 copy-done.23
  158.1 1.0 copy-done.25
  159.1 19.2 %collective-permute-done.19.refs_1_.refs_2_ = bf16[128,4096]{1,0:T(8,128)(2,1)S(1)} collective-permute-done((bf16[128,4096]{1,0:T(8,128)(2,1)}, bf16[128,4096]{1,0:T(8,128)(2,1)S(1)}, u32[]{:S(2)}, u32[]{:S(2)}) %collective-permute-start.19) | collective-permute-done | bytes 1048608 | tf_op jit(solution)/shard_map/projections/ppermute | solution.py:411
  178.3 1.8 collective-permute-done.21.refs_3_
  180.2 2.2 copy-done.2
  182.3 1.2 copy-done.17
  183.6 1.2 copy-done.24
  184.8 1.2 copy-done.26
  186.0 3.7 %out_projection.4 = (bf16[256,512]{1,0:T(8,128)(2,1)S(1)}, bf16[256,512]{1,0:T(8,128)(2,1)S(1)}) custom-call(s32[1]{0:T(128)} %bitcast.refs_0_, bf16[128,4096]{1,0:T(8,128)(2,1)S(1)} %copy-done.17, bf16[128,4096]{1,0:T(8,128)(2,1)S(1)} %copy-done.24, bf16[128,4096]{1,0:T(8,128)(2,1)} %get-tuple-element.39.refs_3_.refs_0_, bf16[128,4096]{1,0:T(8,128)(2,1)S(1)} %copy-done.26, ...), custom_call_target="tpu_custom_call" | custom-call | tf_op jit(solution)/shard_map/projections/out_projection/pallas_call | solution.py:347
  189.8 4.6 %out_projection.5 = (bf16[256,512]{1,0:T(8,128)(2,1)S(1)}, bf16[256,512]{1,0:T(8,128)(2,1)S(1)}) custom-call(s32[1]{0:T(128)} %bitcast.refs_0_, bf16[128,4096]{1,0:T(8,128)(2,1)} %collective-permute-done.12.refs_7_.refs_1_, bf16[128,4096]{1,0:T(8,128)(2,1)} %collective-permute-done.16.refs_2_, bf16[128,4096]{1,0:T(8,128)(2,1)} %collective-permute-done.13.refs_8_.refs_3_, ...), custom_call_target="tpu_custom_call" | custom-call | tf_op jit(solution)/shard_map/projections/out_projection/pallas_call | solution.py:347
  194.8 1.7 collective-permute-start.25
  196.6 2.0 multiply_convert_fusion.1.refs_2_
  198.6 4.2 %out_projection.6 = (bf16[256,512]{1,0:T(8,128)(2,1)S(1)}, bf16[256,512]{1,0:T(8,128)(2,1)S(1)}) custom-call(s32[1]{0:T(128)} %bitcast.refs_0_, bf16[128,4096]{1,0:T(8,128)(2,1)S(1)} %collective-permute-done.19.refs_1_.refs_2_, bf16[128,4096]{1,0:T(8,128)(2,1)} %collective-permute-done.20.refs_2_, bf16[128,4096]{1,0:T(8,128)(2,1)} %collective-permute-done.21.refs_3_, ...), custom_call_target="tpu_custom_call" | custom-call | tf_op jit(solution)/shard_map/projections/out_projection/pallas_call | solution.py:347
  203.4 2.0 multiply_convert_fusion.refs_3_
  205.4 1.3 cache_projection.4
  206.7 1.3 cache_projection.5
  207.9 12.1 %collective-permute-done.27.refs_0_ = bf16[128,4096]{1,0:T(8,128)(2,1)S(1)} collective-permute-done((bf16[128,4096]{1,0:T(8,128)(2,1)S(1)}, bf16[128,4096]{1,0:T(8,128)(2,1)S(1)}, u32[]{:S(2)}, u32[]{:S(2)}) %collective-permute-start.27) | collective-permute-done | bytes 1048608 | tf_op jit(solution)/shard_map/projections/ppermute | solution.py:411
  220.5 1.6 collective-permute-start.24
  222.7 1.4 collective-permute-start.30
  224.6 2.3 out_projection.7
  227.0 9.0 %collective-permute-done.24.refs_6_.refs_4_ = bf16[128,2176]{1,0:T(8,128)(2,1)S(1)} collective-permute-done((bf16[128,2176]{1,0:T(8,128)(2,1)S(1)}, bf16[128,2176]{1,0:T(8,128)(2,1)S(1)}, u32[]{:S(2)}, u32[]{:S(2)}) %collective-permute-start.24) | collective-permute-done | bytes 557088 | tf_op jit(solution)/shard_map/projections/ppermute | solution.py:411
  236.0 1.6 collective-permute-done.32.refs_7_
  237.6 11.2 %collective-permute-done.30.refs_4_ = bf16[128,2176]{1,0:T(8,128)(2,1)S(1)} collective-permute-done((bf16[128,2176]{1,0:T(8,128)(2,1)S(1)}, bf16[128,2176]{1,0:T(8,128)(2,1)S(1)}, u32[]{:S(2)}, u32[]{:S(2)}) %collective-permute-start.30) | collective-permute-done | bytes 557088 | tf_op jit(solution)/shard_map/projections/ppermute | solution.py:411
  248.8 1.3 cache_projection.6
  250.5 1.6 collective-permute-start.34
  252.1 1.5 collective-permute-done.14.refs_1_
  253.6 10.5 %collective-permute-done.33.refs_5_ = bf16[128,2176]{1,0:T(8,128)(2,1)S(1)} collective-permute-done((bf16[128,2176]{1,0:T(8,128)(2,1)S(1)}, bf16[128,2176]{1,0:T(8,128)(2,1)S(1)}, u32[]{:S(2)}, u32[]{:S(2)}) %collective-permute-start.33) | collective-permute-done | bytes 557088 | tf_op jit(solution)/shard_map/projections/ppermute | solution.py:411
  264.4 2.4 cache_projection.7
  (125 shorter events, 13.3 us)
Async XLA Ops:
  7.2 5.0 %copy-start.10 = (bf16[256,4096]{1,0:T(8,128)(2,1)S(1)}, bf16[256,4096]{1,0:T(8,128)(2,1)}, u32[]{:S(2)}) copy-start(bf16[256,4096]{1,0:T(8,128)(2,1)} %refs_1_.5) | copy-start | bytes 6291460
  7.2 47.2 %all-gather.3.cloned.1.call-start = ((), (), s32[]{:S(2)}) async-start(), calls=%async_computation.3 | async-start | bytes 2621440 | tf_op jit(solution)/shard_map/kv_weight_gather/all_gather | solution.py:433
  9.2 1.2 copy-start.27
  12.1 7.1 %copy-start.34 = (bf16[128,512]{1,0:T(8,128)(2,1)}, bf16[128,512]{1,0:T(8,128)(2,1)S(1)}, u32[]{:S(2)}) copy-start(bf16[128,512]{1,0:T(8,128)(2,1)S(1)} %get-tuple-element.31) | copy-start | bytes 393220
  12.1 1.6 copy-start.12
  19.2 4.8 %copy-start.33 = (bf16[128,512]{1,0:T(8,128)(2,1)S(1)}, bf16[128,512]{1,0:T(8,128)(2,1)}, u32[]{:S(2)}) copy-start(bf16[128,512]{1,0:T(8,128)(2,1)} %copy-done.32) | copy-start | bytes 393220
  19.2 26.6 %all-to-all-start = ((bf16[8,576,128]{2,1,0:T(8,128)(2,1)}), bf16[8,576,128]{2,1,0:T(8,128)(2,1)}, u32[]{:S(2)}, u32[]{:S(2)}) async-start(bf16[8,576,128]{2,1,0:T(8,128)(2,1)} %local_states.1.refs_1_), calls=%async_computation | async-start | bytes 2359296 | tf_op jit(solution)/shard_map/state_scan/all_to_all | solution.py:444
  23.6 156.6 %all-gather.5.cloned.1.call-start = ((), (), s32[]{:S(2)}) async-start(), calls=%async_computation.4 | async-start | bytes 5242880 | tf_op jit(solution)/shard_map/out_weight_gather/all_gather | solution.py:460
  23.6 3.8 %collective-permute-start.3 = (bf16[128,512]{1,0:T(8,128)(2,1)}, bf16[128,512]{1,0:T(8,128)(2,1)S(1)}, u32[]{:S(2)}, u32[]{:S(2)}) collective-permute-start(bf16[128,512]{1,0:T(8,128)(2,1)} %copy-done.34), channel_id=1, source_target_pairs={{0,1},{1,0},{2,3},{3,2},{4,5},{5,4},{6,7},{7,6},{8,9},{9,8},{10,11... | collective-permute-start | bytes 393224 | tf_op jit(solution)/shard_map/out_weight_gather/ppermute | solution.py:411
  24.0 18.7 %collective-permute-start.4 = (bf16[128,512]{1,0:T(8,128)(2,1)S(1)}, bf16[128,512]{1,0:T(8,128)(2,1)S(1)}, u32[]{:S(2)}, u32[]{:S(2)}) collective-permute-start(bf16[128,512]{1,0:T(8,128)(2,1)S(1)} %copy-done.33), channel_id=1, source_target_pairs={{0,2},{1,3},{2,0},{3,1},{4,6},{5,7},{6,4},{7,5},{8,10},{9,11},{10,... | collective-permute-start | bytes 393224 | tf_op jit(solution)/shard_map/out_weight_gather/ppermute | solution.py:411
  25.6 22.4 %collective-permute-start.5 = (bf16[128,512]{1,0:T(8,128)(2,1)}, bf16[128,512]{1,0:T(8,128)(2,1)}, u32[]{:S(2)}, u32[]{:S(2)}) collective-permute-start(bf16[128,512]{1,0:T(8,128)(2,1)} %get-tuple-element.33), channel_id=1, source_target_pairs={{0,3},{1,2},{2,1},{3,0},{4,7},{5,6},{6,5},{7,4},{8,11},{9,10},{10,... | collective-permute-start | bytes 393224 | tf_op jit(solution)/shard_map/out_weight_gather/ppermute | solution.py:411
  25.6 22.4 %collective-permute-start.6 = (bf16[128,512]{1,0:T(8,128)(2,1)}, bf16[128,512]{1,0:T(8,128)(2,1)}, u32[]{:S(2)}, u32[]{:S(2)}) collective-permute-start(bf16[128,512]{1,0:T(8,128)(2,1)} %get-tuple-element.34), channel_id=1, source_target_pairs={{0,4},{1,5},{2,6},{3,7},{4,0},{5,1},{6,2},{7,3},{8,12},{9,13},{10,... | collective-permute-start | bytes 393224 | tf_op jit(solution)/shard_map/out_weight_gather/ppermute | solution.py:411
  27.4 20.8 %collective-permute-start.7 = (bf16[128,512]{1,0:T(8,128)(2,1)}, bf16[128,512]{1,0:T(8,128)(2,1)}, u32[]{:S(2)}, u32[]{:S(2)}) collective-permute-start(bf16[128,512]{1,0:T(8,128)(2,1)} %get-tuple-element.35), channel_id=1, source_target_pairs={{0,5},{1,4},{2,7},{3,6},{4,1},{5,0},{6,3},{7,2},{8,13},{9,12},{10,... | collective-permute-start | bytes 393224 | tf_op jit(solution)/shard_map/out_weight_gather/ppermute | solution.py:411
  27.4 18.4 %copy-start.28 = (bf16[128,512]{1,0:T(8,128)(2,1)}, bf16[128,512]{1,0:T(8,128)(2,1)S(1)}, u32[]{:S(2)}) copy-start(bf16[128,512]{1,0:T(8,128)(2,1)S(1)} %collective-permute-done.3.refs_2_) | copy-start | bytes 393220
  27.5 21.9 %collective-permute-start.8 = (bf16[128,512]{1,0:T(8,128)(2,1)}, bf16[128,512]{1,0:T(8,128)(2,1)}, u32[]{:S(2)}, u32[]{:S(2)}) collective-permute-start(bf16[128,512]{1,0:T(8,128)(2,1)} %get-tuple-element.36), channel_id=1, source_target_pairs={{0,6},{1,7},{2,4},{3,5},{4,2},{5,3},{6,0},{7,1},{8,14},{9,15},{10,... | collective-permute-start | bytes 393224 | tf_op jit(solution)/shard_map/out_weight_gather/ppermute | solution.py:411
  43.3 7.9 %collective-permute-start.9 = (bf16[128,512]{1,0:T(8,128)(2,1)}, bf16[128,512]{1,0:T(8,128)(2,1)}, u32[]{:S(2)}, u32[]{:S(2)}) collective-permute-start(bf16[128,512]{1,0:T(8,128)(2,1)} %get-tuple-element.37), channel_id=1, source_target_pairs={{0,7},{1,6},{2,5},{3,4},{4,3},{5,2},{6,1},{7,0},{8,15},{9,14},{10,... | collective-permute-start | bytes 393224 | tf_op jit(solution)/shard_map/out_weight_gather/ppermute | solution.py:411
  43.7 1.6 copy-start.21
  58.4 1.3 copy-start.4
  59.8 39.7 %all-to-all-start.1 = ((bf16[8,256,512]{2,1,0:T(8,128)(2,1)}), bf16[8,256,512]{2,1,0:T(8,128)(2,1)S(1)}, u32[]{:S(2)}, u32[]{:S(2)}) async-start(bf16[8,256,512]{2,1,0:T(8,128)(2,1)} %copy-done.4), calls=%async_computation.1 | async-start | bytes 4194304 | tf_op jit(solution)/shard_map/residual_exchange/all_to_all | solution.py:451
  63.5 20.8 %collective-permute-start = (bf16[4,144,128]{2,1,0:T(8,128)(2,1)S(1)}, bf16[4,144,128]{2,1,0:T(8,128)(2,1)S(1)}, u32[]{:S(2)}, u32[]{:S(2)}) collective-permute-start(bf16[4,144,128]{2,1,0:T(8,128)(2,1)S(1)} %plane_total.1.refs_6_.refs_1_.refs_10_), channel_id=1, source_target_pairs={{0,8},{1,9},{2,10},{3,11},{4,12},{5,13},{6,14},{7,15},{8,16},{9,17... | collective-permute-start | bytes 442376 | tf_op jit(solution)/shard_map/state_scan/ppermute | solution.py:418
  64.8 34.6 %collective-permute-start.1 = (bf16[4,144,128]{2,1,0:T(8,128)(2,1)S(1)}, bf16[4,144,128]{2,1,0:T(8,128)(2,1)}, u32[]{:S(2)}, u32[]{:S(2)}) collective-permute-start(bf16[4,144,128]{2,1,0:T(8,128)(2,1)S(1)} %plane_total.1.refs_6_.refs_1_.refs_10_), channel_id=1, source_target_pairs={{0,16},{1,17},{2,18},{3,19},{4,20},{5,21},{6,22},{7,23},{8,24},{9,... | collective-permute-start | bytes 442376 | tf_op jit(solution)/shard_map/state_scan/ppermute | solution.py:418
  66.1 33.3 %collective-permute-start.2 = (bf16[4,144,128]{2,1,0:T(8,128)(2,1)S(1)}, bf16[4,144,128]{2,1,0:T(8,128)(2,1)}, u32[]{:S(2)}, u32[]{:S(2)}) collective-permute-start(bf16[4,144,128]{2,1,0:T(8,128)(2,1)S(1)} %plane_total.1.refs_6_.refs_1_.refs_10_), channel_id=1, source_target_pairs={{0,24},{1,25},{2,26},{3,27},{4,28},{5,29},{6,30},{7,31}} | collective-permute-start | bytes 442376 | tf_op jit(solution)/shard_map/state_scan/ppermute | solution.py:418
  67.5 1.8 copy-start.11
  69.3 1.8 copy-start.13
  71.0 1.6 copy-start.14
  72.6 1.6 copy-start.22
  80.8 2.0 copy-start.5
  82.8 1.4 copy-start.19
  99.4 2.3 copy-start.6
  101.7 3.0 %copy-start.9 = (bf16[1024,512]{1,0:T(8,128)(2,1)S(1)}, bf16[1024,512]{1,0:T(8,128)(2,1)}, u32[]{:S(2)}) copy-start(bf16[1024,512]{1,0:T(8,128)(2,1)} %copy-done.8) | copy-start | bytes 3145732
  101.7 22.6 %copy-start.15 = (bf16[256,4096]{1,0:T(8,128)(2,1)S(1)}, bf16[256,4096]{1,0:T(8,128)(2,1)}, u32[]{:S(2)}) copy-start(bf16[256,4096]{1,0:T(8,128)(2,1)} %refs_0_.7) | copy-start | bytes 6291460
  101.7 22.6 %copy-start.20 = (bf16[256,4096]{1,0:T(8,128)(2,1)S(1)}, bf16[256,4096]{1,0:T(8,128)(2,1)}, u32[]{:S(2)}) copy-start(bf16[256,4096]{1,0:T(8,128)(2,1)} %copy-done.19) | copy-start | bytes 6291460
  104.7 19.5 %copy-start.7 = (f32[256,4096]{1,0:T(8,128)S(1)}, f32[256,4096]{1,0:T(8,128)}, u32[]{:S(2)}) copy-start(f32[256,4096]{1,0:T(8,128)} %copy-done.5) | copy-start | bytes 12582916
  124.2 55.9 %copy-start.35 = (bf16[4096]{0:T(1024)(128)(2,1)S(1)}, bf16[4096]{0:T(1024)(128)(2,1)}, u32[]{:S(2)}) copy-start(bf16[4096]{0:T(1024)(128)(2,1)} %param.16) | copy-start | bytes 24580
  130.2 24.5 %collective-permute-start.12 = (bf16[128,4096]{1,0:T(8,128)(2,1)S(1)}, bf16[128,4096]{1,0:T(8,128)(2,1)}, u32[]{:S(2)}, u32[]{:S(2)}) collective-permute-start(bf16[128,4096]{1,0:T(8,128)(2,1)S(1)} %get-tuple-element.38.refs_1_.refs_0_), channel_id=1, source_target_pairs={{0,2},{1,3},{2,0},{3,1},{4,6},{5,7},{6,4},{7,5},{8,10},{9,11},{10,... | collective-permute-start | bytes 3145736 | tf_op jit(solution)/shard_map/projections/ppermute | solution.py:411
  130.7 25.1 %collective-permute-start.13 = (bf16[128,4096]{1,0:T(8,128)(2,1)}, bf16[128,4096]{1,0:T(8,128)(2,1)}, u32[]{:S(2)}, u32[]{:S(2)}) collective-permute-start(bf16[128,4096]{1,0:T(8,128)(2,1)} %get-tuple-element.39.refs_3_.refs_0_), channel_id=1, source_target_pairs={{0,4},{1,5},{2,6},{3,7},{4,0},{5,1},{6,2},{7,3},{8,12},{9,13},{10,... | collective-permute-start | bytes 3145736 | tf_op jit(solution)/shard_map/projections/ppermute | solution.py:411
  131.3 25.3 %collective-permute-start.10 = (bf16[128,4096]{1,0:T(8,128)(2,1)S(1)}, bf16[128,4096]{1,0:T(8,128)(2,1)S(1)}, u32[]{:S(2)}, u32[]{:S(2)}) collective-permute-start(bf16[128,4096]{1,0:T(8,128)(2,1)S(1)} %get-tuple-element.38.refs_1_.refs_0_), channel_id=1, source_target_pairs={{0,1},{1,0},{2,3},{3,2},{4,5},{5,4},{6,7},{7,6},{8,9},{9,8},{10,11... | collective-permute-start | bytes 3145736 | tf_op jit(solution)/shard_map/projections/ppermute | solution.py:411
  132.3 25.8 %collective-permute-start.11 = (bf16[128,4096]{1,0:T(8,128)(2,1)}, bf16[128,4096]{1,0:T(8,128)(2,1)S(1)}, u32[]{:S(2)}, u32[]{:S(2)}) collective-permute-start(bf16[128,4096]{1,0:T(8,128)(2,1)} %get-tuple-element.39.refs_3_.refs_0_), channel_id=1, source_target_pairs={{0,1},{1,0},{2,3},{3,2},{4,5},{5,4},{6,7},{7,6},{8,9},{9,8},{10,11... | collective-permute-start | bytes 3145736 | tf_op jit(solution)/shard_map/projections/ppermute | solution.py:411
  154.6 23.6 %collective-permute-start.19 = (bf16[128,4096]{1,0:T(8,128)(2,1)}, bf16[128,4096]{1,0:T(8,128)(2,1)S(1)}, u32[]{:S(2)}, u32[]{:S(2)}) collective-permute-start(bf16[128,4096]{1,0:T(8,128)(2,1)} %collective-permute-done.12.refs_7_.refs_1_), channel_id=1, source_target_pairs={{0,4},{1,5},{2,6},{3,7},{4,0},{5,1},{6,2},{7,3},{8,12},{9,13},{10,... | collective-permute-start | bytes 3145736 | tf_op jit(solution)/shard_map/projections/ppermute | solution.py:411
  155.9 24.2 %collective-permute-start.21 = (bf16[128,4096]{1,0:T(8,128)(2,1)}, bf16[128,4096]{1,0:T(8,128)(2,1)}, u32[]{:S(2)}, u32[]{:S(2)}) collective-permute-start(bf16[128,4096]{1,0:T(8,128)(2,1)} %collective-permute-done.13.refs_8_.refs_3_), channel_id=1, source_target_pairs={{0,2},{1,3},{2,0},{3,1},{4,6},{5,7},{6,4},{7,5},{8,10},{9,11},{10,... | collective-permute-start | bytes 3145736 | tf_op jit(solution)/shard_map/projections/ppermute | solution.py:411
  156.6 46.8 %collective-permute-start.15 = (bf16[512,2048]{1,0:T(8,128)(2,1)}, bf16[512,2048]{1,0:T(8,128)(2,1)}, u32[]{:S(2)}, u32[]{:S(2)}) collective-permute-start(bf16[512,2048]{1,0:T(8,128)(2,1)} %all-gather.3.cloned.1.call-done.refs_9_), channel_id=1, source_target_pairs={{0,1},{1,0},{2,3},{3,2},{4,5},{5,4},{6,7},{7,6},{8,9},{9,8},{10,11... | collective-permute-start | bytes 6291464 | tf_op jit(solution)/shard_map/cache_weight/ppermute | solution.py:411
  157.5 32.2 %collective-permute-start.16 = (bf16[128,4096]{1,0:T(8,128)(2,1)}, bf16[128,4096]{1,0:T(8,128)(2,1)}, u32[]{:S(2)}, u32[]{:S(2)}) collective-permute-start(bf16[128,4096]{1,0:T(8,128)(2,1)} %collective-permute-done.12.refs_7_.refs_1_), channel_id=1, source_target_pairs={{0,1},{1,0},{2,3},{3,2},{4,5},{5,4},{6,7},{7,6},{8,9},{9,8},{10,11... | collective-permute-start | bytes 3145736 | tf_op jit(solution)/shard_map/projections/ppermute | solution.py:411
  159.1 30.7 %collective-permute-start.17 = (bf16[128,4096]{1,0:T(8,128)(2,1)}, bf16[128,4096]{1,0:T(8,128)(2,1)}, u32[]{:S(2)}, u32[]{:S(2)}) collective-permute-start(bf16[128,4096]{1,0:T(8,128)(2,1)} %collective-permute-done.13.refs_8_.refs_3_), channel_id=1, source_target_pairs={{0,1},{1,0},{2,3},{3,2},{4,5},{5,4},{6,7},{7,6},{8,9},{9,8},{10,11... | collective-permute-start | bytes 3145736 | tf_op jit(solution)/shard_map/projections/ppermute | solution.py:411
  178.3 20.3 %collective-permute-start.20 = (bf16[128,4096]{1,0:T(8,128)(2,1)S(1)}, bf16[128,4096]{1,0:T(8,128)(2,1)}, u32[]{:S(2)}, u32[]{:S(2)}) collective-permute-start(bf16[128,4096]{1,0:T(8,128)(2,1)S(1)} %collective-permute-done.19.refs_1_.refs_2_), channel_id=1, source_target_pairs={{0,1},{1,0},{2,3},{3,2},{4,5},{5,4},{6,7},{7,6},{8,9},{9,8},{10,11... | collective-permute-start | bytes 3145736 | tf_op jit(solution)/shard_map/projections/ppermute | solution.py:411
  180.1 18.5 %collective-permute-start.22 = (bf16[128,4096]{1,0:T(8,128)(2,1)}, bf16[128,4096]{1,0:T(8,128)(2,1)}, u32[]{:S(2)}, u32[]{:S(2)}) collective-permute-start(bf16[128,4096]{1,0:T(8,128)(2,1)} %collective-permute-done.21.refs_3_), channel_id=1, source_target_pairs={{0,1},{1,0},{2,3},{3,2},{4,5},{5,4},{6,7},{7,6},{8,9},{9,8},{10,11... | collective-permute-start | bytes 3145736 | tf_op jit(solution)/shard_map/projections/ppermute | solution.py:411
  180.1 2.2 copy-start.2
  182.3 1.2 copy-start.17
  186.0 3.7 %copy-start.3 = (bf16[4096,512]{1,0:T(8,128)(2,1)S(1)}, bf16[4096,512]{1,0:T(8,128)(2,1)}, u32[]{:S(2)}) copy-start(bf16[4096,512]{1,0:T(8,128)(2,1)} %all-gather.5.cloned.1.call-done.refs_5_) | copy-start | bytes 12582916
  189.7 4.6 %copy-start.18 = (bf16[128,4096]{1,0:T(8,128)(2,1)S(1)}, bf16[128,4096]{1,0:T(8,128)(2,1)}, u32[]{:S(2)}) copy-start(bf16[128,4096]{1,0:T(8,128)(2,1)} %copy-done.16) | copy-start | bytes 3145732
  194.4 25.6 %collective-permute-start.27 = (bf16[128,4096]{1,0:T(8,128)(2,1)S(1)}, bf16[128,4096]{1,0:T(8,128)(2,1)S(1)}, u32[]{:S(2)}, u32[]{:S(2)}) collective-permute-start(bf16[128,4096]{1,0:T(8,128)(2,1)S(1)} %hold.10), channel_id=1, source_target_pairs={{0,4},{1,5},{2,6},{3,7},{4,0},{5,1},{6,2},{7,3},{8,12},{9,13},{10,... | collective-permute-start | bytes 3145736 | tf_op jit(solution)/shard_map/projections/ppermute | solution.py:411
  194.8 25.5 %collective-permute-start.25 = (bf16[128,4096]{1,0:T(8,128)(2,1)}, bf16[128,4096]{1,0:T(8,128)(2,1)S(1)}, u32[]{:S(2)}, u32[]{:S(2)}) collective-permute-start(bf16[128,4096]{1,0:T(8,128)(2,1)} %hold.8), channel_id=1, source_target_pairs={{0,2},{1,3},{2,0},{3,1},{4,6},{5,7},{6,4},{7,5},{8,10},{9,11},{10,... | collective-permute-start | bytes 3145736 | tf_op jit(solution)/shard_map/projections/ppermute | solution.py:411
  202.8 2.6 collective-permute-start.23
  202.9 3.8 %collective-permute-start.18 = (bf16[256,512]{1,0:T(8,128)(2,1)S(1)}, bf16[256,512]{1,0:T(8,128)(2,1)S(1)}, u32[]{:S(2)}, u32[]{:S(2)}) collective-permute-start(bf16[256,512]{1,0:T(8,128)(2,1)S(1)} %get-tuple-element.43), channel_id=1, source_target_pairs={{0,1},{1,0},{2,3},{3,2},{4,5},{5,4},{6,7},{7,6},{8,9},{9,8},{10,11... | collective-permute-start | bytes 786440 | tf_op jit(solution)/shard_map/projections/ppermute | solution.py:411
  220.0 4.1 %collective-permute-start.28 = (bf16[128,4096]{1,0:T(8,128)(2,1)S(1)}, bf16[128,4096]{1,0:T(8,128)(2,1)S(1)}, u32[]{:S(2)}, u32[]{:S(2)}) collective-permute-start(bf16[128,4096]{1,0:T(8,128)(2,1)S(1)} %hold.11.refs_3_), channel_id=1, source_target_pairs={{0,1},{1,0},{2,3},{3,2},{4,5},{5,4},{6,7},{7,6},{8,9},{9,8},{10,11... | collective-permute-start | bytes 3145736 | tf_op jit(solution)/shard_map/projections/ppermute | solution.py:411
  220.4 4.2 %collective-permute-start.26 = (bf16[128,4096]{1,0:T(8,128)(2,1)S(1)}, bf16[128,4096]{1,0:T(8,128)(2,1)S(1)}, u32[]{:S(2)}, u32[]{:S(2)}) collective-permute-start(bf16[128,4096]{1,0:T(8,128)(2,1)S(1)} %hold.9.refs_1_), channel_id=1, source_target_pairs={{0,1},{1,0},{2,3},{3,2},{4,5},{5,4},{6,7},{7,6},{8,9},{9,8},{10,11... | collective-permute-start | bytes 3145736 | tf_op jit(solution)/shard_map/projections/ppermute | solution.py:411
  220.5 15.4 %collective-permute-start.24 = (bf16[128,2176]{1,0:T(8,128)(2,1)S(1)}, bf16[128,2176]{1,0:T(8,128)(2,1)S(1)}, u32[]{:S(2)}, u32[]{:S(2)}) collective-permute-start(bf16[128,2176]{1,0:T(8,128)(2,1)S(1)} %get-tuple-element.47.refs_1_), channel_id=1, source_target_pairs={{0,2},{1,3},{2,0},{3,1},{4,6},{5,7},{6,4},{7,5},{8,10},{9,11},{10,... | collective-permute-start | bytes 1671176 | tf_op jit(solution)/shard_map/projections/ppermute | solution.py:411
  222.1 15.5 %collective-permute-start.32 = (bf16[128,2176]{1,0:T(8,128)(2,1)S(1)}, bf16[128,2176]{1,0:T(8,128)(2,1)S(1)}, u32[]{:S(2)}, u32[]{:S(2)}) collective-permute-start(bf16[128,2176]{1,0:T(8,128)(2,1)S(1)} %get-tuple-element.51), channel_id=1, source_target_pairs={{0,4},{1,5},{2,6},{3,7},{4,0},{5,1},{6,2},{7,3},{8,12},{9,13},{10,... | collective-permute-start | bytes 1671176 | tf_op jit(solution)/shard_map/projections/ppermute | solution.py:411
  222.7 26.1 %collective-permute-start.30 = (bf16[128,2176]{1,0:T(8,128)(2,1)S(1)}, bf16[128,2176]{1,0:T(8,128)(2,1)S(1)}, u32[]{:S(2)}, u32[]{:S(2)}) collective-permute-start(bf16[128,2176]{1,0:T(8,128)(2,1)S(1)} %get-tuple-element.50), channel_id=1, source_target_pairs={{0,4},{1,5},{2,6},{3,7},{4,0},{5,1},{6,2},{7,3},{8,12},{9,13},{10,... | collective-permute-start | bytes 1671176 | tf_op jit(solution)/shard_map/projections/ppermute | solution.py:411
  224.1 24.7 %collective-permute-start.31 = (bf16[128,2176]{1,0:T(8,128)(2,1)S(1)}, bf16[128,2176]{1,0:T(8,128)(2,1)S(1)}, u32[]{:S(2)}, u32[]{:S(2)}) collective-permute-start(bf16[128,2176]{1,0:T(8,128)(2,1)S(1)} %get-tuple-element.46.refs_4_), channel_id=1, source_target_pairs={{0,2},{1,3},{2,0},{3,1},{4,6},{5,7},{6,4},{7,5},{8,10},{9,11},{10,... | collective-permute-start | bytes 1671176 | tf_op jit(solution)/shard_map/projections/ppermute | solution.py:411
  226.9 21.9 %collective-permute-start.29 = (bf16[256,512]{1,0:T(8,128)(2,1)S(1)}, bf16[256,512]{1,0:T(8,128)(2,1)S(1)}, u32[]{:S(2)}, u32[]{:S(2)}) collective-permute-start(bf16[256,512]{1,0:T(8,128)(2,1)S(1)} %get-tuple-element.49), channel_id=1, source_target_pairs={{0,1},{1,0},{2,3},{3,2},{4,5},{5,4},{6,7},{7,6},{8,9},{9,8},{10,11... | collective-permute-start | bytes 786440 | tf_op jit(solution)/shard_map/projections/ppermute | solution.py:411
  250.1 14.0 %collective-permute-start.33 = (bf16[128,2176]{1,0:T(8,128)(2,1)S(1)}, bf16[128,2176]{1,0:T(8,128)(2,1)S(1)}, u32[]{:S(2)}, u32[]{:S(2)}) collective-permute-start(bf16[128,2176]{1,0:T(8,128)(2,1)S(1)} %get-tuple-element.52), channel_id=1, source_target_pairs={{0,2},{1,3},{2,0},{3,1},{4,6},{5,7},{6,4},{7,5},{8,10},{9,11},{10,... | collective-permute-start | bytes 1671176 | tf_op jit(solution)/shard_map/projections/ppermute | solution.py:411
  250.5 14.0 %collective-permute-start.34 = (bf16[128,2176]{1,0:T(8,128)(2,1)S(1)}, bf16[128,2176]{1,0:T(8,128)(2,1)S(1)}, u32[]{:S(2)}, u32[]{:S(2)}) collective-permute-start(bf16[128,2176]{1,0:T(8,128)(2,1)S(1)} %get-tuple-element.53), channel_id=1, source_target_pairs={{0,4},{1,5},{2,6},{3,7},{4,0},{5,1},{6,2},{7,3},{8,12},{9,13},{10,... | collective-permute-start | bytes 1671176 | tf_op jit(solution)/shard_map/projections/ppermute | solution.py:411
  252.1 14.8 %copy-start.1 = (f32[256,32]{0,1:T(8,128)S(1)}, f32[256,32]{0,1:T(8,128)}, u32[]{:S(2)}) copy-start(f32[256,32]{0,1:T(8,128)} %param.14) | copy-start | bytes 98308
  252.1 1.5 collective-permute-start.14
  (11 other events, 10.3 us)
Sparse Core Ops, SparseCore 0:
  9.6 44.7 all-gather.2
  58.6 91.3 all-gather.4

commit v3 on v2

--- a/solution.py
+++ b/solution.py
@@ -15,7 +15,9 @@
 DECAY_ROWS = 16
 PLANE = ("y", "x", "c")
 SEQ = ("z", "y", "x", "c")
-VMEM_LIMIT = 16 * 1024 * 1024
+MIB = 1024 * 1024
+VMEM_STREAMED = {"local_states": 60 * MIB, "local_intra": 54 * MIB, "mix": 16 * MIB}
+VMEM_RESIDENT = 16 * MIB
 
 
 def split_rows(total):
@@ -63,7 +65,8 @@
         scores = dot(query_ref[:, columns], key_ref[:, columns], ((1,), (1,)))
         spread = within[:, head : head + 1] - across[head : head + 1, :]
         weighted = jnp.where(lower, scores * jnp.exp(jnp.where(lower, spread, 0.0)), 0.0)
-        out_ref[:, columns] = dot(weighted.astype(BF16), value_ref[:, columns], ((1,), (0,)))
+        local = dot(weighted.astype(BF16), value_ref[:, columns], ((1,), (0,)))
+        out_ref[:, columns] = local.astype(BF16)
         gate = gate_ref[:, columns].astype(F32)
         open_ref[:, columns] = (gate / (1.0 + jnp.exp(-gate))).astype(BF16)
 
@@ -74,7 +77,7 @@
     for head in range(state_ref.shape[0]):
         columns = slice(head * width, (head + 1) * width)
         carried = dot(query_ref[:, columns], state_ref[head], ((1,), (0,)))
-        retained = intra_ref[:, columns] + reach[:, head : head + 1] * carried
+        retained = intra_ref[:, columns].astype(F32) + reach[:, head : head + 1] * carried
         scale = lax.rsqrt(jnp.mean(retained * retained, axis=1, keepdims=True) + NORM_EPS)
         mixed = (open_ref[:, columns].astype(F32) * (retained * scale)).astype(BF16)
         for half, out_ref in enumerate(out_refs):
@@ -82,27 +85,38 @@
 
 
 def total_kernel(width, parts_ref, out_ref):
-    state = jnp.zeros((width, width), F32)
-    total = jnp.zeros((1, width), F32)
-    for place in range(parts_ref.shape[0]):
-        ending = join_rows(parts_ref[place, width:, :])
-        state = jnp.exp(ending) * state + parts_ref[place, :width, :].astype(F32)
-        total = total + ending
-    out_ref[0, :width, :] = state.astype(BF16)
-    out_ref[0, width:, :] = split_rows(total)
-
-
-def prefix_kernel(width, planes, parts_ref, *refs):
-    plane_refs, out_ref = refs[:planes], refs[planes]
-    state = jnp.zeros((width, width), F32)
-    reach = jnp.zeros((1, width), F32)
-    for ref in plane_refs:
-        state = state + jnp.exp(reach) * ref[0, :width, :].astype(F32)
-        reach = reach + join_rows(ref[0, width:, :])
-    for place in range(parts_ref.shape[0]):
-        out_ref[place, 0] = state.astype(BF16)
-        ending = join_rows(parts_ref[place, width:, :])
-        state = jnp.exp(ending) * state + parts_ref[place, :width, :].astype(F32)
+    for head in range(out_ref.shape[0]):
+        top = head * (width + DECAY_ROWS)
+        states, decays = slice(top, top + width), slice(top + width, top + width + DECAY_ROWS)
+        state = jnp.zeros((width, width), F32)
+        total = jnp.zeros((1, width), F32)
+        for place in range(parts_ref.shape[0]):
+            ending = join_rows(parts_ref[place, decays, :])
+            state = jnp.exp(ending) * state + parts_ref[place, states, :].astype(F32)
+            total = total + ending
+        out_ref[head, :width, :] = state.astype(BF16)
+        out_ref[head, width:, :] = split_rows(total)
+
+
+def join_kernel(width, earlier_ref, later_ref, out_ref):
+    for head in range(out_ref.shape[0]):
+        ending = join_rows(later_ref[head, width:, :])
+        state = jnp.exp(ending) * earlier_ref[head, :width, :].astype(F32)
+        out_ref[head, :width, :] = (state + later_ref[head, :width, :].astype(F32)).astype(BF16)
+        out_ref[head, width:, :] = split_rows(join_rows(earlier_ref[head, width:, :]) + ending)
+
+
+def prefix_kernel(width, parts_ref, nearest_ref, others_ref, out_ref):
+    for head in range(nearest_ref.shape[0]):
+        top = head * (width + DECAY_ROWS)
+        states, decays = slice(top, top + width), slice(top + width, top + width + DECAY_ROWS)
+        reach = jnp.exp(join_rows(nearest_ref[head, width:, :]))
+        state = reach * others_ref[head, :width, :].astype(F32)
+        state = state + nearest_ref[head, :width, :].astype(F32)
+        for place in range(parts_ref.shape[0]):
+            out_ref[place, head] = state.astype(BF16)
+            ending = join_rows(parts_ref[place, decays, :])
+            state = jnp.exp(ending) * state + parts_ref[place, states, :].astype(F32)
 
 
 def local_call(
@@ -123,7 +137,29 @@
             scratch_shapes=scratch,
         ),
         out_shape=out_shape,
-        compiler_params=pltpu.CompilerParams(vmem_limit_bytes=VMEM_LIMIT),
+        compiler_params=pltpu.CompilerParams(vmem_limit_bytes=VMEM_STREAMED[name]),
+        name=name,
+    )(*scalars, *operands, *after)
+
+
+def resident(count):
+    return [pl.BlockSpec(memory_space=pltpu.VMEM)] * count
+
+
+def resident_call(name, body, operands, out_shape, scalars=(), after=()):
+    taken = len(scalars) + len(operands)
+
+    def kernel(*refs):
+        body(*refs[:taken], *refs[taken + len(after) :])
+
+    return pl.pallas_call(
+        kernel,
+        in_specs=[pl.BlockSpec(memory_space=pltpu.SMEM)] * len(scalars)
+        + resident(len(operands))
+        + [pl.BlockSpec(memory_space=pltpu.HBM)] * len(after),
+        out_specs=resident(len(out_shape)),
+        out_shape=out_shape,
+        compiler_params=pltpu.CompilerParams(vmem_limit_bytes=VMEM_RESIDENT),
         name=name,
     )(*scalars, *operands, *after)
 
@@ -165,10 +201,7 @@
         (queries, keys, values, gate, within, across),
         (heads, heads, heads, heads, group(tokens, per), group(per, tokens)),
         [heads, heads],
-        [
-            jax.ShapeDtypeStruct(queries.shape, F32),
-            jax.ShapeDtypeStruct(queries.shape, BF16),
-        ],
+        [jax.ShapeDtypeStruct(queries.shape, BF16)] * 2,
         after=after,
     )
 
@@ -195,165 +228,131 @@
 
 
 def plane_total(parts, heads, width, after=()):
-    places, rows = parts.shape[0], width + DECAY_ROWS
-    return local_call(
-        "plane_total",
-        functools.partial(total_kernel, width),
-        heads,
-        (parts,),
-        (pl.BlockSpec((places, rows, width), lambda i: (0, i, 0)),),
-        group(rows, width),
-        jax.ShapeDtypeStruct((heads, rows, width), BF16),
-        after=after,
-    )
-
-
-def plane_prefix(parts, planes, width, after=()):
-    places, (heads, rows, _) = parts.shape[0], planes[0].shape
-    return local_call(
-        "plane_prefix",
-        functools.partial(prefix_kernel, width, len(planes)),
-        heads,
-        (parts, *planes),
-        [pl.BlockSpec((places, rows, width), lambda i: (0, i, 0))]
-        + [group(rows, width)] * len(planes),
-        pl.BlockSpec((places, 1, width, width), lambda i: (0, i, 0, 0)),
-        jax.ShapeDtypeStruct((places, heads, width, width), BF16),
-        after=after,
-    )
-
-
-def deal_kernel(ways, block, place_ref, source_ref, *target_refs):
-    for r, target_ref in enumerate(target_refs):
-        for i in range(target_ref.shape[1] // block):
-            start = pl.multiple_of((i * ways + (place_ref[0] ^ r)) * block, block)
-            target_ref[:, i * block : (i + 1) * block] = source_ref[:, pl.ds(start, block)]
-
-
-def deal(array, place, ways, block, after=()):
-    rows, columns = array.shape
-    return local_call(
+    shape = jax.ShapeDtypeStruct((heads, width + DECAY_ROWS, width), BF16)
+    body = functools.partial(total_kernel, width)
+    return resident_call("plane_total", body, (parts,), [shape], after=after)[0]
+
+
+def join(earlier, later, width, after=()):
+    shape = jax.ShapeDtypeStruct(later.shape, BF16)
+    body = functools.partial(join_kernel, width)
+    return resident_call("join", body, (earlier, later), [shape], after=after)[0]
+
+
+def plane_prefix(parts, nearest, others, width, after=()):
+    shape = jax.ShapeDtypeStruct((parts.shape[0], nearest.shape[0], width, width), BF16)
+    body = functools.partial(prefix_kernel, width)
+    return resident_call("plane_prefix", body, (parts, nearest, others), [shape], after=after)[0]
+
+
+def deal_kernel(ways, block, place_ref, *refs):
+    *source_refs, even_ref, odd_ref = refs
+    for r in range(ways):
+        target_ref, top = (even_ref, odd_ref)[r % 2], 0
+        for source_ref in source_refs:
+            rows = slice(top, top + source_ref.shape[0])
+            for i in range(target_ref.shape[2] // block):
+                start = pl.multiple_of((i * ways + (place_ref[0] ^ r)) * block, block)
+                columns = slice(i * block, (i + 1) * block)
+                target_ref[r // 2, rows, columns] = source_ref[:, pl.ds(start, block)]
+            top += source_ref.shape[0]
+
+
+def deal(arrays, place, ways, block, after=()):
+    rows = sum(array.shape[0] for array in arrays)
+    shape = jax.ShapeDtypeStruct((ways // 2, rows, arrays[0].shape[1] // ways), BF16)
+    return resident_call(
         "deal",
         functools.partial(deal_kernel, ways, block),
-        1,
-        (array,),
-        (whole(rows, columns),),
-        [whole(rows, columns // ways)] * ways,
-        [jax.ShapeDtypeStruct((rows, columns // ways), array.dtype)] * ways,
+        arrays,
+        [shape, shape],
         scalars=(place.reshape(1),),
         after=after,
     )
 
 
-def spread_kernel(block, source_ref, target_ref):
-    ways, _, columns = target_ref.shape
-    for place in range(ways):
-        for i in range(columns // block):
-            start = (i * ways + place) * block
-            target_ref[place, :, i * block : (i + 1) * block] = source_ref[:, start : start + block]
-
-
-def spread(array, ways, block, after=()):
-    rows, columns = array.shape
-    return local_call(
-        "spread",
-        functools.partial(spread_kernel, block),
-        2,
-        (array,),
-        (pl.BlockSpec((rows // 2, columns), lambda i: (i, 0)),),
-        pl.BlockSpec((ways, rows // 2, columns // ways), lambda i: (0, i, 0)),
-        jax.ShapeDtypeStruct((ways, rows, columns // ways), array.dtype),
-        after=after,
-    )
+def pair_kernel(heights, even_ref, odd_ref, *target_refs):
+    chips = even_ref.shape[0]
+    for i, target_ref in enumerate(target_refs):
+        top = sum(heights[: i // chips])
+        rows = slice(top, top + heights[i // chips])
+        target_ref[0] = even_ref[i % chips, rows, :]
+        target_ref[1] = odd_ref[i % chips, rows, :]
+
+
+def pair(even, odd, heights, after=()):
+    chips, _, columns = even.shape
+    shapes = [jax.ShapeDtypeStruct((2, rows, columns), even.dtype) for rows in heights]
+    body = functools.partial(pair_kernel, heights)
+    pairs = resident_call(
+        "pair", body, (even, odd), [s for s in shapes for _ in range(chips)], after=after
+    )
+    return [pairs[i : i + chips] for i in range(0, len(pairs), chips)]
 
 
 def order_kernel(place_ref, *refs):
     *sources, target_ref = refs
-    rows = sources[0].shape[0]
-    for r, source in enumerate(sources):
+    rows = sources[0].shape[1]
+    for r in range(2 * len(sources)):
         start = pl.multiple_of((place_ref[0] ^ r) * rows, rows)
-        target_ref[pl.ds(start, rows), :] = source[...]
+        target_ref[pl.ds(start, rows), :] = sources[r // 2][r % 2]
 
 
 def in_order(arrays, place, after=()):
-    rows, columns = arrays[0].shape
-    tall = (len(arrays) * rows, columns)
-    return local_call(
+    _, rows, columns = arrays[0].shape
+    tall = (2 * len(arrays) * rows, columns)
+    return resident_call(
         "in_order",
         order_kernel,
-        1,
         arrays,
-        [whole(rows, columns)] * len(arrays),
-        whole(*tall),
-        jax.ShapeDtypeStruct(tall, arrays[0].dtype),
+        [jax.ShapeDtypeStruct(tall, arrays[0].dtype)],
         scalars=(place.reshape(1),),
         after=after,
-    )
-
-
-def hold(array, after):
-    kept = pl.BlockSpec(memory_space=pltpu.HBM)
+    )[0]
+
+
+def hold(arrays, after):
+    kept, count = pl.BlockSpec(memory_space=pltpu.HBM), len(arrays)
     return pl.pallas_call(
         lambda *refs: None,
-        in_specs=[kept] * (1 + len(after)),
-        out_specs=kept,
-        out_shape=jax.ShapeDtypeStruct(array.shape, array.dtype),
-        input_output_aliases={0: 0},
-        compiler_params=pltpu.CompilerParams(vmem_limit_bytes=VMEM_LIMIT),
+        in_specs=[kept] * (count + len(after)),
+        out_specs=[kept] * count,
+        out_shape=[jax.ShapeDtypeStruct(array.shape, array.dtype) for array in arrays],
+        input_output_aliases={i: i for i in range(count)},
+        compiler_params=pltpu.CompilerParams(vmem_limit_bytes=VMEM_RESIDENT),
         name="hold",
-    )(array, *after)
-
-
-def resident(count):
-    return [pl.BlockSpec(memory_space=pltpu.VMEM)] * count
-
-
-def out_kernel(chips, halves, place_ref, *refs):
-    pieces = 2 * len(chips)
-    mixed, (weight_ref, start_ref, mine_ref, theirs_ref) = refs[:pieces], refs[pieces:]
+    )(*arrays, *after)
+
+
+def out_kernel(halves, *refs):
+    chips, pieces = len(halves), 2 * len(halves)
+    mixed, weight_ref, start_refs = refs[:pieces], refs[pieces], refs[pieces + 1 : -2]
     tokens, depth = mixed[0].shape
     step = min(depth, 512)
     total = jnp.zeros((pieces * tokens, weight_ref.shape[1]), F32)
     for start in range(0, depth, step):
         left = jnp.concatenate([ref[:, start : start + step] for ref in mixed], axis=0)
         total = total + dot(left, weight_ref[start : start + step, :], ((1,), (0,)))
-    for i in range(pieces):
-        rows = ((place_ref[0] ^ (2 * chips[i // 2] + i % 2)) * 2 + halves[i // 2]) * tokens
-        hidden = start_ref[pl.ds(pl.multiple_of(rows, tokens), tokens), :].astype(F32)
-        hidden = (hidden + total[i * tokens : (i + 1) * tokens]).astype(BF16)
-        (mine_ref, theirs_ref)[i % 2][i // 2 * tokens : (i // 2 + 1) * tokens, :] = hidden
-
-
-def out_projection(place, pieces, weight, start, after=()):
-    chips, halves, mixed = zip(*pieces)
+    for chip in range(chips):
+        rows = slice(halves[chip] * tokens, (halves[chip] + 1) * tokens)
+        for core, out_ref in enumerate(refs[-2:]):
+            i = 2 * chip + core
+            hidden = start_refs[chip][core, rows, :].astype(F32)
+            hidden = hidden + total[i * tokens : (i + 1) * tokens]
+            out_ref[chip * tokens : (chip + 1) * tokens, :] = hidden.astype(BF16)
+
+
+def out_projection(pieces, weight, after=()):
+    halves, mixed, starts = zip(*pieces)
     mixed = [array for cores in mixed for array in cores]
     shape = jax.ShapeDtypeStruct((len(pieces) * mixed[0].shape[0], weight.shape[1]), BF16)
     return resident_call(
         "out_projection",
-        functools.partial(out_kernel, chips, halves),
-        (place.reshape(1),),
-        (*mixed, weight, start),
+        functools.partial(out_kernel, halves),
+        (*mixed, weight, *starts),
         [shape, shape],
-        after,
-    )
-
-
-def resident_call(name, body, scalars, operands, out_shape, after):
-    taken = len(scalars) + len(operands)
-
-    def kernel(*refs):
-        body(*refs[:taken], *refs[taken + len(after) :])
-
-    return pl.pallas_call(
-        kernel,
-        in_specs=[pl.BlockSpec(memory_space=pltpu.SMEM)] * len(scalars)
-        + resident(len(operands))
-        + [pl.BlockSpec(memory_space=pltpu.HBM)] * len(after),
-        out_specs=resident(len(out_shape)),
-        out_shape=out_shape,
-        compiler_params=pltpu.CompilerParams(vmem_limit_bytes=VMEM_LIMIT),
-        name=name,
-    )(*scalars, *operands, *after)
+        after=after,
+    )
 
 
 def cache_kernel(width, model, joined, finish, *refs):
@@ -394,10 +393,9 @@
     return resident_call(
         "cache_projection",
         functools.partial(cache_kernel, width, model, [half for _, half in added], finish),
-        (),
         (own, other, *weights, *[array for array, _ in added]),
         [jax.ShapeDtypeStruct(out, BF16)] * 2,
-        after,
+        after=after,
     )
 
 
@@ -431,38 +429,40 @@
 
     with jax.named_scope("kv_weight_gather"):
         kv_mine = lax.all_gather(kv_weight, "z", axis=0, tiled=True)
-    with jax.named_scope("out_weight_gather"):
-        dealt = deal(out_weight, place, PLACES, piece)
-        pieces = [swap(part, r) if r else part for r, part in enumerate(dealt)]
-
     running = jnp.cumsum(log_decay, axis=0)
     per = heads // PLACES
     within = running.reshape(tokens, PLACES, per).transpose(1, 0, 2)
     across = running.T.reshape(PLACES, per, tokens)
-    states = local_states(keys, values, within, width, after=(dealt[0],))
+    states = local_states(keys, values, within, width)
     with jax.named_scope("state_scan"):
         parts = lax.all_to_all(states, PLANE, 0, 0, tiled=True)
+
+    intra, opened = local_intra(
+        queries, keys, values, gate, within, across, width, after=(states,)
+    )
+    with jax.named_scope("state_scan"):
+        total = plane_total(parts, per, width, after=(intra,))
+        nearest = hop(total, {a: a + 1 for a in range(DEPTH - 1)})
+        joined = join(nearest, total, width)
+        others = hop(joined, {a: a + 2 for a in range(DEPTH - 2)})
+
+    def exchange(pairs):
+        return [swap(part, 2 * chip) if chip else part for chip, part in enumerate(pairs)]
+
+    even, odd = deal((residual, out_weight), place, PLACES, piece, after=(total,))
+    starts, weights = pair(even, swap(odd, 1), (tokens, out_weight.shape[0]))
+    with jax.named_scope("out_weight_gather"):
+        shard = in_order(exchange(weights), place, after=(joined,))
+        out_full = lax.all_gather(*hold((shard,), (kv_mine,)), "z", axis=0, tiled=True)
     with jax.named_scope("residual_exchange"):
-        dealt = spread(residual, PLACES, piece, after=(states,))
+        starts = exchange(hold(starts, (shard,)))
     with jax.named_scope("state_scan"):
-        total = plane_total(parts, per, width, after=(dealt,))
-        earlier = [hop(total, {a: a + d for a in range(DEPTH - d)}) for d in range(1, DEPTH)]
-    with jax.named_scope("residual_exchange"):
-        start = lax.all_to_all(hold(dealt, (total,)), PLANE, 0, 0, tiled=True)
-        start = start.reshape(-1, share)
-    intra, opened = local_intra(
-        queries, keys, values, gate, within, across, width, after=(total,)
-    )
-    with jax.named_scope("state_scan"):
-        prefix = plane_prefix(parts, earlier, width, after=(start, intra))
-    with jax.named_scope("out_weight_gather"):
-        shard = in_order(pieces, place, after=(kv_mine, total))
-        out_full = lax.all_gather(shard, "z", axis=0, tiled=True)
-    with jax.named_scope("state_scan"):
-        entering = lax.all_to_all(hold(prefix, (shard,)), PLANE, 0, 0, tiled=True)
+        prefix = plane_prefix(parts, nearest, others, width, after=(kv_mine, shard))
+        entering = lax.all_to_all(prefix, PLANE, 0, 0, tiled=True)
         entering = entering.reshape(heads, width, width)
 
     early, late = mix(queries, opened, intra, within, entering, width)
+    early, late = hold((early, late), tuple(starts[1:]))
 
     with jax.named_scope("cache_weight"):
         gains = norm_gain.reshape(DEPTH, PLACES, piece)
@@ -472,8 +472,8 @@
             kv_full.append((rows.astype(F32) * gain.astype(F32)).astype(BF16))
 
     def hidden_of(*halves, after=()):
-        pieces = [(chip, half, (mixed, swap(mixed, 1))) for chip, half, mixed in halves]
-        mine, theirs = out_projection(place, pieces, out_full, start, after)
+        pieces = [(half, (mixed, swap(mixed, 1)), starts[chip]) for chip, half, mixed in halves]
+        mine, theirs = out_projection(pieces, out_full, after)
         return mine, swap(theirs, 1)
 
     def share_of(hidden, added=(), finish=False, after=()):
@@ -482,19 +482,18 @@
     with jax.named_scope("projections"):
         early_x, late_y = swap(early, 2), swap(late, 4)
         early_far, late_far = swap(early_x, 4), swap(late_y, 2)
-        home = hidden_of((0, 0, early), (0, 1, late), after=(early_x, late_y))
-        near = hidden_of((1, 0, early_x), (2, 1, late_y), after=(home[0],))
-        late_x = swap(hold(late, (near[0], early_far, late_far)), 2)
-        early_y = swap(hold(early, (near[0], early_far, late_far)), 4)
+        near = hidden_of((1, 0, early_x), (2, 1, late_y))
+        early, late = hold((early, late), (early_far, late_far))
+        late_x, early_y = swap(late, 2), swap(early, 4)
         far = hidden_of((3, 0, early_far), (3, 1, late_far), after=(near[0],))
         early_far, late_far = share_of(far)
         early_x, late_y = share_of(near, after=(early_far,))
-        late_x, early_y = hold(late_x, (early_x,)), hold(early_y, (early_x,))
+        late_x, early_y = hold((late_x, early_y), (early_x,))
         early_x, late_y = swap(early_x, 2), swap(late_y, 4)
+        late_far, early_far = swap(late_far, 4), swap(early_far, 2)
         near = hidden_of((1, 1, late_x), (2, 0, early_y))
-        late_x, early_y = share_of(
-            near, [(swap(late_far, 4), 0), (swap(early_far, 2), 1)], after=(early_x, late_y)
-        )
+        late_x, early_y = share_of(near, [(late_far, 0), (early_far, 1)])
+        home = hidden_of((0, 0, early), (0, 1, late), after=(late_x, early_x, late_y))
         late_x, early_y = swap(late_x, 2), swap(early_y, 4)
         added = [(early_x, 0), (late_x, 1), (early_y, 0), (late_y, 1)]
         return share_of(home, added, True)

time: 275 us -> 241 us (0.88)
  blocking collectives: 19.5 us -> 0 us
  local copies, waits for them, and re-layouts: 31.8 us -> 19.9 us
  waiting for transfers between devices: 125 us -> 119 us
  Pallas kernels: 47 us -> 51.5 us
    all_to_all x1 -> x0, blocking collectives: 19.5 us -> none  [shared_on_device(): entering = lax.all_to_all(hold(prefix, (shard,)), PLANE, 0, 0, tiled=True)]
    ppermute x32, waiting for transfers between devices: 106 us -> 89.9 us  [swap(): return lax.ppermute(array, SEQ, [(i, i ^ distance) for i in range(DEVICES)])]
    unnamed x72 -> x52, local copies, waits for them, and re-layouts: 31.2 us -> 17.6 us
    all_to_all x1, waiting for transfers between devices: 0.01 us -> 12.3 us  [shared_on_device(): entering = lax.all_to_all(prefix, PLANE, 0, 0, tiled=True)]
    pallas_call x8 -> x14, Pallas kernels: 21.1 us -> 27.4 us  [resident_call(): pl.pallas_call(kernel, in_specs=[pl.BlockSpec(memory_space=pltpu.SMEM)] *...]
    all_to_all x1, waiting for transfers between devices: 0.01 us -> 5.8 us  [shared_on_device(): parts = lax.all_to_all(states, PLANE, 0, 0, tiled=True)]
    ppermute x3 -> x2, waiting for transfers between devices: 15.1 us -> 9.63 us  [hop(): return lax.ppermute(array, SEQ, pairs)]
    all_gather x1, waiting for transfers between devices: 3.16 us -> 0.01 us  [shared_on_device(): kv_mine = lax.all_gather(kv_weight, 'z', axis=0, tiled=True)]
  transfers between devices with their start and end apart: 39 -> 38, of which waited for: 17 -> 21; matrix products, arithmetic and copies ran while one was open for 2% -> 3% of each run, Pallas kernels for 15% -> 20%
where the time goes in v3:
time: 241 us; the launch traced here: 240 us
  waiting for transfers between devices  119 us (49%)
  Pallas kernels  51.5 us (21%)
  starting transfers between devices  30.2 us (13%)
  local copies, waits for them, and re-layouts  19.9 us (8%)
  between operations  14.4 us (6%)
  other arithmetic  4.77 us (2%)
    ppermute x32, waiting for transfers between devices, swap(): return lax.ppermute(array, SEQ, [(i, i ^ distance) for i in range(DEVICES)])  89.9 us
    pallas_call x14, Pallas kernels, resident_call(): pl.pallas_call(kernel, in_specs=[pl.BlockSpec(memory_space=pltpu.SMEM)] *...  27.4 us
    pallas_call x3, Pallas kernels, local_call(): pl.pallas_call(kernel, grid_spec=pltpu.PrefetchScalarGridSpec(num_scalar_...  24 us
    ppermute x32, starting transfers between devices, swap(): return lax.ppermute(array, SEQ, [(i, i ^ distance) for i in range(DEVICES)])  20.3 us
    unnamed x52, local copies, waits for them, and re-layouts  17.6 us
    all_to_all x1, waiting for transfers between devices, shared_on_device(): entering = lax.all_to_all(prefix, PLANE, 0, 0, tiled=True)  12.3 us
    ppermute x2, waiting for transfers between devices, hop(): return lax.ppermute(array, SEQ, pairs)  9.63 us
    all_to_all x1, waiting for transfers between devices, shared_on_device(): parts = lax.all_to_all(states, PLANE, 0, 0, tiled=True)  5.8 us
  transfers between devices with their start and end apart: 38, of which 21 were waited for; matrix products, arithmetic and copies ran while one was open for 3% of the time, Pallas kernels for 20%

profile of v3, /device:TPU:24, one launch (start us, length us, event | category | flops | bytes accessed | tf_op | source)
XLA Modules:
  0.0 239.7 jit_solution(17438928390429702534)
XLA Ops:
  8.8 1.4 copy.26
  10.2 7.9 %local_states.1.refs_6_ = bf16[8,576,128]{2,1,0:T(8,128)(2,1)} custom-call(bf16[256,4096]{1,0:T(8,128)(2,1)} %refs_1_.4, bf16[256,4096]{1,0:T(8,128)(2,1)} %refs_2_.2, f32[8,256,4]{2,1,0:T(8,128)} %bitcast.21), custom_call_target="tpu_custom_call" | custom-call | tf_op jit(solution)/shard_map/local_states/pallas_call | solution.py:130
  18.1 3.7 %all-to-all-start = ((bf16[8,576,128]{2,1,0:T(8,128)(2,1)}), bf16[8,576,128]{2,1,0:T(8,128)(2,1)S(1)}, u32[]{:S(2)}, u32[]{:S(2)}) async-start(bf16[8,576,128]{2,1,0:T(8,128)(2,1)} %local_states.1.refs_6_), calls=%async_computation | async-start | bytes 2359296 | tf_op jit(solution)/shard_map/state_scan/all_to_all | solution.py:438
  22.6 10.3 %local_intra.1 = (bf16[256,4096]{1,0:T(8,128)(2,1)}, bf16[256,4096]{1,0:T(8,128)(2,1)}) custom-call(bf16[256,4096]{1,0:T(8,128)(2,1)} %refs_0_.5, bf16[256,4096]{1,0:T(8,128)(2,1)} %refs_1_.4, bf16[256,4096]{1,0:T(8,128)(2,1)} %refs_2_.2, bf16[256,4096]{1,0:T(8,128)(2,1)} %refs_3_.1, f32[8,256,4]{2,1,0:T(8,128)} %bitcast.22, ...), custom_call_target="tpu_custom_call" | custom-call | tf_op jit(solution)/shard_map/local_intra/pallas_call | solution.py:130
  32.9 5.8 %all-to-all-done.refs_0_ = bf16[8,576,128]{2,1,0:T(8,128)(2,1)S(1)} async-done(((bf16[8,576,128]{2,1,0:T(8,128)(2,1)}), bf16[8,576,128]{2,1,0:T(8,128)(2,1)S(1)}, u32[]{:S(2)}, u32[]{:S(2)}) %all-to-all-start) | async-done | bytes 1179680 | tf_op jit(solution)/shard_map/state_scan/all_to_all | solution.py:438
  38.7 1.6 copy-done.5
  40.5 1.0 copy-done.22
  41.5 0.8 deal.1
  42.4 1.3 collective-permute-start
  43.7 2.1 collective-permute-done.2.refs_1_
  45.8 1.0 pair.1
  48.0 2.3 collective-permute-start.5
  50.3 6.1 %collective-permute-done.refs_0_.refs_1_ = bf16[4,144,128]{2,1,0:T(8,128)(2,1)S(1)} collective-permute-done((bf16[4,144,128]{2,1,0:T(8,128)(2,1)S(1)}, bf16[4,144,128]{2,1,0:T(8,128)(2,1)S(1)}, u32[]{:S(2)}, u32[]{:S(2)}) %collective-permute-start) | collective-permute-done | bytes 147488 | tf_op jit(solution)/shard_map/state_scan/ppermute | solution.py:416
  56.4 1.3 collective-permute-start.1
  57.7 3.3 %collective-permute-done.4.refs_3_ = bf16[2,128,512]{2,1,0:T(8,128)(2,1)S(1)} collective-permute-done((bf16[2,128,512]{2,1,0:T(8,128)(2,1)S(1)}, bf16[2,128,512]{2,1,0:T(8,128)(2,1)S(1)}, u32[]{:S(2)}, u32[]{:S(2)}) %collective-permute-start.4) | collective-permute-done | bytes 262176 | tf_op jit(solution)/shard_map/out_weight_gather/ppermute | solution.py:409
  61.0 1.1 in_order.1.refs_4_.refs_0_
  62.1 0.8 copy-done.14
  62.9 0.8 copy-done.23
  63.7 0.8 copy-done.24
  64.5 3.6 %collective-permute-done.1.refs_2_ = bf16[4,144,128]{2,1,0:T(8,128)(2,1)S(1)} collective-permute-done((bf16[4,144,128]{2,1,0:T(8,128)(2,1)S(1)}, bf16[4,144,128]{2,1,0:T(8,128)(2,1)S(1)}, u32[]{:S(2)}, u32[]{:S(2)}) %collective-permute-start.1) | collective-permute-done | bytes 147488 | tf_op jit(solution)/shard_map/state_scan/ppermute | solution.py:416
  68.1 1.4 plane_prefix.1
  69.5 0.7 all-gather.5.cloned.1.call-update
  70.3 3.6 %all-to-all-start.1 = ((bf16[8,4,128,128]{3,2,1,0:T(8,128)(2,1)}), bf16[8,4,128,128]{3,2,1,0:T(8,128)(2,1)S(1)}, u32[]{:S(2)}, u32[]{:S(2)}) async-start(bf16[8,4,128,128]{3,2,1,0:T(8,128)(2,1)} %plane_prefix.1), calls=%async_computation.1 | async-start | bytes 2097152 | tf_op jit(solution)/shard_map/state_scan/all_to_all | solution.py:461
  73.8 1.9 collective-permute-start.6
  75.8 1.5 collective-permute-start.7
  77.4 12.3 %all-to-all-done.1 = bf16[8,4,128,128]{3,2,1,0:T(8,128)(2,1)S(1)} async-done(((bf16[8,4,128,128]{3,2,1,0:T(8,128)(2,1)}), bf16[8,4,128,128]{3,2,1,0:T(8,128)(2,1)S(1)}, u32[]{:S(2)}, u32[]{:S(2)}) %all-to-all-start.1) | async-done | bytes 1048608 | tf_op jit(solution)/shard_map/state_scan/all_to_all | solution.py:461
  89.7 1.1 copy-done.16
  90.8 1.6 copy-done.6
  92.4 1.6 copy-done.7
  93.9 1.2 copy-done.17
  95.2 1.6 copy-done.19
  96.8 5.8 %mix.1 = (bf16[128,4096]{1,0:T(8,128)(2,1)S(1)}, bf16[128,4096]{1,0:T(8,128)(2,1)}) custom-call(bf16[256,4096]{1,0:T(8,128)(2,1)S(1)} %copy-done.7, bf16[256,4096]{1,0:T(8,128)(2,1)S(1)} %copy-done.19, bf16[256,4096]{1,0:T(8,128)(2,1)S(1)} %copy-done.6, f32[8,256,4]{2,1,0:T(8,128)S(1)} %bitcast.23, bf16[32,128,128]{2,1,0:T(8,128)(2,1)S(1)} %bitcast.24), custom_call_target="tpu_custom_call" | custom-call | tf_op jit(solution)/shard_map/mix/pallas_call | solution.py:130
  102.7 9.1 %collective-permute-done.8.refs_4_.refs_5_.refs_6_ = bf16[2,256,512]{2,1,0:T(8,128)(2,1)} collective-permute-done((bf16[2,256,512]{2,1,0:T(8,128)(2,1)}, bf16[2,256,512]{2,1,0:T(8,128)(2,1)}, u32[]{:S(2)}, u32[]{:S(2)}) %collective-permute-start.8) | collective-permute-done | bytes 524320 | tf_op jit(solution)/shard_map/residual_exchange/ppermute | solution.py:409
  112.7 23.8 %collective-permute-done.9.refs_0_ = bf16[128,4096]{1,0:T(8,128)(2,1)S(1)} collective-permute-done((bf16[128,4096]{1,0:T(8,128)(2,1)S(1)}, bf16[128,4096]{1,0:T(8,128)(2,1)S(1)}, u32[]{:S(2)}, u32[]{:S(2)}) %collective-permute-start.9) | collective-permute-done | bytes 1048608 | tf_op jit(solution)/shard_map/projections/ppermute | solution.py:409
  137.1 1.5 collective-permute-start.12
  139.1 21.4 %collective-permute-done.10.refs_2_.refs_0_ = bf16[128,4096]{1,0:T(8,128)(2,1)} collective-permute-done((bf16[128,4096]{1,0:T(8,128)(2,1)S(1)}, bf16[128,4096]{1,0:T(8,128)(2,1)}, u32[]{:S(2)}, u32[]{:S(2)}) %collective-permute-start.10) | collective-permute-done | bytes 1048608 | tf_op jit(solution)/shard_map/projections/ppermute | solution.py:409
  161.1 1.4 collective-permute-start.15
  163.2 2.0 multiply_convert_fusion.1.refs_2_
  165.2 2.2 copy-done.2
  167.4 1.0 copy-done.9
  168.4 1.0 copy-done.12
  169.5 1.2 copy-done.21
  170.7 4.3 %out_projection.4 = (bf16[256,512]{1,0:T(8,128)(2,1)S(1)}, bf16[256,512]{1,0:T(8,128)(2,1)S(1)}) custom-call(bf16[128,4096]{1,0:T(8,128)(2,1)S(1)} %copy-done.21, bf16[128,4096]{1,0:T(8,128)(2,1)} %collective-permute-done.17.refs_1_, bf16[128,4096]{1,0:T(8,128)(2,1)} %collective-permute-done.11.refs_2_, bf16[128,4096]{1,0:T(8,128)(2,1)} %collective-permute-done.18.refs_3_, ...), custom_call_target="tpu_custom_call" | custom-call | tf_op jit(solution)/shard_map/projections/out_projection/pallas_call | solution.py:155
  175.1 4.8 %out_projection.5 = (bf16[256,512]{1,0:T(8,128)(2,1)S(1)}, bf16[256,512]{1,0:T(8,128)(2,1)S(1)}) custom-call(bf16[128,4096]{1,0:T(8,128)(2,1)} %collective-permute-done.10.refs_2_.refs_0_, bf16[128,4096]{1,0:T(8,128)(2,1)} %collective-permute-done.21.refs_1_, bf16[128,4096]{1,0:T(8,128)(2,1)} %collective-permute-done.12.refs_3_.refs_2_, ...), custom_call_target="tpu_custom_call" | custom-call | tf_op jit(solution)/shard_map/projections/out_projection/pallas_call | solution.py:155
  180.5 2.0 multiply_convert_fusion.refs_3_
  182.5 1.3 cache_projection.4
  183.7 1.3 cache_projection.5
  185.0 2.0 collective-permute-done.15.refs_0_
  187.0 0.9 collective-permute-done.16.refs_1_
  189.1 1.5 collective-permute-start.28
  190.9 2.9 %collective-permute-done.25.refs_3_ = bf16[128,4096]{1,0:T(8,128)(2,1)S(1)} collective-permute-done((bf16[128,4096]{1,0:T(8,128)(2,1)}, bf16[128,4096]{1,0:T(8,128)(2,1)S(1)}, u32[]{:S(2)}, u32[]{:S(2)}) %collective-permute-start.25) | collective-permute-done | bytes 1048608 | tf_op jit(solution)/shard_map/projections/ppermute | solution.py:409
  194.4 3.9 %out_projection.6 = (bf16[256,512]{1,0:T(8,128)(2,1)S(1)}, bf16[256,512]{1,0:T(8,128)(2,1)S(1)}) custom-call(bf16[128,4096]{1,0:T(8,128)(2,1)} %get-tuple-element.68.refs_0_, bf16[128,4096]{1,0:T(8,128)(2,1)S(1)} %collective-permute-done.24.refs_1_, bf16[128,4096]{1,0:T(8,128)(2,1)} %get-tuple-element.69.refs_2_, ...), custom_call_target="tpu_custom_call" | custom-call | tf_op jit(solution)/shard_map/projections/out_projection/pallas_call | solution.py:155
  198.3 5.1 %collective-permute-done.27.refs_4_ = bf16[128,2176]{1,0:T(8,128)(2,1)S(1)} collective-permute-done((bf16[128,2176]{1,0:T(8,128)(2,1)S(1)}, bf16[128,2176]{1,0:T(8,128)(2,1)S(1)}, u32[]{:S(2)}, u32[]{:S(2)}) %collective-permute-start.27) | collective-permute-done | bytes 557088 | tf_op jit(solution)/shard_map/projections/ppermute | solution.py:409
  203.5 1.1 collective-permute-done.28.refs_5_
  204.5 1.4 collective-permute-start.30
  205.9 1.3 cache_projection.6
  208.0 1.5 collective-permute-start.33
  209.4 7.0 %collective-permute-done.29.refs_8_.refs_4_ = bf16[128,2176]{1,0:T(8,128)(2,1)S(1)} collective-permute-done((bf16[128,2176]{1,0:T(8,128)(2,1)S(1)}, bf16[128,2176]{1,0:T(8,128)(2,1)S(1)}, u32[]{:S(2)}, u32[]{:S(2)}) %collective-permute-start.29) | collective-permute-done | bytes 557088 | tf_op jit(solution)/shard_map/projections/ppermute | solution.py:409
  216.5 3.6 %collective-permute-done.30.refs_9_.refs_7_ = bf16[128,2176]{1,0:T(8,128)(2,1)S(1)} collective-permute-done((bf16[128,2176]{1,0:T(8,128)(2,1)S(1)}, bf16[128,2176]{1,0:T(8,128)(2,1)S(1)}, u32[]{:S(2)}, u32[]{:S(2)}) %collective-permute-start.30) | collective-permute-done | bytes 557088 | tf_op jit(solution)/shard_map/projections/ppermute | solution.py:409
  220.1 3.6 %out_projection.7 = (bf16[256,512]{1,0:T(8,128)(2,1)S(1)}, bf16[256,512]{1,0:T(8,128)(2,1)S(1)}) custom-call(bf16[128,4096]{1,0:T(8,128)(2,1)S(1)} %get-tuple-element.59.refs_0_, bf16[128,4096]{1,0:T(8,128)(2,1)S(1)} %collective-permute-done.13.refs_1_, bf16[128,4096]{1,0:T(8,128)(2,1)} %get-tuple-element.60.refs_2_, ...), custom_call_target="tpu_custom_call" | custom-call | tf_op jit(solution)/shard_map/projections/out_projection/pallas_call | solution.py:155
  223.8 1.5 collective-permute-done.31.refs_1_
  225.3 2.4 %collective-permute-done.32.refs_5_ = bf16[128,2176]{1,0:T(8,128)(2,1)S(1)} collective-permute-done((bf16[128,2176]{1,0:T(8,128)(2,1)S(1)}, bf16[128,2176]{1,0:T(8,128)(2,1)S(1)}, u32[]{:S(2)}, u32[]{:S(2)}) %collective-permute-start.32) | collective-permute-done | bytes 557088 | tf_op jit(solution)/shard_map/projections/ppermute | solution.py:409
  227.7 2.7 %collective-permute-done.33.refs_6_ = bf16[128,2176]{1,0:T(8,128)(2,1)S(1)} collective-permute-done((bf16[128,2176]{1,0:T(8,128)(2,1)S(1)}, bf16[128,2176]{1,0:T(8,128)(2,1)S(1)}, u32[]{:S(2)}, u32[]{:S(2)}) %collective-permute-start.33) | collective-permute-done | bytes 557088 | tf_op jit(solution)/shard_map/projections/ppermute | solution.py:409
  230.5 2.4 %cache_projection.7 = (bf16[256,1024]{1,0:T(8,128)(2,1)}, bf16[256,1024]{1,0:T(8,128)(2,1)}) custom-call(bf16[256,512]{1,0:T(8,128)(2,1)S(1)} %get-tuple-element.75.refs_0_, bf16[256,512]{1,0:T(8,128)(2,1)S(1)} %collective-permute-done.31.refs_1_, bf16[512,2048]{1,0:T(8,128)(2,1)S(1)} %multiply_convert_fusion.1.refs_2_, ...), custom_call_target="tpu_custom_call" | custom-call | tf_op jit(solution)/shard_map/projections/cache_projection/pallas_call | solution.py:155
  (102 shorter events, 10.9 us)
Async XLA Ops:
  7.2 0.8 copy-start
  7.2 60.9 %all-gather.3.cloned.1.call-start = ((), (), s32[]{:S(2)}) async-start(), calls=%async_computation.2 | async-start | bytes 2621440 | tf_op jit(solution)/shard_map/kv_weight_gather/all_gather | solution.py:431
  18.1 20.5 %all-to-all-start = ((bf16[8,576,128]{2,1,0:T(8,128)(2,1)}), bf16[8,576,128]{2,1,0:T(8,128)(2,1)S(1)}, u32[]{:S(2)}, u32[]{:S(2)}) async-start(bf16[8,576,128]{2,1,0:T(8,128)(2,1)} %local_states.1.refs_6_), calls=%async_computation | async-start | bytes 2359296 | tf_op jit(solution)/shard_map/state_scan/all_to_all | solution.py:438
  22.6 17.9 %copy-start.18 = (bf16[256,4096]{1,0:T(8,128)(2,1)S(1)}, bf16[256,4096]{1,0:T(8,128)(2,1)}, u32[]{:S(2)}) copy-start(bf16[256,4096]{1,0:T(8,128)(2,1)} %refs_1_.5) | copy-start | bytes 6291460
  38.7 1.6 copy-start.5
  40.3 1.2 copy-start.22
  42.3 3.5 %collective-permute-start.2 = (bf16[4,384,512]{2,1,0:T(8,128)(2,1)S(1)}, bf16[4,384,512]{2,1,0:T(8,128)(2,1)S(1)}, u32[]{:S(2)}, u32[]{:S(2)}) collective-permute-start(bf16[4,384,512]{2,1,0:T(8,128)(2,1)S(1)} %get-tuple-element.43), channel_id=1, source_target_pairs={{0,1},{1,0},{2,3},{3,2},{4,5},{5,4},{6,7},{7,6},{8,9},{9,8},{10,11... | collective-permute-start | bytes 4718600 | tf_op jit(solution)/shard_map/ppermute | solution.py:409
  42.4 13.9 %collective-permute-start = (bf16[4,144,128]{2,1,0:T(8,128)(2,1)S(1)}, bf16[4,144,128]{2,1,0:T(8,128)(2,1)S(1)}, u32[]{:S(2)}, u32[]{:S(2)}) collective-permute-start(bf16[4,144,128]{2,1,0:T(8,128)(2,1)S(1)} %plane_total.1.refs_1_.refs_3_), channel_id=1, source_target_pairs={{0,8},{1,9},{2,10},{3,11},{4,12},{5,13},{6,14},{7,15},{8,16},{9,17... | collective-permute-start | bytes 442376 | tf_op jit(solution)/shard_map/state_scan/ppermute | solution.py:416
  46.8 10.9 %collective-permute-start.3 = (bf16[2,128,512]{2,1,0:T(8,128)(2,1)S(1)}, bf16[2,128,512]{2,1,0:T(8,128)(2,1)S(1)}, u32[]{:S(2)}, u32[]{:S(2)}) collective-permute-start(bf16[2,128,512]{2,1,0:T(8,128)(2,1)S(1)} %get-tuple-element.45), channel_id=1, source_target_pairs={{0,2},{1,3},{2,0},{3,1},{4,6},{5,7},{6,4},{7,5},{8,10},{9,11},{10,... | collective-permute-start | bytes 786440 | tf_op jit(solution)/shard_map/out_weight_gather/ppermute | solution.py:409
  47.3 13.7 %collective-permute-start.4 = (bf16[2,128,512]{2,1,0:T(8,128)(2,1)S(1)}, bf16[2,128,512]{2,1,0:T(8,128)(2,1)S(1)}, u32[]{:S(2)}, u32[]{:S(2)}) collective-permute-start(bf16[2,128,512]{2,1,0:T(8,128)(2,1)S(1)} %get-tuple-element.46), channel_id=1, source_target_pairs={{0,4},{1,5},{2,6},{3,7},{4,0},{5,1},{6,2},{7,3},{8,12},{9,13},{10,... | collective-permute-start | bytes 786440 | tf_op jit(solution)/shard_map/out_weight_gather/ppermute | solution.py:409
  48.0 13.1 %collective-permute-start.5 = (bf16[2,128,512]{2,1,0:T(8,128)(2,1)S(1)}, bf16[2,128,512]{2,1,0:T(8,128)(2,1)S(1)}, u32[]{:S(2)}, u32[]{:S(2)}) collective-permute-start(bf16[2,128,512]{2,1,0:T(8,128)(2,1)S(1)} %get-tuple-element.47), channel_id=1, source_target_pairs={{0,6},{1,7},{2,4},{3,5},{4,2},{5,3},{6,0},{7,1},{8,14},{9,15},{10,... | collective-permute-start | bytes 786440 | tf_op jit(solution)/shard_map/out_weight_gather/ppermute | solution.py:409
  56.4 11.7 %collective-permute-start.1 = (bf16[4,144,128]{2,1,0:T(8,128)(2,1)S(1)}, bf16[4,144,128]{2,1,0:T(8,128)(2,1)S(1)}, u32[]{:S(2)}, u32[]{:S(2)}) collective-permute-start(bf16[4,144,128]{2,1,0:T(8,128)(2,1)S(1)} %join.1.refs_5_), channel_id=1, source_target_pairs={{0,16},{1,17},{2,18},{3,19},{4,20},{5,21},{6,22},{7,23},{8,24},{9,... | collective-permute-start | bytes 442376 | tf_op jit(solution)/shard_map/state_scan/ppermute | solution.py:416
  62.1 0.8 copy-start.14
  62.9 0.8 copy-start.23
  63.7 0.8 copy-start.24
  69.5 95.7 %all-gather.5.cloned.1.call-start = ((), (), s32[]{:S(2)}) async-start(), calls=%async_computation.3 | async-start | bytes 5242880 | tf_op jit(solution)/shard_map/out_weight_gather/all_gather | solution.py:456
  69.5 21.2 %copy-start.4 = (f32[256,8,4]{2,0,1:T(8,128)S(1)}, f32[256,8,4]{2,0,1:T(8,128)}, u32[]{:S(2)}) copy-start(f32[256,8,4]{2,0,1:T(8,128)} %copy.26) | copy-start | bytes 98308
  70.3 19.4 %all-to-all-start.1 = ((bf16[8,4,128,128]{3,2,1,0:T(8,128)(2,1)}), bf16[8,4,128,128]{3,2,1,0:T(8,128)(2,1)S(1)}, u32[]{:S(2)}, u32[]{:S(2)}) async-start(bf16[8,4,128,128]{3,2,1,0:T(8,128)(2,1)} %plane_prefix.1), calls=%async_computation.1 | async-start | bytes 2097152 | tf_op jit(solution)/shard_map/state_scan/all_to_all | solution.py:461
  73.8 28.8 %collective-permute-start.6 = (bf16[2,256,512]{2,1,0:T(8,128)(2,1)}, bf16[2,256,512]{2,1,0:T(8,128)(2,1)S(1)}, u32[]{:S(2)}, u32[]{:S(2)}) collective-permute-start(bf16[2,256,512]{2,1,0:T(8,128)(2,1)} %get-tuple-element.54), channel_id=1, source_target_pairs={{0,2},{1,3},{2,0},{3,1},{4,6},{5,7},{6,4},{7,5},{8,10},{9,11},{10,... | collective-permute-start | bytes 1572872 | tf_op jit(solution)/shard_map/residual_exchange/ppermute | solution.py:409
  75.8 26.9 %collective-permute-start.7 = (bf16[2,256,512]{2,1,0:T(8,128)(2,1)}, bf16[2,256,512]{2,1,0:T(8,128)(2,1)S(1)}, u32[]{:S(2)}, u32[]{:S(2)}) collective-permute-start(bf16[2,256,512]{2,1,0:T(8,128)(2,1)} %copy-done.23), channel_id=1, source_target_pairs={{0,4},{1,5},{2,6},{3,7},{4,0},{5,1},{6,2},{7,3},{8,12},{9,13},{10,... | collective-permute-start | bytes 1572872 | tf_op jit(solution)/shard_map/residual_exchange/ppermute | solution.py:409
  77.3 34.5 %collective-permute-start.8 = (bf16[2,256,512]{2,1,0:T(8,128)(2,1)}, bf16[2,256,512]{2,1,0:T(8,128)(2,1)}, u32[]{:S(2)}, u32[]{:S(2)}) collective-permute-start(bf16[2,256,512]{2,1,0:T(8,128)(2,1)} %copy-done.24), channel_id=1, source_target_pairs={{0,6},{1,7},{2,4},{3,5},{4,2},{5,3},{6,0},{7,1},{8,14},{9,15},{10,... | collective-permute-start | bytes 1572872 | tf_op jit(solution)/shard_map/residual_exchange/ppermute | solution.py:409
  89.7 1.1 copy-start.16
  90.8 1.6 copy-start.6
  92.4 1.6 copy-start.7
  93.9 1.2 copy-start.17
  95.2 1.6 copy-start.19
  102.6 58.4 %copy-start.25 = (bf16[4096]{0:T(1024)(128)(2,1)S(1)}, bf16[4096]{0:T(1024)(128)(2,1)}, u32[]{:S(2)}) copy-start(bf16[4096]{0:T(1024)(128)(2,1)} %param.16) | copy-start | bytes 24580
  102.6 58.4 %copy-start.8 = (bf16[2,256,512]{2,1,0:T(8,128)(2,1)}, bf16[2,256,512]{2,1,0:T(8,128)(2,1)S(1)}, u32[]{:S(2)}) copy-start(bf16[2,256,512]{2,1,0:T(8,128)(2,1)S(1)} %collective-permute-done.6.refs_2_.refs_5_) | copy-start | bytes 1572868
  102.6 58.4 %copy-start.11 = (bf16[2,256,512]{2,1,0:T(8,128)(2,1)}, bf16[2,256,512]{2,1,0:T(8,128)(2,1)S(1)}, u32[]{:S(2)}) copy-start(bf16[2,256,512]{2,1,0:T(8,128)(2,1)S(1)} %collective-permute-done.7.refs_3_.refs_6_) | copy-start | bytes 1572868
  111.8 24.7 %collective-permute-start.9 = (bf16[128,4096]{1,0:T(8,128)(2,1)S(1)}, bf16[128,4096]{1,0:T(8,128)(2,1)S(1)}, u32[]{:S(2)}, u32[]{:S(2)}) collective-permute-start(bf16[128,4096]{1,0:T(8,128)(2,1)S(1)} %get-tuple-element.57.refs_0_), channel_id=1, source_target_pairs={{0,2},{1,3},{2,0},{3,1},{4,6},{5,7},{6,4},{7,5},{8,10},{9,11},{10,... | collective-permute-start | bytes 3145736 | tf_op jit(solution)/shard_map/projections/ppermute | solution.py:409
  112.4 24.7 %collective-permute-start.11 = (bf16[128,4096]{1,0:T(8,128)(2,1)}, bf16[128,4096]{1,0:T(8,128)(2,1)}, u32[]{:S(2)}, u32[]{:S(2)}) collective-permute-start(bf16[128,4096]{1,0:T(8,128)(2,1)} %get-tuple-element.58.refs_1_), channel_id=1, source_target_pairs={{0,4},{1,5},{2,6},{3,7},{4,0},{5,1},{6,2},{7,3},{8,12},{9,13},{10,... | collective-permute-start | bytes 3145736 | tf_op jit(solution)/shard_map/projections/ppermute | solution.py:409
  136.5 24.6 %copy-start.20 = (bf16[128,4096]{1,0:T(8,128)(2,1)}, bf16[128,4096]{1,0:T(8,128)(2,1)S(1)}, u32[]{:S(2)}) copy-start(bf16[128,4096]{1,0:T(8,128)(2,1)S(1)} %collective-permute-done.9.refs_0_) | copy-start | bytes 3145732
  136.5 24.0 %collective-permute-start.10 = (bf16[128,4096]{1,0:T(8,128)(2,1)S(1)}, bf16[128,4096]{1,0:T(8,128)(2,1)}, u32[]{:S(2)}, u32[]{:S(2)}) collective-permute-start(bf16[128,4096]{1,0:T(8,128)(2,1)S(1)} %collective-permute-done.9.refs_0_), channel_id=1, source_target_pairs={{0,4},{1,5},{2,6},{3,7},{4,0},{5,1},{6,2},{7,3},{8,12},{9,13},{10,... | collective-permute-start | bytes 3145736 | tf_op jit(solution)/shard_map/projections/ppermute | solution.py:409
  137.1 23.9 %collective-permute-start.12 = (bf16[128,4096]{1,0:T(8,128)(2,1)}, bf16[128,4096]{1,0:T(8,128)(2,1)}, u32[]{:S(2)}, u32[]{:S(2)}) collective-permute-start(bf16[128,4096]{1,0:T(8,128)(2,1)} %collective-permute-done.11.refs_2_), channel_id=1, source_target_pairs={{0,2},{1,3},{2,0},{3,1},{4,6},{5,7},{6,4},{7,5},{8,10},{9,11},{10,... | collective-permute-start | bytes 3145736 | tf_op jit(solution)/shard_map/projections/ppermute | solution.py:409
  138.6 41.9 %collective-permute-start.20 = (bf16[512,2048]{1,0:T(8,128)(2,1)}, bf16[512,2048]{1,0:T(8,128)(2,1)}, u32[]{:S(2)}, u32[]{:S(2)}) collective-permute-start(bf16[512,2048]{1,0:T(8,128)(2,1)} %all-gather.3.cloned.1.call-done.refs_3_.refs_1_), channel_id=1, source_target_pairs={{0,1},{1,0},{2,3},{3,2},{4,5},{5,4},{6,7},{7,6},{8,9},{9,8},{10,11... | collective-permute-start | bytes 6291464 | tf_op jit(solution)/shard_map/cache_weight/ppermute | solution.py:409
  138.6 22.5 %collective-permute-start.17 = (bf16[128,4096]{1,0:T(8,128)(2,1)S(1)}, bf16[128,4096]{1,0:T(8,128)(2,1)}, u32[]{:S(2)}, u32[]{:S(2)}) collective-permute-start(bf16[128,4096]{1,0:T(8,128)(2,1)S(1)} %collective-permute-done.9.refs_0_), channel_id=1, source_target_pairs={{0,1},{1,0},{2,3},{3,2},{4,5},{5,4},{6,7},{7,6},{8,9},{9,8},{10,11... | collective-permute-start | bytes 3145736 | tf_op jit(solution)/shard_map/projections/ppermute | solution.py:409
  139.1 23.4 %collective-permute-start.18 = (bf16[128,4096]{1,0:T(8,128)(2,1)}, bf16[128,4096]{1,0:T(8,128)(2,1)}, u32[]{:S(2)}, u32[]{:S(2)}) collective-permute-start(bf16[128,4096]{1,0:T(8,128)(2,1)} %collective-permute-done.11.refs_2_), channel_id=1, source_target_pairs={{0,1},{1,0},{2,3},{3,2},{4,5},{5,4},{6,7},{7,6},{8,9},{9,8},{10,11... | collective-permute-start | bytes 3145736 | tf_op jit(solution)/shard_map/projections/ppermute | solution.py:409
  160.5 14.5 %collective-permute-start.21 = (bf16[128,4096]{1,0:T(8,128)(2,1)}, bf16[128,4096]{1,0:T(8,128)(2,1)}, u32[]{:S(2)}, u32[]{:S(2)}) collective-permute-start(bf16[128,4096]{1,0:T(8,128)(2,1)} %collective-permute-done.10.refs_2_.refs_0_), channel_id=1, source_target_pairs={{0,1},{1,0},{2,3},{3,2},{4,5},{5,4},{6,7},{7,6},{8,9},{9,8},{10,11... | collective-permute-start | bytes 3145736 | tf_op jit(solution)/shard_map/projections/ppermute | solution.py:409
  161.0 14.0 %collective-permute-start.22 = (bf16[128,4096]{1,0:T(8,128)(2,1)}, bf16[128,4096]{1,0:T(8,128)(2,1)}, u32[]{:S(2)}, u32[]{:S(2)}) collective-permute-start(bf16[128,4096]{1,0:T(8,128)(2,1)} %collective-permute-done.12.refs_3_.refs_2_), channel_id=1, source_target_pairs={{0,1},{1,0},{2,3},{3,2},{4,5},{5,4},{6,7},{7,6},{8,9},{9,8},{10,11... | collective-permute-start | bytes 3145736 | tf_op jit(solution)/shard_map/projections/ppermute | solution.py:409
  161.1 25.9 %collective-permute-start.15 = (bf16[128,4096]{1,0:T(8,128)(2,1)}, bf16[128,4096]{1,0:T(8,128)(2,1)}, u32[]{:S(2)}, u32[]{:S(2)}) collective-permute-start(bf16[128,4096]{1,0:T(8,128)(2,1)} %get-tuple-element.60.refs_2_), channel_id=1, source_target_pairs={{0,2},{1,3},{2,0},{3,1},{4,6},{5,7},{6,4},{7,5},{8,10},{9,11},{10,... | collective-permute-start | bytes 3145736 | tf_op jit(solution)/shard_map/projections/ppermute | solution.py:409
  162.5 25.4 %collective-permute-start.16 = (bf16[128,4096]{1,0:T(8,128)(2,1)S(1)}, bf16[128,4096]{1,0:T(8,128)(2,1)}, u32[]{:S(2)}, u32[]{:S(2)}) collective-permute-start(bf16[128,4096]{1,0:T(8,128)(2,1)S(1)} %get-tuple-element.59.refs_0_), channel_id=1, source_target_pairs={{0,4},{1,5},{2,6},{3,7},{4,0},{5,1},{6,2},{7,3},{8,12},{9,13},{10,... | collective-permute-start | bytes 3145736 | tf_op jit(solution)/shard_map/projections/ppermute | solution.py:409
  165.2 2.2 copy-start.2
  167.4 1.0 copy-start.9
  168.4 1.0 copy-start.12
  169.5 1.2 copy-start.21
  170.7 4.4 %copy-start.3 = (bf16[4096,512]{1,0:T(8,128)(2,1)S(1)}, bf16[4096,512]{1,0:T(8,128)(2,1)}, u32[]{:S(2)}) copy-start(bf16[4096,512]{1,0:T(8,128)(2,1)} %all-gather.5.cloned.1.call-done.refs_4_) | copy-start | bytes 12582916
  179.9 2.6 %collective-permute-start.23 = (bf16[256,512]{1,0:T(8,128)(2,1)S(1)}, bf16[256,512]{1,0:T(8,128)(2,1)S(1)}, u32[]{:S(2)}, u32[]{:S(2)}) collective-permute-start(bf16[256,512]{1,0:T(8,128)(2,1)S(1)} %get-tuple-element.65), channel_id=1, source_target_pairs={{0,1},{1,0},{2,3},{3,2},{4,5},{5,4},{6,7},{7,6},{8,9},{9,8},{10,11... | collective-permute-start | bytes 786440 | tf_op jit(solution)/shard_map/projections/ppermute | solution.py:409
  180.0 3.8 %collective-permute-start.19 = (bf16[256,512]{1,0:T(8,128)(2,1)S(1)}, bf16[256,512]{1,0:T(8,128)(2,1)S(1)}, u32[]{:S(2)}, u32[]{:S(2)}) collective-permute-start(bf16[256,512]{1,0:T(8,128)(2,1)S(1)} %get-tuple-element.63), channel_id=1, source_target_pairs={{0,1},{1,0},{2,3},{3,2},{4,5},{5,4},{6,7},{7,6},{8,9},{9,8},{10,11... | collective-permute-start | bytes 786440 | tf_op jit(solution)/shard_map/projections/ppermute | solution.py:409
  185.0 9.4 %copy-start.10 = (bf16[2,256,512]{2,1,0:T(8,128)(2,1)S(1)}, bf16[2,256,512]{2,1,0:T(8,128)(2,1)}, u32[]{:S(2)}) copy-start(bf16[2,256,512]{2,1,0:T(8,128)(2,1)} %copy-done.8) | copy-start | bytes 1572868
  185.0 9.4 %copy-start.13 = (bf16[2,256,512]{2,1,0:T(8,128)(2,1)S(1)}, bf16[2,256,512]{2,1,0:T(8,128)(2,1)}, u32[]{:S(2)}) copy-start(bf16[2,256,512]{2,1,0:T(8,128)(2,1)} %copy-done.11) | copy-start | bytes 1572868
  187.9 2.9 %collective-permute-start.24 = (bf16[128,4096]{1,0:T(8,128)(2,1)}, bf16[128,4096]{1,0:T(8,128)(2,1)S(1)}, u32[]{:S(2)}, u32[]{:S(2)}) collective-permute-start(bf16[128,4096]{1,0:T(8,128)(2,1)} %get-tuple-element.68.refs_0_), channel_id=1, source_target_pairs={{0,1},{1,0},{2,3},{3,2},{4,5},{5,4},{6,7},{7,6},{8,9},{9,8},{10,11... | collective-permute-start | bytes 3145736 | tf_op jit(solution)/shard_map/projections/ppermute | solution.py:409
  187.9 5.9 %collective-permute-start.25 = (bf16[128,4096]{1,0:T(8,128)(2,1)}, bf16[128,4096]{1,0:T(8,128)(2,1)S(1)}, u32[]{:S(2)}, u32[]{:S(2)}) collective-permute-start(bf16[128,4096]{1,0:T(8,128)(2,1)} %get-tuple-element.69.refs_2_), channel_id=1, source_target_pairs={{0,1},{1,0},{2,3},{3,2},{4,5},{5,4},{6,7},{7,6},{8,9},{9,8},{10,11... | collective-permute-start | bytes 3145736 | tf_op jit(solution)/shard_map/projections/ppermute | solution.py:409
  188.4 19.5 %collective-permute-start.13 = (bf16[128,4096]{1,0:T(8,128)(2,1)S(1)}, bf16[128,4096]{1,0:T(8,128)(2,1)S(1)}, u32[]{:S(2)}, u32[]{:S(2)}) collective-permute-start(bf16[128,4096]{1,0:T(8,128)(2,1)S(1)} %get-tuple-element.59.refs_0_), channel_id=1, source_target_pairs={{0,1},{1,0},{2,3},{3,2},{4,5},{5,4},{6,7},{7,6},{8,9},{9,8},{10,11... | collective-permute-start | bytes 3145736 | tf_op jit(solution)/shard_map/projections/ppermute | solution.py:409
  188.4 15.0 %collective-permute-start.27 = (bf16[128,2176]{1,0:T(8,128)(2,1)S(1)}, bf16[128,2176]{1,0:T(8,128)(2,1)S(1)}, u32[]{:S(2)}, u32[]{:S(2)}) collective-permute-start(bf16[128,2176]{1,0:T(8,128)(2,1)S(1)} %get-tuple-element.72), channel_id=1, source_target_pairs={{0,4},{1,5},{2,6},{3,7},{4,0},{5,1},{6,2},{7,3},{8,12},{9,13},{10,... | collective-permute-start | bytes 1671176 | tf_op jit(solution)/shard_map/projections/ppermute | solution.py:409
  189.1 15.5 %collective-permute-start.28 = (bf16[128,2176]{1,0:T(8,128)(2,1)S(1)}, bf16[128,2176]{1,0:T(8,128)(2,1)S(1)}, u32[]{:S(2)}, u32[]{:S(2)}) collective-permute-start(bf16[128,2176]{1,0:T(8,128)(2,1)S(1)} %get-tuple-element.66.refs_4_), channel_id=1, source_target_pairs={{0,2},{1,3},{2,0},{3,1},{4,6},{5,7},{6,4},{7,5},{8,10},{9,11},{10,... | collective-permute-start | bytes 1671176 | tf_op jit(solution)/shard_map/projections/ppermute | solution.py:409
  190.8 18.6 %collective-permute-start.14 = (bf16[128,4096]{1,0:T(8,128)(2,1)}, bf16[128,4096]{1,0:T(8,128)(2,1)S(1)}, u32[]{:S(2)}, u32[]{:S(2)}) collective-permute-start(bf16[128,4096]{1,0:T(8,128)(2,1)} %get-tuple-element.60.refs_2_), channel_id=1, source_target_pairs={{0,1},{1,0},{2,3},{3,2},{4,5},{5,4},{6,7},{7,6},{8,9},{9,8},{10,11... | collective-permute-start | bytes 3145736 | tf_op jit(solution)/shard_map/projections/ppermute | solution.py:409
  193.8 22.7 %collective-permute-start.29 = (bf16[128,2176]{1,0:T(8,128)(2,1)S(1)}, bf16[128,2176]{1,0:T(8,128)(2,1)S(1)}, u32[]{:S(2)}, u32[]{:S(2)}) collective-permute-start(bf16[128,2176]{1,0:T(8,128)(2,1)S(1)} %get-tuple-element.67.refs_2_), channel_id=1, source_target_pairs={{0,2},{1,3},{2,0},{3,1},{4,6},{5,7},{6,4},{7,5},{8,10},{9,11},{10,... | collective-permute-start | bytes 1671176 | tf_op jit(solution)/shard_map/projections/ppermute | solution.py:409
  203.5 2.5 %collective-permute-start.26 = (bf16[256,512]{1,0:T(8,128)(2,1)S(1)}, bf16[256,512]{1,0:T(8,128)(2,1)S(1)}, u32[]{:S(2)}, u32[]{:S(2)}) collective-permute-start(bf16[256,512]{1,0:T(8,128)(2,1)S(1)} %get-tuple-element.71), channel_id=1, source_target_pairs={{0,1},{1,0},{2,3},{3,2},{4,5},{5,4},{6,7},{7,6},{8,9},{9,8},{10,11... | collective-permute-start | bytes 786440 | tf_op jit(solution)/shard_map/projections/ppermute | solution.py:409
  204.5 15.6 %collective-permute-start.30 = (bf16[128,2176]{1,0:T(8,128)(2,1)S(1)}, bf16[128,2176]{1,0:T(8,128)(2,1)S(1)}, u32[]{:S(2)}, u32[]{:S(2)}) collective-permute-start(bf16[128,2176]{1,0:T(8,128)(2,1)S(1)} %get-tuple-element.74), channel_id=1, source_target_pairs={{0,4},{1,5},{2,6},{3,7},{4,0},{5,1},{6,2},{7,3},{8,12},{9,13},{10,... | collective-permute-start | bytes 1671176 | tf_op jit(solution)/shard_map/projections/ppermute | solution.py:409
  205.9 14.2 %copy-start.15 = (bf16[2,256,512]{2,1,0:T(8,128)(2,1)S(1)}, bf16[2,256,512]{2,1,0:T(8,128)(2,1)}, u32[]{:S(2)}) copy-start(bf16[2,256,512]{2,1,0:T(8,128)(2,1)} %copy-done.14) | copy-start | bytes 1572868
  207.2 20.5 %collective-permute-start.32 = (bf16[128,2176]{1,0:T(8,128)(2,1)S(1)}, bf16[128,2176]{1,0:T(8,128)(2,1)S(1)}, u32[]{:S(2)}, u32[]{:S(2)}) collective-permute-start(bf16[128,2176]{1,0:T(8,128)(2,1)S(1)} %get-tuple-element.73.refs_7_), channel_id=1, source_target_pairs={{0,2},{1,3},{2,0},{3,1},{4,6},{5,7},{6,4},{7,5},{8,10},{9,11},{10,... | collective-permute-start | bytes 1671176 | tf_op jit(solution)/shard_map/projections/ppermute | solution.py:409
  208.0 22.5 %collective-permute-start.33 = (bf16[128,2176]{1,0:T(8,128)(2,1)S(1)}, bf16[128,2176]{1,0:T(8,128)(2,1)S(1)}, u32[]{:S(2)}, u32[]{:S(2)}) collective-permute-start(bf16[128,2176]{1,0:T(8,128)(2,1)S(1)} %get-tuple-element.77), channel_id=1, source_target_pairs={{0,4},{1,5},{2,6},{3,7},{4,0},{5,1},{6,2},{7,3},{8,12},{9,13},{10,... | collective-permute-start | bytes 1671176 | tf_op jit(solution)/shard_map/projections/ppermute | solution.py:409
  223.7 1.6 collective-permute-start.31
  230.5 2.4 %copy-start.1 = (f32[256,32]{0,1:T(8,128)S(1)}, f32[256,32]{0,1:T(8,128)}, u32[]{:S(2)}) copy-start(f32[256,32]{0,1:T(8,128)} %param.14) | copy-start | bytes 98308
Sparse Core Ops, SparseCore 0:
  9.6 47.7 all-gather.2
  71.9 77.5 all-gather.4

commit v4 on v3

--- a/solution.py
+++ b/solution.py
@@ -16,7 +16,7 @@
 PLANE = ("y", "x", "c")
 SEQ = ("z", "y", "x", "c")
 MIB = 1024 * 1024
-VMEM_STREAMED = {"local_states": 60 * MIB, "local_intra": 54 * MIB, "mix": 16 * MIB}
+VMEM_STREAMED = {"local_states": 60 * MIB, "local_intra": 54 * MIB, "mix": 60 * MIB}
 VMEM_RESIDENT = 16 * MIB
 
 
@@ -37,19 +37,40 @@
     return lax.dot_general(a, b, (contract, ((), ())), preferred_element_type=F32)
 
 
-def state_kernel(width, key_ref, value_ref, within_ref, out_ref):
+def state_kernel(width, key_ref, value_ref, decay_ref, out_ref, fade_ref, ending_ref):
     tokens = key_ref.shape[0]
-    within = within_ref[0]
-    ending = within[tokens - 1 : tokens, :]
-    fade = jnp.exp(ending - within)
+    groups, _, per = fade_ref.shape
+
+    @pl.when(pl.program_id(0) == 0)
+    def _():
+        decay = decay_ref[...]
+        later = lax.broadcasted_iota(jnp.int32, (tokens, tokens), 0) < lax.broadcasted_iota(
+            jnp.int32, (tokens, tokens), 1
+        )
+        rest = lax.dot_general(
+            later.astype(F32),
+            decay,
+            (((1,), (0,)), ((), ())),
+            precision=HIGHEST,
+            preferred_element_type=F32,
+        )
+        fade = jnp.exp(rest)
+        ending = rest[:1] + decay[:1]
+        for i in range(groups):
+            fade_ref[i] = fade[:, i * per : (i + 1) * per]
+            ending_ref[i] = ending[:, i * per : (i + 1) * per]
+
     rows = width + DECAY_ROWS
-    for head in range(within.shape[1]):
-        columns = slice(head * width, (head + 1) * width)
-        faded = (key_ref[:, columns].astype(F32) * fade[:, head : head + 1]).astype(BF16)
-        state = dot(faded, value_ref[:, columns], ((0,), (0,)))
-        out_ref[0, head * rows : head * rows + width, :] = state.astype(BF16)
-        total = jnp.broadcast_to(ending[:, head : head + 1], (1, width))
-        out_ref[0, head * rows + width : (head + 1) * rows, :] = split_rows(total)
+    for i in range(out_ref.shape[0]):
+        place = pl.program_id(0) * out_ref.shape[0] + i
+        fade, ending = fade_ref[place], ending_ref[place]
+        for head in range(per):
+            columns = slice((i * per + head) * width, (i * per + head + 1) * width)
+            faded = (key_ref[:, columns].astype(F32) * fade[:, head : head + 1]).astype(BF16)
+            state = dot(faded, value_ref[:, columns], ((0,), (0,)))
+            out_ref[i, head * rows : head * rows + width, :] = state.astype(BF16)
+            total = jnp.broadcast_to(ending[:, head : head + 1], (1, width))
+            out_ref[i, head * rows + width : (head + 1) * rows, :] = split_rows(total)
 
 
 def intra_kernel(
@@ -176,17 +197,20 @@
     return pl.BlockSpec((1,) + shape, lambda i, *_: (i, 0, 0))
 
 
-def local_states(keys, values, within, width, after=()):
-    tokens, groups, per = keys.shape[0], within.shape[0], within.shape[2]
+def local_states(keys, values, log_decay, groups, width, after=()):
+    tokens, heads = log_decay.shape
+    per, steps = heads // groups, groups // 2
     tall = per * (width + DECAY_ROWS)
+    wider = wide(tokens, 2 * per * width)
     return local_call(
         "local_states",
         functools.partial(state_kernel, width),
-        groups,
-        (keys, values, within),
-        (wide(tokens, per * width), wide(tokens, per * width), group(tokens, per)),
-        group(tall, width),
+        steps,
+        (keys, values, log_decay),
+        (wider, wider, whole(tokens, heads)),
+        pl.BlockSpec((2, tall, width), lambda i: (i, 0, 0)),
         jax.ShapeDtypeStruct((groups, tall, width), BF16),
+        scratch=(pltpu.VMEM((groups, tokens, per), F32), pltpu.VMEM((groups, 1, per), F32)),
         after=after,
     )
 
@@ -433,36 +457,39 @@
     per = heads // PLACES
     within = running.reshape(tokens, PLACES, per).transpose(1, 0, 2)
     across = running.T.reshape(PLACES, per, tokens)
-    states = local_states(keys, values, within, width)
+    states = local_states(keys, values, log_decay, PLACES, width)
     with jax.named_scope("state_scan"):
         parts = lax.all_to_all(states, PLANE, 0, 0, tiled=True)
 
-    intra, opened = local_intra(
-        queries, keys, values, gate, within, across, width, after=(states,)
-    )
+    even, odd = deal((residual, out_weight), place, PLACES, piece, after=(states,))
+    starts, weights = pair(even, swap(odd, 1), (tokens, out_weight.shape[0]))
+    with jax.named_scope("out_weight_gather"):
+        weights = [swap(part, 2 * chip) if chip else part for chip, part in enumerate(weights)]
+    with jax.named_scope("residual_exchange"):
+        starts = [starts[0], swap(starts[1], 2), swap(starts[2], 4), starts[3]]
     with jax.named_scope("state_scan"):
-        total = plane_total(parts, per, width, after=(intra,))
+        total = plane_total(parts, per, width, after=(starts[0],))
         nearest = hop(total, {a: a + 1 for a in range(DEPTH - 1)})
         joined = join(nearest, total, width)
         others = hop(joined, {a: a + 2 for a in range(DEPTH - 2)})
-
-    def exchange(pairs):
-        return [swap(part, 2 * chip) if chip else part for chip, part in enumerate(pairs)]
-
-    even, odd = deal((residual, out_weight), place, PLACES, piece, after=(total,))
-    starts, weights = pair(even, swap(odd, 1), (tokens, out_weight.shape[0]))
     with jax.named_scope("out_weight_gather"):
-        shard = in_order(exchange(weights), place, after=(joined,))
+        shard = in_order(weights, place, after=(total,))
         out_full = lax.all_gather(*hold((shard,), (kv_mine,)), "z", axis=0, tiled=True)
-    with jax.named_scope("residual_exchange"):
-        starts = exchange(hold(starts, (shard,)))
     with jax.named_scope("state_scan"):
-        prefix = plane_prefix(parts, nearest, others, width, after=(kv_mine, shard))
+        prefix = plane_prefix(
+            parts, nearest, others, width, after=(kv_mine, shard, starts[1], starts[2])
+        )
         entering = lax.all_to_all(prefix, PLANE, 0, 0, tiled=True)
         entering = entering.reshape(heads, width, width)
+    intra, opened = local_intra(
+        queries, keys, values, gate, within, across, width, after=(prefix,)
+    )
+    with jax.named_scope("residual_exchange"):
+        (starts[3],) = hold((starts[3],), (prefix,))
+        starts[3] = swap(starts[3], 6)
 
     early, late = mix(queries, opened, intra, within, entering, width)
-    early, late = hold((early, late), tuple(starts[1:]))
+    early, late = hold((early, late), (starts[3],))
 
     with jax.named_scope("cache_weight"):
         gains = norm_gain.reshape(DEPTH, PLACES, piece)

time: 241 us -> 231 us (0.959)
  waiting for transfers between devices: 119 us -> 110 us
  local copies, waits for them, and re-layouts: 19.9 us -> 11.9 us
  Pallas kernels: 51.5 us -> 56.1 us
  starting transfers between devices: 30.2 us -> 33 us
    all_to_all x1, waiting for transfers between devices: 12.3 us -> 0.01 us  [shared_on_device(): entering = lax.all_to_all(prefix, PLANE, 0, 0, tiled=True)]
    unnamed x52 -> x41, local copies, waits for them, and re-layouts: 17.6 us -> 9.62 us
    ppermute x32, waiting for transfers between devices: 89.9 us -> 82.8 us  [swap(): return lax.ppermute(array, SEQ, [(i, i ^ distance) for i in range(DEVICES)])]
    ppermute x2, waiting for transfers between devices: 9.63 us -> 15 us  [hop(): return lax.ppermute(array, SEQ, pairs)]
    all_to_all x1, waiting for transfers between devices: 5.8 us -> 10.4 us  [shared_on_device(): parts = lax.all_to_all(states, PLANE, 0, 0, tiled=True)]
    ppermute x32, starting transfers between devices: 20.3 us -> 23 us  [swap(): return lax.ppermute(array, SEQ, [(i, i ^ distance) for i in range(DEVICES)])]
    pallas_call x14, Pallas kernels: 27.4 us -> 30 us  [resident_call(): pl.pallas_call(kernel, in_specs=[pl.BlockSpec(memory_space=pltpu.SMEM)] *...]
  transfers between devices with their start and end apart: 38 -> 38, of which waited for: 21 -> 18; matrix products, arithmetic and copies ran while one was open for 3% -> 4% of each run, Pallas kernels for 20% -> 23%
where the time goes in v4:
time: 231 us; the launch traced here: 230 us
  waiting for transfers between devices  110 us (48%)
  Pallas kernels  56.1 us (24%)
  starting transfers between devices  33 us (14%)
  between operations  14.4 us (6%)
  local copies, waits for them, and re-layouts  11.9 us (5%)
  other arithmetic  4.77 us (2%)
    ppermute x32, waiting for transfers between devices, swap(): return lax.ppermute(array, SEQ, [(i, i ^ distance) for i in range(DEVICES)])  82.8 us
    pallas_call x14, Pallas kernels, resident_call(): pl.pallas_call(kernel, in_specs=[pl.BlockSpec(memory_space=pltpu.SMEM)] *...  30 us
    pallas_call x3, Pallas kernels, local_call(): pl.pallas_call(kernel, grid_spec=pltpu.PrefetchScalarGridSpec(num_scalar_...  26.1 us
    ppermute x32, starting transfers between devices, swap(): return lax.ppermute(array, SEQ, [(i, i ^ distance) for i in range(DEVICES)])  23 us
    ppermute x2, waiting for transfers between devices, hop(): return lax.ppermute(array, SEQ, pairs)  15 us
    all_to_all x1, waiting for transfers between devices, shared_on_device(): parts = lax.all_to_all(states, PLANE, 0, 0, tiled=True)  10.4 us
    unnamed x41, local copies, waits for them, and re-layouts  9.62 us
  transfers between devices with their start and end apart: 38, of which 18 were waited for; matrix products, arithmetic and copies ran while one was open for 4% of the time, Pallas kernels for 23%

profile of v4, /device:TPU:24, one launch (start us, length us, event | category | flops | bytes accessed | tf_op | source)
XLA Modules:
  0.0 229.8 jit_solution(14722460650816811381)
XLA Ops:
  7.2 0.7 all-gather.3.cloned.1.call-update
  7.9 1.5 copy.26.refs_2_
  9.4 7.0 %local_states.1.refs_3_ = bf16[8,576,128]{2,1,0:T(8,128)(2,1)} custom-call(bf16[256,4096]{1,0:T(8,128)(2,1)} %refs_1_.5, bf16[256,4096]{1,0:T(8,128)(2,1)} %refs_2_.4, f32[256,32]{1,0:T(8,128)} %copy.26.refs_2_), custom_call_target="tpu_custom_call" | custom-call | tf_op jit(solution)/shard_map/local_states/pallas_call | solution.py:151
  16.4 1.3 copy-done.7
  17.7 2.0 deal.1
  19.7 3.8 %all-to-all-start = ((bf16[8,576,128]{2,1,0:T(8,128)(2,1)}), bf16[8,576,128]{2,1,0:T(8,128)(2,1)S(1)}, u32[]{:S(2)}, u32[]{:S(2)}) async-start(bf16[8,576,128]{2,1,0:T(8,128)(2,1)} %local_states.1.refs_3_), calls=%async_computation | async-start | bytes 2359296 | tf_op jit(solution)/shard_map/state_scan/all_to_all | solution.py:462
  23.6 2.5 %pair.1 = (bf16[2,256,512]{2,1,0:T(8,128)(2,1)S(1)}, bf16[2,256,512]{2,1,0:T(8,128)(2,1)}, bf16[2,256,512]{2,1,0:T(8,128)(2,1)}, bf16[2,256,512]{2,1,0:T(8,128)(...) custom-call(bf16[4,384,512]{2,1,0:T(8,128)(2,1)S(1)} %get-tuple-elem, ...), custom_call_target="tpu_custom_call" | custom-call | tf_op jit(solution)/shard_map/pair/pallas_call | solution.py:176
  26.1 0.8 copy-done.10
  26.9 2.1 collective-permute-start.6
  29.0 1.5 collective-permute-start.7
  30.5 10.4 %all-to-all-done.refs_0_ = bf16[8,576,128]{2,1,0:T(8,128)(2,1)S(1)} async-done(((bf16[8,576,128]{2,1,0:T(8,128)(2,1)}), bf16[8,576,128]{2,1,0:T(8,128)(2,1)S(1)}, u32[]{:S(2)}, u32[]{:S(2)}) %all-to-all-start) | async-done | bytes 1179680 | tf_op jit(solution)/shard_map/state_scan/all_to_all | solution.py:462
  41.2 1.3 collective-permute-start.1
  42.6 1.1 collective-permute-start.4
  43.7 11.3 %collective-permute-done.1.refs_0_.refs_1_ = bf16[4,144,128]{2,1,0:T(8,128)(2,1)S(1)} collective-permute-done((bf16[4,144,128]{2,1,0:T(8,128)(2,1)S(1)}, bf16[4,144,128]{2,1,0:T(8,128)(2,1)S(1)}, u32[]{:S(2)}, u32[]{:S(2)}) %collective-permute-start.1) | collective-permute-done | bytes 147488 | tf_op jit(solution)/shard_map/state_scan/ppermute | solution.py:440
  55.0 1.9 collective-permute-start.5
  56.9 1.3 collective-permute-start.2
  58.2 4.7 %collective-permute-done.5.refs_4_ = bf16[2,128,512]{2,1,0:T(8,128)(2,1)S(1)} collective-permute-done((bf16[2,128,512]{2,1,0:T(8,128)(2,1)}, bf16[2,128,512]{2,1,0:T(8,128)(2,1)S(1)}, u32[]{:S(2)}, u32[]{:S(2)}) %collective-permute-start.5) | collective-permute-done | bytes 262176 | tf_op jit(solution)/shard_map/out_weight_gather/ppermute | solution.py:433
  62.9 1.1 in_order.1.refs_4_.refs_0_
  64.0 3.7 %collective-permute-done.2.refs_2_ = bf16[4,144,128]{2,1,0:T(8,128)(2,1)S(1)} collective-permute-done((bf16[4,144,128]{2,1,0:T(8,128)(2,1)S(1)}, bf16[4,144,128]{2,1,0:T(8,128)(2,1)S(1)}, u32[]{:S(2)}, u32[]{:S(2)}) %collective-permute-start.2) | collective-permute-done | bytes 147488 | tf_op jit(solution)/shard_map/state_scan/ppermute | solution.py:440
  67.7 0.6 copy-done.12
  68.4 0.9 copy-done.13
  69.3 1.3 plane_prefix.1.refs_6_.refs_1_
  70.6 0.7 all-gather.5.cloned.1.call-update
  71.3 3.6 %all-to-all-start.1 = ((bf16[8,4,128,128]{3,2,1,0:T(8,128)(2,1)}), bf16[8,4,128,128]{3,2,1,0:T(8,128)(2,1)S(1)}, u32[]{:S(2)}, u32[]{:S(2)}) async-start(bf16[8,4,128,128]{3,2,1,0:T(8,128)(2,1)} %plane_prefix.1.refs_6_.refs_1_), calls=%async_computation.1 | async-start | bytes 2097152 | tf_op jit(solution)/shard_map/state_scan/all_to_all | solution.py:482
  74.9 0.6 reduce-window.6
  75.5 2.9 %collective-permute-start.8 = (bf16[2,256,512]{2,1,0:T(8,128)(2,1)S(1)}, bf16[2,256,512]{2,1,0:T(8,128)(2,1)S(1)}, u32[]{:S(2)}, u32[]{:S(2)}) collective-permute-start(bf16[2,256,512]{2,1,0:T(8,128)(2,1)S(1)} %hold.5), channel_id=1, source_target_pairs={{0,6},{1,7},{2,4},{3,5},{4,2},{5,3},{6,0},{7,1},{8,14},{9,15},{10,... | collective-permute-start | bytes 1572872 | tf_op jit(solution)/shard_map/residual_exchange/ppermute | solution.py:433
  78.7 1.4 copy.24
  80.3 0.6 reduce_window_sum.21.refs_5_
  80.9 10.2 %local_intra.1 = (bf16[256,4096]{1,0:T(8,128)(2,1)}, bf16[256,4096]{1,0:T(8,128)(2,1)}) custom-call(bf16[256,4096]{1,0:T(8,128)(2,1)} %refs_0_.5, bf16[256,4096]{1,0:T(8,128)(2,1)} %refs_1_.5, bf16[256,4096]{1,0:T(8,128)(2,1)} %refs_2_.4, bf16[256,4096]{1,0:T(8,128)(2,1)} %refs_3_.1, f32[8,256,4]{2,1,0:T(8,128)} %bitcast.21, ...), custom_call_target="tpu_custom_call" | custom-call | tf_op jit(solution)/shard_map/local_intra/pallas_call | solution.py:151
  91.2 1.0 copy-done.17
  92.2 8.8 %mix.1 = (bf16[128,4096]{1,0:T(8,128)(2,1)}, bf16[128,4096]{1,0:T(8,128)(2,1)}) custom-call(bf16[256,4096]{1,0:T(8,128)(2,1)} %refs_0_.5, bf16[256,4096]{1,0:T(8,128)(2,1)} %get-tuple-element.45.refs_1_, bf16[256,4096]{1,0:T(8,128)(2,1)} %get-tuple-element.46.refs_2_, f32[8,256,4]{2,1,0:T(8,128)} %bitcast.22, bf16[32,128,128]{2,1,0:T(8,128)(2,1)} %bitcast.23), custom_call_target="tpu_custom_call" | custom-call | tf_op jit(solution)/shard_map/mix/pallas_call | solution.py:151
  102.4 24.1 %collective-permute-done.9.refs_0_ = bf16[128,4096]{1,0:T(8,128)(2,1)S(1)} collective-permute-done((bf16[128,4096]{1,0:T(8,128)(2,1)}, bf16[128,4096]{1,0:T(8,128)(2,1)S(1)}, u32[]{:S(2)}, u32[]{:S(2)}) %collective-permute-start.9) | collective-permute-done | bytes 1048608 | tf_op jit(solution)/shard_map/projections/ppermute | solution.py:433
  127.1 1.3 collective-permute-start.12
  128.9 21.8 %collective-permute-done.10.refs_2_.refs_0_ = bf16[128,4096]{1,0:T(8,128)(2,1)} collective-permute-done((bf16[128,4096]{1,0:T(8,128)(2,1)S(1)}, bf16[128,4096]{1,0:T(8,128)(2,1)}, u32[]{:S(2)}, u32[]{:S(2)}) %collective-permute-start.10) | collective-permute-done | bytes 1048608 | tf_op jit(solution)/shard_map/projections/ppermute | solution.py:433
  151.2 1.2 collective-permute-start.15
  152.4 0.9 collective-permute-start.16
  153.3 2.0 multiply_convert_fusion.1.refs_2_
  155.4 2.2 copy-done
  157.6 1.2 copy-done.9
  158.8 4.3 %out_projection.4 = (bf16[256,512]{1,0:T(8,128)(2,1)S(1)}, bf16[256,512]{1,0:T(8,128)(2,1)S(1)}) custom-call(bf16[128,4096]{1,0:T(8,128)(2,1)S(1)} %copy-done.9, bf16[128,4096]{1,0:T(8,128)(2,1)} %collective-permute-done.17.refs_1_, bf16[128,4096]{1,0:T(8,128)(2,1)} %collective-permute-done.11.refs_2_, bf16[128,4096]{1,0:T(8,128)(2,1)} %collective-permute-done.18.refs_3_, ...), custom_call_target="tpu_custom_call" | custom-call | tf_op jit(solution)/shard_map/projections/out_projection/pallas_call | solution.py:176
  163.2 4.5 %out_projection.5 = (bf16[256,512]{1,0:T(8,128)(2,1)S(1)}, bf16[256,512]{1,0:T(8,128)(2,1)S(1)}) custom-call(bf16[128,4096]{1,0:T(8,128)(2,1)} %collective-permute-done.10.refs_2_.refs_0_, bf16[128,4096]{1,0:T(8,128)(2,1)} %collective-permute-done.21.refs_1_, bf16[128,4096]{1,0:T(8,128)(2,1)} %collective-permute-done.12.refs_3_.refs_2_, ...), custom_call_target="tpu_custom_call" | custom-call | tf_op jit(solution)/shard_map/projections/out_projection/pallas_call | solution.py:176
  168.2 2.0 multiply_convert_fusion.refs_3_
  170.2 1.3 cache_projection.4
  171.5 1.3 cache_projection.5
  172.8 4.4 %collective-permute-done.15.refs_0_ = bf16[128,4096]{1,0:T(8,128)(2,1)} collective-permute-done((bf16[128,4096]{1,0:T(8,128)(2,1)}, bf16[128,4096]{1,0:T(8,128)(2,1)}, u32[]{:S(2)}, u32[]{:S(2)}) %collective-permute-start.15) | collective-permute-done | bytes 1048608 | tf_op jit(solution)/shard_map/projections/ppermute | solution.py:433
  177.1 0.9 collective-permute-done.16.refs_1_
  178.5 0.9 collective-permute-start.27
  179.5 1.4 collective-permute-start.28
  181.0 1.4 collective-permute-done.25.refs_3_
  182.4 0.9 collective-permute-start.29
  183.3 3.9 %out_projection.6 = (bf16[256,512]{1,0:T(8,128)(2,1)S(1)}, bf16[256,512]{1,0:T(8,128)(2,1)S(1)}) custom-call(bf16[128,4096]{1,0:T(8,128)(2,1)} %get-tuple-element.60.refs_0_, bf16[128,4096]{1,0:T(8,128)(2,1)S(1)} %collective-permute-done.24.refs_1_, bf16[128,4096]{1,0:T(8,128)(2,1)} %get-tuple-element.61.refs_2_, ...), custom_call_target="tpu_custom_call" | custom-call | tf_op jit(solution)/shard_map/projections/out_projection/pallas_call | solution.py:176
  187.1 6.5 %collective-permute-done.27.refs_4_ = bf16[128,2176]{1,0:T(8,128)(2,1)S(1)} collective-permute-done((bf16[128,2176]{1,0:T(8,128)(2,1)S(1)}, bf16[128,2176]{1,0:T(8,128)(2,1)S(1)}, u32[]{:S(2)}, u32[]{:S(2)}) %collective-permute-start.27) | collective-permute-done | bytes 557088 | tf_op jit(solution)/shard_map/projections/ppermute | solution.py:433
  193.6 1.3 collective-permute-done.28.refs_5_
  194.9 1.1 collective-permute-start.30
  196.0 1.3 cache_projection.6
  197.3 0.9 collective-permute-start.32
  198.3 1.5 collective-permute-start.33
  199.7 7.1 %collective-permute-done.29.refs_8_.refs_4_ = bf16[128,2176]{1,0:T(8,128)(2,1)S(1)} collective-permute-done((bf16[128,2176]{1,0:T(8,128)(2,1)S(1)}, bf16[128,2176]{1,0:T(8,128)(2,1)S(1)}, u32[]{:S(2)}, u32[]{:S(2)}) %collective-permute-start.29) | collective-permute-done | bytes 557088 | tf_op jit(solution)/shard_map/projections/ppermute | solution.py:433
  206.9 3.6 %collective-permute-done.30.refs_9_.refs_7_ = bf16[128,2176]{1,0:T(8,128)(2,1)S(1)} collective-permute-done((bf16[128,2176]{1,0:T(8,128)(2,1)S(1)}, bf16[128,2176]{1,0:T(8,128)(2,1)S(1)}, u32[]{:S(2)}, u32[]{:S(2)}) %collective-permute-start.30) | collective-permute-done | bytes 557088 | tf_op jit(solution)/shard_map/projections/ppermute | solution.py:433
  210.5 3.9 %out_projection.7 = (bf16[256,512]{1,0:T(8,128)(2,1)S(1)}, bf16[256,512]{1,0:T(8,128)(2,1)S(1)}) custom-call(bf16[128,4096]{1,0:T(8,128)(2,1)} %get-tuple-element.52.refs_0_, bf16[128,4096]{1,0:T(8,128)(2,1)S(1)} %collective-permute-done.13.refs_1_, bf16[128,4096]{1,0:T(8,128)(2,1)} %get-tuple-element.53.refs_2_, ...), custom_call_target="tpu_custom_call" | custom-call | tf_op jit(solution)/shard_map/projections/out_projection/pallas_call | solution.py:176
  214.4 1.5 collective-permute-done.31.refs_1_
  215.9 2.1 collective-permute-done.32.refs_5_
  218.1 2.5 %collective-permute-done.33.refs_6_ = bf16[128,2176]{1,0:T(8,128)(2,1)S(1)} collective-permute-done((bf16[128,2176]{1,0:T(8,128)(2,1)S(1)}, bf16[128,2176]{1,0:T(8,128)(2,1)S(1)}, u32[]{:S(2)}, u32[]{:S(2)}) %collective-permute-start.33) | collective-permute-done | bytes 557088 | tf_op jit(solution)/shard_map/projections/ppermute | solution.py:433
  220.6 2.4 %cache_projection.7 = (bf16[256,1024]{1,0:T(8,128)(2,1)}, bf16[256,1024]{1,0:T(8,128)(2,1)}) custom-call(bf16[256,512]{1,0:T(8,128)(2,1)S(1)} %get-tuple-element.67.refs_0_, bf16[256,512]{1,0:T(8,128)(2,1)S(1)} %collective-permute-done.31.refs_1_, bf16[512,2048]{1,0:T(8,128)(2,1)S(1)} %multiply_convert_fusion.1.refs_2_, ...), custom_call_target="tpu_custom_call" | custom-call | tf_op jit(solution)/shard_map/projections/cache_projection/pallas_call | solution.py:176
  (91 shorter events, 5.3 us)
Async XLA Ops:
  7.2 61.2 %all-gather.3.cloned.1.call-start = ((), (), s32[]{:S(2)}) async-start(), calls=%async_computation.2 | async-start | bytes 2621440 | tf_op jit(solution)/shard_map/kv_weight_gather/all_gather | solution.py:455
  9.4 7.0 %copy-start.6 = (bf16[256,4096]{1,0:T(8,128)(2,1)S(1)}, bf16[256,4096]{1,0:T(8,128)(2,1)}, u32[]{:S(2)}) copy-start(bf16[256,4096]{1,0:T(8,128)(2,1)} %refs_1_.4) | copy-start | bytes 6291460
  16.4 1.3 copy-start.7
  19.7 3.8 %collective-permute-start = (bf16[4,384,512]{2,1,0:T(8,128)(2,1)}, bf16[4,384,512]{2,1,0:T(8,128)(2,1)}, u32[]{:S(2)}, u32[]{:S(2)}) collective-permute-start(bf16[4,384,512]{2,1,0:T(8,128)(2,1)} %get-tuple-element.37), channel_id=1, source_target_pairs={{0,1},{1,0},{2,3},{3,2},{4,5},{5,4},{6,7},{7,6},{8,9},{9,8},{10,11... | collective-permute-start | bytes 4718600 | tf_op jit(solution)/shard_map/ppermute | solution.py:433
  19.7 21.2 %all-to-all-start = ((bf16[8,576,128]{2,1,0:T(8,128)(2,1)}), bf16[8,576,128]{2,1,0:T(8,128)(2,1)S(1)}, u32[]{:S(2)}, u32[]{:S(2)}) async-start(bf16[8,576,128]{2,1,0:T(8,128)(2,1)} %local_states.1.refs_3_), calls=%async_computation | async-start | bytes 2359296 | tf_op jit(solution)/shard_map/state_scan/all_to_all | solution.py:462
  26.1 0.8 copy-start.10
  26.9 2.1 copy-start.14
  26.9 2.1 copy-start.15
  26.9 2.1 copy-start.16
  26.9 37.0 %copy-start.4 = (bf16[2,256,512]{2,1,0:T(8,128)(2,1)}, bf16[2,256,512]{2,1,0:T(8,128)(2,1)S(1)}, u32[]{:S(2)}) copy-start(bf16[2,256,512]{2,1,0:T(8,128)(2,1)S(1)} %get-tuple-element.38.refs_1_.refs_5_.refs_6_) | copy-start | bytes 1572868
  26.9 41.4 %collective-permute-start.6 = (bf16[2,256,512]{2,1,0:T(8,128)(2,1)}, bf16[2,256,512]{2,1,0:T(8,128)(2,1)S(1)}, u32[]{:S(2)}, u32[]{:S(2)}) collective-permute-start(bf16[2,256,512]{2,1,0:T(8,128)(2,1)} %get-tuple-element.43), channel_id=1, source_target_pairs={{0,2},{1,3},{2,0},{3,1},{4,6},{5,7},{6,4},{7,5},{8,10},{9,11},{10,... | collective-permute-start | bytes 1572872 | tf_op jit(solution)/shard_map/residual_exchange/ppermute | solution.py:433
  29.0 39.3 %collective-permute-start.7 = (bf16[2,256,512]{2,1,0:T(8,128)(2,1)}, bf16[2,256,512]{2,1,0:T(8,128)(2,1)S(1)}, u32[]{:S(2)}, u32[]{:S(2)}) collective-permute-start(bf16[2,256,512]{2,1,0:T(8,128)(2,1)} %get-tuple-element.44), channel_id=1, source_target_pairs={{0,4},{1,5},{2,6},{3,7},{4,0},{5,1},{6,2},{7,3},{8,12},{9,13},{10,... | collective-permute-start | bytes 1572872 | tf_op jit(solution)/shard_map/residual_exchange/ppermute | solution.py:433
  41.2 13.8 %collective-permute-start.1 = (bf16[4,144,128]{2,1,0:T(8,128)(2,1)S(1)}, bf16[4,144,128]{2,1,0:T(8,128)(2,1)S(1)}, u32[]{:S(2)}, u32[]{:S(2)}) collective-permute-start(bf16[4,144,128]{2,1,0:T(8,128)(2,1)S(1)} %plane_total.1.refs_1_.refs_5_), channel_id=1, source_target_pairs={{0,8},{1,9},{2,10},{3,11},{4,12},{5,13},{6,14},{7,15},{8,16},{9,17... | collective-permute-start | bytes 442376 | tf_op jit(solution)/shard_map/state_scan/ppermute | solution.py:440
  42.5 14.5 %collective-permute-start.3 = (bf16[2,128,512]{2,1,0:T(8,128)(2,1)}, bf16[2,128,512]{2,1,0:T(8,128)(2,1)S(1)}, u32[]{:S(2)}, u32[]{:S(2)}) collective-permute-start(bf16[2,128,512]{2,1,0:T(8,128)(2,1)} %copy-done.16), channel_id=1, source_target_pairs={{0,2},{1,3},{2,0},{3,1},{4,6},{5,7},{6,4},{7,5},{8,10},{9,11},{10,... | collective-permute-start | bytes 786440 | tf_op jit(solution)/shard_map/out_weight_gather/ppermute | solution.py:433
  42.6 15.7 %collective-permute-start.4 = (bf16[2,128,512]{2,1,0:T(8,128)(2,1)}, bf16[2,128,512]{2,1,0:T(8,128)(2,1)S(1)}, u32[]{:S(2)}, u32[]{:S(2)}) collective-permute-start(bf16[2,128,512]{2,1,0:T(8,128)(2,1)} %copy-done.15), channel_id=1, source_target_pairs={{0,4},{1,5},{2,6},{3,7},{4,0},{5,1},{6,2},{7,3},{8,12},{9,13},{10,... | collective-permute-start | bytes 786440 | tf_op jit(solution)/shard_map/out_weight_gather/ppermute | solution.py:433
  55.0 7.9 %collective-permute-start.5 = (bf16[2,128,512]{2,1,0:T(8,128)(2,1)}, bf16[2,128,512]{2,1,0:T(8,128)(2,1)S(1)}, u32[]{:S(2)}, u32[]{:S(2)}) collective-permute-start(bf16[2,128,512]{2,1,0:T(8,128)(2,1)} %copy-done.14), channel_id=1, source_target_pairs={{0,6},{1,7},{2,4},{3,5},{4,2},{5,3},{6,0},{7,1},{8,14},{9,15},{10,... | collective-permute-start | bytes 786440 | tf_op jit(solution)/shard_map/out_weight_gather/ppermute | solution.py:433
  56.9 10.8 %collective-permute-start.2 = (bf16[4,144,128]{2,1,0:T(8,128)(2,1)S(1)}, bf16[4,144,128]{2,1,0:T(8,128)(2,1)S(1)}, u32[]{:S(2)}, u32[]{:S(2)}) collective-permute-start(bf16[4,144,128]{2,1,0:T(8,128)(2,1)S(1)} %join.1), channel_id=1, source_target_pairs={{0,16},{1,17},{2,18},{3,19},{4,20},{5,21},{6,22},{7,23},{8,24},{9,... | collective-permute-start | bytes 442376 | tf_op jit(solution)/shard_map/state_scan/ppermute | solution.py:440
  67.7 0.6 copy-start.12
  68.3 0.9 copy-start.13
  70.6 84.7 %all-gather.5.cloned.1.call-start = ((), (), s32[]{:S(2)}) async-start(), calls=%async_computation.3 | async-start | bytes 5242880 | tf_op jit(solution)/shard_map/out_weight_gather/all_gather | solution.py:477
  70.6 4.3 %copy-start.18 = (f32[256,32]{0,1:T(8,128)S(1)}, f32[256,32]{0,1:T(8,128)}, u32[]{:S(2)}) copy-start(f32[256,32]{0,1:T(8,128)} %param.14) | copy-start | bytes 98308
  70.6 4.9 %copy-start.11 = (bf16[2,256,512]{2,1,0:T(8,128)(2,1)S(1)}, bf16[2,256,512]{2,1,0:T(8,128)(2,1)}, u32[]{:S(2)}) copy-start(bf16[2,256,512]{2,1,0:T(8,128)(2,1)} %copy-done.10) | copy-start | bytes 1572868
  71.3 19.8 %all-to-all-start.1 = ((bf16[8,4,128,128]{3,2,1,0:T(8,128)(2,1)}), bf16[8,4,128,128]{3,2,1,0:T(8,128)(2,1)S(1)}, u32[]{:S(2)}, u32[]{:S(2)}) async-start(bf16[8,4,128,128]{3,2,1,0:T(8,128)(2,1)} %plane_prefix.1.refs_6_.refs_1_), calls=%async_computation.1 | async-start | bytes 2097152 | tf_op jit(solution)/shard_map/state_scan/all_to_all | solution.py:482
  75.5 26.0 %collective-permute-start.8 = (bf16[2,256,512]{2,1,0:T(8,128)(2,1)S(1)}, bf16[2,256,512]{2,1,0:T(8,128)(2,1)S(1)}, u32[]{:S(2)}, u32[]{:S(2)}) collective-permute-start(bf16[2,256,512]{2,1,0:T(8,128)(2,1)S(1)} %hold.5), channel_id=1, source_target_pairs={{0,6},{1,7},{2,4},{3,5},{4,2},{5,3},{6,0},{7,1},{8,14},{9,15},{10,... | collective-permute-start | bytes 1572872 | tf_op jit(solution)/shard_map/residual_exchange/ppermute | solution.py:433
  91.2 1.0 copy-start.17
  101.0 50.2 %copy-start.19 = (bf16[4096]{0:T(1024)(128)(2,1)S(1)}, bf16[4096]{0:T(1024)(128)(2,1)}, u32[]{:S(2)}) copy-start(bf16[4096]{0:T(1024)(128)(2,1)} %param.16) | copy-start | bytes 24580
  101.5 49.7 %copy-start.2 = (bf16[2,256,512]{2,1,0:T(8,128)(2,1)}, bf16[2,256,512]{2,1,0:T(8,128)(2,1)S(1)}, u32[]{:S(2)}) copy-start(bf16[2,256,512]{2,1,0:T(8,128)(2,1)S(1)} %collective-permute-done.8.refs_2_.refs_5_.refs_6_) | copy-start | bytes 1572868
  101.5 25.0 %collective-permute-start.9 = (bf16[128,4096]{1,0:T(8,128)(2,1)}, bf16[128,4096]{1,0:T(8,128)(2,1)S(1)}, u32[]{:S(2)}, u32[]{:S(2)}) collective-permute-start(bf16[128,4096]{1,0:T(8,128)(2,1)} %get-tuple-element.50.refs_0_), channel_id=1, source_target_pairs={{0,2},{1,3},{2,0},{3,1},{4,6},{5,7},{6,4},{7,5},{8,10},{9,11},{10,... | collective-permute-start | bytes 3145736 | tf_op jit(solution)/shard_map/projections/ppermute | solution.py:433
  102.1 25.0 %collective-permute-start.11 = (bf16[128,4096]{1,0:T(8,128)(2,1)}, bf16[128,4096]{1,0:T(8,128)(2,1)}, u32[]{:S(2)}, u32[]{:S(2)}) collective-permute-start(bf16[128,4096]{1,0:T(8,128)(2,1)} %get-tuple-element.51.refs_1_), channel_id=1, source_target_pairs={{0,4},{1,5},{2,6},{3,7},{4,0},{5,1},{6,2},{7,3},{8,12},{9,13},{10,... | collective-permute-start | bytes 3145736 | tf_op jit(solution)/shard_map/projections/ppermute | solution.py:433
  126.5 24.7 %copy-start.8 = (bf16[128,4096]{1,0:T(8,128)(2,1)}, bf16[128,4096]{1,0:T(8,128)(2,1)S(1)}, u32[]{:S(2)}) copy-start(bf16[128,4096]{1,0:T(8,128)(2,1)S(1)} %collective-permute-done.9.refs_0_) | copy-start | bytes 3145732
  126.5 24.1 %collective-permute-start.10 = (bf16[128,4096]{1,0:T(8,128)(2,1)S(1)}, bf16[128,4096]{1,0:T(8,128)(2,1)}, u32[]{:S(2)}, u32[]{:S(2)}) collective-permute-start(bf16[128,4096]{1,0:T(8,128)(2,1)S(1)} %collective-permute-done.9.refs_0_), channel_id=1, source_target_pairs={{0,4},{1,5},{2,6},{3,7},{4,0},{5,1},{6,2},{7,3},{8,12},{9,13},{10,... | collective-permute-start | bytes 3145736 | tf_op jit(solution)/shard_map/projections/ppermute | solution.py:433
  127.1 24.1 %collective-permute-start.12 = (bf16[128,4096]{1,0:T(8,128)(2,1)}, bf16[128,4096]{1,0:T(8,128)(2,1)}, u32[]{:S(2)}, u32[]{:S(2)}) collective-permute-start(bf16[128,4096]{1,0:T(8,128)(2,1)} %collective-permute-done.11.refs_2_), channel_id=1, source_target_pairs={{0,2},{1,3},{2,0},{3,1},{4,6},{5,7},{6,4},{7,5},{8,10},{9,11},{10,... | collective-permute-start | bytes 3145736 | tf_op jit(solution)/shard_map/projections/ppermute | solution.py:433
  128.4 39.9 %collective-permute-start.20 = (bf16[512,2048]{1,0:T(8,128)(2,1)}, bf16[512,2048]{1,0:T(8,128)(2,1)}, u32[]{:S(2)}, u32[]{:S(2)}) collective-permute-start(bf16[512,2048]{1,0:T(8,128)(2,1)} %all-gather.3.cloned.1.call-done.refs_3_.refs_1_), channel_id=1, source_target_pairs={{0,1},{1,0},{2,3},{3,2},{4,5},{5,4},{6,7},{7,6},{8,9},{9,8},{10,11... | collective-permute-start | bytes 6291464 | tf_op jit(solution)/shard_map/cache_weight/ppermute | solution.py:433
  128.4 22.8 %collective-permute-start.17 = (bf16[128,4096]{1,0:T(8,128)(2,1)S(1)}, bf16[128,4096]{1,0:T(8,128)(2,1)}, u32[]{:S(2)}, u32[]{:S(2)}) collective-permute-start(bf16[128,4096]{1,0:T(8,128)(2,1)S(1)} %collective-permute-done.9.refs_0_), channel_id=1, source_target_pairs={{0,1},{1,0},{2,3},{3,2},{4,5},{5,4},{6,7},{7,6},{8,9},{9,8},{10,11... | collective-permute-start | bytes 3145736 | tf_op jit(solution)/shard_map/projections/ppermute | solution.py:433
  128.9 23.5 %collective-permute-start.18 = (bf16[128,4096]{1,0:T(8,128)(2,1)}, bf16[128,4096]{1,0:T(8,128)(2,1)}, u32[]{:S(2)}, u32[]{:S(2)}) collective-permute-start(bf16[128,4096]{1,0:T(8,128)(2,1)} %collective-permute-done.11.refs_2_), channel_id=1, source_target_pairs={{0,1},{1,0},{2,3},{3,2},{4,5},{5,4},{6,7},{7,6},{8,9},{9,8},{10,11... | collective-permute-start | bytes 3145736 | tf_op jit(solution)/shard_map/projections/ppermute | solution.py:433
  150.7 12.5 %collective-permute-start.21 = (bf16[128,4096]{1,0:T(8,128)(2,1)}, bf16[128,4096]{1,0:T(8,128)(2,1)}, u32[]{:S(2)}, u32[]{:S(2)}) collective-permute-start(bf16[128,4096]{1,0:T(8,128)(2,1)} %collective-permute-done.10.refs_2_.refs_0_), channel_id=1, source_target_pairs={{0,1},{1,0},{2,3},{3,2},{4,5},{5,4},{6,7},{7,6},{8,9},{9,8},{10,11... | collective-permute-start | bytes 3145736 | tf_op jit(solution)/shard_map/projections/ppermute | solution.py:433
  151.1 12.0 %collective-permute-start.22 = (bf16[128,4096]{1,0:T(8,128)(2,1)}, bf16[128,4096]{1,0:T(8,128)(2,1)}, u32[]{:S(2)}, u32[]{:S(2)}) collective-permute-start(bf16[128,4096]{1,0:T(8,128)(2,1)} %collective-permute-done.12.refs_3_.refs_2_), channel_id=1, source_target_pairs={{0,1},{1,0},{2,3},{3,2},{4,5},{5,4},{6,7},{7,6},{8,9},{9,8},{10,11... | collective-permute-start | bytes 3145736 | tf_op jit(solution)/shard_map/projections/ppermute | solution.py:433
  151.2 25.9 %collective-permute-start.15 = (bf16[128,4096]{1,0:T(8,128)(2,1)}, bf16[128,4096]{1,0:T(8,128)(2,1)}, u32[]{:S(2)}, u32[]{:S(2)}) collective-permute-start(bf16[128,4096]{1,0:T(8,128)(2,1)} %get-tuple-element.53.refs_2_), channel_id=1, source_target_pairs={{0,2},{1,3},{2,0},{3,1},{4,6},{5,7},{6,4},{7,5},{8,10},{9,11},{10,... | collective-permute-start | bytes 3145736 | tf_op jit(solution)/shard_map/projections/ppermute | solution.py:433
  152.4 25.6 %collective-permute-start.16 = (bf16[128,4096]{1,0:T(8,128)(2,1)}, bf16[128,4096]{1,0:T(8,128)(2,1)}, u32[]{:S(2)}, u32[]{:S(2)}) collective-permute-start(bf16[128,4096]{1,0:T(8,128)(2,1)} %get-tuple-element.52.refs_0_), channel_id=1, source_target_pairs={{0,4},{1,5},{2,6},{3,7},{4,0},{5,1},{6,2},{7,3},{8,12},{9,13},{10,... | collective-permute-start | bytes 3145736 | tf_op jit(solution)/shard_map/projections/ppermute | solution.py:433
  155.4 2.2 copy-start
  157.5 1.2 copy-start.9
  158.8 4.4 %copy-start.1 = (bf16[4096,512]{1,0:T(8,128)(2,1)S(1)}, bf16[4096,512]{1,0:T(8,128)(2,1)}, u32[]{:S(2)}) copy-start(bf16[4096,512]{1,0:T(8,128)(2,1)} %all-gather.5.cloned.1.call-done.refs_4_) | copy-start | bytes 12582916
  158.8 4.4 %copy-start.3 = (bf16[2,256,512]{2,1,0:T(8,128)(2,1)S(1)}, bf16[2,256,512]{2,1,0:T(8,128)(2,1)}, u32[]{:S(2)}) copy-start(bf16[2,256,512]{2,1,0:T(8,128)(2,1)} %copy-done.2) | copy-start | bytes 1572868
  167.7 2.6 %collective-permute-start.23 = (bf16[256,512]{1,0:T(8,128)(2,1)S(1)}, bf16[256,512]{1,0:T(8,128)(2,1)S(1)}, u32[]{:S(2)}, u32[]{:S(2)}) collective-permute-start(bf16[256,512]{1,0:T(8,128)(2,1)S(1)} %get-tuple-element.57), channel_id=1, source_target_pairs={{0,1},{1,0},{2,3},{3,2},{4,5},{5,4},{6,7},{7,6},{8,9},{9,8},{10,11... | collective-permute-start | bytes 786440 | tf_op jit(solution)/shard_map/projections/ppermute | solution.py:433
  167.7 3.8 %collective-permute-start.19 = (bf16[256,512]{1,0:T(8,128)(2,1)S(1)}, bf16[256,512]{1,0:T(8,128)(2,1)S(1)}, u32[]{:S(2)}, u32[]{:S(2)}) collective-permute-start(bf16[256,512]{1,0:T(8,128)(2,1)S(1)} %get-tuple-element.55), channel_id=1, source_target_pairs={{0,1},{1,0},{2,3},{3,2},{4,5},{5,4},{6,7},{7,6},{8,9},{9,8},{10,11... | collective-permute-start | bytes 786440 | tf_op jit(solution)/shard_map/projections/ppermute | solution.py:433
  178.0 2.9 %collective-permute-start.24 = (bf16[128,4096]{1,0:T(8,128)(2,1)}, bf16[128,4096]{1,0:T(8,128)(2,1)S(1)}, u32[]{:S(2)}, u32[]{:S(2)}) collective-permute-start(bf16[128,4096]{1,0:T(8,128)(2,1)} %get-tuple-element.60.refs_0_), channel_id=1, source_target_pairs={{0,1},{1,0},{2,3},{3,2},{4,5},{5,4},{6,7},{7,6},{8,9},{9,8},{10,11... | collective-permute-start | bytes 3145736 | tf_op jit(solution)/shard_map/projections/ppermute | solution.py:433
  178.0 4.4 %collective-permute-start.25 = (bf16[128,4096]{1,0:T(8,128)(2,1)}, bf16[128,4096]{1,0:T(8,128)(2,1)S(1)}, u32[]{:S(2)}, u32[]{:S(2)}) collective-permute-start(bf16[128,4096]{1,0:T(8,128)(2,1)} %get-tuple-element.61.refs_2_), channel_id=1, source_target_pairs={{0,1},{1,0},{2,3},{3,2},{4,5},{5,4},{6,7},{7,6},{8,9},{9,8},{10,11... | collective-permute-start | bytes 3145736 | tf_op jit(solution)/shard_map/projections/ppermute | solution.py:433
  178.5 19.7 %collective-permute-start.13 = (bf16[128,4096]{1,0:T(8,128)(2,1)}, bf16[128,4096]{1,0:T(8,128)(2,1)S(1)}, u32[]{:S(2)}, u32[]{:S(2)}) collective-permute-start(bf16[128,4096]{1,0:T(8,128)(2,1)} %get-tuple-element.52.refs_0_), channel_id=1, source_target_pairs={{0,1},{1,0},{2,3},{3,2},{4,5},{5,4},{6,7},{7,6},{8,9},{9,8},{10,11... | collective-permute-start | bytes 3145736 | tf_op jit(solution)/shard_map/projections/ppermute | solution.py:433
  178.5 15.0 %collective-permute-start.27 = (bf16[128,2176]{1,0:T(8,128)(2,1)S(1)}, bf16[128,2176]{1,0:T(8,128)(2,1)S(1)}, u32[]{:S(2)}, u32[]{:S(2)}) collective-permute-start(bf16[128,2176]{1,0:T(8,128)(2,1)S(1)} %get-tuple-element.64), channel_id=1, source_target_pairs={{0,4},{1,5},{2,6},{3,7},{4,0},{5,1},{6,2},{7,3},{8,12},{9,13},{10,... | collective-permute-start | bytes 1671176 | tf_op jit(solution)/shard_map/projections/ppermute | solution.py:433
  179.5 15.5 %collective-permute-start.28 = (bf16[128,2176]{1,0:T(8,128)(2,1)S(1)}, bf16[128,2176]{1,0:T(8,128)(2,1)S(1)}, u32[]{:S(2)}, u32[]{:S(2)}) collective-permute-start(bf16[128,2176]{1,0:T(8,128)(2,1)S(1)} %get-tuple-element.58.refs_4_), channel_id=1, source_target_pairs={{0,2},{1,3},{2,0},{3,1},{4,6},{5,7},{6,4},{7,5},{8,10},{9,11},{10,... | collective-permute-start | bytes 1671176 | tf_op jit(solution)/shard_map/projections/ppermute | solution.py:433
  180.9 18.9 %collective-permute-start.14 = (bf16[128,4096]{1,0:T(8,128)(2,1)}, bf16[128,4096]{1,0:T(8,128)(2,1)S(1)}, u32[]{:S(2)}, u32[]{:S(2)}) collective-permute-start(bf16[128,4096]{1,0:T(8,128)(2,1)} %get-tuple-element.53.refs_2_), channel_id=1, source_target_pairs={{0,1},{1,0},{2,3},{3,2},{4,5},{5,4},{6,7},{7,6},{8,9},{9,8},{10,11... | collective-permute-start | bytes 3145736 | tf_op jit(solution)/shard_map/projections/ppermute | solution.py:433
  182.4 24.5 %collective-permute-start.29 = (bf16[128,2176]{1,0:T(8,128)(2,1)S(1)}, bf16[128,2176]{1,0:T(8,128)(2,1)S(1)}, u32[]{:S(2)}, u32[]{:S(2)}) collective-permute-start(bf16[128,2176]{1,0:T(8,128)(2,1)S(1)} %get-tuple-element.59.refs_2_), channel_id=1, source_target_pairs={{0,2},{1,3},{2,0},{3,1},{4,6},{5,7},{6,4},{7,5},{8,10},{9,11},{10,... | collective-permute-start | bytes 1671176 | tf_op jit(solution)/shard_map/projections/ppermute | solution.py:433
  193.6 2.5 %collective-permute-start.26 = (bf16[256,512]{1,0:T(8,128)(2,1)S(1)}, bf16[256,512]{1,0:T(8,128)(2,1)S(1)}, u32[]{:S(2)}, u32[]{:S(2)}) collective-permute-start(bf16[256,512]{1,0:T(8,128)(2,1)S(1)} %get-tuple-element.63), channel_id=1, source_target_pairs={{0,1},{1,0},{2,3},{3,2},{4,5},{5,4},{6,7},{7,6},{8,9},{9,8},{10,11... | collective-permute-start | bytes 786440 | tf_op jit(solution)/shard_map/projections/ppermute | solution.py:433
  194.9 15.6 %collective-permute-start.30 = (bf16[128,2176]{1,0:T(8,128)(2,1)S(1)}, bf16[128,2176]{1,0:T(8,128)(2,1)S(1)}, u32[]{:S(2)}, u32[]{:S(2)}) collective-permute-start(bf16[128,2176]{1,0:T(8,128)(2,1)S(1)} %get-tuple-element.66), channel_id=1, source_target_pairs={{0,4},{1,5},{2,6},{3,7},{4,0},{5,1},{6,2},{7,3},{8,12},{9,13},{10,... | collective-permute-start | bytes 1671176 | tf_op jit(solution)/shard_map/projections/ppermute | solution.py:433
  196.0 14.4 %copy-start.5 = (bf16[2,256,512]{2,1,0:T(8,128)(2,1)S(1)}, bf16[2,256,512]{2,1,0:T(8,128)(2,1)}, u32[]{:S(2)}) copy-start(bf16[2,256,512]{2,1,0:T(8,128)(2,1)} %copy-done.4) | copy-start | bytes 1572868
  197.3 20.8 %collective-permute-start.32 = (bf16[128,2176]{1,0:T(8,128)(2,1)S(1)}, bf16[128,2176]{1,0:T(8,128)(2,1)S(1)}, u32[]{:S(2)}, u32[]{:S(2)}) collective-permute-start(bf16[128,2176]{1,0:T(8,128)(2,1)S(1)} %get-tuple-element.65.refs_7_), channel_id=1, source_target_pairs={{0,2},{1,3},{2,0},{3,1},{4,6},{5,7},{6,4},{7,5},{8,10},{9,11},{10,... | collective-permute-start | bytes 1671176 | tf_op jit(solution)/shard_map/projections/ppermute | solution.py:433
  198.3 22.3 %collective-permute-start.33 = (bf16[128,2176]{1,0:T(8,128)(2,1)S(1)}, bf16[128,2176]{1,0:T(8,128)(2,1)S(1)}, u32[]{:S(2)}, u32[]{:S(2)}) collective-permute-start(bf16[128,2176]{1,0:T(8,128)(2,1)S(1)} %get-tuple-element.69), channel_id=1, source_target_pairs={{0,4},{1,5},{2,6},{3,7},{4,0},{5,1},{6,2},{7,3},{8,12},{9,13},{10,... | collective-permute-start | bytes 1671176 | tf_op jit(solution)/shard_map/projections/ppermute | solution.py:433
  214.3 1.6 collective-permute-start.31
Sparse Core Ops, SparseCore 0:
  9.6 47.6 all-gather.2
  73.0 78.0 all-gather.4

commit v5 on v4

--- a/solution.py
+++ b/solution.py
@@ -50,12 +50,12 @@
         rest = lax.dot_general(
             later.astype(F32),
             decay,
-            (((1,), (0,)), ((), ())),
+            (((1,), (1,)), ((), ())),
             precision=HIGHEST,
             preferred_element_type=F32,
         )
         fade = jnp.exp(rest)
-        ending = rest[:1] + decay[:1]
+        ending = rest[:1] + jnp.transpose(decay)[:1]
         for i in range(groups):
             fade_ref[i] = fade[:, i * per : (i + 1) * per]
             ending_ref[i] = ending[:, i * per : (i + 1) * per]
@@ -93,12 +93,13 @@
 
 
 def mix_kernel(width, query_ref, open_ref, intra_ref, within_ref, state_ref, *out_refs):
-    reach = jnp.exp(within_ref[0])
     rows = out_refs[0].shape[0]
-    for head in range(state_ref.shape[0]):
+    groups, _, per = within_ref.shape
+    for head in range(groups * per):
+        reach = jnp.exp(within_ref[head // per])[:, head % per : head % per + 1]
         columns = slice(head * width, (head + 1) * width)
         carried = dot(query_ref[:, columns], state_ref[head], ((1,), (0,)))
-        retained = intra_ref[:, columns].astype(F32) + reach[:, head : head + 1] * carried
+        retained = intra_ref[:, columns].astype(F32) + reach * carried
         scale = lax.rsqrt(jnp.mean(retained * retained, axis=1, keepdims=True) + NORM_EPS)
         mixed = (open_ref[:, columns].astype(F32) * (retained * scale)).astype(BF16)
         for half, out_ref in enumerate(out_refs):
@@ -197,8 +198,8 @@
     return pl.BlockSpec((1,) + shape, lambda i, *_: (i, 0, 0))
 
 
-def local_states(keys, values, log_decay, groups, width, after=()):
-    tokens, heads = log_decay.shape
+def local_states(keys, values, decays, groups, width, after=()):
+    heads, tokens = decays.shape
     per, steps = heads // groups, groups // 2
     tall = per * (width + DECAY_ROWS)
     wider = wide(tokens, 2 * per * width)
@@ -206,8 +207,8 @@
         "local_states",
         functools.partial(state_kernel, width),
         steps,
-        (keys, values, log_decay),
-        (wider, wider, whole(tokens, heads)),
+        (keys, values, decays),
+        (wider, wider, whole(heads, tokens)),
         pl.BlockSpec((2, tall, width), lambda i: (i, 0, 0)),
         jax.ShapeDtypeStruct((groups, tall, width), BF16),
         scratch=(pltpu.VMEM((groups, tokens, per), F32), pltpu.VMEM((groups, 1, per), F32)),
@@ -232,20 +233,21 @@
 
 def mix(queries, opened, intra, within, states, width, after=()):
     groups, tokens, per = within.shape
-    heads = wide(tokens, per * width)
+    heads = 2 * per
+    wider = wide(tokens, heads * width)
     return local_call(
         "mix",
         functools.partial(mix_kernel, width),
-        groups,
+        groups // 2,
         (queries, opened, intra, within, states),
         (
-            heads,
-            heads,
-            heads,
-            group(tokens, per),
-            pl.BlockSpec((per, width, width), lambda i: (i, 0, 0)),
+            wider,
+            wider,
+            wider,
+            pl.BlockSpec((2, tokens, per), lambda i: (i, 0, 0)),
+            pl.BlockSpec((heads, width, width), lambda i: (i, 0, 0)),
         ),
-        [wide(tokens // 2, per * width)] * 2,
+        [wide(tokens // 2, heads * width)] * 2,
         [jax.ShapeDtypeStruct((tokens // 2, queries.shape[1]), BF16)] * 2,
         after=after,
     )
@@ -295,35 +297,37 @@
     )
 
 
-def pair_kernel(heights, even_ref, odd_ref, *target_refs):
-    chips = even_ref.shape[0]
-    for i, target_ref in enumerate(target_refs):
-        top = sum(heights[: i // chips])
-        rows = slice(top, top + heights[i // chips])
-        target_ref[0] = even_ref[i % chips, rows, :]
-        target_ref[1] = odd_ref[i % chips, rows, :]
-
-
-def pair(even, odd, heights, after=()):
-    chips, _, columns = even.shape
-    shapes = [jax.ShapeDtypeStruct((2, rows, columns), even.dtype) for rows in heights]
-    body = functools.partial(pair_kernel, heights)
-    pairs = resident_call(
-        "pair", body, (even, odd), [s for s in shapes for _ in range(chips)], after=after
-    )
-    return [pairs[i : i + chips] for i in range(0, len(pairs), chips)]
+def pair_kernel(parts, even_ref, odd_ref, *target_refs):
+    for (chip, top), target_ref in zip(parts, target_refs):
+        rows = slice(top, top + target_ref.shape[1])
+        target_ref[0] = even_ref[chip, rows, :]
+        target_ref[1] = odd_ref[chip, rows, :]
+
+
+def pair(even, odd, split, after=()):
+    chips, rows, columns = even.shape
+    parts = [(chip, 0) for chip in range(chips)] + [(chips - 1, split)]
+    heights = [rows] * (chips - 1) + [split, rows - split]
+    return resident_call(
+        "pair",
+        functools.partial(pair_kernel, parts),
+        (even, odd),
+        [jax.ShapeDtypeStruct((2, height, columns), even.dtype) for height in heights],
+        after=after,
+    )
 
 
 def order_kernel(place_ref, *refs):
     *sources, target_ref = refs
-    rows = sources[0].shape[1]
+    rows = sources[-1].shape[1]
     for r in range(2 * len(sources)):
+        source = sources[r // 2]
         start = pl.multiple_of((place_ref[0] ^ r) * rows, rows)
-        target_ref[pl.ds(start, rows), :] = sources[r // 2][r % 2]
+        target_ref[pl.ds(start, rows), :] = source[r % 2, source.shape[1] - rows :, :]
 
 
 def in_order(arrays, place, after=()):
-    _, rows, columns = arrays[0].shape
+    _, rows, columns = arrays[-1].shape
     tall = (2 * len(arrays) * rows, columns)
     return resident_call(
         "in_order",
@@ -457,27 +461,26 @@
     per = heads // PLACES
     within = running.reshape(tokens, PLACES, per).transpose(1, 0, 2)
     across = running.T.reshape(PLACES, per, tokens)
-    states = local_states(keys, values, log_decay, PLACES, width)
+    states = local_states(keys, values, log_decay.T, PLACES, width)
     with jax.named_scope("state_scan"):
         parts = lax.all_to_all(states, PLANE, 0, 0, tiled=True)
 
     even, odd = deal((residual, out_weight), place, PLACES, piece, after=(states,))
-    starts, weights = pair(even, swap(odd, 1), (tokens, out_weight.shape[0]))
-    with jax.named_scope("out_weight_gather"):
-        weights = [swap(part, 2 * chip) if chip else part for chip, part in enumerate(weights)]
-    with jax.named_scope("residual_exchange"):
-        starts = [starts[0], swap(starts[1], 2), swap(starts[2], 4), starts[3]]
+    with jax.named_scope("start_exchange"):
+        *starts, far_weight = pair(even, swap(odd, 1), tokens)
+        starts[1:3] = [swap(starts[1], 2), swap(starts[2], 4)]
+        far_weight = swap(far_weight, 6)
     with jax.named_scope("state_scan"):
         total = plane_total(parts, per, width, after=(starts[0],))
         nearest = hop(total, {a: a + 1 for a in range(DEPTH - 1)})
         joined = join(nearest, total, width)
         others = hop(joined, {a: a + 2 for a in range(DEPTH - 2)})
     with jax.named_scope("out_weight_gather"):
-        shard = in_order(weights, place, after=(total,))
+        shard = in_order((*starts[:3], far_weight), place, after=(total,))
         out_full = lax.all_gather(*hold((shard,), (kv_mine,)), "z", axis=0, tiled=True)
     with jax.named_scope("state_scan"):
         prefix = plane_prefix(
-            parts, nearest, others, width, after=(kv_mine, shard, starts[1], starts[2])
+            parts, nearest, others, width, after=(kv_mine, shard)
         )
         entering = lax.all_to_all(prefix, PLANE, 0, 0, tiled=True)
         entering = entering.reshape(heads, width, width)
@@ -498,8 +501,11 @@
             gain = lax.dynamic_index_in_dim(gains, place ^ r, 1, False).reshape(share, 1)
             kv_full.append((rows.astype(F32) * gain.astype(F32)).astype(BF16))
 
+    def cores(mixed):
+        return mixed, swap(mixed, 1)
+
     def hidden_of(*halves, after=()):
-        pieces = [(half, (mixed, swap(mixed, 1)), starts[chip]) for chip, half, mixed in halves]
+        pieces = [(half, mixed, starts[chip]) for chip, half, mixed in halves]
         mine, theirs = out_projection(pieces, out_full, after)
         return mine, swap(theirs, 1)
 
@@ -509,18 +515,22 @@
     with jax.named_scope("projections"):
         early_x, late_y = swap(early, 2), swap(late, 4)
         early_far, late_far = swap(early_x, 4), swap(late_y, 2)
-        near = hidden_of((1, 0, early_x), (2, 1, late_y))
+        crossed = swap(early, 1), swap(late, 1)
+        near = hidden_of(
+            (1, 0, cores(early_x)), (2, 1, cores(late_y)), after=crossed
+        )
         early, late = hold((early, late), (early_far, late_far))
+        home = (0, 0, (early, crossed[0])), (0, 1, (late, crossed[1]))
         late_x, early_y = swap(late, 2), swap(early, 4)
-        far = hidden_of((3, 0, early_far), (3, 1, late_far), after=(near[0],))
+        far = hidden_of((3, 0, cores(early_far)), (3, 1, cores(late_far)), after=(near[0],))
         early_far, late_far = share_of(far)
         early_x, late_y = share_of(near, after=(early_far,))
         late_x, early_y = hold((late_x, early_y), (early_x,))
         early_x, late_y = swap(early_x, 2), swap(late_y, 4)
         late_far, early_far = swap(late_far, 4), swap(early_far, 2)
-        near = hidden_of((1, 1, late_x), (2, 0, early_y))
+        near = hidden_of((1, 1, cores(late_x)), (2, 0, cores(early_y)))
         late_x, early_y = share_of(near, [(late_far, 0), (early_far, 1)])
-        home = hidden_of((0, 0, early), (0, 1, late), after=(late_x, early_x, late_y))
+        home = hidden_of(*home, after=(late_x, early_x, late_y))
         late_x, early_y = swap(late_x, 2), swap(early_y, 4)
         added = [(early_x, 0), (late_x, 1), (early_y, 0), (late_y, 1)]
         return share_of(home, added, True)

time: 231 us -> 225 us (0.974)
  waiting for transfers between devices: 110 us -> 95 us
  local copies, waits for them, and re-layouts: 11.9 us -> 22.9 us
  starting transfers between devices: 33 us -> 30.4 us
    unnamed x41 -> x56, local copies, waits for them, and re-layouts: 9.62 us -> 20.6 us
    ppermute x32 -> x30, waiting for transfers between devices: 82.8 us -> 73.9 us  [swap(): return lax.ppermute(array, SEQ, [(i, i ^ distance) for i in range(DEVICES)])]
    ppermute x2, waiting for transfers between devices: 15 us -> 12 us  [hop(): return lax.ppermute(array, SEQ, pairs)]
    ppermute x32 -> x30, starting transfers between devices: 23 us -> 20.4 us  [swap(): return lax.ppermute(array, SEQ, [(i, i ^ distance) for i in range(DEVICES)])]
    all_to_all x1, waiting for transfers between devices: 10.4 us -> 7.76 us  [shared_on_device(): parts = lax.all_to_all(states, PLANE, 0, 0, tiled=True)]
  transfers between devices with their start and end apart: 38 -> 36, of which waited for: 18 -> 14; matrix products, arithmetic and copies ran while one was open for 4% -> 3% of each run, Pallas kernels for 23% -> 23%
where the time goes in v5:
time: 225 us; the launch traced here: 223 us
  waiting for transfers between devices  95 us (42%)
  Pallas kernels  55.3 us (25%)
  starting transfers between devices  30.4 us (14%)
  local copies, waits for them, and re-layouts  22.9 us (10%)
  between operations  14.4 us (6%)
  other arithmetic  4.77 us (2%)
    ppermute x30, waiting for transfers between devices, swap(): return lax.ppermute(array, SEQ, [(i, i ^ distance) for i in range(DEVICES)])  73.9 us
    pallas_call x14, Pallas kernels, resident_call(): pl.pallas_call(kernel, in_specs=[pl.BlockSpec(memory_space=pltpu.SMEM)] *...  30.6 us
    pallas_call x3, Pallas kernels, local_call(): pl.pallas_call(kernel, grid_spec=pltpu.PrefetchScalarGridSpec(num_scalar_...  24.7 us
    unnamed x56, local copies, waits for them, and re-layouts  20.6 us
    ppermute x30, starting transfers between devices, swap(): return lax.ppermute(array, SEQ, [(i, i ^ distance) for i in range(DEVICES)])  20.4 us
    ppermute x2, waiting for transfers between devices, hop(): return lax.ppermute(array, SEQ, pairs)  12 us
    all_to_all x1, waiting for transfers between devices, shared_on_device(): parts = lax.all_to_all(states, PLANE, 0, 0, tiled=True)  7.76 us
  transfers between devices with their start and end apart: 36, of which 14 were waited for; matrix products, arithmetic and copies ran while one was open for 3% of the time, Pallas kernels for 23%

profile of v5, /device:TPU:24, one launch (start us, length us, event | category | flops | bytes accessed | tf_op | source)
XLA Modules:
  0.0 222.7 jit_solution(4522182477574918952)
XLA Ops:
  7.2 0.7 all-gather.3.cloned.1.call-update
  7.9 7.0 %local_states.1.refs_3_ = bf16[8,576,128]{2,1,0:T(8,128)(2,1)} custom-call(bf16[256,4096]{1,0:T(8,128)(2,1)} %refs_1_.5, bf16[256,4096]{1,0:T(8,128)(2,1)} %refs_2_.3, f32[32,256]{1,0:T(8,128)} %bitcast.24), custom_call_target="tpu_custom_call" | custom-call | tf_op jit(solution)/shard_map/local_states/pallas_call | solution.py:152
  14.9 2.0 deal.1
  16.9 1.2 copy-done.12
  18.1 3.8 %all-to-all-start = ((bf16[8,576,128]{2,1,0:T(8,128)(2,1)}), bf16[8,576,128]{2,1,0:T(8,128)(2,1)S(1)}, u32[]{:S(2)}, u32[]{:S(2)}) async-start(bf16[8,576,128]{2,1,0:T(8,128)(2,1)} %local_states.1.refs_3_), calls=%async_computation | async-start | bytes 2359296 | tf_op jit(solution)/shard_map/state_scan/all_to_all | solution.py:466
  22.0 1.1 copy-done.14
  23.1 1.4 copy-done.13
  24.5 1.4 copy-done.15
  25.9 1.4 pair.1
  27.3 0.7 copy-done.23
  28.0 2.0 collective-permute-start.3
  30.0 1.5 collective-permute-start.4
  31.5 7.8 %all-to-all-done.refs_0_ = bf16[8,576,128]{2,1,0:T(8,128)(2,1)S(1)} async-done(((bf16[8,576,128]{2,1,0:T(8,128)(2,1)}), bf16[8,576,128]{2,1,0:T(8,128)(2,1)S(1)}, u32[]{:S(2)}, u32[]{:S(2)}) %all-to-all-start) | async-done | bytes 1179680 | tf_op jit(solution)/shard_map/state_scan/all_to_all | solution.py:466
  39.5 1.3 collective-permute-start.1
  41.5 12.0 %collective-permute-done.1.refs_0_.refs_1_ = bf16[4,144,128]{2,1,0:T(8,128)(2,1)S(1)} collective-permute-done((bf16[4,144,128]{2,1,0:T(8,128)(2,1)S(1)}, bf16[4,144,128]{2,1,0:T(8,128)(2,1)S(1)}, u32[]{:S(2)}, u32[]{:S(2)}) %collective-permute-start.1) | collective-permute-done | bytes 147488 | tf_op jit(solution)/shard_map/state_scan/ppermute | solution.py:444
  53.5 1.3 collective-permute-start.2
  54.8 6.4 %collective-permute-done.5.refs_4_ = bf16[2,128,512]{2,1,0:T(8,128)(2,1)S(1)} collective-permute-done((bf16[2,128,512]{2,1,0:T(8,128)(2,1)S(1)}, bf16[2,128,512]{2,1,0:T(8,128)(2,1)S(1)}, u32[]{:S(2)}, u32[]{:S(2)}) %collective-permute-start.5) | collective-permute-done | bytes 262176 | tf_op jit(solution)/shard_map/start_exchange/ppermute | solution.py:437
  61.3 2.5 %in_order.1.refs_4_.refs_0_ = bf16[1024,512]{1,0:T(8,128)(2,1)} custom-call(s32[1]{0:T(128)} %bitcast.3.refs_0_, bf16[2,384,512]{2,1,0:T(8,128)(2,1)S(1)} %get-tuple-element.35.refs_1_.refs_5_.refs_6_, bf16[2,384,512]{2,1,0:T(8,128)(2,1)S(1)} %collective-permute-done.3.refs_2_.refs_5_, bf16[2,384,512]{2,1,0:T(8,128)(2,1)} %collective-permute-done.4.refs_3_.refs_6_, ...), custom_call_target="tpu_custom_call" | custom-call | tf_op jit(solution)/shard_map/out_weight_gather/in_order/pallas_call | solution.py:177
  64.4 0.9 copy-done.22
  65.4 1.4 plane_prefix.1.refs_6_.refs_1_
  66.8 0.7 all-gather.5.cloned.1.call-update
  67.5 3.6 %all-to-all-start.1 = ((bf16[8,4,128,128]{3,2,1,0:T(8,128)(2,1)}), bf16[8,4,128,128]{3,2,1,0:T(8,128)(2,1)S(1)}, u32[]{:S(2)}, u32[]{:S(2)}) async-start(bf16[8,4,128,128]{3,2,1,0:T(8,128)(2,1)} %plane_prefix.1.refs_6_.refs_1_), calls=%async_computation.1 | async-start | bytes 2097152 | tf_op jit(solution)/shard_map/state_scan/all_to_all | solution.py:485
  71.7 2.9 %collective-permute-start.6 = (bf16[2,256,512]{2,1,0:T(8,128)(2,1)S(1)}, bf16[2,256,512]{2,1,0:T(8,128)(2,1)S(1)}, u32[]{:S(2)}, u32[]{:S(2)}) collective-permute-start(bf16[2,256,512]{2,1,0:T(8,128)(2,1)S(1)} %hold.5), channel_id=1, source_target_pairs={{0,6},{1,7},{2,4},{3,5},{4,2},{5,3},{6,0},{7,1},{8,14},{9,15},{10,... | collective-permute-start | bytes 1572872 | tf_op jit(solution)/shard_map/residual_exchange/ppermute | solution.py:437
  74.9 1.4 copy.23
  77.0 10.3 %local_intra.1 = (bf16[256,4096]{1,0:T(8,128)(2,1)}, bf16[256,4096]{1,0:T(8,128)(2,1)}) custom-call(bf16[256,4096]{1,0:T(8,128)(2,1)} %refs_0_.5, bf16[256,4096]{1,0:T(8,128)(2,1)} %refs_1_.5, bf16[256,4096]{1,0:T(8,128)(2,1)} %refs_2_.3, bf16[256,4096]{1,0:T(8,128)(2,1)} %refs_3_.1, f32[8,256,4]{2,1,0:T(8,128)} %bitcast.21, ...), custom_call_target="tpu_custom_call" | custom-call | tf_op jit(solution)/shard_map/local_intra/pallas_call | solution.py:152
  87.3 1.1 copy-done.25
  88.4 7.4 %mix.1 = (bf16[128,4096]{1,0:T(8,128)(2,1)}, bf16[128,4096]{1,0:T(8,128)(2,1)}) custom-call(bf16[256,4096]{1,0:T(8,128)(2,1)} %refs_0_.5, bf16[256,4096]{1,0:T(8,128)(2,1)} %get-tuple-element.39.refs_1_, bf16[256,4096]{1,0:T(8,128)(2,1)} %get-tuple-element.40.refs_2_, f32[8,256,4]{2,1,0:T(8,128)} %bitcast.22, bf16[32,128,128]{2,1,0:T(8,128)(2,1)} %bitcast.23), custom_call_target="tpu_custom_call" | custom-call | tf_op jit(solution)/shard_map/mix/pallas_call | solution.py:152
  95.8 1.9 collective-permute-done.6.refs_2_.refs_5_.refs_6_
  99.1 23.6 %collective-permute-done.7.refs_0_ = bf16[128,4096]{1,0:T(8,128)(2,1)S(1)} collective-permute-done((bf16[128,4096]{1,0:T(8,128)(2,1)}, bf16[128,4096]{1,0:T(8,128)(2,1)S(1)}, u32[]{:S(2)}, u32[]{:S(2)}) %collective-permute-start.7) | collective-permute-done | bytes 1048608 | tf_op jit(solution)/shard_map/projections/ppermute | solution.py:437
  123.2 1.2 collective-permute-start.10
  124.4 1.0 copy-done.5
  125.9 1.0 copy-done.17
  126.9 1.0 copy-done.8
  127.9 1.0 copy-done.19
  128.9 17.9 %collective-permute-done.8.refs_2_.refs_0_ = bf16[128,4096]{1,0:T(8,128)(2,1)} collective-permute-done((bf16[128,4096]{1,0:T(8,128)(2,1)S(1)}, bf16[128,4096]{1,0:T(8,128)(2,1)}, u32[]{:S(2)}, u32[]{:S(2)}) %collective-permute-start.8) | collective-permute-done | bytes 1048608 | tf_op jit(solution)/shard_map/projections/ppermute | solution.py:437
  147.4 1.0 collective-permute-start.13
  148.3 0.9 collective-permute-start.14
  149.3 2.0 multiply_convert_fusion.1.refs_2_
  151.3 2.2 copy-done
  153.5 1.1 copy-done.3
  154.6 1.2 copy-done.6
  155.8 1.2 copy-done.9
  157.1 1.2 copy-done.18
  158.3 1.2 copy-done.20
  159.5 4.2 %out_projection.4 = (bf16[256,512]{1,0:T(8,128)(2,1)S(1)}, bf16[256,512]{1,0:T(8,128)(2,1)S(1)}) custom-call(bf16[128,4096]{1,0:T(8,128)(2,1)S(1)} %copy-done.18, bf16[128,4096]{1,0:T(8,128)(2,1)} %collective-permute-done.15.refs_1_, bf16[128,4096]{1,0:T(8,128)(2,1)S(1)} %copy-done.20, bf16[128,4096]{1,0:T(8,128)(2,1)} %collective-permute-done.16.refs_3_, ...), custom_call_target="tpu_custom_call" | custom-call | tf_op jit(solution)/shard_map/projections/out_projection/pallas_call | solution.py:177
  163.8 4.6 %out_projection.5 = (bf16[256,512]{1,0:T(8,128)(2,1)S(1)}, bf16[256,512]{1,0:T(8,128)(2,1)S(1)}) custom-call(bf16[128,4096]{1,0:T(8,128)(2,1)} %collective-permute-done.8.refs_2_.refs_0_, bf16[128,4096]{1,0:T(8,128)(2,1)} %collective-permute-done.19.refs_1_, bf16[128,4096]{1,0:T(8,128)(2,1)} %collective-permute-done.10.refs_3_.refs_2_, ...), custom_call_target="tpu_custom_call" | custom-call | tf_op jit(solution)/shard_map/projections/out_projection/pallas_call | solution.py:177
  168.9 2.0 multiply_convert_fusion.refs_3_
  170.9 1.3 cache_projection.4
  172.2 1.3 cache_projection.5
  174.5 0.9 collective-permute-start.25
  175.4 1.4 collective-permute-start.26
  177.4 0.9 collective-permute-done.23.refs_3_
  178.3 4.1 %out_projection.6 = (bf16[256,512]{1,0:T(8,128)(2,1)S(1)}, bf16[256,512]{1,0:T(8,128)(2,1)S(1)}) custom-call(bf16[128,4096]{1,0:T(8,128)(2,1)} %get-tuple-element.54.refs_0_, bf16[128,4096]{1,0:T(8,128)(2,1)S(1)} %collective-permute-done.22.refs_1_, bf16[128,4096]{1,0:T(8,128)(2,1)} %get-tuple-element.55.refs_2_, ...), custom_call_target="tpu_custom_call" | custom-call | tf_op jit(solution)/shard_map/projections/out_projection/pallas_call | solution.py:177
  182.6 0.9 collective-permute-start.28
  183.6 6.4 %collective-permute-done.25.refs_4_ = bf16[128,2176]{1,0:T(8,128)(2,1)S(1)} collective-permute-done((bf16[128,2176]{1,0:T(8,128)(2,1)S(1)}, bf16[128,2176]{1,0:T(8,128)(2,1)S(1)}, u32[]{:S(2)}, u32[]{:S(2)}) %collective-permute-start.25) | collective-permute-done | bytes 557088 | tf_op jit(solution)/shard_map/projections/ppermute | solution.py:437
  190.0 1.0 collective-permute-done.26.refs_5_
  190.9 1.3 cache_projection.6
  192.2 1.5 collective-permute-start.30
  193.7 0.8 collective-permute-start.31
  194.5 8.3 %collective-permute-done.27.refs_8_.refs_4_ = bf16[128,2176]{1,0:T(8,128)(2,1)S(1)} collective-permute-done((bf16[128,2176]{1,0:T(8,128)(2,1)S(1)}, bf16[128,2176]{1,0:T(8,128)(2,1)S(1)}, u32[]{:S(2)}, u32[]{:S(2)}) %collective-permute-start.27) | collective-permute-done | bytes 557088 | tf_op jit(solution)/shard_map/projections/ppermute | solution.py:437
  202.9 3.9 %out_projection.7 = (bf16[256,512]{1,0:T(8,128)(2,1)S(1)}, bf16[256,512]{1,0:T(8,128)(2,1)S(1)}) custom-call(bf16[128,4096]{1,0:T(8,128)(2,1)} %get-tuple-element.46.refs_0_, bf16[128,4096]{1,0:T(8,128)(2,1)S(1)} %copy-done.7, bf16[128,4096]{1,0:T(8,128)(2,1)} %get-tuple-element.47.refs_2_, bf16[128,4096]{1,0:T(8,128)(2,1)S(1)} %copy-done.10, ...), custom_call_target="tpu_custom_call" | custom-call | tf_op jit(solution)/shard_map/projections/out_projection/pallas_call | solution.py:177
  206.8 1.5 collective-permute-done.29.refs_1_
  208.3 5.2 %collective-permute-done.30.refs_5_ = bf16[128,2176]{1,0:T(8,128)(2,1)S(1)} collective-permute-done((bf16[128,2176]{1,0:T(8,128)(2,1)S(1)}, bf16[128,2176]{1,0:T(8,128)(2,1)S(1)}, u32[]{:S(2)}, u32[]{:S(2)}) %collective-permute-start.30) | collective-permute-done | bytes 557088 | tf_op jit(solution)/shard_map/projections/ppermute | solution.py:437
  213.5 2.4 %cache_projection.7 = (bf16[256,1024]{1,0:T(8,128)(2,1)}, bf16[256,1024]{1,0:T(8,128)(2,1)}) custom-call(bf16[256,512]{1,0:T(8,128)(2,1)S(1)} %get-tuple-element.61.refs_0_, bf16[256,512]{1,0:T(8,128)(2,1)S(1)} %collective-permute-done.29.refs_1_, bf16[512,2048]{1,0:T(8,128)(2,1)S(1)} %multiply_convert_fusion.1.refs_2_, ...), custom_call_target="tpu_custom_call" | custom-call | tf_op jit(solution)/shard_map/projections/cache_projection/pallas_call | solution.py:177
  (102 shorter events, 8.8 us)
Async XLA Ops:
  7.2 57.3 %all-gather.3.cloned.1.call-start = ((), (), s32[]{:S(2)}) async-start(), calls=%async_computation.2 | async-start | bytes 2621440 | tf_op jit(solution)/shard_map/kv_weight_gather/all_gather | solution.py:459
  7.9 7.0 %copy-start.11 = (bf16[256,4096]{1,0:T(8,128)(2,1)S(1)}, bf16[256,4096]{1,0:T(8,128)(2,1)}, u32[]{:S(2)}) copy-start(bf16[256,4096]{1,0:T(8,128)(2,1)} %refs_1_.4) | copy-start | bytes 6291460
  7.9 7.0 %copy-start.16 = (bf16[128,4096]{1,0:T(8,128)(2,1)S(1)}, bf16[128,4096]{1,0:T(8,128)(2,1)}, u32[]{:S(2)}) copy-start(bf16[128,4096]{1,0:T(8,128)(2,1)} %refs_2_.2) | copy-start | bytes 3145732
  16.9 1.2 copy-start.12
  18.1 3.8 %collective-permute-start = (bf16[4,384,512]{2,1,0:T(8,128)(2,1)}, bf16[4,384,512]{2,1,0:T(8,128)(2,1)S(1)}, u32[]{:S(2)}, u32[]{:S(2)}) collective-permute-start(bf16[4,384,512]{2,1,0:T(8,128)(2,1)} %get-tuple-element.34), channel_id=1, source_target_pairs={{0,1},{1,0},{2,3},{3,2},{4,5},{5,4},{6,7},{7,6},{8,9},{9,8},{10,11... | collective-permute-start | bytes 4718600 | tf_op jit(solution)/shard_map/start_exchange/ppermute | solution.py:437
  18.1 21.2 %all-to-all-start = ((bf16[8,576,128]{2,1,0:T(8,128)(2,1)}), bf16[8,576,128]{2,1,0:T(8,128)(2,1)S(1)}, u32[]{:S(2)}, u32[]{:S(2)}) async-start(bf16[8,576,128]{2,1,0:T(8,128)(2,1)} %local_states.1.refs_3_), calls=%async_computation | async-start | bytes 2359296 | tf_op jit(solution)/shard_map/state_scan/all_to_all | solution.py:466
  21.9 1.2 copy-start.14
  23.1 1.4 copy-start.13
  24.5 1.4 copy-start.15
  27.3 0.7 copy-start.23
  28.0 33.3 %collective-permute-start.3 = (bf16[2,384,512]{2,1,0:T(8,128)(2,1)}, bf16[2,384,512]{2,1,0:T(8,128)(2,1)S(1)}, u32[]{:S(2)}, u32[]{:S(2)}) collective-permute-start(bf16[2,384,512]{2,1,0:T(8,128)(2,1)} %get-tuple-element.36), channel_id=1, source_target_pairs={{0,2},{1,3},{2,0},{3,1},{4,6},{5,7},{6,4},{7,5},{8,10},{9,11},{10,... | collective-permute-start | bytes 2359304 | tf_op jit(solution)/shard_map/start_exchange/ppermute | solution.py:437
  30.0 31.2 %collective-permute-start.4 = (bf16[2,384,512]{2,1,0:T(8,128)(2,1)}, bf16[2,384,512]{2,1,0:T(8,128)(2,1)}, u32[]{:S(2)}, u32[]{:S(2)}) collective-permute-start(bf16[2,384,512]{2,1,0:T(8,128)(2,1)} %get-tuple-element.37), channel_id=1, source_target_pairs={{0,4},{1,5},{2,6},{3,7},{4,0},{5,1},{6,2},{7,3},{8,12},{9,13},{10,... | collective-permute-start | bytes 2359304 | tf_op jit(solution)/shard_map/start_exchange/ppermute | solution.py:437
  39.3 1.6 copy-start.24
  39.5 13.9 %collective-permute-start.1 = (bf16[4,144,128]{2,1,0:T(8,128)(2,1)S(1)}, bf16[4,144,128]{2,1,0:T(8,128)(2,1)S(1)}, u32[]{:S(2)}, u32[]{:S(2)}) collective-permute-start(bf16[4,144,128]{2,1,0:T(8,128)(2,1)S(1)} %plane_total.1.refs_1_.refs_5_), channel_id=1, source_target_pairs={{0,8},{1,9},{2,10},{3,11},{4,12},{5,13},{6,14},{7,15},{8,16},{9,17... | collective-permute-start | bytes 442376 | tf_op jit(solution)/shard_map/state_scan/ppermute | solution.py:444
  40.8 20.4 %collective-permute-start.5 = (bf16[2,128,512]{2,1,0:T(8,128)(2,1)S(1)}, bf16[2,128,512]{2,1,0:T(8,128)(2,1)S(1)}, u32[]{:S(2)}, u32[]{:S(2)}) collective-permute-start(bf16[2,128,512]{2,1,0:T(8,128)(2,1)S(1)} %copy-done.24), channel_id=1, source_target_pairs={{0,6},{1,7},{2,4},{3,5},{4,2},{5,3},{6,0},{7,1},{8,14},{9,15},{10,... | collective-permute-start | bytes 786440 | tf_op jit(solution)/shard_map/start_exchange/ppermute | solution.py:437
  53.5 10.2 %collective-permute-start.2 = (bf16[4,144,128]{2,1,0:T(8,128)(2,1)S(1)}, bf16[4,144,128]{2,1,0:T(8,128)(2,1)S(1)}, u32[]{:S(2)}, u32[]{:S(2)}) collective-permute-start(bf16[4,144,128]{2,1,0:T(8,128)(2,1)S(1)} %join.1), channel_id=1, source_target_pairs={{0,16},{1,17},{2,18},{3,19},{4,20},{5,21},{6,22},{7,23},{8,24},{9,... | collective-permute-start | bytes 442376 | tf_op jit(solution)/shard_map/state_scan/ppermute | solution.py:444
  61.3 5.5 %copy-start.2 = (bf16[2,384,512]{2,1,0:T(8,128)(2,1)}, bf16[2,384,512]{2,1,0:T(8,128)(2,1)S(1)}, u32[]{:S(2)}) copy-start(bf16[2,384,512]{2,1,0:T(8,128)(2,1)S(1)} %collective-permute-done.3.refs_2_.refs_5_) | copy-start | bytes 2359300
  63.8 0.7 copy-start.21
  64.4 0.9 copy-start.22
  66.8 84.5 %all-gather.5.cloned.1.call-start = ((), (), s32[]{:S(2)}) async-start(), calls=%async_computation.3 | async-start | bytes 5242880 | tf_op jit(solution)/shard_map/out_weight_gather/all_gather | solution.py:480
  66.8 4.3 %copy-start.26 = (f32[256,32]{0,1:T(8,128)S(1)}, f32[256,32]{0,1:T(8,128)}, u32[]{:S(2)}) copy-start(f32[256,32]{0,1:T(8,128)} %param.14) | copy-start | bytes 98308
  67.5 19.8 %all-to-all-start.1 = ((bf16[8,4,128,128]{3,2,1,0:T(8,128)(2,1)}), bf16[8,4,128,128]{3,2,1,0:T(8,128)(2,1)S(1)}, u32[]{:S(2)}, u32[]{:S(2)}) async-start(bf16[8,4,128,128]{3,2,1,0:T(8,128)(2,1)} %plane_prefix.1.refs_6_.refs_1_), calls=%async_computation.1 | async-start | bytes 2097152 | tf_op jit(solution)/shard_map/state_scan/all_to_all | solution.py:485
  71.7 26.0 %collective-permute-start.6 = (bf16[2,256,512]{2,1,0:T(8,128)(2,1)S(1)}, bf16[2,256,512]{2,1,0:T(8,128)(2,1)S(1)}, u32[]{:S(2)}, u32[]{:S(2)}) collective-permute-start(bf16[2,256,512]{2,1,0:T(8,128)(2,1)S(1)} %hold.5), channel_id=1, source_target_pairs={{0,6},{1,7},{2,4},{3,5},{4,2},{5,3},{6,0},{7,1},{8,14},{9,15},{10,... | collective-permute-start | bytes 1572872 | tf_op jit(solution)/shard_map/residual_exchange/ppermute | solution.py:437
  87.3 1.1 copy-start.25
  95.8 51.6 %copy-start.27 = (bf16[4096]{0:T(1024)(128)(2,1)S(1)}, bf16[4096]{0:T(1024)(128)(2,1)}, u32[]{:S(2)}) copy-start(bf16[4096]{0:T(1024)(128)(2,1)} %param.16) | copy-start | bytes 24580
  97.7 25.0 %collective-permute-start.7 = (bf16[128,4096]{1,0:T(8,128)(2,1)}, bf16[128,4096]{1,0:T(8,128)(2,1)S(1)}, u32[]{:S(2)}, u32[]{:S(2)}) collective-permute-start(bf16[128,4096]{1,0:T(8,128)(2,1)} %get-tuple-element.44.refs_0_), channel_id=1, source_target_pairs={{0,2},{1,3},{2,0},{3,1},{4,6},{5,7},{6,4},{7,5},{8,10},{9,11},{10,... | collective-permute-start | bytes 3145736 | tf_op jit(solution)/shard_map/projections/ppermute | solution.py:437
  98.2 25.0 %collective-permute-start.9 = (bf16[128,4096]{1,0:T(8,128)(2,1)}, bf16[128,4096]{1,0:T(8,128)(2,1)S(1)}, u32[]{:S(2)}, u32[]{:S(2)}) collective-permute-start(bf16[128,4096]{1,0:T(8,128)(2,1)} %get-tuple-element.45.refs_1_), channel_id=1, source_target_pairs={{0,4},{1,5},{2,6},{3,7},{4,0},{5,1},{6,2},{7,3},{8,12},{9,13},{10,... | collective-permute-start | bytes 3145736 | tf_op jit(solution)/shard_map/projections/ppermute | solution.py:437
  98.6 25.8 %collective-permute-start.11 = (bf16[128,4096]{1,0:T(8,128)(2,1)}, bf16[128,4096]{1,0:T(8,128)(2,1)S(1)}, u32[]{:S(2)}, u32[]{:S(2)}) collective-permute-start(bf16[128,4096]{1,0:T(8,128)(2,1)} %get-tuple-element.44.refs_0_), channel_id=1, source_target_pairs={{0,1},{1,0},{2,3},{3,2},{4,5},{5,4},{6,7},{7,6},{8,9},{9,8},{10,11... | collective-permute-start | bytes 3145736 | tf_op jit(solution)/shard_map/projections/ppermute | solution.py:437
  98.6 28.3 %collective-permute-start.12 = (bf16[128,4096]{1,0:T(8,128)(2,1)}, bf16[128,4096]{1,0:T(8,128)(2,1)S(1)}, u32[]{:S(2)}, u32[]{:S(2)}) collective-permute-start(bf16[128,4096]{1,0:T(8,128)(2,1)} %get-tuple-element.45.refs_1_), channel_id=1, source_target_pairs={{0,1},{1,0},{2,3},{3,2},{4,5},{5,4},{6,7},{7,6},{8,9},{9,8},{10,11... | collective-permute-start | bytes 3145736 | tf_op jit(solution)/shard_map/projections/ppermute | solution.py:437
  122.7 24.1 %collective-permute-start.8 = (bf16[128,4096]{1,0:T(8,128)(2,1)S(1)}, bf16[128,4096]{1,0:T(8,128)(2,1)}, u32[]{:S(2)}, u32[]{:S(2)}) collective-permute-start(bf16[128,4096]{1,0:T(8,128)(2,1)S(1)} %collective-permute-done.7.refs_0_), channel_id=1, source_target_pairs={{0,4},{1,5},{2,6},{3,7},{4,0},{5,1},{6,2},{7,3},{8,12},{9,13},{10,... | collective-permute-start | bytes 3145736 | tf_op jit(solution)/shard_map/projections/ppermute | solution.py:437
  123.2 23.9 %collective-permute-start.10 = (bf16[128,4096]{1,0:T(8,128)(2,1)S(1)}, bf16[128,4096]{1,0:T(8,128)(2,1)}, u32[]{:S(2)}, u32[]{:S(2)}) collective-permute-start(bf16[128,4096]{1,0:T(8,128)(2,1)S(1)} %collective-permute-done.9.refs_2_), channel_id=1, source_target_pairs={{0,2},{1,3},{2,0},{3,1},{4,6},{5,7},{6,4},{7,5},{8,10},{9,11},{10,... | collective-permute-start | bytes 3145736 | tf_op jit(solution)/shard_map/projections/ppermute | solution.py:437
  124.4 44.5 %collective-permute-start.18 = (bf16[512,2048]{1,0:T(8,128)(2,1)}, bf16[512,2048]{1,0:T(8,128)(2,1)}, u32[]{:S(2)}, u32[]{:S(2)}) collective-permute-start(bf16[512,2048]{1,0:T(8,128)(2,1)} %all-gather.3.cloned.1.call-done.refs_3_.refs_1_), channel_id=1, source_target_pairs={{0,1},{1,0},{2,3},{3,2},{4,5},{5,4},{6,7},{7,6},{8,9},{9,8},{10,11... | collective-permute-start | bytes 6291464 | tf_op jit(solution)/shard_map/cache_weight/ppermute | solution.py:437
  124.4 1.0 copy-start.5
  125.4 22.0 %collective-permute-start.15 = (bf16[128,4096]{1,0:T(8,128)(2,1)S(1)}, bf16[128,4096]{1,0:T(8,128)(2,1)}, u32[]{:S(2)}, u32[]{:S(2)}) collective-permute-start(bf16[128,4096]{1,0:T(8,128)(2,1)S(1)} %collective-permute-done.7.refs_0_), channel_id=1, source_target_pairs={{0,1},{1,0},{2,3},{3,2},{4,5},{5,4},{6,7},{7,6},{8,9},{9,8},{10,11... | collective-permute-start | bytes 3145736 | tf_op jit(solution)/shard_map/projections/ppermute | solution.py:437
  125.9 1.0 copy-start.17
  126.9 1.0 copy-start.8
  127.9 20.4 %collective-permute-start.16 = (bf16[128,4096]{1,0:T(8,128)(2,1)S(1)}, bf16[128,4096]{1,0:T(8,128)(2,1)}, u32[]{:S(2)}, u32[]{:S(2)}) collective-permute-start(bf16[128,4096]{1,0:T(8,128)(2,1)S(1)} %collective-permute-done.9.refs_2_), channel_id=1, source_target_pairs={{0,1},{1,0},{2,3},{3,2},{4,5},{5,4},{6,7},{7,6},{8,9},{9,8},{10,11... | collective-permute-start | bytes 3145736 | tf_op jit(solution)/shard_map/projections/ppermute | solution.py:437
  127.9 1.0 copy-start.19
  146.8 17.0 %collective-permute-start.19 = (bf16[128,4096]{1,0:T(8,128)(2,1)}, bf16[128,4096]{1,0:T(8,128)(2,1)}, u32[]{:S(2)}, u32[]{:S(2)}) collective-permute-start(bf16[128,4096]{1,0:T(8,128)(2,1)} %collective-permute-done.8.refs_2_.refs_0_), channel_id=1, source_target_pairs={{0,1},{1,0},{2,3},{3,2},{4,5},{5,4},{6,7},{7,6},{8,9},{9,8},{10,11... | collective-permute-start | bytes 3145736 | tf_op jit(solution)/shard_map/projections/ppermute | solution.py:437
  147.1 16.7 %collective-permute-start.20 = (bf16[128,4096]{1,0:T(8,128)(2,1)}, bf16[128,4096]{1,0:T(8,128)(2,1)}, u32[]{:S(2)}, u32[]{:S(2)}) collective-permute-start(bf16[128,4096]{1,0:T(8,128)(2,1)} %collective-permute-done.10.refs_3_.refs_2_), channel_id=1, source_target_pairs={{0,1},{1,0},{2,3},{3,2},{4,5},{5,4},{6,7},{7,6},{8,9},{9,8},{10,11... | collective-permute-start | bytes 3145736 | tf_op jit(solution)/shard_map/projections/ppermute | solution.py:437
  147.4 26.2 %collective-permute-start.13 = (bf16[128,4096]{1,0:T(8,128)(2,1)}, bf16[128,4096]{1,0:T(8,128)(2,1)}, u32[]{:S(2)}, u32[]{:S(2)}) collective-permute-start(bf16[128,4096]{1,0:T(8,128)(2,1)} %get-tuple-element.47.refs_2_), channel_id=1, source_target_pairs={{0,2},{1,3},{2,0},{3,1},{4,6},{5,7},{6,4},{7,5},{8,10},{9,11},{10,... | collective-permute-start | bytes 3145736 | tf_op jit(solution)/shard_map/projections/ppermute | solution.py:437
  148.3 25.6 %collective-permute-start.14 = (bf16[128,4096]{1,0:T(8,128)(2,1)}, bf16[128,4096]{1,0:T(8,128)(2,1)}, u32[]{:S(2)}, u32[]{:S(2)}) collective-permute-start(bf16[128,4096]{1,0:T(8,128)(2,1)} %get-tuple-element.46.refs_0_), channel_id=1, source_target_pairs={{0,4},{1,5},{2,6},{3,7},{4,0},{5,1},{6,2},{7,3},{8,12},{9,13},{10,... | collective-permute-start | bytes 3145736 | tf_op jit(solution)/shard_map/projections/ppermute | solution.py:437
  151.3 2.2 copy-start
  153.5 1.1 copy-start.3
  154.6 1.2 copy-start.6
  155.8 1.2 copy-start.9
  157.1 1.2 copy-start.18
  158.3 1.2 copy-start.20
  159.5 4.3 %copy-start.1 = (bf16[4096,512]{1,0:T(8,128)(2,1)S(1)}, bf16[4096,512]{1,0:T(8,128)(2,1)}, u32[]{:S(2)}) copy-start(bf16[4096,512]{1,0:T(8,128)(2,1)} %all-gather.5.cloned.1.call-done.refs_4_) | copy-start | bytes 12582916
  168.4 2.6 %collective-permute-start.21 = (bf16[256,512]{1,0:T(8,128)(2,1)S(1)}, bf16[256,512]{1,0:T(8,128)(2,1)S(1)}, u32[]{:S(2)}, u32[]{:S(2)}) collective-permute-start(bf16[256,512]{1,0:T(8,128)(2,1)S(1)} %get-tuple-element.51), channel_id=1, source_target_pairs={{0,1},{1,0},{2,3},{3,2},{4,5},{5,4},{6,7},{7,6},{8,9},{9,8},{10,11... | collective-permute-start | bytes 786440 | tf_op jit(solution)/shard_map/projections/ppermute | solution.py:437
  168.4 3.8 %collective-permute-start.17 = (bf16[256,512]{1,0:T(8,128)(2,1)S(1)}, bf16[256,512]{1,0:T(8,128)(2,1)S(1)}, u32[]{:S(2)}, u32[]{:S(2)}) collective-permute-start(bf16[256,512]{1,0:T(8,128)(2,1)S(1)} %get-tuple-element.49), channel_id=1, source_target_pairs={{0,1},{1,0},{2,3},{3,2},{4,5},{5,4},{6,7},{7,6},{8,9},{9,8},{10,11... | collective-permute-start | bytes 786440 | tf_op jit(solution)/shard_map/projections/ppermute | solution.py:437
  173.5 4.8 %copy-start.4 = (bf16[2,384,512]{2,1,0:T(8,128)(2,1)S(1)}, bf16[2,384,512]{2,1,0:T(8,128)(2,1)}, u32[]{:S(2)}) copy-start(bf16[2,384,512]{2,1,0:T(8,128)(2,1)} %copy-done.2) | copy-start | bytes 2359300
  173.9 3.5 %collective-permute-start.22 = (bf16[128,4096]{1,0:T(8,128)(2,1)}, bf16[128,4096]{1,0:T(8,128)(2,1)S(1)}, u32[]{:S(2)}, u32[]{:S(2)}) collective-permute-start(bf16[128,4096]{1,0:T(8,128)(2,1)} %get-tuple-element.54.refs_0_), channel_id=1, source_target_pairs={{0,1},{1,0},{2,3},{3,2},{4,5},{5,4},{6,7},{7,6},{8,9},{9,8},{10,11... | collective-permute-start | bytes 3145736 | tf_op jit(solution)/shard_map/projections/ppermute | solution.py:437
  174.0 4.4 %collective-permute-start.23 = (bf16[128,4096]{1,0:T(8,128)(2,1)}, bf16[128,4096]{1,0:T(8,128)(2,1)S(1)}, u32[]{:S(2)}, u32[]{:S(2)}) collective-permute-start(bf16[128,4096]{1,0:T(8,128)(2,1)} %get-tuple-element.55.refs_2_), channel_id=1, source_target_pairs={{0,1},{1,0},{2,3},{3,2},{4,5},{5,4},{6,7},{7,6},{8,9},{9,8},{10,11... | collective-permute-start | bytes 3145736 | tf_op jit(solution)/shard_map/projections/ppermute | solution.py:437
  174.5 15.5 %collective-permute-start.25 = (bf16[128,2176]{1,0:T(8,128)(2,1)S(1)}, bf16[128,2176]{1,0:T(8,128)(2,1)S(1)}, u32[]{:S(2)}, u32[]{:S(2)}) collective-permute-start(bf16[128,2176]{1,0:T(8,128)(2,1)S(1)} %get-tuple-element.58), channel_id=1, source_target_pairs={{0,4},{1,5},{2,6},{3,7},{4,0},{5,1},{6,2},{7,3},{8,12},{9,13},{10,... | collective-permute-start | bytes 1671176 | tf_op jit(solution)/shard_map/projections/ppermute | solution.py:437
  175.4 15.5 %collective-permute-start.26 = (bf16[128,2176]{1,0:T(8,128)(2,1)S(1)}, bf16[128,2176]{1,0:T(8,128)(2,1)S(1)}, u32[]{:S(2)}, u32[]{:S(2)}) collective-permute-start(bf16[128,2176]{1,0:T(8,128)(2,1)S(1)} %get-tuple-element.52.refs_4_), channel_id=1, source_target_pairs={{0,2},{1,3},{2,0},{3,1},{4,6},{5,7},{6,4},{7,5},{8,10},{9,11},{10,... | collective-permute-start | bytes 1671176 | tf_op jit(solution)/shard_map/projections/ppermute | solution.py:437
  176.8 26.0 %collective-permute-start.27 = (bf16[128,2176]{1,0:T(8,128)(2,1)S(1)}, bf16[128,2176]{1,0:T(8,128)(2,1)S(1)}, u32[]{:S(2)}, u32[]{:S(2)}) collective-permute-start(bf16[128,2176]{1,0:T(8,128)(2,1)S(1)} %get-tuple-element.53.refs_2_), channel_id=1, source_target_pairs={{0,2},{1,3},{2,0},{3,1},{4,6},{5,7},{6,4},{7,5},{8,10},{9,11},{10,... | collective-permute-start | bytes 1671176 | tf_op jit(solution)/shard_map/projections/ppermute | solution.py:437
  182.4 8.5 %collective-permute-start.24 = (bf16[256,512]{1,0:T(8,128)(2,1)S(1)}, bf16[256,512]{1,0:T(8,128)(2,1)S(1)}, u32[]{:S(2)}, u32[]{:S(2)}) collective-permute-start(bf16[256,512]{1,0:T(8,128)(2,1)S(1)} %get-tuple-element.57), channel_id=1, source_target_pairs={{0,1},{1,0},{2,3},{3,2},{4,5},{5,4},{6,7},{7,6},{8,9},{9,8},{10,11... | collective-permute-start | bytes 786440 | tf_op jit(solution)/shard_map/projections/ppermute | solution.py:437
  182.6 20.2 %collective-permute-start.28 = (bf16[128,2176]{1,0:T(8,128)(2,1)S(1)}, bf16[128,2176]{1,0:T(8,128)(2,1)S(1)}, u32[]{:S(2)}, u32[]{:S(2)}) collective-permute-start(bf16[128,2176]{1,0:T(8,128)(2,1)S(1)} %get-tuple-element.60), channel_id=1, source_target_pairs={{0,4},{1,5},{2,6},{3,7},{4,0},{5,1},{6,2},{7,3},{8,12},{9,13},{10,... | collective-permute-start | bytes 1671176 | tf_op jit(solution)/shard_map/projections/ppermute | solution.py:437
  190.9 11.9 %copy-start.7 = (bf16[128,4096]{1,0:T(8,128)(2,1)S(1)}, bf16[128,4096]{1,0:T(8,128)(2,1)}, u32[]{:S(2)}) copy-start(bf16[128,4096]{1,0:T(8,128)(2,1)} %copy-done.5) | copy-start | bytes 3145732
  190.9 11.9 %copy-start.10 = (bf16[128,4096]{1,0:T(8,128)(2,1)S(1)}, bf16[128,4096]{1,0:T(8,128)(2,1)}, u32[]{:S(2)}) copy-start(bf16[128,4096]{1,0:T(8,128)(2,1)} %copy-done.8) | copy-start | bytes 3145732
  192.2 21.3 %collective-permute-start.30 = (bf16[128,2176]{1,0:T(8,128)(2,1)S(1)}, bf16[128,2176]{1,0:T(8,128)(2,1)S(1)}, u32[]{:S(2)}, u32[]{:S(2)}) collective-permute-start(bf16[128,2176]{1,0:T(8,128)(2,1)S(1)} %get-tuple-element.59.refs_7_), channel_id=1, source_target_pairs={{0,2},{1,3},{2,0},{3,1},{4,6},{5,7},{6,4},{7,5},{8,10},{9,11},{10,... | collective-permute-start | bytes 1671176 | tf_op jit(solution)/shard_map/projections/ppermute | solution.py:437
  193.7 19.8 %collective-permute-start.31 = (bf16[128,2176]{1,0:T(8,128)(2,1)S(1)}, bf16[128,2176]{1,0:T(8,128)(2,1)S(1)}, u32[]{:S(2)}, u32[]{:S(2)}) collective-permute-start(bf16[128,2176]{1,0:T(8,128)(2,1)S(1)} %get-tuple-element.63), channel_id=1, source_target_pairs={{0,4},{1,5},{2,6},{3,7},{4,0},{5,1},{6,2},{7,3},{8,12},{9,13},{10,... | collective-permute-start | bytes 1671176 | tf_op jit(solution)/shard_map/projections/ppermute | solution.py:437
  206.7 1.6 collective-permute-start.29
Sparse Core Ops, SparseCore 0:
  9.6 49.9 all-gather.2
  69.2 78.5 all-gather.4

commit v6 on v5

--- a/solution.py
+++ b/solution.py
@@ -488,7 +488,7 @@
         queries, keys, values, gate, within, across, width, after=(prefix,)
     )
     with jax.named_scope("residual_exchange"):
-        (starts[3],) = hold((starts[3],), (prefix,))
+        (starts[3],) = hold((starts[3],), (joined,))
         starts[3] = swap(starts[3], 6)
 
     early, late = mix(queries, opened, intra, within, entering, width)

time: 225 us -> 224 us (level)
    unnamed x56 -> x52, local copies, waits for them, and re-layouts: 20.6 us -> 19.2 us
where the time goes in v6:
time: 224 us; the launch traced here: 221 us
  waiting for transfers between devices  95.3 us (43%)
  Pallas kernels  55.1 us (25%)
  starting transfers between devices  30.3 us (14%)
  local copies, waits for them, and re-layouts  21.4 us (10%)
  between operations  14.4 us (6%)
  other arithmetic  4.77 us (2%)
    ppermute x30, waiting for transfers between devices, swap(): return lax.ppermute(array, SEQ, [(i, i ^ distance) for i in range(DEVICES)])  74.1 us
    pallas_call x14, Pallas kernels, resident_call(): pl.pallas_call(kernel, in_specs=[pl.BlockSpec(memory_space=pltpu.SMEM)] *...  30.4 us
    pallas_call x3, Pallas kernels, local_call(): pl.pallas_call(kernel, grid_spec=pltpu.PrefetchScalarGridSpec(num_scalar_...  24.7 us
    ppermute x30, starting transfers between devices, swap(): return lax.ppermute(array, SEQ, [(i, i ^ distance) for i in range(DEVICES)])  20.2 us
    unnamed x52, local copies, waits for them, and re-layouts  19.2 us
    ppermute x2, waiting for transfers between devices, hop(): return lax.ppermute(array, SEQ, pairs)  12.1 us
    all_to_all x1, waiting for transfers between devices, shared_on_device(): parts = lax.all_to_all(states, PLANE, 0, 0, tiled=True)  7.71 us
  transfers between devices with their start and end apart: 36, of which 14 were waited for; matrix products, arithmetic and copies ran while one was open for 3% of the time, Pallas kernels for 23%

profile of v6, /device:TPU:24, one launch (start us, length us, event | category | flops | bytes accessed | tf_op | source)
XLA Modules:
  0.0 221.2 jit_solution(6920557086714109042)
XLA Ops:
  7.2 0.7 all-gather.3.cloned.1.call-update
  7.9 7.0 %local_states.1.refs_3_ = bf16[8,576,128]{2,1,0:T(8,128)(2,1)} custom-call(bf16[256,4096]{1,0:T(8,128)(2,1)} %refs_1_.5, bf16[256,4096]{1,0:T(8,128)(2,1)} %refs_2_.3, f32[32,256]{1,0:T(8,128)} %bitcast.24), custom_call_target="tpu_custom_call" | custom-call | tf_op jit(solution)/shard_map/local_states/pallas_call | solution.py:152
  14.9 2.0 deal.1
  16.9 1.2 copy-done.12
  18.1 3.8 %all-to-all-start = ((bf16[8,576,128]{2,1,0:T(8,128)(2,1)}), bf16[8,576,128]{2,1,0:T(8,128)(2,1)S(1)}, u32[]{:S(2)}, u32[]{:S(2)}) async-start(bf16[8,576,128]{2,1,0:T(8,128)(2,1)} %local_states.1.refs_3_), calls=%async_computation | async-start | bytes 2359296 | tf_op jit(solution)/shard_map/state_scan/all_to_all | solution.py:466
  22.0 1.2 copy-done.14
  23.1 1.4 copy-done.13
  24.6 1.4 copy-done.15
  26.0 1.3 pair.1
  27.3 0.8 copy-done.21
  28.1 2.0 collective-permute-start.3
  30.1 1.5 collective-permute-start.4
  31.6 7.7 %all-to-all-done.refs_0_ = bf16[8,576,128]{2,1,0:T(8,128)(2,1)S(1)} async-done(((bf16[8,576,128]{2,1,0:T(8,128)(2,1)}), bf16[8,576,128]{2,1,0:T(8,128)(2,1)S(1)}, u32[]{:S(2)}, u32[]{:S(2)}) %all-to-all-start) | async-done | bytes 1179680 | tf_op jit(solution)/shard_map/state_scan/all_to_all | solution.py:466
  39.6 1.3 collective-permute-start.1
  41.5 12.0 %collective-permute-done.1.refs_0_.refs_1_ = bf16[4,144,128]{2,1,0:T(8,128)(2,1)S(1)} collective-permute-done((bf16[4,144,128]{2,1,0:T(8,128)(2,1)S(1)}, bf16[4,144,128]{2,1,0:T(8,128)(2,1)S(1)}, u32[]{:S(2)}, u32[]{:S(2)}) %collective-permute-start.1) | collective-permute-done | bytes 147488 | tf_op jit(solution)/shard_map/state_scan/ppermute | solution.py:444
  53.6 1.3 collective-permute-start.2
  54.9 6.4 %collective-permute-done.5.refs_4_ = bf16[2,128,512]{2,1,0:T(8,128)(2,1)S(1)} collective-permute-done((bf16[2,128,512]{2,1,0:T(8,128)(2,1)}, bf16[2,128,512]{2,1,0:T(8,128)(2,1)S(1)}, u32[]{:S(2)}, u32[]{:S(2)}) %collective-permute-start.5) | collective-permute-done | bytes 262176 | tf_op jit(solution)/shard_map/start_exchange/ppermute | solution.py:437
  61.3 2.5 %in_order.1.refs_4_.refs_0_ = bf16[1024,512]{1,0:T(8,128)(2,1)} custom-call(s32[1]{0:T(128)} %bitcast.3.refs_0_, bf16[2,384,512]{2,1,0:T(8,128)(2,1)S(1)} %get-tuple-element.35.refs_1_.refs_5_.refs_6_, bf16[2,384,512]{2,1,0:T(8,128)(2,1)S(1)} %collective-permute-done.3.refs_2_.refs_5_, bf16[2,384,512]{2,1,0:T(8,128)(2,1)} %collective-permute-done.4.refs_3_.refs_6_, ...), custom_call_target="tpu_custom_call" | custom-call | tf_op jit(solution)/shard_map/out_weight_gather/in_order/pallas_call | solution.py:177
  63.8 1.4 plane_prefix.1.refs_6_
  65.2 0.7 all-gather.5.cloned.1.call-update
  66.0 3.6 %all-to-all-start.1 = ((bf16[8,4,128,128]{3,2,1,0:T(8,128)(2,1)}), bf16[8,4,128,128]{3,2,1,0:T(8,128)(2,1)S(1)}, u32[]{:S(2)}, u32[]{:S(2)}) async-start(bf16[8,4,128,128]{3,2,1,0:T(8,128)(2,1)} %plane_prefix.1.refs_6_), calls=%async_computation.1 | async-start | bytes 2097152 | tf_op jit(solution)/shard_map/state_scan/all_to_all | solution.py:485
  70.2 2.9 %collective-permute-start.6 = (bf16[2,256,512]{2,1,0:T(8,128)(2,1)S(1)}, bf16[2,256,512]{2,1,0:T(8,128)(2,1)S(1)}, u32[]{:S(2)}, u32[]{:S(2)}) collective-permute-start(bf16[2,256,512]{2,1,0:T(8,128)(2,1)S(1)} %hold.5), channel_id=1, source_target_pairs={{0,6},{1,7},{2,4},{3,5},{4,2},{5,3},{6,0},{7,1},{8,14},{9,15},{10,... | collective-permute-start | bytes 1572872 | tf_op jit(solution)/shard_map/residual_exchange/ppermute | solution.py:437
  73.4 1.4 copy.23
  74.8 0.6 reduce_window_sum.21.refs_5_
  75.5 10.3 %local_intra.1 = (bf16[256,4096]{1,0:T(8,128)(2,1)}, bf16[256,4096]{1,0:T(8,128)(2,1)}) custom-call(bf16[256,4096]{1,0:T(8,128)(2,1)} %refs_0_.5, bf16[256,4096]{1,0:T(8,128)(2,1)} %refs_1_.5, bf16[256,4096]{1,0:T(8,128)(2,1)} %refs_2_.3, bf16[256,4096]{1,0:T(8,128)(2,1)} %refs_3_.1, f32[8,256,4]{2,1,0:T(8,128)} %bitcast.21, ...), custom_call_target="tpu_custom_call" | custom-call | tf_op jit(solution)/shard_map/local_intra/pallas_call | solution.py:152
  85.8 1.0 copy-done.23
  86.8 7.4 %mix.1 = (bf16[128,4096]{1,0:T(8,128)(2,1)}, bf16[128,4096]{1,0:T(8,128)(2,1)}) custom-call(bf16[256,4096]{1,0:T(8,128)(2,1)} %refs_0_.5, bf16[256,4096]{1,0:T(8,128)(2,1)} %get-tuple-element.39.refs_1_, bf16[256,4096]{1,0:T(8,128)(2,1)} %get-tuple-element.40.refs_2_, f32[8,256,4]{2,1,0:T(8,128)} %bitcast.22, bf16[32,128,128]{2,1,0:T(8,128)(2,1)} %bitcast.23), custom_call_target="tpu_custom_call" | custom-call | tf_op jit(solution)/shard_map/mix/pallas_call | solution.py:152
  94.2 1.9 collective-permute-done.6.refs_2_.refs_5_.refs_6_
  97.6 23.6 %collective-permute-done.7.refs_0_ = bf16[128,4096]{1,0:T(8,128)(2,1)S(1)} collective-permute-done((bf16[128,4096]{1,0:T(8,128)(2,1)}, bf16[128,4096]{1,0:T(8,128)(2,1)S(1)}, u32[]{:S(2)}, u32[]{:S(2)}) %collective-permute-start.7) | collective-permute-done | bytes 1048608 | tf_op jit(solution)/shard_map/projections/ppermute | solution.py:437
  121.7 1.2 collective-permute-start.10
  122.9 1.0 copy-done.5
  124.3 1.0 copy-done.17
  125.3 1.0 copy-done.8
  126.3 1.0 copy-done.19
  127.3 18.0 %collective-permute-done.8.refs_2_.refs_0_ = bf16[128,4096]{1,0:T(8,128)(2,1)} collective-permute-done((bf16[128,4096]{1,0:T(8,128)(2,1)S(1)}, bf16[128,4096]{1,0:T(8,128)(2,1)}, u32[]{:S(2)}, u32[]{:S(2)}) %collective-permute-start.8) | collective-permute-done | bytes 1048608 | tf_op jit(solution)/shard_map/projections/ppermute | solution.py:437
  145.8 1.0 collective-permute-start.13
  146.8 0.9 collective-permute-start.14
  147.7 2.0 multiply_convert_fusion.1.refs_2_
  149.7 2.2 copy-done
  151.9 1.1 copy-done.3
  153.1 1.2 copy-done.6
  154.3 1.2 copy-done.9
  155.5 1.2 copy-done.18
  156.7 1.2 copy-done.20
  158.0 4.2 %out_projection.4 = (bf16[256,512]{1,0:T(8,128)(2,1)S(1)}, bf16[256,512]{1,0:T(8,128)(2,1)S(1)}) custom-call(bf16[128,4096]{1,0:T(8,128)(2,1)S(1)} %copy-done.18, bf16[128,4096]{1,0:T(8,128)(2,1)} %collective-permute-done.15.refs_1_, bf16[128,4096]{1,0:T(8,128)(2,1)S(1)} %copy-done.20, bf16[128,4096]{1,0:T(8,128)(2,1)} %collective-permute-done.16.refs_3_, ...), custom_call_target="tpu_custom_call" | custom-call | tf_op jit(solution)/shard_map/projections/out_projection/pallas_call | solution.py:177
  162.2 4.5 %out_projection.5 = (bf16[256,512]{1,0:T(8,128)(2,1)S(1)}, bf16[256,512]{1,0:T(8,128)(2,1)S(1)}) custom-call(bf16[128,4096]{1,0:T(8,128)(2,1)} %collective-permute-done.8.refs_2_.refs_0_, bf16[128,4096]{1,0:T(8,128)(2,1)} %collective-permute-done.19.refs_1_, bf16[128,4096]{1,0:T(8,128)(2,1)} %collective-permute-done.10.refs_3_.refs_2_, ...), custom_call_target="tpu_custom_call" | custom-call | tf_op jit(solution)/shard_map/projections/out_projection/pallas_call | solution.py:177
  167.3 2.0 multiply_convert_fusion.refs_3_
  169.3 1.3 cache_projection.4
  170.6 1.3 cache_projection.5
  172.9 0.9 collective-permute-start.25
  173.8 1.4 collective-permute-start.26
  175.9 0.9 collective-permute-done.23.refs_3_
  176.8 4.1 %out_projection.6 = (bf16[256,512]{1,0:T(8,128)(2,1)S(1)}, bf16[256,512]{1,0:T(8,128)(2,1)S(1)}) custom-call(bf16[128,4096]{1,0:T(8,128)(2,1)} %get-tuple-element.54.refs_0_, bf16[128,4096]{1,0:T(8,128)(2,1)S(1)} %collective-permute-done.22.refs_1_, bf16[128,4096]{1,0:T(8,128)(2,1)} %get-tuple-element.55.refs_2_, ...), custom_call_target="tpu_custom_call" | custom-call | tf_op jit(solution)/shard_map/projections/out_projection/pallas_call | solution.py:177
  181.1 0.9 collective-permute-start.28
  182.0 6.4 %collective-permute-done.25.refs_4_ = bf16[128,2176]{1,0:T(8,128)(2,1)S(1)} collective-permute-done((bf16[128,2176]{1,0:T(8,128)(2,1)S(1)}, bf16[128,2176]{1,0:T(8,128)(2,1)S(1)}, u32[]{:S(2)}, u32[]{:S(2)}) %collective-permute-start.25) | collective-permute-done | bytes 557088 | tf_op jit(solution)/shard_map/projections/ppermute | solution.py:437
  188.4 1.0 collective-permute-done.26.refs_5_
  189.4 1.3 cache_projection.6
  190.7 1.5 collective-permute-start.30
  192.2 0.7 collective-permute-start.31
  192.8 8.5 %collective-permute-done.27.refs_8_.refs_4_ = bf16[128,2176]{1,0:T(8,128)(2,1)S(1)} collective-permute-done((bf16[128,2176]{1,0:T(8,128)(2,1)S(1)}, bf16[128,2176]{1,0:T(8,128)(2,1)S(1)}, u32[]{:S(2)}, u32[]{:S(2)}) %collective-permute-start.27) | collective-permute-done | bytes 557088 | tf_op jit(solution)/shard_map/projections/ppermute | solution.py:437
  201.3 3.9 %out_projection.7 = (bf16[256,512]{1,0:T(8,128)(2,1)S(1)}, bf16[256,512]{1,0:T(8,128)(2,1)S(1)}) custom-call(bf16[128,4096]{1,0:T(8,128)(2,1)} %get-tuple-element.46.refs_0_, bf16[128,4096]{1,0:T(8,128)(2,1)S(1)} %copy-done.7, bf16[128,4096]{1,0:T(8,128)(2,1)} %get-tuple-element.47.refs_2_, bf16[128,4096]{1,0:T(8,128)(2,1)S(1)} %copy-done.10, ...), custom_call_target="tpu_custom_call" | custom-call | tf_op jit(solution)/shard_map/projections/out_projection/pallas_call | solution.py:177
  205.3 1.5 collective-permute-done.29.refs_1_
  206.8 5.2 %collective-permute-done.30.refs_5_ = bf16[128,2176]{1,0:T(8,128)(2,1)S(1)} collective-permute-done((bf16[128,2176]{1,0:T(8,128)(2,1)S(1)}, bf16[128,2176]{1,0:T(8,128)(2,1)S(1)}, u32[]{:S(2)}, u32[]{:S(2)}) %collective-permute-start.30) | collective-permute-done | bytes 557088 | tf_op jit(solution)/shard_map/projections/ppermute | solution.py:437
  212.0 2.4 %cache_projection.7 = (bf16[256,1024]{1,0:T(8,128)(2,1)}, bf16[256,1024]{1,0:T(8,128)(2,1)}) custom-call(bf16[256,512]{1,0:T(8,128)(2,1)S(1)} %get-tuple-element.61.refs_0_, bf16[256,512]{1,0:T(8,128)(2,1)S(1)} %collective-permute-done.29.refs_1_, bf16[512,2048]{1,0:T(8,128)(2,1)S(1)} %multiply_convert_fusion.1.refs_2_, ...), custom_call_target="tpu_custom_call" | custom-call | tf_op jit(solution)/shard_map/projections/cache_projection/pallas_call | solution.py:177
  (98 shorter events, 7.6 us)
Async XLA Ops:
  7.2 56.7 %all-gather.3.cloned.1.call-start = ((), (), s32[]{:S(2)}) async-start(), calls=%async_computation.2 | async-start | bytes 2621440 | tf_op jit(solution)/shard_map/kv_weight_gather/all_gather | solution.py:459
  7.9 7.0 %copy-start.11 = (bf16[256,4096]{1,0:T(8,128)(2,1)S(1)}, bf16[256,4096]{1,0:T(8,128)(2,1)}, u32[]{:S(2)}) copy-start(bf16[256,4096]{1,0:T(8,128)(2,1)} %refs_1_.4) | copy-start | bytes 6291460
  7.9 7.0 %copy-start.16 = (bf16[128,4096]{1,0:T(8,128)(2,1)S(1)}, bf16[128,4096]{1,0:T(8,128)(2,1)}, u32[]{:S(2)}) copy-start(bf16[128,4096]{1,0:T(8,128)(2,1)} %refs_2_.2) | copy-start | bytes 3145732
  16.9 1.2 copy-start.12
  18.1 3.8 %collective-permute-start = (bf16[4,384,512]{2,1,0:T(8,128)(2,1)}, bf16[4,384,512]{2,1,0:T(8,128)(2,1)S(1)}, u32[]{:S(2)}, u32[]{:S(2)}) collective-permute-start(bf16[4,384,512]{2,1,0:T(8,128)(2,1)} %get-tuple-element.34), channel_id=1, source_target_pairs={{0,1},{1,0},{2,3},{3,2},{4,5},{5,4},{6,7},{7,6},{8,9},{9,8},{10,11... | collective-permute-start | bytes 4718600 | tf_op jit(solution)/shard_map/start_exchange/ppermute | solution.py:437
  18.1 21.2 %all-to-all-start = ((bf16[8,576,128]{2,1,0:T(8,128)(2,1)}), bf16[8,576,128]{2,1,0:T(8,128)(2,1)S(1)}, u32[]{:S(2)}, u32[]{:S(2)}) async-start(bf16[8,576,128]{2,1,0:T(8,128)(2,1)} %local_states.1.refs_3_), calls=%async_computation | async-start | bytes 2359296 | tf_op jit(solution)/shard_map/state_scan/all_to_all | solution.py:466
  22.0 1.2 copy-start.14
  23.1 1.4 copy-start.13
  24.6 1.4 copy-start.15
  27.3 0.8 copy-start.21
  28.1 33.2 %collective-permute-start.3 = (bf16[2,384,512]{2,1,0:T(8,128)(2,1)}, bf16[2,384,512]{2,1,0:T(8,128)(2,1)S(1)}, u32[]{:S(2)}, u32[]{:S(2)}) collective-permute-start(bf16[2,384,512]{2,1,0:T(8,128)(2,1)} %get-tuple-element.36), channel_id=1, source_target_pairs={{0,2},{1,3},{2,0},{3,1},{4,6},{5,7},{6,4},{7,5},{8,10},{9,11},{10,... | collective-permute-start | bytes 2359304 | tf_op jit(solution)/shard_map/start_exchange/ppermute | solution.py:437
  30.1 31.2 %collective-permute-start.4 = (bf16[2,384,512]{2,1,0:T(8,128)(2,1)}, bf16[2,384,512]{2,1,0:T(8,128)(2,1)}, u32[]{:S(2)}, u32[]{:S(2)}) collective-permute-start(bf16[2,384,512]{2,1,0:T(8,128)(2,1)} %get-tuple-element.37), channel_id=1, source_target_pairs={{0,4},{1,5},{2,6},{3,7},{4,0},{5,1},{6,2},{7,3},{8,12},{9,13},{10,... | collective-permute-start | bytes 2359304 | tf_op jit(solution)/shard_map/start_exchange/ppermute | solution.py:437
  39.6 14.0 %collective-permute-start.1 = (bf16[4,144,128]{2,1,0:T(8,128)(2,1)S(1)}, bf16[4,144,128]{2,1,0:T(8,128)(2,1)S(1)}, u32[]{:S(2)}, u32[]{:S(2)}) collective-permute-start(bf16[4,144,128]{2,1,0:T(8,128)(2,1)S(1)} %plane_total.1.refs_1_.refs_5_), channel_id=1, source_target_pairs={{0,8},{1,9},{2,10},{3,11},{4,12},{5,13},{6,14},{7,15},{8,16},{9,17... | collective-permute-start | bytes 442376 | tf_op jit(solution)/shard_map/state_scan/ppermute | solution.py:444
  40.9 20.4 %collective-permute-start.5 = (bf16[2,128,512]{2,1,0:T(8,128)(2,1)}, bf16[2,128,512]{2,1,0:T(8,128)(2,1)S(1)}, u32[]{:S(2)}, u32[]{:S(2)}) collective-permute-start(bf16[2,128,512]{2,1,0:T(8,128)(2,1)} %get-tuple-element.38), channel_id=1, source_target_pairs={{0,6},{1,7},{2,4},{3,5},{4,2},{5,3},{6,0},{7,1},{8,14},{9,15},{10,... | collective-permute-start | bytes 786440 | tf_op jit(solution)/shard_map/start_exchange/ppermute | solution.py:437
  53.6 10.2 %collective-permute-start.2 = (bf16[4,144,128]{2,1,0:T(8,128)(2,1)S(1)}, bf16[4,144,128]{2,1,0:T(8,128)(2,1)S(1)}, u32[]{:S(2)}, u32[]{:S(2)}) collective-permute-start(bf16[4,144,128]{2,1,0:T(8,128)(2,1)S(1)} %join.1.refs_1_), channel_id=1, source_target_pairs={{0,16},{1,17},{2,18},{3,19},{4,20},{5,21},{6,22},{7,23},{8,24},{9,... | collective-permute-start | bytes 442376 | tf_op jit(solution)/shard_map/state_scan/ppermute | solution.py:444
  61.3 3.9 %copy-start.2 = (bf16[2,384,512]{2,1,0:T(8,128)(2,1)}, bf16[2,384,512]{2,1,0:T(8,128)(2,1)S(1)}, u32[]{:S(2)}) copy-start(bf16[2,384,512]{2,1,0:T(8,128)(2,1)S(1)} %collective-permute-done.3.refs_2_.refs_5_) | copy-start | bytes 2359300
  65.2 84.5 %all-gather.5.cloned.1.call-start = ((), (), s32[]{:S(2)}) async-start(), calls=%async_computation.3 | async-start | bytes 5242880 | tf_op jit(solution)/shard_map/out_weight_gather/all_gather | solution.py:480
  65.2 4.3 %copy-start.24 = (f32[256,32]{0,1:T(8,128)S(1)}, f32[256,32]{0,1:T(8,128)}, u32[]{:S(2)}) copy-start(f32[256,32]{0,1:T(8,128)} %param.14) | copy-start | bytes 98308
  65.2 4.9 %copy-start.22 = (bf16[2,256,512]{2,1,0:T(8,128)(2,1)S(1)}, bf16[2,256,512]{2,1,0:T(8,128)(2,1)}, u32[]{:S(2)}) copy-start(bf16[2,256,512]{2,1,0:T(8,128)(2,1)} %copy-done.21) | copy-start | bytes 1572868
  66.0 19.8 %all-to-all-start.1 = ((bf16[8,4,128,128]{3,2,1,0:T(8,128)(2,1)}), bf16[8,4,128,128]{3,2,1,0:T(8,128)(2,1)S(1)}, u32[]{:S(2)}, u32[]{:S(2)}) async-start(bf16[8,4,128,128]{3,2,1,0:T(8,128)(2,1)} %plane_prefix.1.refs_6_), calls=%async_computation.1 | async-start | bytes 2097152 | tf_op jit(solution)/shard_map/state_scan/all_to_all | solution.py:485
  70.2 26.0 %collective-permute-start.6 = (bf16[2,256,512]{2,1,0:T(8,128)(2,1)S(1)}, bf16[2,256,512]{2,1,0:T(8,128)(2,1)S(1)}, u32[]{:S(2)}, u32[]{:S(2)}) collective-permute-start(bf16[2,256,512]{2,1,0:T(8,128)(2,1)S(1)} %hold.5), channel_id=1, source_target_pairs={{0,6},{1,7},{2,4},{3,5},{4,2},{5,3},{6,0},{7,1},{8,14},{9,15},{10,... | collective-permute-start | bytes 1572872 | tf_op jit(solution)/shard_map/residual_exchange/ppermute | solution.py:437
  85.8 1.1 copy-start.23
  94.2 51.6 %copy-start.25 = (bf16[4096]{0:T(1024)(128)(2,1)S(1)}, bf16[4096]{0:T(1024)(128)(2,1)}, u32[]{:S(2)}) copy-start(bf16[4096]{0:T(1024)(128)(2,1)} %param.16) | copy-start | bytes 24580
  96.1 25.0 %collective-permute-start.7 = (bf16[128,4096]{1,0:T(8,128)(2,1)}, bf16[128,4096]{1,0:T(8,128)(2,1)S(1)}, u32[]{:S(2)}, u32[]{:S(2)}) collective-permute-start(bf16[128,4096]{1,0:T(8,128)(2,1)} %get-tuple-element.44.refs_0_), channel_id=1, source_target_pairs={{0,2},{1,3},{2,0},{3,1},{4,6},{5,7},{6,4},{7,5},{8,10},{9,11},{10,... | collective-permute-start | bytes 3145736 | tf_op jit(solution)/shard_map/projections/ppermute | solution.py:437
  96.7 25.0 %collective-permute-start.9 = (bf16[128,4096]{1,0:T(8,128)(2,1)}, bf16[128,4096]{1,0:T(8,128)(2,1)S(1)}, u32[]{:S(2)}, u32[]{:S(2)}) collective-permute-start(bf16[128,4096]{1,0:T(8,128)(2,1)} %get-tuple-element.45.refs_1_), channel_id=1, source_target_pairs={{0,4},{1,5},{2,6},{3,7},{4,0},{5,1},{6,2},{7,3},{8,12},{9,13},{10,... | collective-permute-start | bytes 3145736 | tf_op jit(solution)/shard_map/projections/ppermute | solution.py:437
  97.0 25.8 %collective-permute-start.11 = (bf16[128,4096]{1,0:T(8,128)(2,1)}, bf16[128,4096]{1,0:T(8,128)(2,1)S(1)}, u32[]{:S(2)}, u32[]{:S(2)}) collective-permute-start(bf16[128,4096]{1,0:T(8,128)(2,1)} %get-tuple-element.44.refs_0_), channel_id=1, source_target_pairs={{0,1},{1,0},{2,3},{3,2},{4,5},{5,4},{6,7},{7,6},{8,9},{9,8},{10,11... | collective-permute-start | bytes 3145736 | tf_op jit(solution)/shard_map/projections/ppermute | solution.py:437
  97.0 28.3 %collective-permute-start.12 = (bf16[128,4096]{1,0:T(8,128)(2,1)}, bf16[128,4096]{1,0:T(8,128)(2,1)S(1)}, u32[]{:S(2)}, u32[]{:S(2)}) collective-permute-start(bf16[128,4096]{1,0:T(8,128)(2,1)} %get-tuple-element.45.refs_1_), channel_id=1, source_target_pairs={{0,1},{1,0},{2,3},{3,2},{4,5},{5,4},{6,7},{7,6},{8,9},{9,8},{10,11... | collective-permute-start | bytes 3145736 | tf_op jit(solution)/shard_map/projections/ppermute | solution.py:437
  121.1 24.1 %collective-permute-start.8 = (bf16[128,4096]{1,0:T(8,128)(2,1)S(1)}, bf16[128,4096]{1,0:T(8,128)(2,1)}, u32[]{:S(2)}, u32[]{:S(2)}) collective-permute-start(bf16[128,4096]{1,0:T(8,128)(2,1)S(1)} %collective-permute-done.7.refs_0_), channel_id=1, source_target_pairs={{0,4},{1,5},{2,6},{3,7},{4,0},{5,1},{6,2},{7,3},{8,12},{9,13},{10,... | collective-permute-start | bytes 3145736 | tf_op jit(solution)/shard_map/projections/ppermute | solution.py:437
  121.7 23.9 %collective-permute-start.10 = (bf16[128,4096]{1,0:T(8,128)(2,1)S(1)}, bf16[128,4096]{1,0:T(8,128)(2,1)}, u32[]{:S(2)}, u32[]{:S(2)}) collective-permute-start(bf16[128,4096]{1,0:T(8,128)(2,1)S(1)} %collective-permute-done.9.refs_2_), channel_id=1, source_target_pairs={{0,2},{1,3},{2,0},{3,1},{4,6},{5,7},{6,4},{7,5},{8,10},{9,11},{10,... | collective-permute-start | bytes 3145736 | tf_op jit(solution)/shard_map/projections/ppermute | solution.py:437
  122.9 44.4 %collective-permute-start.18 = (bf16[512,2048]{1,0:T(8,128)(2,1)}, bf16[512,2048]{1,0:T(8,128)(2,1)}, u32[]{:S(2)}, u32[]{:S(2)}) collective-permute-start(bf16[512,2048]{1,0:T(8,128)(2,1)} %all-gather.3.cloned.1.call-done.refs_3_.refs_1_), channel_id=1, source_target_pairs={{0,1},{1,0},{2,3},{3,2},{4,5},{5,4},{6,7},{7,6},{8,9},{9,8},{10,11... | collective-permute-start | bytes 6291464 | tf_op jit(solution)/shard_map/cache_weight/ppermute | solution.py:437
  122.9 1.0 copy-start.5
  123.8 22.0 %collective-permute-start.15 = (bf16[128,4096]{1,0:T(8,128)(2,1)S(1)}, bf16[128,4096]{1,0:T(8,128)(2,1)}, u32[]{:S(2)}, u32[]{:S(2)}) collective-permute-start(bf16[128,4096]{1,0:T(8,128)(2,1)S(1)} %collective-permute-done.7.refs_0_), channel_id=1, source_target_pairs={{0,1},{1,0},{2,3},{3,2},{4,5},{5,4},{6,7},{7,6},{8,9},{9,8},{10,11... | collective-permute-start | bytes 3145736 | tf_op jit(solution)/shard_map/projections/ppermute | solution.py:437
  124.3 1.0 copy-start.17
  125.3 1.0 copy-start.8
  126.3 20.5 %collective-permute-start.16 = (bf16[128,4096]{1,0:T(8,128)(2,1)S(1)}, bf16[128,4096]{1,0:T(8,128)(2,1)}, u32[]{:S(2)}, u32[]{:S(2)}) collective-permute-start(bf16[128,4096]{1,0:T(8,128)(2,1)S(1)} %collective-permute-done.9.refs_2_), channel_id=1, source_target_pairs={{0,1},{1,0},{2,3},{3,2},{4,5},{5,4},{6,7},{7,6},{8,9},{9,8},{10,11... | collective-permute-start | bytes 3145736 | tf_op jit(solution)/shard_map/projections/ppermute | solution.py:437
  126.3 1.0 copy-start.19
  145.3 16.9 %collective-permute-start.19 = (bf16[128,4096]{1,0:T(8,128)(2,1)}, bf16[128,4096]{1,0:T(8,128)(2,1)}, u32[]{:S(2)}, u32[]{:S(2)}) collective-permute-start(bf16[128,4096]{1,0:T(8,128)(2,1)} %collective-permute-done.8.refs_2_.refs_0_), channel_id=1, source_target_pairs={{0,1},{1,0},{2,3},{3,2},{4,5},{5,4},{6,7},{7,6},{8,9},{9,8},{10,11... | collective-permute-start | bytes 3145736 | tf_op jit(solution)/shard_map/projections/ppermute | solution.py:437
  145.5 16.7 %collective-permute-start.20 = (bf16[128,4096]{1,0:T(8,128)(2,1)}, bf16[128,4096]{1,0:T(8,128)(2,1)}, u32[]{:S(2)}, u32[]{:S(2)}) collective-permute-start(bf16[128,4096]{1,0:T(8,128)(2,1)} %collective-permute-done.10.refs_3_.refs_2_), channel_id=1, source_target_pairs={{0,1},{1,0},{2,3},{3,2},{4,5},{5,4},{6,7},{7,6},{8,9},{9,8},{10,11... | collective-permute-start | bytes 3145736 | tf_op jit(solution)/shard_map/projections/ppermute | solution.py:437
  145.8 26.1 %collective-permute-start.13 = (bf16[128,4096]{1,0:T(8,128)(2,1)}, bf16[128,4096]{1,0:T(8,128)(2,1)}, u32[]{:S(2)}, u32[]{:S(2)}) collective-permute-start(bf16[128,4096]{1,0:T(8,128)(2,1)} %get-tuple-element.47.refs_2_), channel_id=1, source_target_pairs={{0,2},{1,3},{2,0},{3,1},{4,6},{5,7},{6,4},{7,5},{8,10},{9,11},{10,... | collective-permute-start | bytes 3145736 | tf_op jit(solution)/shard_map/projections/ppermute | solution.py:437
  146.8 25.6 %collective-permute-start.14 = (bf16[128,4096]{1,0:T(8,128)(2,1)}, bf16[128,4096]{1,0:T(8,128)(2,1)}, u32[]{:S(2)}, u32[]{:S(2)}) collective-permute-start(bf16[128,4096]{1,0:T(8,128)(2,1)} %get-tuple-element.46.refs_0_), channel_id=1, source_target_pairs={{0,4},{1,5},{2,6},{3,7},{4,0},{5,1},{6,2},{7,3},{8,12},{9,13},{10,... | collective-permute-start | bytes 3145736 | tf_op jit(solution)/shard_map/projections/ppermute | solution.py:437
  149.7 2.2 copy-start
  151.9 1.1 copy-start.3
  153.1 1.2 copy-start.6
  154.3 1.2 copy-start.9
  155.5 1.2 copy-start.18
  156.7 1.2 copy-start.20
  158.0 4.3 %copy-start.1 = (bf16[4096,512]{1,0:T(8,128)(2,1)S(1)}, bf16[4096,512]{1,0:T(8,128)(2,1)}, u32[]{:S(2)}) copy-start(bf16[4096,512]{1,0:T(8,128)(2,1)} %all-gather.5.cloned.1.call-done.refs_4_) | copy-start | bytes 12582916
  166.7 2.6 %collective-permute-start.21 = (bf16[256,512]{1,0:T(8,128)(2,1)S(1)}, bf16[256,512]{1,0:T(8,128)(2,1)S(1)}, u32[]{:S(2)}, u32[]{:S(2)}) collective-permute-start(bf16[256,512]{1,0:T(8,128)(2,1)S(1)} %get-tuple-element.51), channel_id=1, source_target_pairs={{0,1},{1,0},{2,3},{3,2},{4,5},{5,4},{6,7},{7,6},{8,9},{9,8},{10,11... | collective-permute-start | bytes 786440 | tf_op jit(solution)/shard_map/projections/ppermute | solution.py:437
  166.8 3.8 %collective-permute-start.17 = (bf16[256,512]{1,0:T(8,128)(2,1)S(1)}, bf16[256,512]{1,0:T(8,128)(2,1)S(1)}, u32[]{:S(2)}, u32[]{:S(2)}) collective-permute-start(bf16[256,512]{1,0:T(8,128)(2,1)S(1)} %get-tuple-element.49), channel_id=1, source_target_pairs={{0,1},{1,0},{2,3},{3,2},{4,5},{5,4},{6,7},{7,6},{8,9},{9,8},{10,11... | collective-permute-start | bytes 786440 | tf_op jit(solution)/shard_map/projections/ppermute | solution.py:437
  171.9 4.9 %copy-start.4 = (bf16[2,384,512]{2,1,0:T(8,128)(2,1)S(1)}, bf16[2,384,512]{2,1,0:T(8,128)(2,1)}, u32[]{:S(2)}) copy-start(bf16[2,384,512]{2,1,0:T(8,128)(2,1)} %copy-done.2) | copy-start | bytes 2359300
  172.4 3.5 %collective-permute-start.22 = (bf16[128,4096]{1,0:T(8,128)(2,1)}, bf16[128,4096]{1,0:T(8,128)(2,1)S(1)}, u32[]{:S(2)}, u32[]{:S(2)}) collective-permute-start(bf16[128,4096]{1,0:T(8,128)(2,1)} %get-tuple-element.54.refs_0_), channel_id=1, source_target_pairs={{0,1},{1,0},{2,3},{3,2},{4,5},{5,4},{6,7},{7,6},{8,9},{9,8},{10,11... | collective-permute-start | bytes 3145736 | tf_op jit(solution)/shard_map/projections/ppermute | solution.py:437
  172.4 4.4 %collective-permute-start.23 = (bf16[128,4096]{1,0:T(8,128)(2,1)}, bf16[128,4096]{1,0:T(8,128)(2,1)S(1)}, u32[]{:S(2)}, u32[]{:S(2)}) collective-permute-start(bf16[128,4096]{1,0:T(8,128)(2,1)} %get-tuple-element.55.refs_2_), channel_id=1, source_target_pairs={{0,1},{1,0},{2,3},{3,2},{4,5},{5,4},{6,7},{7,6},{8,9},{9,8},{10,11... | collective-permute-start | bytes 3145736 | tf_op jit(solution)/shard_map/projections/ppermute | solution.py:437
  172.9 15.5 %collective-permute-start.25 = (bf16[128,2176]{1,0:T(8,128)(2,1)S(1)}, bf16[128,2176]{1,0:T(8,128)(2,1)S(1)}, u32[]{:S(2)}, u32[]{:S(2)}) collective-permute-start(bf16[128,2176]{1,0:T(8,128)(2,1)S(1)} %get-tuple-element.58), channel_id=1, source_target_pairs={{0,4},{1,5},{2,6},{3,7},{4,0},{5,1},{6,2},{7,3},{8,12},{9,13},{10,... | collective-permute-start | bytes 1671176 | tf_op jit(solution)/shard_map/projections/ppermute | solution.py:437
  173.8 15.5 %collective-permute-start.26 = (bf16[128,2176]{1,0:T(8,128)(2,1)S(1)}, bf16[128,2176]{1,0:T(8,128)(2,1)S(1)}, u32[]{:S(2)}, u32[]{:S(2)}) collective-permute-start(bf16[128,2176]{1,0:T(8,128)(2,1)S(1)} %get-tuple-element.52.refs_4_), channel_id=1, source_target_pairs={{0,2},{1,3},{2,0},{3,1},{4,6},{5,7},{6,4},{7,5},{8,10},{9,11},{10,... | collective-permute-start | bytes 1671176 | tf_op jit(solution)/shard_map/projections/ppermute | solution.py:437
  175.3 26.0 %collective-permute-start.27 = (bf16[128,2176]{1,0:T(8,128)(2,1)S(1)}, bf16[128,2176]{1,0:T(8,128)(2,1)S(1)}, u32[]{:S(2)}, u32[]{:S(2)}) collective-permute-start(bf16[128,2176]{1,0:T(8,128)(2,1)S(1)} %get-tuple-element.53.refs_2_), channel_id=1, source_target_pairs={{0,2},{1,3},{2,0},{3,1},{4,6},{5,7},{6,4},{7,5},{8,10},{9,11},{10,... | collective-permute-start | bytes 1671176 | tf_op jit(solution)/shard_map/projections/ppermute | solution.py:437
  180.9 8.5 %collective-permute-start.24 = (bf16[256,512]{1,0:T(8,128)(2,1)S(1)}, bf16[256,512]{1,0:T(8,128)(2,1)S(1)}, u32[]{:S(2)}, u32[]{:S(2)}) collective-permute-start(bf16[256,512]{1,0:T(8,128)(2,1)S(1)} %get-tuple-element.57), channel_id=1, source_target_pairs={{0,1},{1,0},{2,3},{3,2},{4,5},{5,4},{6,7},{7,6},{8,9},{9,8},{10,11... | collective-permute-start | bytes 786440 | tf_op jit(solution)/shard_map/projections/ppermute | solution.py:437
  181.1 20.2 %collective-permute-start.28 = (bf16[128,2176]{1,0:T(8,128)(2,1)S(1)}, bf16[128,2176]{1,0:T(8,128)(2,1)S(1)}, u32[]{:S(2)}, u32[]{:S(2)}) collective-permute-start(bf16[128,2176]{1,0:T(8,128)(2,1)S(1)} %get-tuple-element.60), channel_id=1, source_target_pairs={{0,4},{1,5},{2,6},{3,7},{4,0},{5,1},{6,2},{7,3},{8,12},{9,13},{10,... | collective-permute-start | bytes 1671176 | tf_op jit(solution)/shard_map/projections/ppermute | solution.py:437
  189.4 11.9 %copy-start.7 = (bf16[128,4096]{1,0:T(8,128)(2,1)S(1)}, bf16[128,4096]{1,0:T(8,128)(2,1)}, u32[]{:S(2)}) copy-start(bf16[128,4096]{1,0:T(8,128)(2,1)} %copy-done.5) | copy-start | bytes 3145732
  189.4 11.9 %copy-start.10 = (bf16[128,4096]{1,0:T(8,128)(2,1)S(1)}, bf16[128,4096]{1,0:T(8,128)(2,1)}, u32[]{:S(2)}) copy-start(bf16[128,4096]{1,0:T(8,128)(2,1)} %copy-done.8) | copy-start | bytes 3145732
  190.7 21.3 %collective-permute-start.30 = (bf16[128,2176]{1,0:T(8,128)(2,1)S(1)}, bf16[128,2176]{1,0:T(8,128)(2,1)S(1)}, u32[]{:S(2)}, u32[]{:S(2)}) collective-permute-start(bf16[128,2176]{1,0:T(8,128)(2,1)S(1)} %get-tuple-element.59.refs_7_), channel_id=1, source_target_pairs={{0,2},{1,3},{2,0},{3,1},{4,6},{5,7},{6,4},{7,5},{8,10},{9,11},{10,... | collective-permute-start | bytes 1671176 | tf_op jit(solution)/shard_map/projections/ppermute | solution.py:437
  192.2 19.8 %collective-permute-start.31 = (bf16[128,2176]{1,0:T(8,128)(2,1)S(1)}, bf16[128,2176]{1,0:T(8,128)(2,1)S(1)}, u32[]{:S(2)}, u32[]{:S(2)}) collective-permute-start(bf16[128,2176]{1,0:T(8,128)(2,1)S(1)} %get-tuple-element.63), channel_id=1, source_target_pairs={{0,4},{1,5},{2,6},{3,7},{4,0},{5,1},{6,2},{7,3},{8,12},{9,13},{10,... | collective-permute-start | bytes 1671176 | tf_op jit(solution)/shard_map/projections/ppermute | solution.py:437
  205.2 1.6 collective-permute-start.29
Sparse Core Ops, SparseCore 0:
  9.6 49.9 all-gather.2
  67.6 78.4 all-gather.4

commit v7 on v6

--- a/solution.py
+++ b/solution.py
@@ -271,17 +271,21 @@
     return resident_call("plane_prefix", body, (parts, nearest, others), [shape], after=after)[0]
 
 
+def dealt_blocks(ways, block, source_refs, place):
+    top = 0
+    for source_ref in source_refs:
+        rows = source_ref.shape[0]
+        for i in range(source_ref.shape[1] // (ways * block)):
+            start = pl.multiple_of((i * ways + place) * block, block)
+            yield slice(top, top + rows), slice(i * block, (i + 1) * block), source_ref[:, pl.ds(start, block)]
+        top += rows
+
+
 def deal_kernel(ways, block, place_ref, *refs):
-    *source_refs, even_ref, odd_ref = refs
-    for r in range(ways):
-        target_ref, top = (even_ref, odd_ref)[r % 2], 0
-        for source_ref in source_refs:
-            rows = slice(top, top + source_ref.shape[0])
-            for i in range(target_ref.shape[2] // block):
-                start = pl.multiple_of((i * ways + (place_ref[0] ^ r)) * block, block)
-                columns = slice(i * block, (i + 1) * block)
-                target_ref[r // 2, rows, columns] = source_ref[:, pl.ds(start, block)]
-            top += source_ref.shape[0]
+    *source_refs, target_ref = refs
+    for r in range(1, ways, 2):
+        for rows, columns, part in dealt_blocks(ways, block, source_refs, place_ref[0] ^ r):
+            target_ref[r // 2, rows, columns] = part
 
 
 def deal(arrays, place, ways, block, after=()):
@@ -291,28 +295,36 @@
         "deal",
         functools.partial(deal_kernel, ways, block),
         arrays,
-        [shape, shape],
+        [shape],
         scalars=(place.reshape(1),),
         after=after,
-    )
-
-
-def pair_kernel(parts, even_ref, odd_ref, *target_refs):
-    for (chip, top), target_ref in zip(parts, target_refs):
-        rows = slice(top, top + target_ref.shape[1])
-        target_ref[0] = even_ref[chip, rows, :]
-        target_ref[1] = odd_ref[chip, rows, :]
-
-
-def pair(even, odd, split, after=()):
-    chips, rows, columns = even.shape
-    parts = [(chip, 0) for chip in range(chips)] + [(chips - 1, split)]
+    )[0]
+
+
+def pair_kernel(ways, block, split, place_ref, *refs):
+    chips, sources = ways // 2, len(refs) - ways // 2 - 2
+    source_refs, odd_ref, target_refs = refs[:sources], refs[sources], refs[sources + 1 :]
+    for chip in range(chips):
+        for rows, columns, part in dealt_blocks(ways, block, source_refs, place_ref[0] ^ (2 * chip)):
+            target_ref = target_refs[chip]
+            if rows.start >= target_ref.shape[1]:
+                target_ref, rows = target_refs[chips], slice(rows.start - split, rows.stop - split)
+            target_ref[0, rows, columns] = part
+        height = target_refs[chip].shape[1]
+        target_refs[chip][1] = odd_ref[chip, :height, :]
+    target_refs[chips][1] = odd_ref[chips - 1, split:, :]
+
+
+def pair(arrays, odd, place, ways, block, after=()):
+    chips, rows, columns = odd.shape
+    split = rows - arrays[-1].shape[0]
     heights = [rows] * (chips - 1) + [split, rows - split]
     return resident_call(
         "pair",
-        functools.partial(pair_kernel, parts),
-        (even, odd),
-        [jax.ShapeDtypeStruct((2, height, columns), even.dtype) for height in heights],
+        functools.partial(pair_kernel, ways, block, split),
+        (*arrays, odd),
+        [jax.ShapeDtypeStruct((2, height, columns), odd.dtype) for height in heights],
+        scalars=(place.reshape(1),),
         after=after,
     )
 
@@ -383,7 +395,7 @@
     )
 
 
-def cache_kernel(width, model, joined, finish, *refs):
+def cache_kernel(width, joined, *refs):
     own_ref, other_ref, own_weight_ref, other_weight_ref, *refs = refs
     added, out_refs = refs[: len(joined)], refs[len(joined) :]
     tokens, columns = own_ref.shape[0] // 2, own_weight_ref.shape[1]
@@ -399,30 +411,45 @@
             if half == i:
                 sums = sums + ref[:, :columns].astype(F32)
                 norm = norm + jnp.sum(ref[:, columns:].astype(F32), axis=1, keepdims=True)
-        if finish:
-            sums = (sums * lax.rsqrt(norm / model + NORM_EPS)).astype(BF16)
-            for head in range(columns // (2 * width)):
-                for kind, out_ref in enumerate(out_refs):
-                    start = (2 * head + kind) * width
-                    out_ref[rows, head * width : (head + 1) * width] = sums[:, start : start + width]
-        else:
-            high = norm.astype(BF16).astype(F32)
-            middle = (norm - high).astype(BF16).astype(F32)
-            low = norm - high - middle
-            lane = lax.broadcasted_iota(jnp.int32, (tokens, width), 1)
-            lanes = jnp.where(lane == 0, high, jnp.where(lane == 1, middle, 0.0))
-            out_refs[i][:, :columns] = sums.astype(BF16)
-            out_refs[i][:, columns:] = jnp.where(lane == 2, low, lanes).astype(BF16)
-
-
-def cache_projection(own, other, weights, width, model, added=(), finish=False, after=()):
+        high = norm.astype(BF16).astype(F32)
+        middle = (norm - high).astype(BF16).astype(F32)
+        low = norm - high - middle
+        lane = lax.broadcasted_iota(jnp.int32, (tokens, width), 1)
+        lanes = jnp.where(lane == 0, high, jnp.where(lane == 1, middle, 0.0))
+        out_refs[i][:, :columns] = sums.astype(BF16)
+        out_refs[i][:, columns:] = jnp.where(lane == 2, low, lanes).astype(BF16)
+
+
+def finish_kernel(width, model, *refs):
+    *share_refs, keys_ref, values_ref = refs
+    tokens, columns = share_refs[0].shape[0], 2 * keys_ref.shape[1]
+    for half in range(2):
+        shares = [ref[...].astype(F32) for ref in share_refs[half::2]]
+        norm = sum(jnp.sum(share[:, columns:], axis=1, keepdims=True) for share in shares)
+        sums = sum(share[:, :columns] for share in shares)
+        sums = (sums * lax.rsqrt(norm / model + NORM_EPS)).astype(BF16)
+        rows = slice(half * tokens, (half + 1) * tokens)
+        for head in range(columns // (2 * width)):
+            for kind, out_ref in enumerate((keys_ref, values_ref)):
+                start = (2 * head + kind) * width
+                out_ref[rows, head * width : (head + 1) * width] = sums[:, start : start + width]
+
+
+def finish(shares, width, model):
+    tokens, columns = shares[0].shape
+    out = jax.ShapeDtypeStruct((2 * tokens, (columns - width) // 2), BF16)
+    body = functools.partial(finish_kernel, width, model)
+    return resident_call("finish", body, shares, [out, out])
+
+
+def cache_projection(own, other, weights, width, joined=(), added=(), after=()):
     tokens, columns = own.shape[0], weights[0].shape[1]
-    out = (tokens, columns // 2) if finish else (tokens // 2, columns + width)
+    out = jax.ShapeDtypeStruct((tokens // 2, columns + width), BF16)
     return resident_call(
         "cache_projection",
-        functools.partial(cache_kernel, width, model, [half for _, half in added], finish),
-        (own, other, *weights, *[array for array, _ in added]),
-        [jax.ShapeDtypeStruct(out, BF16)] * 2,
+        functools.partial(cache_kernel, width, joined),
+        (own, other, *weights, *added),
+        [out, out],
         after=after,
     )
 
@@ -465,9 +492,10 @@
     with jax.named_scope("state_scan"):
         parts = lax.all_to_all(states, PLANE, 0, 0, tiled=True)
 
-    even, odd = deal((residual, out_weight), place, PLACES, piece, after=(states,))
+    dealt = (residual, out_weight)
+    odd = deal(dealt, place, PLACES, piece, after=(states,))
     with jax.named_scope("start_exchange"):
-        *starts, far_weight = pair(even, swap(odd, 1), tokens)
+        *starts, far_weight = pair(dealt, swap(odd, 1), place, PLACES, piece)
         starts[1:3] = [swap(starts[1], 2), swap(starts[2], 4)]
         far_weight = swap(far_weight, 6)
     with jax.named_scope("state_scan"):
@@ -509,8 +537,8 @@
         mine, theirs = out_projection(pieces, out_full, after)
         return mine, swap(theirs, 1)
 
-    def share_of(hidden, added=(), finish=False, after=()):
-        return cache_projection(*hidden, kv_full, width, model, added, finish, after)
+    def share_of(hidden, joined=(), added=(), after=()):
+        return cache_projection(*hidden, kv_full, width, joined, added, after)
 
     with jax.named_scope("projections"):
         early_x, late_y = swap(early, 2), swap(late, 4)
@@ -529,11 +557,11 @@
         early_x, late_y = swap(early_x, 2), swap(late_y, 4)
         late_far, early_far = swap(late_far, 4), swap(early_far, 2)
         near = hidden_of((1, 1, cores(late_x)), (2, 0, cores(early_y)))
-        late_x, early_y = share_of(near, [(late_far, 0), (early_far, 1)])
+        late_x, early_y = share_of(near, (0, 1), (late_far, early_far))
         home = hidden_of(*home, after=(late_x, early_x, late_y))
         late_x, early_y = swap(late_x, 2), swap(early_y, 4)
-        added = [(early_x, 0), (late_x, 1), (early_y, 0), (late_y, 1)]
-        return share_of(home, added, True)
+        home = share_of(home, (0, 1), (early_x, late_y))
+        return finish((*home, early_y, late_x), width, model)
 
 
 def entering(part, axis, combine, identity):

time: 224 us -> 222 us (level)
    pallas_call x14 -> x15, Pallas kernels: 30.4 us -> 30.5 us  [resident_call(): pl.pallas_call(kernel, in_specs=[pl.BlockSpec(memory_space=pltpu.SMEM)] *...]
  transfers between devices with their start and end apart: 36 -> 36, of which waited for: 14 -> 15; matrix products, arithmetic and copies ran while one was open for 3% -> 3% of each run, Pallas kernels for 23% -> 24%
where the time goes in v7:
time: 222 us; the launch traced here: 220 us
  waiting for transfers between devices  93.2 us (42%)
  Pallas kernels  55.2 us (25%)
  starting transfers between devices  30.7 us (14%)
  local copies, waits for them, and re-layouts  21.6 us (10%)
  between operations  14.4 us (6%)
  other arithmetic  4.77 us (2%)
    ppermute x30, waiting for transfers between devices, swap(): return lax.ppermute(array, SEQ, [(i, i ^ distance) for i in range(DEVICES)])  72.6 us
    pallas_call x15, Pallas kernels, resident_call(): pl.pallas_call(kernel, in_specs=[pl.BlockSpec(memory_space=pltpu.SMEM)] *...  30.5 us
    pallas_call x3, Pallas kernels, local_call(): pl.pallas_call(kernel, grid_spec=pltpu.PrefetchScalarGridSpec(num_scalar_...  24.7 us
    ppermute x30, starting transfers between devices, swap(): return lax.ppermute(array, SEQ, [(i, i ^ distance) for i in range(DEVICES)])  20.4 us
    unnamed x52, local copies, waits for them, and re-layouts  19.4 us
    ppermute x2, waiting for transfers between devices, hop(): return lax.ppermute(array, SEQ, pairs)  13.1 us
    all_to_all x1, waiting for transfers between devices, shared_on_device(): parts = lax.all_to_all(states, PLANE, 0, 0, tiled=True)  6.08 us
  transfers between devices with their start and end apart: 36, of which 15 were waited for; matrix products, arithmetic and copies ran while one was open for 3% of the time, Pallas kernels for 24%

profile of v7, /device:TPU:24, one launch (start us, length us, event | category | flops | bytes accessed | tf_op | source)
XLA Modules:
  0.0 219.9 jit_solution(2940979842108934273)
XLA Ops:
  7.2 0.7 all-gather.3.cloned.1.call-update
  7.9 7.0 %local_states.1.refs_3_ = bf16[8,576,128]{2,1,0:T(8,128)(2,1)} custom-call(bf16[256,4096]{1,0:T(8,128)(2,1)} %refs_1_.7, bf16[256,4096]{1,0:T(8,128)(2,1)} %refs_2_.5, f32[32,256]{1,0:T(8,128)} %bitcast.24), custom_call_target="tpu_custom_call" | custom-call | tf_op jit(solution)/shard_map/local_states/pallas_call | solution.py:152
  14.9 1.6 deal.1
  16.5 3.8 %all-to-all-start = ((bf16[8,576,128]{2,1,0:T(8,128)(2,1)}), bf16[8,576,128]{2,1,0:T(8,128)(2,1)S(1)}, u32[]{:S(2)}, u32[]{:S(2)}) async-start(bf16[8,576,128]{2,1,0:T(8,128)(2,1)} %local_states.1.refs_3_), calls=%async_computation | async-start | bytes 2359296 | tf_op jit(solution)/shard_map/state_scan/all_to_all | solution.py:493
  20.4 1.2 copy-done.15
  21.6 1.6 copy-done.3
  23.2 1.2 copy-done.8
  24.4 1.4 copy-done.16
  25.8 1.5 pair.1
  27.3 0.8 copy-done.21
  28.1 2.0 collective-permute-start.3
  30.1 1.5 collective-permute-start.4
  31.6 6.1 %all-to-all-done.refs_0_ = bf16[8,576,128]{2,1,0:T(8,128)(2,1)S(1)} async-done(((bf16[8,576,128]{2,1,0:T(8,128)(2,1)}), bf16[8,576,128]{2,1,0:T(8,128)(2,1)S(1)}, u32[]{:S(2)}, u32[]{:S(2)}) %all-to-all-start) | async-done | bytes 1179680 | tf_op jit(solution)/shard_map/state_scan/all_to_all | solution.py:493
  38.0 1.3 collective-permute-start.1
  39.9 12.1 %collective-permute-done.1.refs_0_.refs_1_ = bf16[4,144,128]{2,1,0:T(8,128)(2,1)S(1)} collective-permute-done((bf16[4,144,128]{2,1,0:T(8,128)(2,1)S(1)}, bf16[4,144,128]{2,1,0:T(8,128)(2,1)S(1)}, u32[]{:S(2)}, u32[]{:S(2)}) %collective-permute-start.1) | collective-permute-done | bytes 147488 | tf_op jit(solution)/shard_map/state_scan/ppermute | solution.py:471
  52.1 1.3 collective-permute-start.2
  53.4 6.3 %collective-permute-done.5.refs_4_ = bf16[2,128,512]{2,1,0:T(8,128)(2,1)S(1)} collective-permute-done((bf16[2,128,512]{2,1,0:T(8,128)(2,1)}, bf16[2,128,512]{2,1,0:T(8,128)(2,1)S(1)}, u32[]{:S(2)}, u32[]{:S(2)}) %collective-permute-start.5) | collective-permute-done | bytes 262176 | tf_op jit(solution)/shard_map/start_exchange/ppermute | solution.py:464
  59.7 2.5 %in_order.1.refs_4_.refs_0_ = bf16[1024,512]{1,0:T(8,128)(2,1)} custom-call(s32[1]{0:T(128)} %bitcast.3.refs_0_, bf16[2,384,512]{2,1,0:T(8,128)(2,1)S(1)} %get-tuple-element.33.refs_1_.refs_5_.refs_6_, bf16[2,384,512]{2,1,0:T(8,128)(2,1)S(1)} %collective-permute-done.3.refs_2_.refs_5_, bf16[2,384,512]{2,1,0:T(8,128)(2,1)} %collective-permute-done.4.refs_3_.refs_6_, ...), custom_call_target="tpu_custom_call" | custom-call | tf_op jit(solution)/shard_map/out_weight_gather/in_order/pallas_call | solution.py:177
  62.2 1.0 collective-permute-done.2.refs_2_
  63.2 1.4 plane_prefix.1.refs_6_
  64.6 0.7 all-gather.5.cloned.1.call-update
  65.3 3.8 %all-to-all-start.1 = ((bf16[8,4,128,128]{3,2,1,0:T(8,128)(2,1)}), bf16[8,4,128,128]{3,2,1,0:T(8,128)(2,1)S(1)}, u32[]{:S(2)}, u32[]{:S(2)}) async-start(bf16[8,4,128,128]{3,2,1,0:T(8,128)(2,1)} %plane_prefix.1.refs_6_), calls=%async_computation.1 | async-start | bytes 2097152 | tf_op jit(solution)/shard_map/state_scan/all_to_all | solution.py:513
  69.8 3.0 %collective-permute-start.6 = (bf16[2,256,512]{2,1,0:T(8,128)(2,1)S(1)}, bf16[2,256,512]{2,1,0:T(8,128)(2,1)S(1)}, u32[]{:S(2)}, u32[]{:S(2)}) collective-permute-start(bf16[2,256,512]{2,1,0:T(8,128)(2,1)S(1)} %hold.5), channel_id=1, source_target_pairs={{0,6},{1,7},{2,4},{3,5},{4,2},{5,3},{6,0},{7,1},{8,14},{9,15},{10,... | collective-permute-start | bytes 1572872 | tf_op jit(solution)/shard_map/residual_exchange/ppermute | solution.py:464
  73.1 1.4 copy.23
  75.2 10.3 %local_intra.1 = (bf16[256,4096]{1,0:T(8,128)(2,1)}, bf16[256,4096]{1,0:T(8,128)(2,1)}) custom-call(bf16[256,4096]{1,0:T(8,128)(2,1)} %refs_0_.5, bf16[256,4096]{1,0:T(8,128)(2,1)} %refs_1_.7, bf16[256,4096]{1,0:T(8,128)(2,1)} %refs_2_.5, bf16[256,4096]{1,0:T(8,128)(2,1)} %refs_3_.1, f32[8,256,4]{2,1,0:T(8,128)} %bitcast.21, ...), custom_call_target="tpu_custom_call" | custom-call | tf_op jit(solution)/shard_map/local_intra/pallas_call | solution.py:152
  85.5 1.0 copy-done.23
  86.6 7.4 %mix.1 = (bf16[128,4096]{1,0:T(8,128)(2,1)}, bf16[128,4096]{1,0:T(8,128)(2,1)}) custom-call(bf16[256,4096]{1,0:T(8,128)(2,1)} %refs_0_.5, bf16[256,4096]{1,0:T(8,128)(2,1)} %get-tuple-element.37.refs_1_, bf16[256,4096]{1,0:T(8,128)(2,1)} %get-tuple-element.38.refs_2_, f32[8,256,4]{2,1,0:T(8,128)} %bitcast.22, bf16[32,128,128]{2,1,0:T(8,128)(2,1)} %bitcast.23), custom_call_target="tpu_custom_call" | custom-call | tf_op jit(solution)/shard_map/mix/pallas_call | solution.py:152
  94.0 1.8 collective-permute-done.6.refs_2_.refs_5_.refs_6_
  97.3 23.5 %collective-permute-done.7.refs_0_ = bf16[128,4096]{1,0:T(8,128)(2,1)S(1)} collective-permute-done((bf16[128,4096]{1,0:T(8,128)(2,1)}, bf16[128,4096]{1,0:T(8,128)(2,1)S(1)}, u32[]{:S(2)}, u32[]{:S(2)}) %collective-permute-start.7) | collective-permute-done | bytes 1048608 | tf_op jit(solution)/shard_map/projections/ppermute | solution.py:464
  121.4 1.2 collective-permute-start.10
  122.6 1.0 copy-done.9
  124.0 1.0 copy-done.17
  125.0 1.0 copy-done.12
  126.0 1.0 copy-done.19
  127.0 18.0 %collective-permute-done.8.refs_2_.refs_0_ = bf16[128,4096]{1,0:T(8,128)(2,1)} collective-permute-done((bf16[128,4096]{1,0:T(8,128)(2,1)S(1)}, bf16[128,4096]{1,0:T(8,128)(2,1)}, u32[]{:S(2)}, u32[]{:S(2)}) %collective-permute-start.8) | collective-permute-done | bytes 1048608 | tf_op jit(solution)/shard_map/projections/ppermute | solution.py:464
  145.5 1.0 collective-permute-start.13
  146.5 0.9 collective-permute-start.14
  147.4 2.0 multiply_convert_fusion.1.refs_2_
  149.5 2.2 copy-done
  151.6 1.1 copy-done.5
  152.8 1.2 copy-done.10
  154.0 1.2 copy-done.13
  155.2 1.2 copy-done.18
  156.4 1.2 copy-done.20
  157.7 4.2 %out_projection.4 = (bf16[256,512]{1,0:T(8,128)(2,1)S(1)}, bf16[256,512]{1,0:T(8,128)(2,1)S(1)}) custom-call(bf16[128,4096]{1,0:T(8,128)(2,1)S(1)} %copy-done.18, bf16[128,4096]{1,0:T(8,128)(2,1)} %collective-permute-done.15.refs_1_, bf16[128,4096]{1,0:T(8,128)(2,1)S(1)} %copy-done.20, bf16[128,4096]{1,0:T(8,128)(2,1)} %collective-permute-done.16.refs_3_, ...), custom_call_target="tpu_custom_call" | custom-call | tf_op jit(solution)/shard_map/projections/out_projection/pallas_call | solution.py:177
  161.9 4.5 %out_projection.5 = (bf16[256,512]{1,0:T(8,128)(2,1)S(1)}, bf16[256,512]{1,0:T(8,128)(2,1)S(1)}) custom-call(bf16[128,4096]{1,0:T(8,128)(2,1)} %collective-permute-done.8.refs_2_.refs_0_, bf16[128,4096]{1,0:T(8,128)(2,1)} %collective-permute-done.19.refs_1_, bf16[128,4096]{1,0:T(8,128)(2,1)} %collective-permute-done.10.refs_3_.refs_2_, ...), custom_call_target="tpu_custom_call" | custom-call | tf_op jit(solution)/shard_map/projections/out_projection/pallas_call | solution.py:177
  167.0 2.0 multiply_convert_fusion.refs_3_
  169.0 1.3 cache_projection.4
  170.3 1.3 cache_projection.5
  172.6 0.9 collective-permute-start.25
  173.5 1.4 collective-permute-start.26
  175.6 1.1 collective-permute-start.28
  176.7 4.1 %out_projection.6 = (bf16[256,512]{1,0:T(8,128)(2,1)S(1)}, bf16[256,512]{1,0:T(8,128)(2,1)S(1)}) custom-call(bf16[128,4096]{1,0:T(8,128)(2,1)} %get-tuple-element.52.refs_0_, bf16[128,4096]{1,0:T(8,128)(2,1)S(1)} %collective-permute-done.22.refs_1_, bf16[128,4096]{1,0:T(8,128)(2,1)} %get-tuple-element.53.refs_2_, ...), custom_call_target="tpu_custom_call" | custom-call | tf_op jit(solution)/shard_map/projections/out_projection/pallas_call | solution.py:177
  180.8 7.3 %collective-permute-done.25.refs_4_ = bf16[128,2176]{1,0:T(8,128)(2,1)S(1)} collective-permute-done((bf16[128,2176]{1,0:T(8,128)(2,1)S(1)}, bf16[128,2176]{1,0:T(8,128)(2,1)S(1)}, u32[]{:S(2)}, u32[]{:S(2)}) %collective-permute-start.25) | collective-permute-done | bytes 557088 | tf_op jit(solution)/shard_map/projections/ppermute | solution.py:464
  188.1 1.0 collective-permute-done.26.refs_5_
  189.1 1.3 cache_projection.6
  190.4 1.2 collective-permute-start.30
  191.5 1.0 collective-permute-start.31
  192.5 8.5 %collective-permute-done.27.refs_8_.refs_4_ = bf16[128,2176]{1,0:T(8,128)(2,1)S(1)} collective-permute-done((bf16[128,2176]{1,0:T(8,128)(2,1)S(1)}, bf16[128,2176]{1,0:T(8,128)(2,1)S(1)}, u32[]{:S(2)}, u32[]{:S(2)}) %collective-permute-start.27) | collective-permute-done | bytes 557088 | tf_op jit(solution)/shard_map/projections/ppermute | solution.py:464
  201.0 3.9 %out_projection.7 = (bf16[256,512]{1,0:T(8,128)(2,1)S(1)}, bf16[256,512]{1,0:T(8,128)(2,1)S(1)}) custom-call(bf16[128,4096]{1,0:T(8,128)(2,1)} %get-tuple-element.44.refs_0_, bf16[128,4096]{1,0:T(8,128)(2,1)S(1)} %copy-done.11, bf16[128,4096]{1,0:T(8,128)(2,1)} %get-tuple-element.45.refs_2_, bf16[128,4096]{1,0:T(8,128)(2,1)S(1)} %copy-done.14, ...), custom_call_target="tpu_custom_call" | custom-call | tf_op jit(solution)/shard_map/projections/out_projection/pallas_call | solution.py:177
  205.0 1.5 collective-permute-done.29.refs_1_
  206.5 1.3 cache_projection.7
  207.8 3.2 %collective-permute-done.30.refs_2_ = bf16[128,2176]{1,0:T(8,128)(2,1)S(1)} collective-permute-done((bf16[128,2176]{1,0:T(8,128)(2,1)S(1)}, bf16[128,2176]{1,0:T(8,128)(2,1)S(1)}, u32[]{:S(2)}, u32[]{:S(2)}) %collective-permute-start.30) | collective-permute-done | bytes 557088 | tf_op jit(solution)/shard_map/projections/ppermute | solution.py:464
  211.7 1.4 finish.1
  (99 shorter events, 8.8 us)
Async XLA Ops:
  7.2 56.0 %all-gather.3.cloned.1.call-start = ((), (), s32[]{:S(2)}) async-start(), calls=%async_computation.2 | async-start | bytes 2621440 | tf_op jit(solution)/shard_map/kv_weight_gather/all_gather | solution.py:486
  7.9 7.0 %copy-start.2 = (bf16[256,4096]{1,0:T(8,128)(2,1)S(1)}, bf16[256,4096]{1,0:T(8,128)(2,1)}, u32[]{:S(2)}) copy-start(bf16[256,4096]{1,0:T(8,128)(2,1)} %refs_1_.6) | copy-start | bytes 6291460
  7.9 7.0 %copy-start.7 = (bf16[128,4096]{1,0:T(8,128)(2,1)S(1)}, bf16[128,4096]{1,0:T(8,128)(2,1)}, u32[]{:S(2)}) copy-start(bf16[128,4096]{1,0:T(8,128)(2,1)} %refs_2_.4) | copy-start | bytes 3145732
  16.5 3.8 %collective-permute-start = (bf16[4,384,512]{2,1,0:T(8,128)(2,1)}, bf16[4,384,512]{2,1,0:T(8,128)(2,1)S(1)}, u32[]{:S(2)}, u32[]{:S(2)}) collective-permute-start(bf16[4,384,512]{2,1,0:T(8,128)(2,1)} %deal.1), channel_id=1, source_target_pairs={{0,1},{1,0},{2,3},{3,2},{4,5},{5,4},{6,7},{7,6},{8,9},{9,8},{10,11... | collective-permute-start | bytes 4718600 | tf_op jit(solution)/shard_map/start_exchange/ppermute | solution.py:464
  16.5 21.2 %all-to-all-start = ((bf16[8,576,128]{2,1,0:T(8,128)(2,1)}), bf16[8,576,128]{2,1,0:T(8,128)(2,1)S(1)}, u32[]{:S(2)}, u32[]{:S(2)}) async-start(bf16[8,576,128]{2,1,0:T(8,128)(2,1)} %local_states.1.refs_3_), calls=%async_computation | async-start | bytes 2359296 | tf_op jit(solution)/shard_map/state_scan/all_to_all | solution.py:493
  20.4 1.2 copy-start.15
  21.6 1.6 copy-start.3
  23.2 1.2 copy-start.8
  24.4 1.4 copy-start.16
  27.3 0.8 copy-start.21
  28.1 31.6 %collective-permute-start.3 = (bf16[2,384,512]{2,1,0:T(8,128)(2,1)}, bf16[2,384,512]{2,1,0:T(8,128)(2,1)S(1)}, u32[]{:S(2)}, u32[]{:S(2)}) collective-permute-start(bf16[2,384,512]{2,1,0:T(8,128)(2,1)} %get-tuple-element.34), channel_id=1, source_target_pairs={{0,2},{1,3},{2,0},{3,1},{4,6},{5,7},{6,4},{7,5},{8,10},{9,11},{10,... | collective-permute-start | bytes 2359304 | tf_op jit(solution)/shard_map/start_exchange/ppermute | solution.py:464
  30.1 29.6 %collective-permute-start.4 = (bf16[2,384,512]{2,1,0:T(8,128)(2,1)}, bf16[2,384,512]{2,1,0:T(8,128)(2,1)}, u32[]{:S(2)}, u32[]{:S(2)}) collective-permute-start(bf16[2,384,512]{2,1,0:T(8,128)(2,1)} %get-tuple-element.35), channel_id=1, source_target_pairs={{0,4},{1,5},{2,6},{3,7},{4,0},{5,1},{6,2},{7,3},{8,12},{9,13},{10,... | collective-permute-start | bytes 2359304 | tf_op jit(solution)/shard_map/start_exchange/ppermute | solution.py:464
  38.0 14.0 %collective-permute-start.1 = (bf16[4,144,128]{2,1,0:T(8,128)(2,1)S(1)}, bf16[4,144,128]{2,1,0:T(8,128)(2,1)S(1)}, u32[]{:S(2)}, u32[]{:S(2)}) collective-permute-start(bf16[4,144,128]{2,1,0:T(8,128)(2,1)S(1)} %plane_total.1.refs_1_.refs_5_), channel_id=1, source_target_pairs={{0,8},{1,9},{2,10},{3,11},{4,12},{5,13},{6,14},{7,15},{8,16},{9,17... | collective-permute-start | bytes 442376 | tf_op jit(solution)/shard_map/state_scan/ppermute | solution.py:471
  39.3 20.4 %collective-permute-start.5 = (bf16[2,128,512]{2,1,0:T(8,128)(2,1)}, bf16[2,128,512]{2,1,0:T(8,128)(2,1)S(1)}, u32[]{:S(2)}, u32[]{:S(2)}) collective-permute-start(bf16[2,128,512]{2,1,0:T(8,128)(2,1)} %get-tuple-element.36), channel_id=1, source_target_pairs={{0,6},{1,7},{2,4},{3,5},{4,2},{5,3},{6,0},{7,1},{8,14},{9,15},{10,... | collective-permute-start | bytes 786440 | tf_op jit(solution)/shard_map/start_exchange/ppermute | solution.py:464
  52.1 11.1 %collective-permute-start.2 = (bf16[4,144,128]{2,1,0:T(8,128)(2,1)S(1)}, bf16[4,144,128]{2,1,0:T(8,128)(2,1)S(1)}, u32[]{:S(2)}, u32[]{:S(2)}) collective-permute-start(bf16[4,144,128]{2,1,0:T(8,128)(2,1)S(1)} %join.1.refs_1_), channel_id=1, source_target_pairs={{0,16},{1,17},{2,18},{3,19},{4,20},{5,21},{6,22},{7,23},{8,24},{9,... | collective-permute-start | bytes 442376 | tf_op jit(solution)/shard_map/state_scan/ppermute | solution.py:471
  59.7 4.9 %copy-start.4 = (bf16[2,384,512]{2,1,0:T(8,128)(2,1)}, bf16[2,384,512]{2,1,0:T(8,128)(2,1)S(1)}, u32[]{:S(2)}) copy-start(bf16[2,384,512]{2,1,0:T(8,128)(2,1)S(1)} %collective-permute-done.3.refs_2_.refs_5_) | copy-start | bytes 2359300
  64.6 84.8 %all-gather.5.cloned.1.call-start = ((), (), s32[]{:S(2)}) async-start(), calls=%async_computation.3 | async-start | bytes 5242880 | tf_op jit(solution)/shard_map/out_weight_gather/all_gather | solution.py:508
  64.6 4.5 %copy-start.24 = (f32[256,32]{0,1:T(8,128)S(1)}, f32[256,32]{0,1:T(8,128)}, u32[]{:S(2)}) copy-start(f32[256,32]{0,1:T(8,128)} %param.14) | copy-start | bytes 98308
  64.6 5.2 %copy-start.22 = (bf16[2,256,512]{2,1,0:T(8,128)(2,1)S(1)}, bf16[2,256,512]{2,1,0:T(8,128)(2,1)}, u32[]{:S(2)}) copy-start(bf16[2,256,512]{2,1,0:T(8,128)(2,1)} %copy-done.21) | copy-start | bytes 1572868
  65.3 20.2 %all-to-all-start.1 = ((bf16[8,4,128,128]{3,2,1,0:T(8,128)(2,1)}), bf16[8,4,128,128]{3,2,1,0:T(8,128)(2,1)S(1)}, u32[]{:S(2)}, u32[]{:S(2)}) async-start(bf16[8,4,128,128]{3,2,1,0:T(8,128)(2,1)} %plane_prefix.1.refs_6_), calls=%async_computation.1 | async-start | bytes 2097152 | tf_op jit(solution)/shard_map/state_scan/all_to_all | solution.py:513
  69.8 26.0 %collective-permute-start.6 = (bf16[2,256,512]{2,1,0:T(8,128)(2,1)S(1)}, bf16[2,256,512]{2,1,0:T(8,128)(2,1)S(1)}, u32[]{:S(2)}, u32[]{:S(2)}) collective-permute-start(bf16[2,256,512]{2,1,0:T(8,128)(2,1)S(1)} %hold.5), channel_id=1, source_target_pairs={{0,6},{1,7},{2,4},{3,5},{4,2},{5,3},{6,0},{7,1},{8,14},{9,15},{10,... | collective-permute-start | bytes 1572872 | tf_op jit(solution)/shard_map/residual_exchange/ppermute | solution.py:464
  85.5 1.1 copy-start.23
  94.0 51.5 %copy-start.25 = (bf16[4096]{0:T(1024)(128)(2,1)S(1)}, bf16[4096]{0:T(1024)(128)(2,1)}, u32[]{:S(2)}) copy-start(bf16[4096]{0:T(1024)(128)(2,1)} %param.16) | copy-start | bytes 24580
  95.8 25.0 %collective-permute-start.7 = (bf16[128,4096]{1,0:T(8,128)(2,1)}, bf16[128,4096]{1,0:T(8,128)(2,1)S(1)}, u32[]{:S(2)}, u32[]{:S(2)}) collective-permute-start(bf16[128,4096]{1,0:T(8,128)(2,1)} %get-tuple-element.42.refs_0_), channel_id=1, source_target_pairs={{0,2},{1,3},{2,0},{3,1},{4,6},{5,7},{6,4},{7,5},{8,10},{9,11},{10,... | collective-permute-start | bytes 3145736 | tf_op jit(solution)/shard_map/projections/ppermute | solution.py:464
  96.4 25.0 %collective-permute-start.9 = (bf16[128,4096]{1,0:T(8,128)(2,1)}, bf16[128,4096]{1,0:T(8,128)(2,1)S(1)}, u32[]{:S(2)}, u32[]{:S(2)}) collective-permute-start(bf16[128,4096]{1,0:T(8,128)(2,1)} %get-tuple-element.43.refs_1_), channel_id=1, source_target_pairs={{0,4},{1,5},{2,6},{3,7},{4,0},{5,1},{6,2},{7,3},{8,12},{9,13},{10,... | collective-permute-start | bytes 3145736 | tf_op jit(solution)/shard_map/projections/ppermute | solution.py:464
  96.8 25.8 %collective-permute-start.11 = (bf16[128,4096]{1,0:T(8,128)(2,1)}, bf16[128,4096]{1,0:T(8,128)(2,1)S(1)}, u32[]{:S(2)}, u32[]{:S(2)}) collective-permute-start(bf16[128,4096]{1,0:T(8,128)(2,1)} %get-tuple-element.42.refs_0_), channel_id=1, source_target_pairs={{0,1},{1,0},{2,3},{3,2},{4,5},{5,4},{6,7},{7,6},{8,9},{9,8},{10,11... | collective-permute-start | bytes 3145736 | tf_op jit(solution)/shard_map/projections/ppermute | solution.py:464
  96.8 28.3 %collective-permute-start.12 = (bf16[128,4096]{1,0:T(8,128)(2,1)}, bf16[128,4096]{1,0:T(8,128)(2,1)S(1)}, u32[]{:S(2)}, u32[]{:S(2)}) collective-permute-start(bf16[128,4096]{1,0:T(8,128)(2,1)} %get-tuple-element.43.refs_1_), channel_id=1, source_target_pairs={{0,1},{1,0},{2,3},{3,2},{4,5},{5,4},{6,7},{7,6},{8,9},{9,8},{10,11... | collective-permute-start | bytes 3145736 | tf_op jit(solution)/shard_map/projections/ppermute | solution.py:464
  120.8 24.1 %collective-permute-start.8 = (bf16[128,4096]{1,0:T(8,128)(2,1)S(1)}, bf16[128,4096]{1,0:T(8,128)(2,1)}, u32[]{:S(2)}, u32[]{:S(2)}) collective-permute-start(bf16[128,4096]{1,0:T(8,128)(2,1)S(1)} %collective-permute-done.7.refs_0_), channel_id=1, source_target_pairs={{0,4},{1,5},{2,6},{3,7},{4,0},{5,1},{6,2},{7,3},{8,12},{9,13},{10,... | collective-permute-start | bytes 3145736 | tf_op jit(solution)/shard_map/projections/ppermute | solution.py:464
  121.4 23.9 %collective-permute-start.10 = (bf16[128,4096]{1,0:T(8,128)(2,1)S(1)}, bf16[128,4096]{1,0:T(8,128)(2,1)}, u32[]{:S(2)}, u32[]{:S(2)}) collective-permute-start(bf16[128,4096]{1,0:T(8,128)(2,1)S(1)} %collective-permute-done.9.refs_2_), channel_id=1, source_target_pairs={{0,2},{1,3},{2,0},{3,1},{4,6},{5,7},{6,4},{7,5},{8,10},{9,11},{10,... | collective-permute-start | bytes 3145736 | tf_op jit(solution)/shard_map/projections/ppermute | solution.py:464
  122.6 44.5 %collective-permute-start.18 = (bf16[512,2048]{1,0:T(8,128)(2,1)}, bf16[512,2048]{1,0:T(8,128)(2,1)}, u32[]{:S(2)}, u32[]{:S(2)}) collective-permute-start(bf16[512,2048]{1,0:T(8,128)(2,1)} %all-gather.3.cloned.1.call-done.refs_3_.refs_1_), channel_id=1, source_target_pairs={{0,1},{1,0},{2,3},{3,2},{4,5},{5,4},{6,7},{7,6},{8,9},{9,8},{10,11... | collective-permute-start | bytes 6291464 | tf_op jit(solution)/shard_map/cache_weight/ppermute | solution.py:464
  122.6 1.0 copy-start.9
  123.5 22.0 %collective-permute-start.15 = (bf16[128,4096]{1,0:T(8,128)(2,1)S(1)}, bf16[128,4096]{1,0:T(8,128)(2,1)}, u32[]{:S(2)}, u32[]{:S(2)}) collective-permute-start(bf16[128,4096]{1,0:T(8,128)(2,1)S(1)} %collective-permute-done.7.refs_0_), channel_id=1, source_target_pairs={{0,1},{1,0},{2,3},{3,2},{4,5},{5,4},{6,7},{7,6},{8,9},{9,8},{10,11... | collective-permute-start | bytes 3145736 | tf_op jit(solution)/shard_map/projections/ppermute | solution.py:464
  124.0 1.0 copy-start.17
  125.0 1.0 copy-start.12
  126.0 20.5 %collective-permute-start.16 = (bf16[128,4096]{1,0:T(8,128)(2,1)S(1)}, bf16[128,4096]{1,0:T(8,128)(2,1)}, u32[]{:S(2)}, u32[]{:S(2)}) collective-permute-start(bf16[128,4096]{1,0:T(8,128)(2,1)S(1)} %collective-permute-done.9.refs_2_), channel_id=1, source_target_pairs={{0,1},{1,0},{2,3},{3,2},{4,5},{5,4},{6,7},{7,6},{8,9},{9,8},{10,11... | collective-permute-start | bytes 3145736 | tf_op jit(solution)/shard_map/projections/ppermute | solution.py:464
  126.0 1.0 copy-start.19
  145.0 17.0 %collective-permute-start.19 = (bf16[128,4096]{1,0:T(8,128)(2,1)}, bf16[128,4096]{1,0:T(8,128)(2,1)}, u32[]{:S(2)}, u32[]{:S(2)}) collective-permute-start(bf16[128,4096]{1,0:T(8,128)(2,1)} %collective-permute-done.8.refs_2_.refs_0_), channel_id=1, source_target_pairs={{0,1},{1,0},{2,3},{3,2},{4,5},{5,4},{6,7},{7,6},{8,9},{9,8},{10,11... | collective-permute-start | bytes 3145736 | tf_op jit(solution)/shard_map/projections/ppermute | solution.py:464
  145.2 16.7 %collective-permute-start.20 = (bf16[128,4096]{1,0:T(8,128)(2,1)}, bf16[128,4096]{1,0:T(8,128)(2,1)}, u32[]{:S(2)}, u32[]{:S(2)}) collective-permute-start(bf16[128,4096]{1,0:T(8,128)(2,1)} %collective-permute-done.10.refs_3_.refs_2_), channel_id=1, source_target_pairs={{0,1},{1,0},{2,3},{3,2},{4,5},{5,4},{6,7},{7,6},{8,9},{9,8},{10,11... | collective-permute-start | bytes 3145736 | tf_op jit(solution)/shard_map/projections/ppermute | solution.py:464
  145.5 26.1 %collective-permute-start.13 = (bf16[128,4096]{1,0:T(8,128)(2,1)}, bf16[128,4096]{1,0:T(8,128)(2,1)}, u32[]{:S(2)}, u32[]{:S(2)}) collective-permute-start(bf16[128,4096]{1,0:T(8,128)(2,1)} %get-tuple-element.45.refs_2_), channel_id=1, source_target_pairs={{0,2},{1,3},{2,0},{3,1},{4,6},{5,7},{6,4},{7,5},{8,10},{9,11},{10,... | collective-permute-start | bytes 3145736 | tf_op jit(solution)/shard_map/projections/ppermute | solution.py:464
  146.5 25.6 %collective-permute-start.14 = (bf16[128,4096]{1,0:T(8,128)(2,1)}, bf16[128,4096]{1,0:T(8,128)(2,1)}, u32[]{:S(2)}, u32[]{:S(2)}) collective-permute-start(bf16[128,4096]{1,0:T(8,128)(2,1)} %get-tuple-element.44.refs_0_), channel_id=1, source_target_pairs={{0,4},{1,5},{2,6},{3,7},{4,0},{5,1},{6,2},{7,3},{8,12},{9,13},{10,... | collective-permute-start | bytes 3145736 | tf_op jit(solution)/shard_map/projections/ppermute | solution.py:464
  149.4 2.2 copy-start
  151.6 1.1 copy-start.5
  152.8 1.2 copy-start.10
  154.0 1.2 copy-start.13
  155.2 1.2 copy-start.18
  156.4 1.2 copy-start.20
  157.7 4.3 %copy-start.1 = (bf16[4096,512]{1,0:T(8,128)(2,1)S(1)}, bf16[4096,512]{1,0:T(8,128)(2,1)}, u32[]{:S(2)}) copy-start(bf16[4096,512]{1,0:T(8,128)(2,1)} %all-gather.5.cloned.1.call-done.refs_4_) | copy-start | bytes 12582916
  166.5 2.6 %collective-permute-start.21 = (bf16[256,512]{1,0:T(8,128)(2,1)S(1)}, bf16[256,512]{1,0:T(8,128)(2,1)S(1)}, u32[]{:S(2)}, u32[]{:S(2)}) collective-permute-start(bf16[256,512]{1,0:T(8,128)(2,1)S(1)} %get-tuple-element.49), channel_id=1, source_target_pairs={{0,1},{1,0},{2,3},{3,2},{4,5},{5,4},{6,7},{7,6},{8,9},{9,8},{10,11... | collective-permute-start | bytes 786440 | tf_op jit(solution)/shard_map/projections/ppermute | solution.py:464
  166.5 3.8 %collective-permute-start.17 = (bf16[256,512]{1,0:T(8,128)(2,1)S(1)}, bf16[256,512]{1,0:T(8,128)(2,1)S(1)}, u32[]{:S(2)}, u32[]{:S(2)}) collective-permute-start(bf16[256,512]{1,0:T(8,128)(2,1)S(1)} %get-tuple-element.47), channel_id=1, source_target_pairs={{0,1},{1,0},{2,3},{3,2},{4,5},{5,4},{6,7},{7,6},{8,9},{9,8},{10,11... | collective-permute-start | bytes 786440 | tf_op jit(solution)/shard_map/projections/ppermute | solution.py:464
  171.6 5.1 %copy-start.6 = (bf16[2,384,512]{2,1,0:T(8,128)(2,1)S(1)}, bf16[2,384,512]{2,1,0:T(8,128)(2,1)}, u32[]{:S(2)}) copy-start(bf16[2,384,512]{2,1,0:T(8,128)(2,1)} %copy-done.4) | copy-start | bytes 2359300
  172.1 3.5 %collective-permute-start.22 = (bf16[128,4096]{1,0:T(8,128)(2,1)}, bf16[128,4096]{1,0:T(8,128)(2,1)S(1)}, u32[]{:S(2)}, u32[]{:S(2)}) collective-permute-start(bf16[128,4096]{1,0:T(8,128)(2,1)} %get-tuple-element.52.refs_0_), channel_id=1, source_target_pairs={{0,1},{1,0},{2,3},{3,2},{4,5},{5,4},{6,7},{7,6},{8,9},{9,8},{10,11... | collective-permute-start | bytes 3145736 | tf_op jit(solution)/shard_map/projections/ppermute | solution.py:464
  172.1 4.6 %collective-permute-start.23 = (bf16[128,4096]{1,0:T(8,128)(2,1)}, bf16[128,4096]{1,0:T(8,128)(2,1)S(1)}, u32[]{:S(2)}, u32[]{:S(2)}) collective-permute-start(bf16[128,4096]{1,0:T(8,128)(2,1)} %get-tuple-element.53.refs_2_), channel_id=1, source_target_pairs={{0,1},{1,0},{2,3},{3,2},{4,5},{5,4},{6,7},{7,6},{8,9},{9,8},{10,11... | collective-permute-start | bytes 3145736 | tf_op jit(solution)/shard_map/projections/ppermute | solution.py:464
  172.6 15.5 %collective-permute-start.25 = (bf16[128,2176]{1,0:T(8,128)(2,1)S(1)}, bf16[128,2176]{1,0:T(8,128)(2,1)S(1)}, u32[]{:S(2)}, u32[]{:S(2)}) collective-permute-start(bf16[128,2176]{1,0:T(8,128)(2,1)S(1)} %get-tuple-element.56), channel_id=1, source_target_pairs={{0,4},{1,5},{2,6},{3,7},{4,0},{5,1},{6,2},{7,3},{8,12},{9,13},{10,... | collective-permute-start | bytes 1671176 | tf_op jit(solution)/shard_map/projections/ppermute | solution.py:464
  173.5 15.5 %collective-permute-start.26 = (bf16[128,2176]{1,0:T(8,128)(2,1)S(1)}, bf16[128,2176]{1,0:T(8,128)(2,1)S(1)}, u32[]{:S(2)}, u32[]{:S(2)}) collective-permute-start(bf16[128,2176]{1,0:T(8,128)(2,1)S(1)} %get-tuple-element.50.refs_4_), channel_id=1, source_target_pairs={{0,2},{1,3},{2,0},{3,1},{4,6},{5,7},{6,4},{7,5},{8,10},{9,11},{10,... | collective-permute-start | bytes 1671176 | tf_op jit(solution)/shard_map/projections/ppermute | solution.py:464
  175.0 26.0 %collective-permute-start.27 = (bf16[128,2176]{1,0:T(8,128)(2,1)S(1)}, bf16[128,2176]{1,0:T(8,128)(2,1)S(1)}, u32[]{:S(2)}, u32[]{:S(2)}) collective-permute-start(bf16[128,2176]{1,0:T(8,128)(2,1)S(1)} %get-tuple-element.51.refs_2_), channel_id=1, source_target_pairs={{0,2},{1,3},{2,0},{3,1},{4,6},{5,7},{6,4},{7,5},{8,10},{9,11},{10,... | collective-permute-start | bytes 1671176 | tf_op jit(solution)/shard_map/projections/ppermute | solution.py:464
  175.6 25.4 %collective-permute-start.28 = (bf16[128,2176]{1,0:T(8,128)(2,1)S(1)}, bf16[128,2176]{1,0:T(8,128)(2,1)S(1)}, u32[]{:S(2)}, u32[]{:S(2)}) collective-permute-start(bf16[128,2176]{1,0:T(8,128)(2,1)S(1)} %get-tuple-element.58), channel_id=1, source_target_pairs={{0,4},{1,5},{2,6},{3,7},{4,0},{5,1},{6,2},{7,3},{8,12},{9,13},{10,... | collective-permute-start | bytes 1671176 | tf_op jit(solution)/shard_map/projections/ppermute | solution.py:464
  180.8 8.3 %collective-permute-start.24 = (bf16[256,512]{1,0:T(8,128)(2,1)S(1)}, bf16[256,512]{1,0:T(8,128)(2,1)S(1)}, u32[]{:S(2)}, u32[]{:S(2)}) collective-permute-start(bf16[256,512]{1,0:T(8,128)(2,1)S(1)} %get-tuple-element.55), channel_id=1, source_target_pairs={{0,1},{1,0},{2,3},{3,2},{4,5},{5,4},{6,7},{7,6},{8,9},{9,8},{10,11... | collective-permute-start | bytes 786440 | tf_op jit(solution)/shard_map/projections/ppermute | solution.py:464
  189.1 11.9 %copy-start.11 = (bf16[128,4096]{1,0:T(8,128)(2,1)S(1)}, bf16[128,4096]{1,0:T(8,128)(2,1)}, u32[]{:S(2)}) copy-start(bf16[128,4096]{1,0:T(8,128)(2,1)} %copy-done.9) | copy-start | bytes 3145732
  189.1 11.9 %copy-start.14 = (bf16[128,4096]{1,0:T(8,128)(2,1)S(1)}, bf16[128,4096]{1,0:T(8,128)(2,1)}, u32[]{:S(2)}) copy-start(bf16[128,4096]{1,0:T(8,128)(2,1)} %copy-done.12) | copy-start | bytes 3145732
  190.4 20.7 %collective-permute-start.30 = (bf16[128,2176]{1,0:T(8,128)(2,1)S(1)}, bf16[128,2176]{1,0:T(8,128)(2,1)S(1)}, u32[]{:S(2)}, u32[]{:S(2)}) collective-permute-start(bf16[128,2176]{1,0:T(8,128)(2,1)S(1)} %get-tuple-element.63), channel_id=1, source_target_pairs={{0,4},{1,5},{2,6},{3,7},{4,0},{5,1},{6,2},{7,3},{8,12},{9,13},{10,... | collective-permute-start | bytes 1671176 | tf_op jit(solution)/shard_map/projections/ppermute | solution.py:464
  191.5 20.1 %collective-permute-start.31 = (bf16[128,2176]{1,0:T(8,128)(2,1)S(1)}, bf16[128,2176]{1,0:T(8,128)(2,1)S(1)}, u32[]{:S(2)}, u32[]{:S(2)}) collective-permute-start(bf16[128,2176]{1,0:T(8,128)(2,1)S(1)} %get-tuple-element.57.refs_7_), channel_id=1, source_target_pairs={{0,2},{1,3},{2,0},{3,1},{4,6},{5,7},{6,4},{7,5},{8,10},{9,11},{10,... | collective-permute-start | bytes 1671176 | tf_op jit(solution)/shard_map/projections/ppermute | solution.py:464
  204.9 1.6 collective-permute-start.29
Sparse Core Ops, SparseCore 0:
  9.6 52.0 all-gather.2
  67.0 79.0 all-gather.4
